TPU v7x, 512 devices: a whole 4x8x8 slice. The times are simulated.
512 devices in a mesh: role: 2 (over core), grp: 64 (over y, z), tp: 4 (over x).
Axes of the slice: x: 4, y: 8, z: 8, core: 2. Of those that a mesh axis runs over, the one named last changes fastest.
Arguments:
- q_latent: bfloat16 [256, 128, 576], P(('role', 'grp')), may hold values from -6 to 6
- key_value_cache: bfloat16 [256, 1024, 576], P(('role', 'grp'), 'tp'), may hold values from -6 to 6
- cache_lengths: int32 [256], P(('role', 'grp')), may hold values from 2 to 1024, as said below
- hidden: bfloat16 [8192, 7168], P('grp', ('role', 'tp')), may hold values from -6 to 6
- expert_ids: int32 [8192, 8], P('grp'), may hold values from 0 to 63, all different within a row; in each aligned block of 128 rows (0 to 127, 128 to 255, ...) at most 24 rows name the same one
- route_logits: float32 [8192, 8], P('grp'), may hold values from -6 to 6
- up_weight: bfloat16 [64, 7168, 1024], P('grp', ('role', 'tp')), may hold values from -0.0625 to 0.0625
- down_weight: bfloat16 [64, 1024, 7168], P('grp', None, ('role', 'tp')), may hold values from -0.1875 to 0.1875
Outputs:
- attn_context: bfloat16 [256, 128, 512], P(('role', 'grp'), 'tp')
- moe_output: bfloat16 [8192, 7168], P('grp', ('role', 'tp'))
Inputs may be any that keep to these rules, and one draw needn't show every extreme that they name: `cache_lengths`: each request has 2 to 1024 cached positions; some request has exactly 1024. `expert_ids`: each row names 8 different experts; among the rows of one batch shard no expert is named more than 24 times, a bound that some block reaches.
All inputs are finite; a program needn't handle non-finite values.
Results may differ from a plain program's by a relative error of at most 0.025.
Values may be sent and summed in bfloat16 or wider, within the bound.
No kernel may reach another device: no remote copies, remote signals or barrier semaphores. Data moves between devices by JAX's collectives and lax.ppermute only.
A program may use at most 64 MiB of HBM per device.

v0:
```python
import jax
import jax.numpy as jnp
from jax import lax
from jax.sharding import PartitionSpec as P

KEY_VALUE_LATENT = 512
ROPE = 64
QK_NOPE = 128
EXPERTS = 64
CAP = 24


NEGATIVE = -1e30


def combined_all(value, axis, combine):
    everything = jax.tree.map(
        lambda part, kind: lax.all_gather(part.astype(kind), axis),
        value,
        (jnp.bfloat16, jnp.bfloat16, jnp.bfloat16),
    )

    def take(k):
        return jax.tree.map(lambda part, own: part[k].astype(own.dtype), everything, value)

    return lax.fori_loop(
        1, lax.axis_size(axis), lambda k, so_far: combine(so_far, take(k)), take(0)
    )


def block_ranks(id_rows, experts):
    flat_ids = id_rows.reshape(-1)
    onehot = (flat_ids[:, None] == jnp.arange(experts, dtype=jnp.int32)[None, :]).astype(jnp.int32)
    before = jnp.cumsum(onehot, axis=0) - onehot
    return jnp.sum(before * onehot, axis=1).reshape(id_rows.shape)


def join_parts(part_one, part_two):
    peak_one, total_one, sum_one = part_one
    peak_two, second_total, sum_two = part_two
    peak_both = jnp.maximum(peak_one, peak_two)
    factor_one = jnp.exp(peak_one - peak_both)
    factor_two = jnp.exp(peak_two - peak_both)
    total_both = total_one * factor_one + second_total * factor_two
    sum_both = sum_one * factor_one[..., None] + sum_two * factor_two[..., None]
    return (peak_both, total_both, sum_both)


def shards(
    q_latent,
    key_value_cache,
    cache_lengths,
    hidden,
    expert_ids,
    route_logits,
    up_weight,
    down_weight,
):
    score_scale = 1.0 / (QK_NOPE + ROPE) ** 0.5
    local_len = key_value_cache.shape[1]
    offset = lax.axis_index("tp") * local_len
    positions = offset + jnp.arange(local_len, dtype=jnp.int32)
    is_valid = positions[None, None, :] < cache_lengths[:, None, None]
    scores = (
        jnp.einsum("rhc,rlc->rhl", q_latent, key_value_cache, preferred_element_type=jnp.float32)
        * score_scale
    )
    scores = jnp.where(is_valid, scores, NEGATIVE)
    row_peak = jnp.max(scores, axis=-1)
    exp_terms = jnp.where(is_valid, jnp.exp(scores - row_peak[..., None]), 0.0)
    row_total = jnp.sum(exp_terms, axis=-1)
    context_total = jnp.einsum(
        "wzj,wjp->wzp",
        exp_terms.astype(jnp.bfloat16),
        key_value_cache[:, :, :KEY_VALUE_LATENT],
        preferred_element_type=jnp.float32,
    )
    head_group = q_latent.shape[1] // lax.axis_size("tp")
    peak_all, total_all, sum_all = combined_all(
        (row_peak, row_total, context_total), "tp", join_parts
    )
    first_head_index = lax.axis_index("tp") * head_group
    sum_mine = lax.dynamic_slice_in_dim(sum_all, first_head_index, head_group, 1)
    total_mine = lax.dynamic_slice_in_dim(total_all, first_head_index, head_group, 1)
    attn_context = (sum_mine / total_mine[..., None]).astype(jnp.bfloat16)
    experts_here = up_weight.shape[0]
    owners = lax.axis_size("grp")
    slot_rank = block_ranks(expert_ids, EXPERTS)
    owner_of = expert_ids // experts_here
    local_index = expert_ids % experts_here
    slot_index = (owner_of * CAP + slot_rank) * experts_here + local_index
    total_slots = owners * CAP * experts_here
    slot_numbers = jnp.arange(total_slots, dtype=jnp.int32)
    placed = slot_index[None, :, :] == slot_numbers[:, None, None]
    dispatch_rows = jnp.any(placed, axis=2).astype(jnp.bfloat16)
    outgoing = jnp.dot(dispatch_rows, hidden, preferred_element_type=jnp.float32).astype(
        jnp.bfloat16
    )
    outgoing = outgoing.reshape(owners, CAP, experts_here, hidden.shape[1])
    incoming = lax.all_to_all(outgoing, "grp", split_axis=0, concat_axis=0, tiled=True)
    arrived = incoming.reshape(owners * CAP, experts_here, hidden.shape[1])
    partial_value = jnp.einsum(
        "sed,edf->sef", arrived, up_weight, preferred_element_type=jnp.float32
    )
    summed = lax.psum(partial_value.astype(jnp.bfloat16), ("role", "tp")).astype(jnp.float32)
    activated = jax.nn.silu(summed).astype(jnp.bfloat16)
    produced = jnp.einsum(
        "sef,efd->sed", activated, down_weight, preferred_element_type=jnp.float32
    )
    sending = produced.astype(jnp.bfloat16).reshape(owners, CAP, experts_here, hidden.shape[1])
    returned = lax.all_to_all(sending, "grp", split_axis=0, concat_axis=0, tiled=True)
    flat_back = returned.reshape(total_slots, hidden.shape[1])
    sigmoid_terms = jax.nn.sigmoid(route_logits)
    route_weights = 2.5 * sigmoid_terms / jnp.sum(sigmoid_terms, axis=-1, keepdims=True)
    picked = jnp.take(flat_back, slot_index, axis=0)
    moe_output = jnp.sum(route_weights[:, :, None] * picked.astype(jnp.float32), axis=1).astype(
        jnp.bfloat16
    )
    return (attn_context, moe_output)


def solution(mesh):
    return jax.shard_map(
        shards,
        mesh=mesh,
        in_specs=(
            P(("role", "grp"), None, None),
            P(("role", "grp"), "tp", None),
            P(("role", "grp")),
            P("grp", ("role", "tp")),
            P("grp", None),
            P("grp", None),
            P("grp", ("role", "tp"), None),
            P("grp", None, ("role", "tp")),
        ),
        out_specs=(P(("role", "grp"), "tp", None), P("grp", ("role", "tp"))),
        check_vma=False,
    )
```

profile of v0, /device:TPU:45, one launch (start us, length us, event | category | flops | bytes accessed | tf_op | source)
XLA Modules:
  0.0 329.7 jit_solution(17629614727698891177)
XLA Ops:
  8.0 0.0 copy-start
  8.0 0.0 copy-start.4
  8.0 0.0 copy-start.3
  8.0 0.0 all-reduce.2.cloned.1.call-start
  8.1 0.9 copy.45
  9.0 0.1 eq.44
  9.1 0.1 eq.40
  9.2 18.0 %reduce-window.6 = s32[64,8,128]{2,1,0:T(8,128)S(1)} reduce-window(s32[64,8,128]{2,1,0:T(8,128)S(1)} %fusion.21, s32[]{:T(128)} %constant.90.clone.1), window={size=1x1x128 pad=0_0x0_0x127_0}, to_apply=%region_5.6 | reduce-window | flops 8323072 | bytes 524292 | tf_op jit(solution)/shard_map/reduce-window
  27.2 0.1 slice.34
  27.4 0.1 copy.47
  27.5 0.1 copy.48
  27.6 0.1 broadcast_add_fusion
  27.8 0.1 fusion.20
  27.8 0.1 reshape.125
  28.0 0.0 copy-done.4
  28.0 5.6 %fusion.9 = pred[1536,128]{1,0:T(8,128)(4,1)S(1)} fusion(s32[128,8]{0,1:T(8,128)S(1)} %get-tuple-element.200), kind=kLoop, calls=%fused_computation.20 | loop fusion | flops 2949120 | bytes 200704 | tf_op jit(solution)/shard_map/reduce_or | solution.py:95
  33.6 0.0 copy-done.3
  33.6 0.9 convolution_convert_fusion.1
  34.5 83.8 %all_to_all.10 = bf16[64,24,1,896]{3,1,2,0:T(8,128)(2,1)S(1)} all-to-all(bf16[64,24,1,896]{3,1,2,0:T(8,128)(2,1)S(1)} %bitcast.93), channel_id=1, replica_groups=mesh['role'=2,'grp'=64,'tp'=4] {'grp'}, dimensions={0} | all-to-all | bytes 5505024 | tf_op jit(solution)/shard_map/all_to_all | solution.py:100
  118.3 0.0 copy-done
  118.3 4.8 %fusion.10 = bf16[1536,1,1024]{2,0,1:T(8,128)(2,1)} fusion(bf16[1536,896]{1,0:T(8,128)(2,1)S(1)} %bitcast.95, bf16[1,896,1024]{2,1,0:T(8,128)(2,1)S(1)} %copy-done), kind=kOutput, calls=%fused_computation.25 | convolution fusion | flops 2820145152 | bytes 7733248 | tf_op jit(solution)/shard_map/sed,edf->sef/dot_general | solution.py:102
  123.1 0.0 all-reduce.2.cloned.1.call-update
  123.1 74.2 %all-reduce.2.cloned.1.call-done = bf16[1536,1,1024]{2,0,1:T(8,128)(2,1)} async-done(((bf16[1536,1,1024]{2,0,1:T(8,128)(2,1)}), bf16[1536,1,1024]{2,0,1:T(8,128)(2,1)}) %all-reduce.2.cloned.1.call-update) | async-done | bytes 3145744 | tf_op jit(solution)/shard_map/psum | solution.py:105
  197.3 7.6 %convolution_convert_fusion.2 = bf16[1536,896]{1,0:T(8,128)(2,1)} fusion(bf16[1536,1,1024]{2,0,1:T(8,128)(2,1)} %all-reduce.2.cloned.1.call-done, bf16[1,1024,896]{2,1,0:T(8,128)(2,1)} %param.17), kind=kOutput, calls=%fused_computation.24 | convolution fusion | flops 2829385728 | bytes 7733248 | tf_op jit(solution)/shard_map/sef,efd->sed/dot_general | solution.py:107
  205.0 0.0 copy-start.6
  205.0 0.0 copy-start.1
  205.0 0.0 copy-start.2
  205.0 0.0 copy-start.5
  205.0 13.2 %all-to-all-start.1 = ((bf16[64,24,1,896]{3,1,2,0:T(8,128)(2,1)}), bf16[64,24,1,896]{3,1,2,0:T(8,128)(2,1)}, u32[]{:S(2)}, u32[]{:S(2)}) async-start(bf16[64,24,1,896]{3,1,2,0:T(8,128)(2,1)} %bitcast.94), calls=%async_computation.1 | async-start | bytes 5505024 | tf_op jit(solution)/shard_map/all_to_all | solution.py:111
  218.2 0.0 all-gather.7.cloned.1.call-start
  218.2 0.0 copy-done.6
  218.2 0.1 broadcast_compare_fusion
  218.3 0.0 copy-done.1
  218.3 0.0 copy-done.2
  218.3 0.4 fusion.34
  218.7 1.0 convolution_convert_fusion.3
  219.7 0.0 all-gather.7.cloned.1.call-update
  219.8 0.1 copy.53
  219.9 0.1 reshape.141
  220.0 0.1 copy.50
  220.1 0.0 copy-done.5
  220.1 0.1 copy.44
  220.3 0.2 fusion.23
  220.5 8.5 %all-gather.4 = bf16[4,2,128]{2,1,0:T(2,128)(2,1)S(1)} all-gather(bf16[1,2,128]{2,1,0:T(2,128)(2,1)S(1)} %bitcast.99), channel_id=3, replica_groups=mesh['role'=2,'grp'=64,'tp'=4] {'tp'}, dimensions={0}, use_global_device_ids=true | all-gather | bytes 2560 | tf_op jit(solution)/shard_map/all_gather | solution.py:18
  229.0 6.0 %all-gather.3 = bf16[4,2,128]{2,1,0:T(2,128)(2,1)S(1)} all-gather(bf16[1,2,128]{2,1,0:T(2,128)(2,1)S(1)} %convert_bitcast_fusion.1), channel_id=2, replica_groups=mesh['role'=2,'grp'=64,'tp'=4] {'tp'}, dimensions={0}, use_global_device_ids=true | all-gather | bytes 2560 | tf_op jit(solution)/shard_map/all_gather | solution.py:18
  235.0 14.8 %all-gather.7.cloned.1.call-done = bf16[8,128,512]{2,1,0:T(8,128)(2,1)} async-done(((bf16[2,128,512]{2,1,0:T(8,128)(2,1)}), bf16[8,128,512]{2,1,0:T(8,128)(2,1)}) %all-gather.7.cloned.1.call-update) | async-done | bytes 1048592 | tf_op jit(solution)/shard_map/all_gather | solution.py:18
  249.8 1.0 slice_convert_fusion
  250.8 3.5 %while.19 = (s32[]{:T(128)}, f32[2,128]{1,0:T(2,128)S(1)}, f32[2,128]{1,0:T(2,128)S(1)}, f32[2,128,512]{2,1,0:T(8,128)S(1)}, bf16[4,2,128]{2,1,0:T(2,128)(2,1)S(...) while((s32[]{:T(128)}, f32[2,128]{1,0:T(2,128)S(1)}, ...), condition=%wide.region_3.4_spmd, body=%wide.region_2.3_spmd.sunk | while | flops 526341 | bytes 1320087 | solution.py:26
  250.8 1.1 fusion.43
  252.0 1.1 fusion.43
  253.2 1.1 fusion.43
  254.3 0.1 constant_dynamic-slice_fusion.2
  254.4 0.7 divide_convert_fusion
  255.1 55.7 %all-to-all-done.1 = bf16[64,24,1,896]{3,1,2,0:T(8,128)(2,1)} async-done(((bf16[64,24,1,896]{3,1,2,0:T(8,128)(2,1)}), bf16[64,24,1,896]{3,1,2,0:T(8,128)(2,1)}, u32[]{:S(2)}, u32[]{:S(2)}) %all-to-all-start.1) | async-done | bytes 2752544 | tf_op jit(solution)/shard_map/all_to_all | solution.py:111
  310.8 7.9 %gather_fusion = bf16[1024,896]{1,0:T(8,128)(2,1)} fusion(bf16[1536,896]{1,0:T(8,128)(2,1)} %bitcast.25, s32[1024]{0:T(1024)S(1)} %broadcast_clamp_fusion), kind=kCustom, calls=%fused_computation | custom fusion | bytes 3674112 | tf_op jit(solution)/shard_map/jit(_take)/gather | solution.py:115
  318.7 3.5 %multiply_reduce_fusion = bf16[128,896]{1,0:T(8,128)(2,1)} fusion(bf16[1024,896]{1,0:T(8,128)(2,1)} %gather_fusion, f32[128,8]{1,0:T(8,128)S(1)} %copy.44, pred[128,8]{1,0:T(8,128)(4,1)S(1)} %copy.50), kind=kLoop, calls=%fused_computation.22 | loop fusion | flops 3555328 | bytes 2069504 | tf_op jit(solution)/shard_map/reduce_sum | solution.py:116
  (16 shorter events, 0.3 us)
Async XLA Ops:
  8.0 110.3 %copy-start = (bf16[1,896,1024]{2,1,0:T(8,128)(2,1)S(1)}, bf16[1,896,1024]{2,1,0:T(8,128)(2,1)}, u32[]{:S(2)}) copy-start(bf16[1,896,1024]{2,1,0:T(8,128)(2,1)} %param.16) | copy-start | bytes 5505028
  8.0 20.0 %copy-start.4 = (s32[128,8]{0,1:T(8,128)S(1)}, s32[128,8]{0,1:T(8,128)}, u32[]{:S(2)}) copy-start(s32[128,8]{0,1:T(8,128)} %param.14) | copy-start | bytes 12292
  8.0 25.6 %copy-start.3 = (bf16[128,896]{1,0:T(8,128)(2,1)S(1)}, bf16[128,896]{1,0:T(8,128)(2,1)}, u32[]{:S(2)}) copy-start(bf16[128,896]{1,0:T(8,128)(2,1)} %param.13) | copy-start | bytes 688132
  8.0 189.3 %all-reduce.2.cloned.1.call-start = ((), (), s32[]{:S(2)}) async-start(), calls=%async_computation.2 | async-start | bytes 6291456 | tf_op jit(solution)/shard_map/psum | solution.py:105
  205.0 13.3 %copy-start.6 = (s32[2]{0:T(128)S(1)}, s32[2]{0:T(128)}, u32[]{:S(2)}) copy-start(s32[2]{0:T(128)} %param.12) | copy-start | bytes 28
  205.0 13.4 %copy-start.1 = (bf16[2,256,576]{1,2,0:T(8,128)(2,1)S(1)}, bf16[2,256,576]{1,2,0:T(8,128)(2,1)}, u32[]{:S(2)}) copy-start(bf16[2,256,576]{1,2,0:T(8,128)(2,1)} %param.11) | copy-start | bytes 1769476
  205.0 13.4 %copy-start.2 = (bf16[2,128,576]{1,2,0:T(8,128)(2,1)S(1)}, bf16[2,128,576]{1,2,0:T(8,128)(2,1)}, u32[]{:S(2)}) copy-start(bf16[2,128,576]{1,2,0:T(8,128)(2,1)} %param.10) | copy-start | bytes 884740
  205.0 15.1 %copy-start.5 = (f32[128,8]{0,1:T(8,128)S(1)}, f32[128,8]{0,1:T(8,128)}, u32[]{:S(2)}) copy-start(f32[128,8]{0,1:T(8,128)} %param.15) | copy-start | bytes 12292
  205.0 105.9 %all-to-all-start.1 = ((bf16[64,24,1,896]{3,1,2,0:T(8,128)(2,1)}), bf16[64,24,1,896]{3,1,2,0:T(8,128)(2,1)}, u32[]{:S(2)}, u32[]{:S(2)}) async-start(bf16[64,24,1,896]{3,1,2,0:T(8,128)(2,1)} %bitcast.94), calls=%async_computation.1 | async-start | bytes 5505024 | tf_op jit(solution)/shard_map/all_to_all | solution.py:111
  218.2 31.6 %all-gather.7.cloned.1.call-start = ((), (), s32[]{:S(2)}) async-start(), calls=%async_computation.3 | async-start | bytes 1310720 | tf_op jit(solution)/shard_map/all_gather | solution.py:18
Sparse Core Ops, SparseCore 0:
  123.2 74.0 all-reduce.1
Sparse Core Ops, SparseCore 1:
  220.7 29.0 all-gather.6
where the time goes:
time: 330 us
  waiting for transfers between devices  145 us (44%)
  blocking collectives  98.3 us (30%)
  other arithmetic  32.9 us (10%)
  between operations  15.7 us (5%)
  matrix products  14.7 us (4%)
  starting transfers between devices  13.3 us (4%)
  local copies, waits for them, and re-layouts  10 us (3%)
    all_to_all x1, blocking collectives, shards(): lax.all_to_all(outgoing, 'grp', split_axis=0, concat_axis=0, tiled=True)  83.8 us
    psum x1, waiting for transfers between devices, shards(): lax.psum(partial_value.astype(jnp.bfloat16), ('role', 'tp'))  74.2 us
    all_to_all x1, waiting for transfers between devices, shards(): lax.all_to_all(sending, 'grp', split_axis=0, concat_axis=0, tiled=True)  55.7 us
    another operation x3, other arithmetic  18.2 us
    all_gather x1, waiting for transfers between devices, combined_all(): lax.all_gather(part.astype(kind), axis)  14.8 us
    all_gather x2, blocking collectives, combined_all(): lax.all_gather(part.astype(kind), axis)  14.5 us
    all_to_all x1, starting transfers between devices, shards(): lax.all_to_all(sending, 'grp', split_axis=0, concat_axis=0, tiled=True)  13.2 us
    gather x1, local copies, waits for them, and re-layouts, shards(): picked = jnp.take(flat_back, slot_index, axis=0)  7.9 us
  transfers between devices with their start and end apart: 3, of which 3 were waited for; matrix products, arithmetic and copies ran while one was open for 2% of the time, Pallas kernels for 0%

commit v1 on v0

v1 whole, which is shorter than its diff:
```python
import jax
import jax.numpy as jnp
from jax import lax
from jax.sharding import PartitionSpec as P

KEY_VALUE_LATENT = 512
ROPE = 64
QK_NOPE = 128
EXPERTS = 64
CAP = 24
PARTS = ((0, 16), (16, 24))
LANES = 128

NEGATIVE = -1e30


def two_halves(value):
    high = value.astype(jnp.bfloat16)
    low = (value - high.astype(jnp.float32)).astype(jnp.bfloat16)
    return high, low


def attention_part(q_latent, key_value_cache, cache_lengths):
    score_scale = 1.0 / (QK_NOPE + ROPE) ** 0.5
    local_len = key_value_cache.shape[1]
    offset = lax.axis_index("tp") * local_len
    positions = offset + jnp.arange(local_len, dtype=jnp.int32)
    is_valid = positions[None, None, :] < cache_lengths[:, None, None]
    scores = (
        jnp.einsum("rhc,rlc->rhl", q_latent, key_value_cache, preferred_element_type=jnp.float32)
        * score_scale
    )
    scores = jnp.where(is_valid, scores, NEGATIVE)
    shift = jnp.max(scores, axis=-1).astype(jnp.bfloat16)
    exp_terms = jnp.where(
        is_valid, jnp.exp(scores - shift.astype(jnp.float32)[..., None]), 0.0
    )
    row_total = jnp.sum(exp_terms, axis=-1)
    context_total = jnp.einsum(
        "wzj,wjp->wzp",
        exp_terms.astype(jnp.bfloat16),
        key_value_cache[:, :, :KEY_VALUE_LATENT],
        preferred_element_type=jnp.float32,
    )
    total_high, total_low = two_halves(row_total)
    stats = jnp.stack([shift, total_high, total_low], axis=-1)
    stats = jnp.pad(stats, ((0, 0), (0, 0), (0, LANES - stats.shape[-1])))
    return jnp.concatenate([context_total.astype(jnp.bfloat16), stats], axis=-1)


def attention_join(everything, head_group):
    first = lax.axis_index("tp") * head_group
    mine = lax.dynamic_slice_in_dim(everything, first, head_group, 2)
    mine = lax.optimization_barrier(mine)
    context = mine[..., :KEY_VALUE_LATENT].astype(jnp.float32)
    stats = mine[..., KEY_VALUE_LATENT : KEY_VALUE_LATENT + 3].astype(jnp.float32)
    shift = stats[..., 0]
    total = stats[..., 1] + stats[..., 2]
    factor = jnp.exp(shift - jnp.max(shift, axis=0, keepdims=True))
    total_all = jnp.sum(total * factor, axis=0)
    context_all = jnp.sum(context * factor[..., None], axis=0)
    return (context_all / total_all[..., None]).astype(jnp.bfloat16)


def turned(value, axis, step):
    size = lax.axis_size(axis)
    return lax.ppermute(value, axis, [(k, (k + step) % size) for k in range(size)])


def summed_products(rows_in, weight):
    role = lax.axis_index("role")
    place = lax.axis_index("tp")
    size = lax.axis_size("tp")
    half = rows_in.shape[0] // 2
    share = half // size
    theirs = lax.dynamic_slice_in_dim(rows_in, (1 - role) * half, half, 0)
    mine = lax.dynamic_slice_in_dim(rows_in, role * half, half, 0)
    sent = jnp.dot(theirs, weight, preferred_element_type=jnp.float32).astype(jnp.bfloat16)
    arrived = turned(sent, "role", 1)
    total = jnp.dot(mine, weight, preferred_element_type=jnp.float32) + arrived.astype(jnp.float32)
    rounded = total.astype(jnp.bfloat16)
    shares = []
    for step in (2, 1, 3):
        piece = lax.dynamic_slice_in_dim(rounded, (place + step) % size * share, share, 0)
        shares.append(turned(piece, "tp", step))
    own = lax.dynamic_slice_in_dim(total, place * share, share, 0)
    for piece in shares:
        own = own + piece.astype(jnp.float32)
    return own


def spread(value, rows_all):
    place = lax.axis_index("tp")
    size = lax.axis_size("tp")
    share = value.shape[0]
    half = jnp.zeros((rows_all // 2, value.shape[1]), value.dtype)
    half = lax.dynamic_update_slice_in_dim(half, value, place * share, 0)
    for step in (2, 1, 3):
        piece = turned(value, "tp", step)
        half = lax.dynamic_update_slice_in_dim(half, piece, (place - step) % size * share, 0)
    return half, turned(half, "role", 1)


def shards(
    q_latent,
    key_value_cache,
    cache_lengths,
    hidden,
    expert_ids,
    route_logits,
    up_weight,
    down_weight,
):
    rows, width = hidden.shape
    owners = lax.axis_size("grp")
    role = lax.axis_index("role")
    experts = jnp.arange(EXPERTS, dtype=jnp.int32)
    up = up_weight[0]
    down = down_weight[0]

    named = expert_ids[:, None, :] == experts[None, :, None]
    named_any = jnp.any(named, axis=2)
    row_numbers = jnp.arange(rows, dtype=jnp.int32)
    lower = (row_numbers[None, :] < row_numbers[:, None]).astype(jnp.bfloat16)
    before = jnp.dot(
        lower, named_any.astype(jnp.bfloat16), preferred_element_type=jnp.float32
    ).astype(jnp.int32)
    rank = jnp.where(named_any, before, -1)
    rank_by_expert = rank.T

    arrivals = []
    for first, last in PARTS:
        slots = jnp.arange(first, last, dtype=jnp.int32)
        placed = rank_by_expert[:, None, :] == slots[None, :, None]
        placed = placed.reshape(-1, rows).astype(jnp.bfloat16)
        outgoing = jnp.dot(placed, hidden, preferred_element_type=jnp.float32).astype(jnp.bfloat16)
        if arrivals:
            outgoing, arrivals[-1] = lax.optimization_barrier((outgoing, arrivals[-1]))
        arrivals.append(
            lax.all_to_all(
                outgoing.reshape(owners, last - first, width),
                "grp",
                split_axis=0,
                concat_axis=0,
                tiled=True,
            )
        )

    packed = attention_part(q_latent, key_value_cache, cache_lengths)
    everything = lax.all_gather(packed, "tp")
    attn_context = attention_join(everything, q_latent.shape[1] // lax.axis_size("tp"))

    sigmoid_terms = jax.nn.sigmoid(route_logits)
    route_weights = 2.5 * sigmoid_terms / jnp.sum(sigmoid_terms, axis=-1, keepdims=True)
    weight_of = jnp.sum(jnp.where(named, route_weights[:, None, :], 0.0), axis=2)

    result = jnp.zeros((2 * rows, width), jnp.float32)
    earlier = None
    for (first, last), incoming in zip(PARTS, arrivals):
        slots = jnp.arange(first, last, dtype=jnp.int32)
        count = owners * (last - first)
        if earlier is not None:
            incoming, _ = lax.optimization_barrier((incoming, earlier))
        own = summed_products(incoming.reshape(count, width), up)
        activated = jax.nn.silu(own).astype(jnp.bfloat16)
        produced = jnp.zeros((count, width), jnp.bfloat16)
        halves = spread(activated, count)
        for which, half in zip((role, 1 - role), halves):
            out = jnp.dot(half, down, preferred_element_type=jnp.float32).astype(jnp.bfloat16)
            produced = lax.dynamic_update_slice_in_dim(produced, out, which * (count // 2), 0)
        earlier = produced
        returned = lax.all_to_all(
            produced.reshape(owners, last - first, width),
            "grp",
            split_axis=0,
            concat_axis=0,
            tiled=True,
        )
        taken = rank[:, :, None] == slots[None, None, :]
        weights = jnp.where(taken, weight_of[:, :, None], 0.0).reshape(rows, -1)
        both = jnp.concatenate(two_halves(weights), axis=0)
        result = result + jnp.dot(
            both, returned.reshape(count, width), preferred_element_type=jnp.float32
        )
    moe_output = (result[:rows] + result[rows:]).astype(jnp.bfloat16)
    return (attn_context, moe_output)


def solution(mesh):
    return jax.shard_map(
        shards,
        mesh=mesh,
        in_specs=(
            P(("role", "grp"), None, None),
            P(("role", "grp"), "tp", None),
            P(("role", "grp")),
            P("grp", ("role", "tp")),
            P("grp", None),
            P("grp", None),
            P("grp", ("role", "tp"), None),
            P("grp", None, ("role", "tp")),
        ),
        out_specs=(P(("role", "grp"), "tp", None), P("grp", ("role", "tp"))),
        check_vma=False,
    )
```

time: 330 us -> 267 us (0.81)
  the two profiles are of different devices: /device:TPU:45 before, /device:TPU:22 now
where the time goes in v1:
time: 267 us; the launch traced here: 266 us
  waiting for transfers between devices  101 us (38%)
  starting transfers between devices  88.9 us (33%)
  matrix products  33.8 us (13%)
  local copies, waits for them, and re-layouts  16.8 us (6%)
  between operations  14.7 us (6%)
  other arithmetic  11 us (4%)
    all_to_all x2, waiting for transfers between devices, shards(): lax.all_to_all(outgoing.reshape(owners, last - first, width), 'grp', spli...  50.8 us
    ppermute x16, starting transfers between devices, turned(): lax.ppermute(value, axis, [(k, (k + step) % size) for k in range(size)])  42.2 us
    ppermute x16, waiting for transfers between devices, turned(): lax.ppermute(value, axis, [(k, (k + step) % size) for k in range(size)])  32.8 us
    all_to_all x2, starting transfers between devices, shards(): lax.all_to_all(outgoing.reshape(owners, last - first, width), 'grp', spli...  26.6 us
    all_to_all x2, starting transfers between devices, shards(): lax.all_to_all(produced.reshape(owners, last - first, width), 'grp', spli...  20.1 us
    all_to_all x2, waiting for transfers between devices, shards(): lax.all_to_all(produced.reshape(owners, last - first, width), 'grp', spli...  17.1 us
    dot_general x4, matrix products, shards(): jnp.dot(half, down, preferred_element_type=jnp.float32).astype(jnp.bfloat16)  10.9 us
    dot_general x2, matrix products, summed_products(): jnp.dot(theirs, weight, preferred_element_type=jnp.float32)  7.21 us
  transfers between devices with their start and end apart: 21, of which 13 were waited for; matrix products, arithmetic and copies ran while one was open for 16% of the time, Pallas kernels for 0%

profile of v1, /device:TPU:22, one launch (start us, length us, event | category | flops | bytes accessed | tf_op | source)
XLA Modules:
  0.0 265.9 jit_solution(6811555614853409143)
XLA Ops:
  7.2 0.9 fusion.76
  8.5 2.8 %convolution_convert_fusion = bf16[1024,896]{1,0:T(8,128)(2,1)} fusion(pred[1024,128]{1,0:T(32,128)(4,1)S(1)} %bitcast_compare_fusion, bf16[128,896]{1,0:T(8,128)(2,1)} %param.11), kind=kOutput, calls=%fused_computation.18 | convolution fusion | flops 235798528 | bytes 2195456 | tf_op jit(solution)/shard_map/dot_general | solution.py:136
  11.4 16.8 %all-to-all-start = ((bf16[64,16,896]{2,1,0:T(8,128)(2,1)}), bf16[64,16,896]{2,1,0:T(8,128)(2,1)}, u32[]{:S(2)}, u32[]{:S(2)}) async-start(bf16[64,16,896]{2,1,0:T(8,128)(2,1)} %bitcast.135), calls=%async_computation | async-start | bytes 3670016 | tf_op jit(solution)/shard_map/all_to_all | solution.py:140
  28.3 1.4 convolution_convert_fusion.1
  29.7 44.8 %all-to-all-done = bf16[64,16,896]{2,1,0:T(8,128)(2,1)} async-done(((bf16[64,16,896]{2,1,0:T(8,128)(2,1)}), bf16[64,16,896]{2,1,0:T(8,128)(2,1)}, u32[]{:S(2)}, u32[]{:S(2)}) %all-to-all-start) | async-done | bytes 1835040 | tf_op jit(solution)/shard_map/all_to_all | solution.py:140
  74.6 4.0 %fusion.18 = bf16[512,1024]{1,0:T(8,128)(2,1)} fusion(bf16[1,896,1024]{2,1,0:T(8,128)(2,1)} %param.14, bf16[1024,896]{1,0:T(8,128)(2,1)} %bitcast.12, s32[]{:T(128)S(6)} %select_n.139), kind=kOutput, calls=%fused_computation.19 | convolution fusion | flops 940048384 | bytes 3801092 | tf_op jit(solution)/shard_map/dot_general | solution.py:78
  78.6 1.9 collective-permute-start
  80.6 2.8 %collective-permute-done = bf16[512,1024]{1,0:T(8,128)(2,1)S(1)} collective-permute-done((bf16[512,1024]{1,0:T(8,128)(2,1)}, bf16[512,1024]{1,0:T(8,128)(2,1)S(1)}, u32[]{:S(2)}, u32[]{:S(2)}) %collective-permute-start) | collective-permute-done | bytes 1048608 | tf_op jit(solution)/shard_map/ppermute | solution.py:67
  83.4 4.4 %fusion.99 = (bf16[512,1024]{1,0:T(8,128)(2,1)S(1)}, f32[512,1024]{1,0:T(8,128)}) fusion(bf16[512,1024]{1,0:T(8,128)(2,1)S(1)} %collective-permute-done, bf16[1,896,1024]{2,1,0:T(8,128)(2,1)} %param.14, bf16[1024,896]{1,0:T(8,128)(2,1)} %bitcast.12, s32[]{:T(128)S(6)} %select_n.138), kind=kOutput, calls=%fused_computation.126 | convolution fusion | flops 941096960 | bytes 6946820 | tf_op jit(solution)/shard_map/dot_general | solution.py:80
  87.8 3.3 %collective-permute-start.1 = (bf16[128,1024]{1,0:T(8,128)(2,1)S(1)}, bf16[128,1024]{1,0:T(8,128)(2,1)S(1)}, u32[]{:S(2)}, u32[]{:S(2)}) collective-permute-start(bf16[128,1024]{1,0:T(8,128)(2,1)S(1)} %get-tuple-element.18), channel_id=1, source_target_pairs={{0,2},{1,3},{2,0},{3,1},{4,6},{5,7},{6,4},{7,5},{8,10},{9,11},{10,... | collective-permute-start | bytes 786440 | tf_op jit(solution)/shard_map/ppermute | solution.py:67
  91.1 4.0 %collective-permute-start.2 = (bf16[128,1024]{1,0:T(8,128)(2,1)S(1)}, bf16[128,1024]{1,0:T(8,128)(2,1)S(1)}, u32[]{:S(2)}, u32[]{:S(2)}) collective-permute-start(bf16[128,1024]{1,0:T(8,128)(2,1)S(1)} %get-tuple-element.20), channel_id=1, source_target_pairs={{0,1},{1,2},{2,3},{3,0},{4,5},{5,6},{6,7},{7,4},{8,9},{9,10},{10,1... | collective-permute-start | bytes 786440 | tf_op jit(solution)/shard_map/ppermute | solution.py:67
  95.1 1.9 collective-permute-start.3
  97.1 2.7 %collective-permute-done.1 = bf16[128,1024]{1,0:T(8,128)(2,1)S(1)} collective-permute-done((bf16[128,1024]{1,0:T(8,128)(2,1)S(1)}, bf16[128,1024]{1,0:T(8,128)(2,1)S(1)}, u32[]{:S(2)}, u32[]{:S(2)}) %collective-permute-start.1) | collective-permute-done | bytes 262176 | tf_op jit(solution)/shard_map/ppermute | solution.py:67
  99.8 3.2 %collective-permute-done.2 = bf16[128,1024]{1,0:T(8,128)(2,1)S(1)} collective-permute-done((bf16[128,1024]{1,0:T(8,128)(2,1)S(1)}, bf16[128,1024]{1,0:T(8,128)(2,1)S(1)}, u32[]{:S(2)}, u32[]{:S(2)}) %collective-permute-start.2) | collective-permute-done | bytes 262176 | tf_op jit(solution)/shard_map/ppermute | solution.py:67
  103.0 3.1 %collective-permute-done.3 = bf16[128,1024]{1,0:T(8,128)(2,1)S(1)} collective-permute-done((bf16[128,1024]{1,0:T(8,128)(2,1)S(1)}, bf16[128,1024]{1,0:T(8,128)(2,1)S(1)}, u32[]{:S(2)}, u32[]{:S(2)}) %collective-permute-start.3) | collective-permute-done | bytes 262176 | tf_op jit(solution)/shard_map/ppermute | solution.py:67
  106.0 1.1 broadcast_in_dim.106
  107.1 2.1 constant_dynamic-update-slice_fusion.7
  109.2 2.7 collective-permute-start.4
  111.9 3.9 %collective-permute-start.5 = (bf16[128,1024]{1,0:T(8,128)(2,1)}, bf16[128,1024]{1,0:T(8,128)(2,1)S(1)}, u32[]{:S(2)}, u32[]{:S(2)}) collective-permute-start(bf16[128,1024]{1,0:T(8,128)(2,1)} %get-tuple-element.15), channel_id=1, source_target_pairs={{0,1},{1,2},{2,3},{3,0},{4,5},{5,6},{6,7},{7,4},{8,9},{9,10},{10,1... | collective-permute-start | bytes 786440 | tf_op jit(solution)/shard_map/ppermute | solution.py:67
  115.8 9.8 %all-to-all-start.2 = ((bf16[64,8,896]{2,1,0:T(8,128)(2,1)}), bf16[64,8,896]{2,1,0:T(8,128)(2,1)S(1)}, u32[]{:S(2)}, u32[]{:S(2)}) async-start(bf16[64,8,896]{2,1,0:T(8,128)(2,1)} %bitcast.19), calls=%async_computation.2 | async-start | bytes 1835008 | tf_op jit(solution)/shard_map/all_to_all | solution.py:140
  125.6 1.9 collective-permute-start.6
  127.6 1.7 constant_dynamic-update-slice_fusion.6
  129.3 0.7 constant_dynamic-update-slice_fusion.5
  130.0 6.0 %collective-permute-done.6 = bf16[128,1024]{1,0:T(8,128)(2,1)S(1)} collective-permute-done((bf16[128,1024]{1,0:T(8,128)(2,1)}, bf16[128,1024]{1,0:T(8,128)(2,1)S(1)}, u32[]{:S(2)}, u32[]{:S(2)}) %collective-permute-start.6) | collective-permute-done | bytes 262176 | tf_op jit(solution)/shard_map/ppermute | solution.py:67
  136.7 1.9 collective-permute-start.7
  138.8 1.4 broadcast_in_dim.105
  140.1 3.4 %fusion.24 = bf16[1024,896]{1,0:T(8,128)(2,1)} fusion(bf16[1024,896]{1,0:T(8,128)(2,1)} %broadcast_in_dim.105, s32[]{:T(128)S(6)} %select_n.138, bf16[512,1024]{1,0:T(8,128)(2,1)} %constant_dynamic-update-slice_fusion.4, bf16[1,1024,896]{2,1,0:T(8,128)(2,1)S(1)} %copy-done), kind=kOutput, calls=%fused_computation.21 | convolution fusion | flops 939982848 | bytes 3801092 | tf_op jit(solution)/shard_map/dot_general | solution.py:169
  143.6 3.4 %fusion.30 = bf16[1024,896]{1,0:T(8,128)(2,1)} fusion(bf16[1024,896]{1,0:T(8,128)(2,1)} %fusion.24, s32[]{:T(128)S(6)} %select_n.139, bf16[512,1024]{1,0:T(8,128)(2,1)} %collective-permute-done.7, bf16[1,1024,896]{2,1,0:T(8,128)(2,1)S(1)} %copy-done), kind=kOutput, calls=%fused_computation.23 | convolution fusion | flops 939982848 | bytes 3801092 | tf_op jit(solution)/shard_map/dot_general | solution.py:169
  147.0 6.0 %all-to-all-done.2 = bf16[64,8,896]{2,1,0:T(8,128)(2,1)S(1)} async-done(((bf16[64,8,896]{2,1,0:T(8,128)(2,1)}), bf16[64,8,896]{2,1,0:T(8,128)(2,1)S(1)}, u32[]{:S(2)}, u32[]{:S(2)}) %all-to-all-start.2) | async-done | bytes 917536 | tf_op jit(solution)/shard_map/all_to_all | solution.py:140
  153.0 0.9 copy-done.2
  153.9 7.0 %all-to-all-start.1 = ((bf16[64,16,896]{2,1,0:T(8,128)(2,1)}), bf16[64,16,896]{2,1,0:T(8,128)(2,1)}, u32[]{:S(2)}, u32[]{:S(2)}) async-start(bf16[64,16,896]{2,1,0:T(8,128)(2,1)} %bitcast.15), calls=%async_computation.1 | async-start | bytes 3670016 | tf_op jit(solution)/shard_map/all_to_all | solution.py:172
  161.6 3.2 %fusion.33 = bf16[256,1024]{1,0:T(8,128)(2,1)} fusion(bf16[1,896,1024]{2,1,0:T(8,128)(2,1)} %param.14, bf16[512,896]{1,0:T(8,128)(2,1)} %bitcast.137, s32[]{:T(128)S(6)} %select_n.155), kind=kOutput, calls=%fused_computation.26 | convolution fusion | flops 470024192 | bytes 2818052 | tf_op jit(solution)/shard_map/dot_general | solution.py:78
  164.7 1.9 collective-permute-start.8
  167.2 1.6 collective-permute-done.8
  168.8 2.4 fusion.100
  171.1 0.8 constant_dynamic-slice_fusion.2
  171.9 1.9 collective-permute-start.10
  173.8 3.9 %collective-permute-start.11 = (bf16[64,1024]{1,0:T(8,128)(2,1)}, bf16[64,1024]{1,0:T(8,128)(2,1)S(1)}, u32[]{:S(2)}, u32[]{:S(2)}) collective-permute-start(bf16[64,1024]{1,0:T(8,128)(2,1)} %get-tuple-element.22), channel_id=1, source_target_pairs={{0,3},{1,0},{2,1},{3,2},{4,7},{5,4},{6,5},{7,6},{8,11},{9,8},{10,9... | collective-permute-start | bytes 393224 | tf_op jit(solution)/shard_map/ppermute | solution.py:67
  177.8 1.9 collective-permute-start.9
  179.7 0.8 fusion.69
  180.5 2.2 collective-permute-done.11
  182.7 3.7 %collective-permute-done.9 = bf16[64,1024]{1,0:T(8,128)(2,1)S(1)} collective-permute-done((bf16[64,1024]{1,0:T(8,128)(2,1)}, bf16[64,1024]{1,0:T(8,128)(2,1)S(1)}, u32[]{:S(2)}, u32[]{:S(2)}) %collective-permute-start.9) | collective-permute-done | bytes 131104 | tf_op jit(solution)/shard_map/ppermute | solution.py:67
  187.0 0.9 broadcast_in_dim.111
  187.9 1.7 constant_dynamic-update-slice_fusion.3
  189.5 3.1 %collective-permute-start.12 = (bf16[64,1024]{1,0:T(8,128)(2,1)S(1)}, bf16[64,1024]{1,0:T(8,128)(2,1)S(1)}, u32[]{:S(2)}, u32[]{:S(2)}) collective-permute-start(bf16[64,1024]{1,0:T(8,128)(2,1)S(1)} %get-tuple-element.13), channel_id=1, source_target_pairs={{0,2},{1,3},{2,0},{3,1},{4,6},{5,7},{6,4},{7,5},{8,10},{9,11},{10,... | collective-permute-start | bytes 393224 | tf_op jit(solution)/shard_map/ppermute | solution.py:67
  192.6 3.7 %collective-permute-start.13 = (bf16[64,1024]{1,0:T(8,128)(2,1)S(1)}, bf16[64,1024]{1,0:T(8,128)(2,1)S(1)}, u32[]{:S(2)}, u32[]{:S(2)}) collective-permute-start(bf16[64,1024]{1,0:T(8,128)(2,1)S(1)} %get-tuple-element.13), channel_id=1, source_target_pairs={{0,1},{1,2},{2,3},{3,0},{4,5},{5,6},{6,7},{7,4},{8,9},{9,10},{10,1... | collective-permute-start | bytes 393224 | tf_op jit(solution)/shard_map/ppermute | solution.py:67
  196.5 2.2 collective-permute-start.14
  199.3 0.9 collective-permute-done.13
  200.8 6.8 %collective-permute-done.14 = bf16[64,1024]{1,0:T(8,128)(2,1)S(1)} collective-permute-done((bf16[64,1024]{1,0:T(8,128)(2,1)S(1)}, bf16[64,1024]{1,0:T(8,128)(2,1)S(1)}, u32[]{:S(2)}, u32[]{:S(2)}) %collective-permute-start.14) | collective-permute-done | bytes 131104 | tf_op jit(solution)/shard_map/ppermute | solution.py:67
  208.2 2.1 collective-permute-start.15
  210.5 1.0 broadcast_in_dim.110
  211.5 2.6 fusion.45
  214.1 1.5 fusion.42
  215.6 13.0 %all-to-all-start.3 = ((bf16[64,8,896]{2,1,0:T(8,128)(2,1)}), bf16[64,8,896]{2,1,0:T(8,128)(2,1)}, u32[]{:S(2)}, u32[]{:S(2)}) async-start(bf16[64,8,896]{2,1,0:T(8,128)(2,1)} %bitcast.21), calls=%async_computation.3 | async-start | bytes 1835008 | tf_op jit(solution)/shard_map/all_to_all | solution.py:172
  228.6 0.8 fusion.75
  229.6 0.9 fusion.60
  230.5 2.3 copy.31
  232.9 1.5 constant_dynamic-slice_fusion.6
  234.4 1.9 multiply_reduce_fusion
  236.6 0.8 copy.32
  237.4 2.2 fusion.54
  239.6 17.1 %all-to-all-done.3 = bf16[64,8,896]{2,1,0:T(8,128)(2,1)} async-done(((bf16[64,8,896]{2,1,0:T(8,128)(2,1)}), bf16[64,8,896]{2,1,0:T(8,128)(2,1)}, u32[]{:S(2)}, u32[]{:S(2)}) %all-to-all-start.3) | async-done | bytes 917536 | tf_op jit(solution)/shard_map/all_to_all | solution.py:172
  256.6 1.6 convolution_add_fusion
  258.3 0.7 fusion.62
  (62 shorter events, 5.9 us)
Async XLA Ops:
  7.2 133.0 %copy-start = (bf16[1,1024,896]{2,1,0:T(8,128)(2,1)S(1)}, bf16[1,1024,896]{2,1,0:T(8,128)(2,1)}, u32[]{:S(2)}) copy-start(bf16[1,1024,896]{2,1,0:T(8,128)(2,1)} %param.15) | copy-start | bytes 5505028
  11.4 16.9 %copy-start.4 = (bf16[128,896]{1,0:T(8,128)(2,1)S(1)}, bf16[128,896]{1,0:T(8,128)(2,1)}, u32[]{:S(2)}) copy-start(bf16[128,896]{1,0:T(8,128)(2,1)} %param.11) | copy-start | bytes 688132
  11.4 63.2 %all-to-all-start = ((bf16[64,16,896]{2,1,0:T(8,128)(2,1)}), bf16[64,16,896]{2,1,0:T(8,128)(2,1)}, u32[]{:S(2)}, u32[]{:S(2)}) async-start(bf16[64,16,896]{2,1,0:T(8,128)(2,1)} %bitcast.135), calls=%async_computation | async-start | bytes 3670016 | tf_op jit(solution)/shard_map/all_to_all | solution.py:140
  78.6 4.8 %collective-permute-start = (bf16[512,1024]{1,0:T(8,128)(2,1)}, bf16[512,1024]{1,0:T(8,128)(2,1)S(1)}, u32[]{:S(2)}, u32[]{:S(2)}) collective-permute-start(bf16[512,1024]{1,0:T(8,128)(2,1)} %fusion.18), channel_id=1, source_target_pairs={{0,256},{256,0},{1,257},{257,1},{2,258},{258,2},{3,259},{259,3},{4... | collective-permute-start | bytes 3145736 | tf_op jit(solution)/shard_map/ppermute | solution.py:67
  87.8 12.0 %collective-permute-start.1 = (bf16[128,1024]{1,0:T(8,128)(2,1)S(1)}, bf16[128,1024]{1,0:T(8,128)(2,1)S(1)}, u32[]{:S(2)}, u32[]{:S(2)}) collective-permute-start(bf16[128,1024]{1,0:T(8,128)(2,1)S(1)} %get-tuple-element.18), channel_id=1, source_target_pairs={{0,2},{1,3},{2,0},{3,1},{4,6},{5,7},{6,4},{7,5},{8,10},{9,11},{10,... | collective-permute-start | bytes 786440 | tf_op jit(solution)/shard_map/ppermute | solution.py:67
  91.1 11.8 %collective-permute-start.2 = (bf16[128,1024]{1,0:T(8,128)(2,1)S(1)}, bf16[128,1024]{1,0:T(8,128)(2,1)S(1)}, u32[]{:S(2)}, u32[]{:S(2)}) collective-permute-start(bf16[128,1024]{1,0:T(8,128)(2,1)S(1)} %get-tuple-element.20), channel_id=1, source_target_pairs={{0,1},{1,2},{2,3},{3,0},{4,5},{5,6},{6,7},{7,4},{8,9},{9,10},{10,1... | collective-permute-start | bytes 786440 | tf_op jit(solution)/shard_map/ppermute | solution.py:67
  95.1 10.9 %collective-permute-start.3 = (bf16[128,1024]{1,0:T(8,128)(2,1)S(1)}, bf16[128,1024]{1,0:T(8,128)(2,1)S(1)}, u32[]{:S(2)}, u32[]{:S(2)}) collective-permute-start(bf16[128,1024]{1,0:T(8,128)(2,1)S(1)} %get-tuple-element.19), channel_id=1, source_target_pairs={{0,3},{1,0},{2,1},{3,2},{4,7},{5,4},{6,5},{7,6},{8,11},{9,8},{10,9... | collective-permute-start | bytes 786440 | tf_op jit(solution)/shard_map/ppermute | solution.py:67
  109.2 29.5 %copy-start.10 = (s32[2]{0:T(128)S(1)}, s32[2]{0:T(128)}, u32[]{:S(2)}) copy-start(s32[2]{0:T(128)} %param.10) | copy-start | bytes 28
  109.2 18.4 %collective-permute-start.4 = (bf16[128,1024]{1,0:T(8,128)(2,1)}, bf16[128,1024]{1,0:T(8,128)(2,1)}, u32[]{:S(2)}, u32[]{:S(2)}) collective-permute-start(bf16[128,1024]{1,0:T(8,128)(2,1)} %get-tuple-element.15), channel_id=1, source_target_pairs={{0,2},{1,3},{2,0},{3,1},{4,6},{5,7},{6,4},{7,5},{8,10},{9,11},{10,... | collective-permute-start | bytes 786440 | tf_op jit(solution)/shard_map/ppermute | solution.py:67
  111.9 17.4 %collective-permute-start.5 = (bf16[128,1024]{1,0:T(8,128)(2,1)}, bf16[128,1024]{1,0:T(8,128)(2,1)S(1)}, u32[]{:S(2)}, u32[]{:S(2)}) collective-permute-start(bf16[128,1024]{1,0:T(8,128)(2,1)} %get-tuple-element.15), channel_id=1, source_target_pairs={{0,1},{1,2},{2,3},{3,0},{4,5},{5,6},{6,7},{7,4},{8,9},{9,10},{10,1... | collective-permute-start | bytes 786440 | tf_op jit(solution)/shard_map/ppermute | solution.py:67
  115.8 37.2 %all-to-all-start.2 = ((bf16[64,8,896]{2,1,0:T(8,128)(2,1)}), bf16[64,8,896]{2,1,0:T(8,128)(2,1)S(1)}, u32[]{:S(2)}, u32[]{:S(2)}) async-start(bf16[64,8,896]{2,1,0:T(8,128)(2,1)} %bitcast.19), calls=%async_computation.2 | async-start | bytes 1835008 | tf_op jit(solution)/shard_map/all_to_all | solution.py:140
  125.6 10.4 %collective-permute-start.6 = (bf16[128,1024]{1,0:T(8,128)(2,1)}, bf16[128,1024]{1,0:T(8,128)(2,1)S(1)}, u32[]{:S(2)}, u32[]{:S(2)}) collective-permute-start(bf16[128,1024]{1,0:T(8,128)(2,1)} %get-tuple-element.15), channel_id=1, source_target_pairs={{0,3},{1,0},{2,1},{3,2},{4,7},{5,4},{6,5},{7,6},{8,11},{9,8},{10,9... | collective-permute-start | bytes 786440 | tf_op jit(solution)/shard_map/ppermute | solution.py:67
  136.7 6.8 %collective-permute-start.7 = (bf16[512,1024]{1,0:T(8,128)(2,1)}, bf16[512,1024]{1,0:T(8,128)(2,1)}, u32[]{:S(2)}, u32[]{:S(2)}) collective-permute-start(bf16[512,1024]{1,0:T(8,128)(2,1)} %constant_dynamic-update-slice_fusion.4), channel_id=1, source_target_pairs={{0,256},{256,0},{1,257},{257,1},{2,258},{258,2},{3,259},{259,3},{4... | collective-permute-start | bytes 3145736 | tf_op jit(solution)/shard_map/ppermute | solution.py:67
  153.0 0.9 copy-start.2
  153.9 7.1 %copy-start.1 = (bf16[2,256,576]{1,2,0:T(8,128)(2,1)S(1)}, bf16[2,256,576]{1,2,0:T(8,128)(2,1)}, u32[]{:S(2)}) copy-start(bf16[2,256,576]{1,2,0:T(8,128)(2,1)} %param.9) | copy-start | bytes 1769476
  153.9 7.1 %copy-start.6 = (bf16[2,128,576]{1,2,0:T(8,128)(2,1)S(1)}, bf16[2,128,576]{1,2,0:T(8,128)(2,1)}, u32[]{:S(2)}) copy-start(bf16[2,128,576]{1,2,0:T(8,128)(2,1)} %param.8) | copy-start | bytes 884740
  153.9 61.7 %all-to-all-start.1 = ((bf16[64,16,896]{2,1,0:T(8,128)(2,1)}), bf16[64,16,896]{2,1,0:T(8,128)(2,1)}, u32[]{:S(2)}, u32[]{:S(2)}) async-start(bf16[64,16,896]{2,1,0:T(8,128)(2,1)} %bitcast.15), calls=%async_computation.1 | async-start | bytes 3670016 | tf_op jit(solution)/shard_map/all_to_all | solution.py:172
  160.9 69.6 %all-gather.3.cloned.1.call-start = ((), (), s32[]{:S(2)}) async-start(), calls=%async_computation.4 | async-start | bytes 1638400 | tf_op jit(solution)/shard_map/all_gather | solution.py:150
  164.7 4.0 %collective-permute-start.8 = (bf16[256,1024]{1,0:T(8,128)(2,1)}, bf16[256,1024]{1,0:T(8,128)(2,1)S(1)}, u32[]{:S(2)}, u32[]{:S(2)}) collective-permute-start(bf16[256,1024]{1,0:T(8,128)(2,1)} %fusion.33), channel_id=1, source_target_pairs={{0,256},{256,0},{1,257},{257,1},{2,258},{258,2},{3,259},{259,3},{4... | collective-permute-start | bytes 1572872 | tf_op jit(solution)/shard_map/ppermute | solution.py:67
  167.2 13.3 %copy-start.9 = (f32[128,8]{0,1:T(8,128)S(1)}, f32[128,8]{0,1:T(8,128)}, u32[]{:S(2)}) copy-start(f32[128,8]{0,1:T(8,128)} %param.13) | copy-start | bytes 12292
  171.1 25.2 %copy-start.8 = (s32[128,8]{0,1:T(8,128)S(1)}, s32[128,8]{0,1:T(8,128)}, u32[]{:S(2)}) copy-start(s32[128,8]{0,1:T(8,128)} %param.12) | copy-start | bytes 12292
  171.9 8.6 %collective-permute-start.10 = (bf16[64,1024]{1,0:T(8,128)(2,1)}, bf16[64,1024]{1,0:T(8,128)(2,1)S(1)}, u32[]{:S(2)}, u32[]{:S(2)}) collective-permute-start(bf16[64,1024]{1,0:T(8,128)(2,1)} %get-tuple-element.23), channel_id=1, source_target_pairs={{0,1},{1,2},{2,3},{3,0},{4,5},{5,6},{6,7},{7,4},{8,9},{9,10},{10,1... | collective-permute-start | bytes 393224 | tf_op jit(solution)/shard_map/ppermute | solution.py:67
  173.8 8.9 %collective-permute-start.11 = (bf16[64,1024]{1,0:T(8,128)(2,1)}, bf16[64,1024]{1,0:T(8,128)(2,1)S(1)}, u32[]{:S(2)}, u32[]{:S(2)}) collective-permute-start(bf16[64,1024]{1,0:T(8,128)(2,1)} %get-tuple-element.22), channel_id=1, source_target_pairs={{0,3},{1,0},{2,1},{3,2},{4,7},{5,4},{6,5},{7,6},{8,11},{9,8},{10,9... | collective-permute-start | bytes 393224 | tf_op jit(solution)/shard_map/ppermute | solution.py:67
  177.8 8.6 %collective-permute-start.9 = (bf16[64,1024]{1,0:T(8,128)(2,1)}, bf16[64,1024]{1,0:T(8,128)(2,1)S(1)}, u32[]{:S(2)}, u32[]{:S(2)}) collective-permute-start(bf16[64,1024]{1,0:T(8,128)(2,1)} %get-tuple-element.21), channel_id=1, source_target_pairs={{0,2},{1,3},{2,0},{3,1},{4,6},{5,7},{6,4},{7,5},{8,10},{9,11},{10,... | collective-permute-start | bytes 393224 | tf_op jit(solution)/shard_map/ppermute | solution.py:67
  186.3 0.7 copy-start.7
  189.5 9.1 %collective-permute-start.12 = (bf16[64,1024]{1,0:T(8,128)(2,1)S(1)}, bf16[64,1024]{1,0:T(8,128)(2,1)S(1)}, u32[]{:S(2)}, u32[]{:S(2)}) collective-permute-start(bf16[64,1024]{1,0:T(8,128)(2,1)S(1)} %get-tuple-element.13), channel_id=1, source_target_pairs={{0,2},{1,3},{2,0},{3,1},{4,6},{5,7},{6,4},{7,5},{8,10},{9,11},{10,... | collective-permute-start | bytes 393224 | tf_op jit(solution)/shard_map/ppermute | solution.py:67
  192.6 7.5 %collective-permute-start.13 = (bf16[64,1024]{1,0:T(8,128)(2,1)S(1)}, bf16[64,1024]{1,0:T(8,128)(2,1)S(1)}, u32[]{:S(2)}, u32[]{:S(2)}) collective-permute-start(bf16[64,1024]{1,0:T(8,128)(2,1)S(1)} %get-tuple-element.13), channel_id=1, source_target_pairs={{0,1},{1,2},{2,3},{3,0},{4,5},{5,6},{6,7},{7,4},{8,9},{9,10},{10,1... | collective-permute-start | bytes 393224 | tf_op jit(solution)/shard_map/ppermute | solution.py:67
  196.5 11.1 %collective-permute-start.14 = (bf16[64,1024]{1,0:T(8,128)(2,1)S(1)}, bf16[64,1024]{1,0:T(8,128)(2,1)S(1)}, u32[]{:S(2)}, u32[]{:S(2)}) collective-permute-start(bf16[64,1024]{1,0:T(8,128)(2,1)S(1)} %get-tuple-element.13), channel_id=1, source_target_pairs={{0,3},{1,0},{2,1},{3,2},{4,7},{5,4},{6,5},{7,6},{8,11},{9,8},{10,9... | collective-permute-start | bytes 393224 | tf_op jit(solution)/shard_map/ppermute | solution.py:67
  208.2 5.8 %collective-permute-start.15 = (bf16[256,1024]{1,0:T(8,128)(2,1)}, bf16[256,1024]{1,0:T(8,128)(2,1)S(1)}, u32[]{:S(2)}, u32[]{:S(2)}) collective-permute-start(bf16[256,1024]{1,0:T(8,128)(2,1)} %constant_dynamic-update-slice_fusion), channel_id=1, source_target_pairs={{0,256},{256,0},{1,257},{257,1},{2,258},{258,2},{3,259},{259,3},{4... | collective-permute-start | bytes 1572872 | tf_op jit(solution)/shard_map/ppermute | solution.py:67
  215.6 41.1 %all-to-all-start.3 = ((bf16[64,8,896]{2,1,0:T(8,128)(2,1)}), bf16[64,8,896]{2,1,0:T(8,128)(2,1)}, u32[]{:S(2)}, u32[]{:S(2)}) async-start(bf16[64,8,896]{2,1,0:T(8,128)(2,1)} %bitcast.21), calls=%async_computation.3 | async-start | bytes 1835008 | tf_op jit(solution)/shard_map/all_to_all | solution.py:172
  234.3 3.0 %copy-start.3 = (bf16[128,1024]{0,1:T(8,128)(2,1)S(1)}, bf16[128,1024]{0,1:T(8,128)(2,1)}, u32[]{:S(2)}) copy-start(bf16[128,1024]{0,1:T(8,128)(2,1)} %fusion.60) | copy-start | bytes 786436
  236.6 20.1 %copy-start.5 = (bf16[128,512]{0,1:T(8,128)(2,1)S(1)}, bf16[128,512]{0,1:T(8,128)(2,1)}, u32[]{:S(2)}) copy-start(bf16[128,512]{0,1:T(8,128)(2,1)} %fusion.75) | copy-start | bytes 393220
Sparse Core Ops, SparseCore 0:
  180.6 32.5 all-gather.2

commit v2 on v1

v2 whole, which is shorter than its diff:
```python
import functools

import jax
import jax.numpy as jnp
from jax import lax
from jax.experimental import pallas as pl
from jax.experimental.pallas import tpu as pltpu
from jax.sharding import PartitionSpec as P

KEY_VALUE_LATENT = 512
ROPE = 64
QK_NOPE = 128
EXPERTS = 64
CAP = 24
PARTS = ((0, 8), (8, 24))
VMEM = 40 * 1024 * 1024
LANES = 128

NEGATIVE = -1e30


def two_halves(value):
    high = value.astype(jnp.bfloat16)
    low = (value - high.astype(jnp.float32)).astype(jnp.bfloat16)
    return high, low


def attention_part(q_latent, key_value_cache, cache_lengths):
    score_scale = 1.0 / (QK_NOPE + ROPE) ** 0.5
    local_len = key_value_cache.shape[1]
    offset = lax.axis_index("tp") * local_len
    positions = offset + jnp.arange(local_len, dtype=jnp.int32)
    is_valid = positions[None, None, :] < cache_lengths[:, None, None]
    scores = (
        jnp.einsum("rhc,rlc->rhl", q_latent, key_value_cache, preferred_element_type=jnp.float32)
        * score_scale
    )
    scores = jnp.where(is_valid, scores, NEGATIVE)
    shift = jnp.max(scores, axis=-1).astype(jnp.bfloat16)
    exp_terms = jnp.where(
        is_valid, jnp.exp(scores - shift.astype(jnp.float32)[..., None]), 0.0
    )
    row_total = jnp.sum(exp_terms, axis=-1)
    context_total = jnp.einsum(
        "wzj,wjp->wzp",
        exp_terms.astype(jnp.bfloat16),
        key_value_cache[:, :, :KEY_VALUE_LATENT],
        preferred_element_type=jnp.float32,
    )
    total_high, total_low = two_halves(row_total)
    stats = jnp.stack([shift, total_high, total_low], axis=-1)
    stats = jnp.pad(stats, ((0, 0), (0, 0), (0, LANES - stats.shape[-1])))
    return jnp.concatenate([context_total.astype(jnp.bfloat16), stats], axis=-1)


def attention_join(everything, head_group):
    first = lax.axis_index("tp") * head_group
    mine = lax.dynamic_slice_in_dim(everything, first, head_group, 2)
    mine = lax.optimization_barrier(mine)
    context = mine[..., :KEY_VALUE_LATENT].astype(jnp.float32)
    stats = mine[..., KEY_VALUE_LATENT : KEY_VALUE_LATENT + 3].astype(jnp.float32)
    shift = stats[..., 0]
    total = stats[..., 1] + stats[..., 2]
    factor = jnp.exp(shift - jnp.max(shift, axis=0, keepdims=True))
    total_all = jnp.sum(total * factor, axis=0)
    context_all = jnp.sum(context * factor[..., None], axis=0)
    return (context_all / total_all[..., None]).astype(jnp.bfloat16)


def turned(value, axis, step):
    size = lax.axis_size(axis)
    return lax.ppermute(value, axis, [(k, (k + step) % size) for k in range(size)])


def cost(rows, depth, columns):
    return pl.CostEstimate(
        flops=2 * rows * depth * columns,
        bytes_accessed=2 * (rows * depth + depth * columns + rows * columns),
        transcendentals=0,
    )


def their_kernel(where, rows_ref, weight_ref, out_ref):
    out_ref[...] = jnp.dot(
        rows_ref[...], weight_ref[...], preferred_element_type=jnp.float32
    ).astype(out_ref.dtype)


def their_half(where, rows_in, weight):
    half, depth = rows_in.shape[0] // 2, rows_in.shape[1]
    columns = weight.shape[1]
    tile = min(256, half)
    steps = half // tile
    return pl.pallas_call(
        their_kernel,
        out_shape=jax.ShapeDtypeStruct((half, columns), jnp.bfloat16),
        grid_spec=pltpu.PrefetchScalarGridSpec(
            num_scalar_prefetch=1,
            grid=(steps,),
            in_specs=[
                pl.BlockSpec((tile, depth), lambda i, where: ((1 - where[0]) * steps + i, 0)),
                pl.BlockSpec((depth, columns), lambda i, where: (0, 0)),
            ],
            out_specs=pl.BlockSpec((tile, columns), lambda i, where: (i, 0)),
        ),
        compiler_params=pltpu.CompilerParams(vmem_limit_bytes=VMEM),
        cost_estimate=cost(half, depth, columns),
        name="their_half",
    )(where, rows_in, weight)


def own_kernel(where, rows_ref, weight_ref, arrived_ref, own_ref, *rest):
    piece_refs, total = rest[:-1], rest[-1]
    tile = rows_ref.shape[0]
    share = own_ref.shape[0]
    size = total.shape[0] // share
    step = pl.program_id(0)
    here = pl.ds(pl.multiple_of(step * tile, tile), tile)
    total[here, :] = jnp.dot(
        rows_ref[...], weight_ref[...], preferred_element_type=jnp.float32
    ) + arrived_ref[...].astype(jnp.float32)

    @pl.when(step == pl.num_programs(0) - 1)
    def _():
        if size == 1:
            own_ref[...] = total[...]
            piece_refs[0][...] = total[...].astype(jnp.bfloat16)
        else:
            for ahead in range(size):
                place = lax.rem(where[1] + ahead, size)
                piece = total[pl.ds(pl.multiple_of(place * share, share), share), :]
                if ahead == 0:
                    own_ref[...] = piece
                else:
                    piece_refs[ahead - 1][...] = piece.astype(jnp.bfloat16)


def own_half(where, rows_in, weight, arrived, size):
    half, depth = rows_in.shape[0] // 2, rows_in.shape[1]
    columns = weight.shape[1]
    tile = min(256, half)
    steps = half // tile
    share = half // size
    return pl.pallas_call(
        own_kernel,
        out_shape=[jax.ShapeDtypeStruct((share, columns), jnp.float32)]
        + [jax.ShapeDtypeStruct((share, columns), jnp.bfloat16)] * max(1, size - 1),
        grid_spec=pltpu.PrefetchScalarGridSpec(
            num_scalar_prefetch=1,
            grid=(steps,),
            in_specs=[
                pl.BlockSpec((tile, depth), lambda i, where: (where[0] * steps + i, 0)),
                pl.BlockSpec((depth, columns), lambda i, where: (0, 0)),
                pl.BlockSpec((tile, columns), lambda i, where: (i, 0)),
            ],
            out_specs=[pl.BlockSpec((share, columns), lambda i, where: (0, 0))]
            * max(2, size),
            scratch_shapes=[pltpu.VMEM((half, columns), jnp.float32)],
        ),
        compiler_params=pltpu.CompilerParams(vmem_limit_bytes=VMEM),
        cost_estimate=cost(half, depth, columns),
        name="own_half",
    )(where, rows_in, weight, arrived)


def down_kernel(where, mine_ref, theirs_ref, weight_ref, out_ref):
    @pl.when(pl.program_id(0) == 0)
    def _():
        out_ref[...] = jnp.dot(
            mine_ref[...], weight_ref[...], preferred_element_type=jnp.float32
        ).astype(out_ref.dtype)

    @pl.when(pl.program_id(0) == 1)
    def _():
        out_ref[...] = jnp.dot(
            theirs_ref[...], weight_ref[...], preferred_element_type=jnp.float32
        ).astype(out_ref.dtype)


def down_both(where, mine, theirs, weight, size):
    half, depth = mine.shape
    columns = weight.shape[1]
    share = half // size

    def place(core, back, where):
        which = where[0] + core - 2 * where[0] * core
        return which * size + lax.rem(where[1] * (size > 1) + size - back, size), 0

    return pl.pallas_call(
        down_kernel,
        out_shape=jax.ShapeDtypeStruct((2 * half, columns), jnp.bfloat16),
        grid_spec=pltpu.PrefetchScalarGridSpec(
            num_scalar_prefetch=1,
            grid=(2, size),
            in_specs=[
                pl.BlockSpec((share, depth), lambda h, i, where: (i * (1 - h) + (size - 1) * h, 0)),
                pl.BlockSpec((share, depth), lambda h, i, where: (i * h, 0)),
                pl.BlockSpec((depth, columns), lambda h, i, where: (0, 0)),
            ],
            out_specs=pl.BlockSpec((share, columns), place),
        ),
        compiler_params=pltpu.CompilerParams(vmem_limit_bytes=VMEM),
        cost_estimate=cost(2 * half, depth, columns),
        name="down_both",
    )(where, mine, theirs, weight)


def expert_rows(where, rows_in, up, down, one_step):
    size = lax.axis_size("tp")
    arrived = turned(their_half(where, rows_in, up), "role", 1)
    if one_step:
        own, rounded = own_half(where, rows_in, up, arrived, 1)
        pieces = [turned(rounded, "tp", step) for step in (2, 1, 3)]
    else:
        own, *pieces = own_half(where, rows_in, up, arrived, size)
        pieces = [turned(pieces[step - 1], "tp", step) for step in (2, 1, 3)]
    for piece in pieces:
        own = own + piece.astype(jnp.float32)
    mine = jax.nn.silu(own).astype(jnp.bfloat16)
    if not one_step:
        others = {step: turned(mine, "tp", step) for step in (2, 1, 3)}
        mine = jnp.concatenate([mine] + [others[step] for step in range(1, size)], axis=0)
    theirs = turned(mine, "role", 1)
    return down_both(where, mine, theirs, down, 1 if one_step else size)


def shards(
    q_latent,
    key_value_cache,
    cache_lengths,
    hidden,
    expert_ids,
    route_logits,
    up_weight,
    down_weight,
):
    rows, width = hidden.shape
    owners = lax.axis_size("grp")
    experts = jnp.arange(EXPERTS, dtype=jnp.int32)
    where = jnp.stack([lax.axis_index("role"), lax.axis_index("tp")]).astype(jnp.int32)
    up = up_weight[0]
    down = down_weight[0]

    named = expert_ids[:, None, :] == experts[None, :, None]
    named_any = jnp.any(named, axis=2)
    row_numbers = jnp.arange(rows, dtype=jnp.int32)
    lower = (row_numbers[None, :] < row_numbers[:, None]).astype(jnp.bfloat16)
    before = jnp.dot(
        lower, named_any.astype(jnp.bfloat16), preferred_element_type=jnp.float32
    ).astype(jnp.int32)
    rank = jnp.where(named_any, before, -1)
    rank_by_expert = rank.T

    def exchanged(value, count):
        return lax.all_to_all(
            value.reshape(owners, count, width), "grp", split_axis=0, concat_axis=0, tiled=True
        ).reshape(owners * count, width)

    def outgoing(part):
        slots = jnp.arange(*part, dtype=jnp.int32)
        placed = rank_by_expert[:, None, :] == slots[None, :, None]
        placed = placed.reshape(-1, rows).astype(jnp.bfloat16)
        return jnp.dot(placed, hidden, preferred_element_type=jnp.float32).astype(jnp.bfloat16)

    def weights(part):
        slots = jnp.arange(*part, dtype=jnp.int32)
        taken = rank[:, :, None] == slots[None, None, :]
        return jnp.concatenate(
            two_halves(jnp.where(taken, weight_of[:, :, None], 0.0).reshape(rows, -1)), axis=0
        )

    counts = [last - first for first, last in PARTS]
    first_in = exchanged(outgoing(PARTS[0]), counts[0])

    packed = attention_part(q_latent, key_value_cache, cache_lengths)
    everything = lax.all_gather(packed, "tp")

    sigmoid_terms = jax.nn.sigmoid(route_logits)
    route_weights = 2.5 * sigmoid_terms / jnp.sum(sigmoid_terms, axis=-1, keepdims=True)
    weight_of = jnp.sum(jnp.where(named, route_weights[:, None, :], 0.0), axis=2)
    weights_of = [weights(part) for part in PARTS]

    second_out, first_in, *weights_of, packed = lax.optimization_barrier(
        (outgoing(PARTS[1]), first_in, *weights_of, packed)
    )
    second_in = exchanged(second_out, counts[1])
    first_out = expert_rows(where, first_in, up, down, True)
    second_in, first_out = lax.optimization_barrier((second_in, first_out))
    first_back = exchanged(first_out, counts[0])
    second_out = expert_rows(where, second_in, up, down, False)
    second_back = exchanged(second_out, counts[1])

    everything, second_out = lax.optimization_barrier((everything, second_out))
    attn_context = attention_join(everything, q_latent.shape[1] // lax.axis_size("tp"))
    result = jnp.dot(weights_of[0], first_back, preferred_element_type=jnp.float32)
    result = result + jnp.dot(weights_of[1], second_back, preferred_element_type=jnp.float32)
    moe_output = (result[:rows] + result[rows:]).astype(jnp.bfloat16)
    return (attn_context, moe_output)


def solution(mesh):
    return jax.shard_map(
        shards,
        mesh=mesh,
        in_specs=(
            P(("role", "grp"), None, None),
            P(("role", "grp"), "tp", None),
            P(("role", "grp")),
            P("grp", ("role", "tp")),
            P("grp", None),
            P("grp", None),
            P("grp", ("role", "tp"), None),
            P("grp", None, ("role", "tp")),
        ),
        out_specs=(P(("role", "grp"), "tp", None), P("grp", ("role", "tp"))),
        check_vma=False,
    )
```

time: 267 us -> 241 us (0.903)
  the two profiles are of different devices: /device:TPU:22 before, /device:TPU:24 now
where the time goes in v2:
time: 241 us; the launch traced here: 240 us
  waiting for transfers between devices  97.9 us (41%)
  starting transfers between devices  83.5 us (35%)
  Pallas kernels  18.9 us (8%)
  between operations  14.5 us (6%)
  matrix products  9.54 us (4%)
  other arithmetic  9.46 us (4%)
  local copies, waits for them, and re-layouts  6.37 us (3%)
    all_to_all x4, waiting for transfers between devices, exchanged(): lax.all_to_all(value.reshape(owners, count, width), 'grp', split_axis=0,...  58.6 us
    all_to_all x4, starting transfers between devices, exchanged(): lax.all_to_all(value.reshape(owners, count, width), 'grp', split_axis=0,...  43.2 us
    ppermute x13, starting transfers between devices, turned(): lax.ppermute(value, axis, [(k, (k + step) % size) for k in range(size)])  40.3 us
    ppermute x13, waiting for transfers between devices, turned(): lax.ppermute(value, axis, [(k, (k + step) % size) for k in range(size)])  33.2 us
    pallas_call x2, Pallas kernels, down_both(): pl.pallas_call(down_kernel, out_shape=jax.ShapeDtypeStruct((2 * half, col...  10.2 us
    all_gather x1, waiting for transfers between devices, shards(): everything = lax.all_gather(packed, 'tp')  6.06 us
  transfers between devices with their start and end apart: 18, of which 14 were waited for; matrix products, arithmetic and copies ran while one was open for 7% of the time, Pallas kernels for 5%

profile of v2, /device:TPU:24, one launch (start us, length us, event | category | flops | bytes accessed | tf_op | source)
XLA Modules:
  0.0 240.1 jit_solution(8519330534809466384)
XLA Ops:
  7.2 0.8 fusion.15
  8.0 0.1 fusion.2
  8.3 2.4 fusion
  10.7 16.4 %all-to-all-start = ((bf16[64,8,896]{2,1,0:T(8,128)(2,1)}), bf16[64,8,896]{2,1,0:T(8,128)(2,1)S(1)}, u32[]{:S(2)}, u32[]{:S(2)}) async-start(bf16[64,8,896]{2,1,0:T(8,128)(2,1)} %fusion), calls=%async_computation | async-start | bytes 1835008 | tf_op jit(solution)/shard_map/all_to_all | solution.py:255
  27.3 0.2 fusion.7
  27.6 0.2 fusion.8
  27.8 0.2 bitcast_compare_fusion.1
  28.1 0.4 fusion.31
  28.5 0.2 fusion.16
  28.7 0.1 copy.30
  28.9 0.1 fusion.13
  29.0 0.1 fusion.14
  29.1 0.7 pad_maximum_fusion.2
  29.9 0.3 convolution_convert_fusion.2
  30.2 0.8 fusion.11
  31.0 0.9 pad_maximum_fusion.1
  31.8 1.9 convolution_convert_fusion
  33.7 20.3 %all-to-all-done = bf16[64,8,896]{2,1,0:T(8,128)(2,1)S(1)} async-done(((bf16[64,8,896]{2,1,0:T(8,128)(2,1)}), bf16[64,8,896]{2,1,0:T(8,128)(2,1)S(1)}, u32[]{:S(2)}, u32[]{:S(2)}) %all-to-all-start) | async-done | bytes 917536 | tf_op jit(solution)/shard_map/all_to_all | solution.py:255
  54.0 6.5 %all-to-all-start.1 = ((bf16[64,16,896]{2,1,0:T(8,128)(2,1)}), bf16[64,16,896]{2,1,0:T(8,128)(2,1)}, u32[]{:S(2)}, u32[]{:S(2)}) async-start(bf16[64,16,896]{2,1,0:T(8,128)(2,1)} %bitcast.100), calls=%async_computation.1 | async-start | bytes 3670016 | tf_op jit(solution)/shard_map/all_to_all | solution.py:255
  60.6 1.2 their_half.2
  61.9 1.9 collective-permute-start
  63.8 1.9 collective-permute-done.arrived_ref
  65.7 1.3 own_half.2
  67.0 5.1 %collective-permute-start.1 = (bf16[256,1024]{1,0:T(8,128)(2,1)S(1)}, bf16[256,1024]{1,0:T(8,128)(2,1)S(1)}, u32[]{:S(2)}, u32[]{:S(2)}) collective-permute-start(bf16[256,1024]{1,0:T(8,128)(2,1)S(1)} %get-tuple-element.18), channel_id=1, source_target_pairs={{0,2},{1,3},{2,0},{3,1},{4,6},{5,7},{6,4},{7,5},{8,10},{9,11},{10,... | collective-permute-start | bytes 1572872 | tf_op jit(solution)/shard_map/ppermute | solution.py:72
  72.0 2.5 %collective-permute-start.2 = (bf16[256,1024]{1,0:T(8,128)(2,1)S(1)}, bf16[256,1024]{1,0:T(8,128)(2,1)S(1)}, u32[]{:S(2)}, u32[]{:S(2)}) collective-permute-start(bf16[256,1024]{1,0:T(8,128)(2,1)S(1)} %get-tuple-element.18), channel_id=1, source_target_pairs={{0,1},{1,2},{2,3},{3,0},{4,5},{5,6},{6,7},{7,4},{8,9},{9,10},{10,1... | collective-permute-start | bytes 1572872 | tf_op jit(solution)/shard_map/ppermute | solution.py:72
  74.5 4.6 %collective-permute-start.3 = (bf16[256,1024]{1,0:T(8,128)(2,1)S(1)}, bf16[256,1024]{1,0:T(8,128)(2,1)S(1)}, u32[]{:S(2)}, u32[]{:S(2)}) collective-permute-start(bf16[256,1024]{1,0:T(8,128)(2,1)S(1)} %get-tuple-element.18), channel_id=1, source_target_pairs={{0,3},{1,0},{2,1},{3,2},{4,7},{5,4},{6,5},{7,6},{8,11},{9,8},{10,9... | collective-permute-start | bytes 1572872 | tf_op jit(solution)/shard_map/ppermute | solution.py:72
  79.1 6.2 %collective-permute-done.1 = bf16[256,1024]{1,0:T(8,128)(2,1)S(1)} collective-permute-done((bf16[256,1024]{1,0:T(8,128)(2,1)S(1)}, bf16[256,1024]{1,0:T(8,128)(2,1)S(1)}, u32[]{:S(2)}, u32[]{:S(2)}) %collective-permute-start.1) | collective-permute-done | bytes 524320 | tf_op jit(solution)/shard_map/ppermute | solution.py:72
  85.3 10.4 %collective-permute-done.2 = bf16[256,1024]{1,0:T(8,128)(2,1)S(1)} collective-permute-done((bf16[256,1024]{1,0:T(8,128)(2,1)S(1)}, bf16[256,1024]{1,0:T(8,128)(2,1)S(1)}, u32[]{:S(2)}, u32[]{:S(2)}) %collective-permute-start.2) | collective-permute-done | bytes 524320 | tf_op jit(solution)/shard_map/ppermute | solution.py:72
  95.8 0.4 multiply_convert_fusion.mine_ref
  96.3 1.9 collective-permute-start.4
  98.2 1.9 collective-permute-done.4.theirs_ref
  100.1 2.8 %down_both.2 = bf16[512,896]{1,0:T(8,128)(2,1)} custom-call(s32[2]{0:T(128)S(1)} %pad_add_fusion.where, bf16[256,1024]{1,0:T(8,128)(2,1)S(1)} %multiply_convert_fusion.mine_ref, bf16[256,1024]{1,0:T(8,128)(2,1)S(1)} %collective-permute-done.4.theirs_ref, bf16[1024,896]{1,0:T(8,128)(2,1)S(1)} %bitcast.98), custom_call_target="tpu_custom_call" | custom-call | flops 939524096 | bytes 3801088 | tf_op jit(solution)/shard_map/down_both/pallas_call | solution.py:189
  102.9 6.0 %all-to-all-done.1 = bf16[64,16,896]{2,1,0:T(8,128)(2,1)} async-done(((bf16[64,16,896]{2,1,0:T(8,128)(2,1)}), bf16[64,16,896]{2,1,0:T(8,128)(2,1)}, u32[]{:S(2)}, u32[]{:S(2)}) %all-to-all-start.1) | async-done | bytes 1835040 | tf_op jit(solution)/shard_map/all_to_all | solution.py:255
  108.9 3.0 %their_half.3 = bf16[512,1024]{1,0:T(8,128)(2,1)S(1)} custom-call(s32[2]{0:T(128)S(1)} %pad_add_fusion.where, bf16[1024,896]{1,0:T(8,128)(2,1)} %bitcast.15.rows_ref, bf16[896,1024]{1,0:T(8,128)(2,1)S(1)} %bitcast.94), custom_call_target="tpu_custom_call" | custom-call | flops 939524096 | bytes 3801088 | tf_op jit(solution)/shard_map/their_half/pallas_call | solution.py:94
  111.9 1.9 collective-permute-start.5
  113.8 2.6 %collective-permute-done.5.arrived_ref = bf16[512,1024]{1,0:T(8,128)(2,1)S(1)} collective-permute-done((bf16[512,1024]{1,0:T(8,128)(2,1)S(1)}, bf16[512,1024]{1,0:T(8,128)(2,1)S(1)}, u32[]{:S(2)}, u32[]{:S(2)}) %collective-permute-start.5) | collective-permute-done | bytes 1048608 | tf_op jit(solution)/shard_map/ppermute | solution.py:72
  116.4 3.1 %own_half.3 = (f32[128,1024]{1,0:T(8,128)S(1)}, bf16[128,1024]{1,0:T(8,128)(2,1)S(1)}, bf16[128,1024]{1,0:T(8,128)(2,1)S(1)}, bf16[128,1024]{1,0:T(8,128)(2,1)S(1)}) custom-call(s32[2]{0:T(128)S(1)} %pad_add_fusion.where, bf16[1024,896]{1,0:T(8,128)(2,1)} %bitcast.15.rows_ref, bf16[896,1024]{1,0:T(8,128)(2,1)S(1)} %bitcast.95, ...), custom_call_target="tpu_custom_call" | custom-call | flops 939524096 | bytes 3801088 | tf_op jit(solution)/shard_map/own_half/pallas_call | solution.py:144
  119.6 4.9 %collective-permute-start.6 = (bf16[128,1024]{1,0:T(8,128)(2,1)S(1)}, bf16[128,1024]{1,0:T(8,128)(2,1)S(1)}, u32[]{:S(2)}, u32[]{:S(2)}) collective-permute-start(bf16[128,1024]{1,0:T(8,128)(2,1)S(1)} %get-tuple-element.21), channel_id=1, source_target_pairs={{0,2},{1,3},{2,0},{3,1},{4,6},{5,7},{6,4},{7,5},{8,10},{9,11},{10,... | collective-permute-start | bytes 786440 | tf_op jit(solution)/shard_map/ppermute | solution.py:72
  124.5 2.5 %collective-permute-start.7 = (bf16[128,1024]{1,0:T(8,128)(2,1)S(1)}, bf16[128,1024]{1,0:T(8,128)(2,1)S(1)}, u32[]{:S(2)}, u32[]{:S(2)}) collective-permute-start(bf16[128,1024]{1,0:T(8,128)(2,1)S(1)} %get-tuple-element.22), channel_id=1, source_target_pairs={{0,1},{1,2},{2,3},{3,0},{4,5},{5,6},{6,7},{7,4},{8,9},{9,10},{10,1... | collective-permute-start | bytes 786440 | tf_op jit(solution)/shard_map/ppermute | solution.py:72
  127.0 4.6 %collective-permute-start.8 = (bf16[128,1024]{1,0:T(8,128)(2,1)S(1)}, bf16[128,1024]{1,0:T(8,128)(2,1)S(1)}, u32[]{:S(2)}, u32[]{:S(2)}) collective-permute-start(bf16[128,1024]{1,0:T(8,128)(2,1)S(1)} %get-tuple-element.23), channel_id=1, source_target_pairs={{0,3},{1,0},{2,1},{3,2},{4,7},{5,4},{6,5},{7,6},{8,11},{9,8},{10,9... | collective-permute-start | bytes 786440 | tf_op jit(solution)/shard_map/ppermute | solution.py:72
  131.5 7.6 %all-to-all-start.2 = ((bf16[64,8,896]{2,1,0:T(8,128)(2,1)}), bf16[64,8,896]{2,1,0:T(8,128)(2,1)}, u32[]{:S(2)}, u32[]{:S(2)}) async-start(bf16[64,8,896]{2,1,0:T(8,128)(2,1)} %bitcast.21), calls=%async_computation.2 | async-start | bytes 1835008 | tf_op jit(solution)/shard_map/all_to_all | solution.py:255
  139.2 0.7 copy-done.7
  140.0 0.7 copy-done.9
  140.7 1.5 multiply_convert_fusion.1
  142.1 2.5 %collective-permute-start.10 = (bf16[128,1024]{1,0:T(8,128)(2,1)S(1)}, bf16[128,1024]{1,0:T(8,128)(2,1)S(1)}, u32[]{:S(2)}, u32[]{:S(2)}) collective-permute-start(bf16[128,1024]{1,0:T(8,128)(2,1)S(1)} %multiply_convert_fusion.1), channel_id=1, source_target_pairs={{0,2},{1,3},{2,0},{3,1},{4,6},{5,7},{6,4},{7,5},{8,10},{9,11},{10,... | collective-permute-start | bytes 786440 | tf_op jit(solution)/shard_map/ppermute | solution.py:72
  144.7 3.3 %collective-permute-start.11 = (bf16[128,1024]{1,0:T(8,128)(2,1)S(1)}, bf16[128,1024]{1,0:T(8,128)(2,1)S(1)}, u32[]{:S(2)}, u32[]{:S(2)}) collective-permute-start(bf16[128,1024]{1,0:T(8,128)(2,1)S(1)} %multiply_convert_fusion.1), channel_id=1, source_target_pairs={{0,3},{1,0},{2,1},{3,2},{4,7},{5,4},{6,5},{7,6},{8,11},{9,8},{10,9... | collective-permute-start | bytes 786440 | tf_op jit(solution)/shard_map/ppermute | solution.py:72
  148.0 2.5 %collective-permute-start.9 = (bf16[128,1024]{1,0:T(8,128)(2,1)S(1)}, bf16[128,1024]{1,0:T(8,128)(2,1)S(1)}, u32[]{:S(2)}, u32[]{:S(2)}) collective-permute-start(bf16[128,1024]{1,0:T(8,128)(2,1)S(1)} %multiply_convert_fusion.1), channel_id=1, source_target_pairs={{0,1},{1,2},{2,3},{3,0},{4,5},{5,6},{6,7},{7,4},{8,9},{9,10},{10,1... | collective-permute-start | bytes 786440 | tf_op jit(solution)/shard_map/ppermute | solution.py:72
  150.5 2.2 collective-permute-done.10
  152.7 3.2 %collective-permute-done.11 = bf16[128,1024]{1,0:T(8,128)(2,1)S(1)} collective-permute-done((bf16[128,1024]{1,0:T(8,128)(2,1)S(1)}, bf16[128,1024]{1,0:T(8,128)(2,1)S(1)}, u32[]{:S(2)}, u32[]{:S(2)}) %collective-permute-start.11) | collective-permute-done | bytes 262176 | tf_op jit(solution)/shard_map/ppermute | solution.py:72
  155.9 2.2 collective-permute-done.9
  158.2 2.1 collective-permute-start.12
  160.3 2.6 %collective-permute-done.12.theirs_ref = bf16[512,1024]{1,0:T(8,128)(2,1)} collective-permute-done((bf16[512,1024]{1,0:T(8,128)(2,1)S(1)}, bf16[512,1024]{1,0:T(8,128)(2,1)}, u32[]{:S(2)}, u32[]{:S(2)}) %collective-permute-start.12) | collective-permute-done | bytes 1048608 | tf_op jit(solution)/shard_map/ppermute | solution.py:72
  162.9 7.4 %down_both.3 = bf16[1024,896]{1,0:T(8,128)(2,1)} custom-call(s32[2]{0:T(128)S(1)} %pad_add_fusion.where, bf16[512,1024]{1,0:T(8,128)(2,1)S(1)} %pad_maximum_fusion.mine_ref, bf16[512,1024]{1,0:T(8,128)(2,1)} %collective-permute-done.12.theirs_ref, bf16[1024,896]{1,0:T(8,128)(2,1)S(1)} %bitcast.99), custom_call_target="tpu_custom_call" | custom-call | flops 1879048192 | bytes 5767168 | tf_op jit(solution)/shard_map/down_both/pallas_call | solution.py:189
  170.3 12.7 %all-to-all-start.3 = ((bf16[64,16,896]{2,1,0:T(8,128)(2,1)}), bf16[64,16,896]{2,1,0:T(8,128)(2,1)S(1)}, u32[]{:S(2)}, u32[]{:S(2)}) async-start(bf16[64,16,896]{2,1,0:T(8,128)(2,1)} %bitcast.23), calls=%async_computation.3 | async-start | bytes 3670016 | tf_op jit(solution)/shard_map/all_to_all | solution.py:255
  183.0 6.1 %all-gather.3.cloned.1.call-done = bf16[8,128,640]{2,1,0:T(8,128)(2,1)} async-done(((bf16[2,128,640]{2,1,0:T(8,128)(2,1)}), bf16[8,128,640]{2,1,0:T(8,128)(2,1)}) %all-gather.3.cloned.1.call-update) | async-done | bytes 1310736 | tf_op jit(solution)/shard_map/all_gather | solution.py:276
  189.0 2.3 copy.31
  191.4 2.7 %fusion.3 = f32[256,896]{1,0:T(8,128)} fusion(bf16[256,512]{0,1:T(8,128)(2,1)} %pad_maximum_fusion.2, bf16[64,8,896]{2,1,0:T(8,128)(2,1)} %all-to-all-done.2), kind=kOutput, calls=%fused_computation.12 | convolution fusion | flops 234881024 | bytes 2097152 | tf_op jit(solution)/shard_map/dot_general | solution.py:295
  194.0 1.4 constant_dynamic-slice_fusion
  195.6 1.9 multiply_reduce_fusion
  197.5 0.2 divide_convert_fusion
  197.7 0.8 copy.32
  198.5 32.3 %all-to-all-done.3 = bf16[64,16,896]{2,1,0:T(8,128)(2,1)S(1)} async-done(((bf16[64,16,896]{2,1,0:T(8,128)(2,1)}), bf16[64,16,896]{2,1,0:T(8,128)(2,1)S(1)}, u32[]{:S(2)}, u32[]{:S(2)}) %all-to-all-start.3) | async-done | bytes 1835040 | tf_op jit(solution)/shard_map/all_to_all | solution.py:255
  230.7 1.8 convolution_add_fusion
  232.5 0.7 fusion.10
  (50 shorter events, 0.9 us)
Async XLA Ops:
  7.2 20.9 %copy-start = (bf16[2,128,576]{1,2,0:T(8,128)(2,1)S(1)}, bf16[2,128,576]{1,2,0:T(8,128)(2,1)}, u32[]{:S(2)}) copy-start(bf16[2,128,576]{1,2,0:T(8,128)(2,1)} %param.8) | copy-start | bytes 884740
  7.2 20.0 %copy-start.10 = (s32[128,8]{0,1:T(8,128)S(1)}, s32[128,8]{0,1:T(8,128)}, u32[]{:S(2)}) copy-start(s32[128,8]{0,1:T(8,128)} %param.12) | copy-start | bytes 12292
  7.2 19.9 %copy-start.11 = (f32[128,8]{0,1:T(8,128)S(1)}, f32[128,8]{0,1:T(8,128)}, u32[]{:S(2)}) copy-start(f32[128,8]{0,1:T(8,128)} %param.13) | copy-start | bytes 12292
  8.3 19.7 %copy-start.12 = (s32[2]{0:T(128)S(1)}, s32[2]{0:T(128)}, u32[]{:S(2)}) copy-start(s32[2]{0:T(128)} %param.10) | copy-start | bytes 28
  8.3 19.8 %copy-start.5 = (bf16[2,256,576]{1,2,0:T(8,128)(2,1)S(1)}, bf16[2,256,576]{1,2,0:T(8,128)(2,1)}, u32[]{:S(2)}) copy-start(bf16[2,256,576]{1,2,0:T(8,128)(2,1)} %param.9) | copy-start | bytes 1769476
  10.7 43.3 %all-to-all-start = ((bf16[64,8,896]{2,1,0:T(8,128)(2,1)}), bf16[64,8,896]{2,1,0:T(8,128)(2,1)S(1)}, u32[]{:S(2)}, u32[]{:S(2)}) async-start(bf16[64,8,896]{2,1,0:T(8,128)(2,1)} %fusion), calls=%async_computation | async-start | bytes 1835008 | tf_op jit(solution)/shard_map/all_to_all | solution.py:255
  28.9 3.0 %copy-start.6 = (bf16[128,896]{1,0:T(8,128)(2,1)S(1)}, bf16[128,896]{1,0:T(8,128)(2,1)}, u32[]{:S(2)}) copy-start(bf16[128,896]{1,0:T(8,128)(2,1)} %param.11) | copy-start | bytes 688132
  54.0 6.6 %copy-start.1 = (bf16[1,896,1024]{2,1,0:T(8,128)(2,1)S(1)}, bf16[1,896,1024]{2,1,0:T(8,128)(2,1)}, u32[]{:S(2)}) copy-start(bf16[1,896,1024]{2,1,0:T(8,128)(2,1)} %param.14) | copy-start | bytes 5505028
  54.0 54.8 %all-to-all-start.1 = ((bf16[64,16,896]{2,1,0:T(8,128)(2,1)}), bf16[64,16,896]{2,1,0:T(8,128)(2,1)}, u32[]{:S(2)}, u32[]{:S(2)}) async-start(bf16[64,16,896]{2,1,0:T(8,128)(2,1)} %bitcast.100), calls=%async_computation.1 | async-start | bytes 3670016 | tf_op jit(solution)/shard_map/all_to_all | solution.py:255
  61.9 3.8 %collective-permute-start = (bf16[256,1024]{1,0:T(8,128)(2,1)S(1)}, bf16[256,1024]{1,0:T(8,128)(2,1)S(1)}, u32[]{:S(2)}, u32[]{:S(2)}) collective-permute-start(bf16[256,1024]{1,0:T(8,128)(2,1)S(1)} %their_half.2), channel_id=1, source_target_pairs={{0,256},{256,0},{1,257},{257,1},{2,258},{258,2},{3,259},{259,3},{4... | collective-permute-start | bytes 1572872 | tf_op jit(solution)/shard_map/ppermute | solution.py:72
  67.0 33.1 %copy-start.2 = (bf16[1,1024,896]{2,1,0:T(8,128)(2,1)S(1)}, bf16[1,1024,896]{2,1,0:T(8,128)(2,1)}, u32[]{:S(2)}) copy-start(bf16[1,1024,896]{2,1,0:T(8,128)(2,1)} %param.15) | copy-start | bytes 5505028
  67.0 18.3 %collective-permute-start.1 = (bf16[256,1024]{1,0:T(8,128)(2,1)S(1)}, bf16[256,1024]{1,0:T(8,128)(2,1)S(1)}, u32[]{:S(2)}, u32[]{:S(2)}) collective-permute-start(bf16[256,1024]{1,0:T(8,128)(2,1)S(1)} %get-tuple-element.18), channel_id=1, source_target_pairs={{0,2},{1,3},{2,0},{3,1},{4,6},{5,7},{6,4},{7,5},{8,10},{9,11},{10,... | collective-permute-start | bytes 1572872 | tf_op jit(solution)/shard_map/ppermute | solution.py:72
  72.0 23.7 %collective-permute-start.2 = (bf16[256,1024]{1,0:T(8,128)(2,1)S(1)}, bf16[256,1024]{1,0:T(8,128)(2,1)S(1)}, u32[]{:S(2)}, u32[]{:S(2)}) collective-permute-start(bf16[256,1024]{1,0:T(8,128)(2,1)S(1)} %get-tuple-element.18), channel_id=1, source_target_pairs={{0,1},{1,2},{2,3},{3,0},{4,5},{5,6},{6,7},{7,4},{8,9},{9,10},{10,1... | collective-permute-start | bytes 1572872 | tf_op jit(solution)/shard_map/ppermute | solution.py:72
  74.5 21.3 %collective-permute-start.3 = (bf16[256,1024]{1,0:T(8,128)(2,1)S(1)}, bf16[256,1024]{1,0:T(8,128)(2,1)S(1)}, u32[]{:S(2)}, u32[]{:S(2)}) collective-permute-start(bf16[256,1024]{1,0:T(8,128)(2,1)S(1)} %get-tuple-element.18), channel_id=1, source_target_pairs={{0,3},{1,0},{2,1},{3,2},{4,7},{5,4},{6,5},{7,6},{8,11},{9,8},{10,9... | collective-permute-start | bytes 1572872 | tf_op jit(solution)/shard_map/ppermute | solution.py:72
  96.3 3.8 %collective-permute-start.4 = (bf16[256,1024]{1,0:T(8,128)(2,1)S(1)}, bf16[256,1024]{1,0:T(8,128)(2,1)S(1)}, u32[]{:S(2)}, u32[]{:S(2)}) collective-permute-start(bf16[256,1024]{1,0:T(8,128)(2,1)S(1)} %multiply_convert_fusion.mine_ref), channel_id=1, source_target_pairs={{0,256},{256,0},{1,257},{257,1},{2,258},{258,2},{3,259},{259,3},{4... | collective-permute-start | bytes 1572872 | tf_op jit(solution)/shard_map/ppermute | solution.py:72
  111.9 4.6 %collective-permute-start.5 = (bf16[512,1024]{1,0:T(8,128)(2,1)S(1)}, bf16[512,1024]{1,0:T(8,128)(2,1)S(1)}, u32[]{:S(2)}, u32[]{:S(2)}) collective-permute-start(bf16[512,1024]{1,0:T(8,128)(2,1)S(1)} %their_half.3), channel_id=1, source_target_pairs={{0,256},{256,0},{1,257},{257,1},{2,258},{258,2},{3,259},{259,3},{4... | collective-permute-start | bytes 3145736 | tf_op jit(solution)/shard_map/ppermute | solution.py:72
  119.6 19.6 %collective-permute-start.6 = (bf16[128,1024]{1,0:T(8,128)(2,1)S(1)}, bf16[128,1024]{1,0:T(8,128)(2,1)S(1)}, u32[]{:S(2)}, u32[]{:S(2)}) collective-permute-start(bf16[128,1024]{1,0:T(8,128)(2,1)S(1)} %get-tuple-element.21), channel_id=1, source_target_pairs={{0,2},{1,3},{2,0},{3,1},{4,6},{5,7},{6,4},{7,5},{8,10},{9,11},{10,... | collective-permute-start | bytes 786440 | tf_op jit(solution)/shard_map/ppermute | solution.py:72
  124.5 14.7 %collective-permute-start.7 = (bf16[128,1024]{1,0:T(8,128)(2,1)S(1)}, bf16[128,1024]{1,0:T(8,128)(2,1)S(1)}, u32[]{:S(2)}, u32[]{:S(2)}) collective-permute-start(bf16[128,1024]{1,0:T(8,128)(2,1)S(1)} %get-tuple-element.22), channel_id=1, source_target_pairs={{0,1},{1,2},{2,3},{3,0},{4,5},{5,6},{6,7},{7,4},{8,9},{9,10},{10,1... | collective-permute-start | bytes 786440 | tf_op jit(solution)/shard_map/ppermute | solution.py:72
  127.0 12.2 %collective-permute-start.8 = (bf16[128,1024]{1,0:T(8,128)(2,1)S(1)}, bf16[128,1024]{1,0:T(8,128)(2,1)S(1)}, u32[]{:S(2)}, u32[]{:S(2)}) collective-permute-start(bf16[128,1024]{1,0:T(8,128)(2,1)S(1)} %get-tuple-element.23), channel_id=1, source_target_pairs={{0,3},{1,0},{2,1},{3,2},{4,7},{5,4},{6,5},{7,6},{8,11},{9,8},{10,9... | collective-permute-start | bytes 786440 | tf_op jit(solution)/shard_map/ppermute | solution.py:72
  131.5 38.8 %all-to-all-start.2 = ((bf16[64,8,896]{2,1,0:T(8,128)(2,1)}), bf16[64,8,896]{2,1,0:T(8,128)(2,1)}, u32[]{:S(2)}, u32[]{:S(2)}) async-start(bf16[64,8,896]{2,1,0:T(8,128)(2,1)} %bitcast.21), calls=%async_computation.2 | async-start | bytes 1835008 | tf_op jit(solution)/shard_map/all_to_all | solution.py:255
  139.1 49.9 %all-gather.3.cloned.1.call-start = ((), (), s32[]{:S(2)}) async-start(), calls=%async_computation.4 | async-start | bytes 1638400 | tf_op jit(solution)/shard_map/all_gather | solution.py:276
  139.2 0.7 copy-start.7
  139.2 0.8 copy-start.8
  140.0 0.7 copy-start.9
  140.6 22.2 %copy-start.3 = (bf16[1,1024,896]{2,1,0:T(8,128)(2,1)S(1)}, bf16[1,1024,896]{2,1,0:T(8,128)(2,1)}, u32[]{:S(2)}) copy-start(bf16[1,1024,896]{2,1,0:T(8,128)(2,1)} %param.15) | copy-start | bytes 5505028
  142.1 10.6 %collective-permute-start.10 = (bf16[128,1024]{1,0:T(8,128)(2,1)S(1)}, bf16[128,1024]{1,0:T(8,128)(2,1)S(1)}, u32[]{:S(2)}, u32[]{:S(2)}) collective-permute-start(bf16[128,1024]{1,0:T(8,128)(2,1)S(1)} %multiply_convert_fusion.1), channel_id=1, source_target_pairs={{0,2},{1,3},{2,0},{3,1},{4,6},{5,7},{6,4},{7,5},{8,10},{9,11},{10,... | collective-permute-start | bytes 786440 | tf_op jit(solution)/shard_map/ppermute | solution.py:72
  144.7 11.2 %collective-permute-start.11 = (bf16[128,1024]{1,0:T(8,128)(2,1)S(1)}, bf16[128,1024]{1,0:T(8,128)(2,1)S(1)}, u32[]{:S(2)}, u32[]{:S(2)}) collective-permute-start(bf16[128,1024]{1,0:T(8,128)(2,1)S(1)} %multiply_convert_fusion.1), channel_id=1, source_target_pairs={{0,3},{1,0},{2,1},{3,2},{4,7},{5,4},{6,5},{7,6},{8,11},{9,8},{10,9... | collective-permute-start | bytes 786440 | tf_op jit(solution)/shard_map/ppermute | solution.py:72
  148.0 10.1 %collective-permute-start.9 = (bf16[128,1024]{1,0:T(8,128)(2,1)S(1)}, bf16[128,1024]{1,0:T(8,128)(2,1)S(1)}, u32[]{:S(2)}, u32[]{:S(2)}) collective-permute-start(bf16[128,1024]{1,0:T(8,128)(2,1)S(1)} %multiply_convert_fusion.1), channel_id=1, source_target_pairs={{0,1},{1,2},{2,3},{3,0},{4,5},{5,6},{6,7},{7,4},{8,9},{9,10},{10,1... | collective-permute-start | bytes 786440 | tf_op jit(solution)/shard_map/ppermute | solution.py:72
  158.2 4.7 %collective-permute-start.12 = (bf16[512,1024]{1,0:T(8,128)(2,1)S(1)}, bf16[512,1024]{1,0:T(8,128)(2,1)}, u32[]{:S(2)}, u32[]{:S(2)}) collective-permute-start(bf16[512,1024]{1,0:T(8,128)(2,1)S(1)} %pad_maximum_fusion.mine_ref), channel_id=1, source_target_pairs={{0,256},{256,0},{1,257},{257,1},{2,258},{258,2},{3,259},{259,3},{4... | collective-permute-start | bytes 3145736 | tf_op jit(solution)/shard_map/ppermute | solution.py:72
  170.3 60.5 %all-to-all-start.3 = ((bf16[64,16,896]{2,1,0:T(8,128)(2,1)}), bf16[64,16,896]{2,1,0:T(8,128)(2,1)S(1)}, u32[]{:S(2)}, u32[]{:S(2)}) async-start(bf16[64,16,896]{2,1,0:T(8,128)(2,1)} %bitcast.23), calls=%async_computation.3 | async-start | bytes 3670016 | tf_op jit(solution)/shard_map/all_to_all | solution.py:255
  195.5 35.3 %copy-start.4 = (f32[256,896]{1,0:T(8,128)S(1)}, f32[256,896]{1,0:T(8,128)}, u32[]{:S(2)}) copy-start(f32[256,896]{1,0:T(8,128)} %fusion.3) | copy-start | bytes 2752516
Sparse Core Ops, SparseCore 0:
  160.4 28.5 all-gather.2

commit v3 on v2

--- a/solution.py
+++ b/solution.py
@@ -12,8 +12,8 @@
 QK_NOPE = 128
 EXPERTS = 64
 CAP = 24
-PARTS = ((0, 8), (8, 24))
-VMEM = 40 * 1024 * 1024
+FIRST = 8
+VMEM = 32 * 1024 * 1024
 LANES = 128
 
 NEGATIVE = -1e30
@@ -53,10 +53,8 @@
     return jnp.concatenate([context_total.astype(jnp.bfloat16), stats], axis=-1)
 
 
-def attention_join(everything, head_group):
-    first = lax.axis_index("tp") * head_group
-    mine = lax.dynamic_slice_in_dim(everything, first, head_group, 2)
-    mine = lax.optimization_barrier(mine)
+def attention_join(pieces):
+    mine = jnp.stack(pieces)
     context = mine[..., :KEY_VALUE_LATENT].astype(jnp.float32)
     stats = mine[..., KEY_VALUE_LATENT : KEY_VALUE_LATENT + 3].astype(jnp.float32)
     shift = stats[..., 0]
@@ -205,23 +203,127 @@
     )(where, mine, theirs, weight)
 
 
-def expert_rows(where, rows_in, up, down, one_step):
-    size = lax.axis_size("tp")
+def wide_kernel(where, rows_ref, weight_ref, other_ref, own_ref, *rest):
+    piece_refs, total = rest[:-1], rest[-1]
+    tile = rows_ref.shape[0]
+    depth = weight_ref.shape[0]
+    share = own_ref.shape[0]
+    size = total.shape[0] // share
+    step = pl.program_id(0)
+    here = pl.ds(pl.multiple_of(step * tile, tile), tile)
+    total[here, :] = jnp.dot(
+        rows_ref[:, :depth], weight_ref[...], preferred_element_type=jnp.float32
+    ) + jnp.dot(rows_ref[:, depth:], other_ref[...], preferred_element_type=jnp.float32)
+
+    @pl.when(step == pl.num_programs(0) - 1)
+    def _():
+        for ahead in range(size):
+            place = lax.rem(where[1] + ahead, size)
+            piece = total[pl.ds(pl.multiple_of(place * share, share), share), :]
+            if ahead == 0:
+                own_ref[...] = piece
+            else:
+                piece_refs[ahead - 1][...] = piece.astype(jnp.bfloat16)
+
+
+def wide_product(where, rows_in, weight, other, size):
+    rows, width = rows_in.shape
+    depth, columns = weight.shape
+    tile = 256
+    share = rows // size
+    return pl.pallas_call(
+        wide_kernel,
+        out_shape=[jax.ShapeDtypeStruct((share, columns), jnp.float32)]
+        + [jax.ShapeDtypeStruct((share, columns), jnp.bfloat16)] * (size - 1),
+        grid_spec=pltpu.PrefetchScalarGridSpec(
+            num_scalar_prefetch=1,
+            grid=(rows // tile,),
+            in_specs=[
+                pl.BlockSpec((tile, width), lambda i, where: (i, 0)),
+                pl.BlockSpec((depth, columns), lambda i, where: (0, 0)),
+                pl.BlockSpec((depth, columns), lambda i, where: (0, 0)),
+            ],
+            out_specs=[pl.BlockSpec((share, columns), lambda i, where: (0, 0))] * size,
+            scratch_shapes=[pltpu.VMEM((rows, columns), jnp.float32)],
+        ),
+        compiler_params=pltpu.CompilerParams(vmem_limit_bytes=VMEM),
+        cost_estimate=cost(rows, width, columns),
+        name="wide_product",
+    )(where, rows_in, weight, other)
+
+
+def down_half_kernel(where, rows_ref, weight_ref, *rest):
+    out_ref = rest[-1]
+    sources, _, slots, columns = out_ref.shape
+    size = 4
+    share = sources // size
+    together = rows_ref.shape[0] // (share * slots)
+    made = jnp.dot(rows_ref[...], weight_ref[...], preferred_element_type=jnp.float32)
+    for k in range(together):
+        back = pl.program_id(0) * together + k
+        place = lax.rem(where[1] + size - back, size)
+        piece = made[k * share * slots : (k + 1) * share * slots]
+        out_ref[pl.ds(place * share, share), 0] = piece.reshape(share, slots, columns).astype(
+            out_ref.dtype
+        )
+
+
+def down_half(where, core, rows_in, weight, made, sources):
+    rows, depth = rows_in.shape
+    columns = weight.shape[1]
+    slots = rows // sources
+    tile = rows // 2
+    in_specs = [
+        pl.BlockSpec((tile, depth), lambda i, where: (i, 0)),
+        pl.BlockSpec((depth, columns), lambda i, where: (0, 0)),
+    ]
+    inputs = [rows_in, weight]
+    aliases = {}
+    if made is not None:
+        in_specs.append(pl.BlockSpec(memory_space=pl.ANY))
+        inputs.append(made)
+        aliases = {3: 0}
+
+    def half(i, where):
+        return 0, where[0] + core - 2 * where[0] * core, 0, 0
+
+    return pl.pallas_call(
+        down_half_kernel,
+        out_shape=jax.ShapeDtypeStruct((sources, 2, slots, columns), jnp.bfloat16),
+        grid_spec=pltpu.PrefetchScalarGridSpec(
+            num_scalar_prefetch=1,
+            grid=(rows // tile,),
+            in_specs=in_specs,
+            out_specs=pl.BlockSpec((sources, 1, slots, columns), half),
+        ),
+        input_output_aliases=aliases,
+        compiler_params=pltpu.CompilerParams(vmem_limit_bytes=VMEM),
+        cost_estimate=cost(rows, depth, columns),
+        name="down_half",
+    )(where, *inputs)
+
+
+def narrow_rows(where, rows_in, up, down):
     arrived = turned(their_half(where, rows_in, up), "role", 1)
-    if one_step:
-        own, rounded = own_half(where, rows_in, up, arrived, 1)
-        pieces = [turned(rounded, "tp", step) for step in (2, 1, 3)]
-    else:
-        own, *pieces = own_half(where, rows_in, up, arrived, size)
-        pieces = [turned(pieces[step - 1], "tp", step) for step in (2, 1, 3)]
+    own, rounded = own_half(where, rows_in, up, arrived, 1)
+    pieces = [turned(rounded, "tp", step) for step in (2, 1, 3)]
     for piece in pieces:
         own = own + piece.astype(jnp.float32)
     mine = jax.nn.silu(own).astype(jnp.bfloat16)
-    if not one_step:
-        others = {step: turned(mine, "tp", step) for step in (2, 1, 3)}
-        mine = jnp.concatenate([mine] + [others[step] for step in range(1, size)], axis=0)
+    return down_both(where, mine, turned(mine, "role", 1), down, 1)
+
+
+def wide_rows(where, rows_in, up, other_up, down, sources):
+    size = lax.axis_size("tp")
+    own, *pieces = wide_product(where, rows_in, up, other_up, size)
+    for step in (2, 1, 3):
+        own = own + turned(pieces[step - 1], "tp", step).astype(jnp.float32)
+    mine = jax.nn.silu(own).astype(jnp.bfloat16)
+    others = {step: turned(mine, "tp", step) for step in (2, 1, 3)}
+    mine = jnp.concatenate([mine] + [others[step] for step in range(1, size)], axis=0)
     theirs = turned(mine, "role", 1)
-    return down_both(where, mine, theirs, down, 1 if one_step else size)
+    made = down_half(where, 0, mine, down, None, sources)
+    return down_half(where, 1, theirs, down, made, sources)
 
 
 def shards(
@@ -251,47 +353,60 @@
     rank = jnp.where(named_any, before, -1)
     rank_by_expert = rank.T
 
-    def exchanged(value, count):
-        return lax.all_to_all(
-            value.reshape(owners, count, width), "grp", split_axis=0, concat_axis=0, tiled=True
-        ).reshape(owners * count, width)
-
-    def outgoing(part):
-        slots = jnp.arange(*part, dtype=jnp.int32)
+    def exchanged(value):
+        return lax.all_to_all(value, "grp", split_axis=0, concat_axis=0, tiled=True)
+
+    def outgoing(first, count, source):
+        slots = first + jnp.arange(count, dtype=jnp.int32)
         placed = rank_by_expert[:, None, :] == slots[None, :, None]
         placed = placed.reshape(-1, rows).astype(jnp.bfloat16)
-        return jnp.dot(placed, hidden, preferred_element_type=jnp.float32).astype(jnp.bfloat16)
-
-    def weights(part):
-        slots = jnp.arange(*part, dtype=jnp.int32)
+        made = jnp.dot(placed, source, preferred_element_type=jnp.float32).astype(jnp.bfloat16)
+        return made.reshape(owners, count, source.shape[1])
+
+    def weights(first, last):
+        slots = jnp.arange(first, last, dtype=jnp.int32)
         taken = rank[:, :, None] == slots[None, None, :]
         return jnp.concatenate(
             two_halves(jnp.where(taken, weight_of[:, :, None], 0.0).reshape(rows, -1)), axis=0
         )
 
-    counts = [last - first for first, last in PARTS]
-    first_in = exchanged(outgoing(PARTS[0]), counts[0])
-
-    packed = attention_part(q_latent, key_value_cache, cache_lengths)
-    everything = lax.all_gather(packed, "tp")
+    first_out = outgoing(0, FIRST, hidden)
+    first_out, hidden = lax.optimization_barrier((first_out, hidden))
+    first_in = exchanged(first_out)
+
+    wide = jnp.concatenate([hidden, turned(hidden, "role", 1)], axis=1)
 
     sigmoid_terms = jax.nn.sigmoid(route_logits)
     route_weights = 2.5 * sigmoid_terms / jnp.sum(sigmoid_terms, axis=-1, keepdims=True)
     weight_of = jnp.sum(jnp.where(named, route_weights[:, None, :], 0.0), axis=2)
-    weights_of = [weights(part) for part in PARTS]
-
-    second_out, first_in, *weights_of, packed = lax.optimization_barrier(
-        (outgoing(PARTS[1]), first_in, *weights_of, packed)
-    )
-    second_in = exchanged(second_out, counts[1])
-    first_out = expert_rows(where, first_in, up, down, True)
+    weights_of = [weights(0, FIRST), weights(FIRST, CAP)]
+
+    half = (CAP - FIRST) // 2
+    begin = FIRST + where[0] * half
+    second_out, first_in, passed_up, *weights_of = lax.optimization_barrier(
+        (outgoing(begin, half, wide), first_in, up, *weights_of)
+    )
+    second_in = exchanged(second_out)
+    other_up = turned(passed_up, "role", 1)
+    first_out = narrow_rows(where, first_in.reshape(-1, width), up, down)
     second_in, first_out = lax.optimization_barrier((second_in, first_out))
-    first_back = exchanged(first_out, counts[0])
-    second_out = expert_rows(where, second_in, up, down, False)
-    second_back = exchanged(second_out, counts[1])
-
-    everything, second_out = lax.optimization_barrier((everything, second_out))
-    attn_context = attention_join(everything, q_latent.shape[1] // lax.axis_size("tp"))
+    first_back = exchanged(first_out.reshape(owners, FIRST, width))
+    second_out = wide_rows(where, second_in.reshape(-1, 2 * width), up, other_up, down, owners)
+    second_out, first_back, q_latent = lax.optimization_barrier((second_out, first_back, q_latent))
+    second_back = exchanged(second_out)
+
+    packed = attention_part(q_latent, key_value_cache, cache_lengths)
+    size = lax.axis_size("tp")
+    heads = q_latent.shape[1] // size
+    place = lax.axis_index("tp")
+    pieces = [
+        lax.dynamic_slice_in_dim(packed, (place + step) % size * heads, heads, 1)
+        for step in range(size)
+    ]
+    pieces = [pieces[0]] + [turned(pieces[step], "tp", step) for step in (2, 1, 3)]
+    attn_context = attention_join(pieces)
+    first_back = first_back.reshape(-1, width)
+    second_back = second_back.reshape(-1, width)
     result = jnp.dot(weights_of[0], first_back, preferred_element_type=jnp.float32)
     result = result + jnp.dot(weights_of[1], second_back, preferred_element_type=jnp.float32)
     moe_output = (result[:rows] + result[rows:]).astype(jnp.bfloat16)

time: 241 us -> 222 us (0.921)
  starting transfers between devices: 83.5 us -> 99 us
  waiting for transfers between devices: 97.9 us -> 84.6 us
  between operations: 14.5 us -> 1.2 us
  local copies, waits for them, and re-layouts: 6.37 us -> 0.51 us
    ppermute x13 -> x17, starting transfers between devices: 40.3 us -> 53 us  [turned(): lax.ppermute(value, axis, [(k, (k + step) % size) for k in range(size)])]
    pallas_call x0 -> x3, Pallas kernels: none -> 11.4 us  [the longest x2 5.91 us: down_half(): pl.pallas_call(down_half_kernel, out_shape=jax.ShapeDtypeStruct((sources,...]
    pallas_call x2 -> x1, Pallas kernels: 10.2 us -> 2.83 us  [down_both(): pl.pallas_call(down_kernel, out_shape=jax.ShapeDtypeStruct((2 * half, col...]
    all_gather x1 -> x0, waiting for transfers between devices: 6.06 us -> none  [shards(): everything = lax.all_gather(packed, 'tp')]
    all_to_all x4, waiting for transfers between devices: 58.6 us -> 54.8 us  [exchanged(): return lax.all_to_all(value, 'grp', split_axis=0, concat_axis=0, tiled=True)]
    ppermute x13 -> x17, waiting for transfers between devices: 33.2 us -> 29.8 us  [turned(): lax.ppermute(value, axis, [(k, (k + step) % size) for k in range(size)])]
    all_to_all x4, starting transfers between devices: 43.2 us -> 45.9 us  [exchanged(): return lax.all_to_all(value, 'grp', split_axis=0, concat_axis=0, tiled=True)]
  transfers between devices with their start and end apart: 18 -> 21, of which waited for: 14 -> 10; matrix products, arithmetic and copies ran while one was open for 7% -> 5% of each run, Pallas kernels for 5% -> 6%
where the time goes in v3:
time: 222 us; the launch traced here: 221 us
  starting transfers between devices  99 us (45%)
  waiting for transfers between devices  84.6 us (38%)
  Pallas kernels  19.8 us (9%)
  matrix products  8.52 us (4%)
  other arithmetic  7.55 us (3%)
    all_to_all x4, waiting for transfers between devices, exchanged(): return lax.all_to_all(value, 'grp', split_axis=0, concat_axis=0, tiled=True)  54.8 us
    ppermute x17, starting transfers between devices, turned(): lax.ppermute(value, axis, [(k, (k + step) % size) for k in range(size)])  53 us
    all_to_all x4, starting transfers between devices, exchanged(): return lax.all_to_all(value, 'grp', split_axis=0, concat_axis=0, tiled=True)  45.9 us
    ppermute x17, waiting for transfers between devices, turned(): lax.ppermute(value, axis, [(k, (k + step) % size) for k in range(size)])  29.8 us
    pallas_call x2, Pallas kernels, down_half(): pl.pallas_call(down_half_kernel, out_shape=jax.ShapeDtypeStruct((sources,...  5.91 us
    pallas_call x1, Pallas kernels, wide_product(): pl.pallas_call(wide_kernel, out_shape=[jax.ShapeDtypeStruct((share, colum...  5.53 us
  transfers between devices with their start and end apart: 21, of which 10 were waited for; matrix products, arithmetic and copies ran while one was open for 5% of the time, Pallas kernels for 6%

profile of v3, /device:TPU:24, one launch (start us, length us, event | category | flops | bytes accessed | tf_op | source)
XLA Modules:
  0.0 221.2 jit_solution(15073432538239502421)
XLA Ops:
  0.7 0.8 fusion.19
  1.5 0.1 fusion.3
  1.7 0.1 eq.104
  1.8 2.3 %fusion.1 = bf16[64,8,896]{2,1,0:T(8,128)(2,1)} fusion(bf16[128,896]{1,0:T(8,128)(2,1)} %param.11, s32[512]{0:T(512)S(1)} %eq.104, s32[64,128]{1,0:T(8,128)S(1)} %bitcast.84), kind=kOutput, calls=%fused_computation.3 | convolution fusion | flops 117964800 | bytes 1181696 | tf_op jit(solution)/shard_map/dot_general | solution.py:363
  4.1 16.4 %all-to-all-start = ((bf16[64,8,896]{2,1,0:T(8,128)(2,1)}), bf16[64,8,896]{2,1,0:T(8,128)(2,1)S(1)}, u32[]{:S(2)}, u32[]{:S(2)}) async-start(bf16[64,8,896]{2,1,0:T(8,128)(2,1)} %fusion.1), calls=%async_computation | async-start | bytes 1835008 | tf_op jit(solution)/shard_map/all_to_all | solution.py:357
  20.5 1.9 collective-permute-start
  22.5 0.1 eq.114
  22.6 0.1 select_reduce_fusion
  22.7 0.2 fusion.8
  22.9 0.2 fusion.9
  23.1 0.1 eq.100
  23.2 0.1 fusion.17
  23.4 0.1 fusion.18
  23.5 0.8 pad_maximum_fusion.3
  24.3 0.9 pad_maximum_fusion.1
  25.1 1.9 fusion
  27.0 20.4 %all-to-all-done = bf16[64,8,896]{2,1,0:T(8,128)(2,1)S(1)} async-done(((bf16[64,8,896]{2,1,0:T(8,128)(2,1)}), bf16[64,8,896]{2,1,0:T(8,128)(2,1)S(1)}, u32[]{:S(2)}, u32[]{:S(2)}) %all-to-all-start) | async-done | bytes 917536 | tf_op jit(solution)/shard_map/all_to_all | solution.py:357
  47.4 6.4 %all-to-all-start.1 = ((bf16[64,8,1792]{2,1,0:T(8,128)(2,1)}), bf16[64,8,1792]{2,1,0:T(8,128)(2,1)}, u32[]{:S(2)}, u32[]{:S(2)}) async-start(bf16[64,8,1792]{2,1,0:T(8,128)(2,1)} %fusion), calls=%async_computation.1 | async-start | bytes 3670016 | tf_op jit(solution)/shard_map/all_to_all | solution.py:357
  53.9 2.8 %their_half.1 = bf16[256,1024]{1,0:T(8,128)(2,1)S(1)} custom-call(s32[2]{0:T(128)S(1)} %pad_add_fusion.where, bf16[512,896]{1,0:T(8,128)(2,1)S(1)} %bitcast.81, bf16[896,1024]{1,0:T(8,128)(2,1)} %bitcast.6.weight_ref), custom_call_target="tpu_custom_call" | custom-call | flops 469762048 | bytes 2818048 | tf_op jit(solution)/shard_map/their_half/pallas_call | solution.py:92
  56.7 1.9 collective-permute-start.1
  58.6 2.4 %collective-permute-start.6 = (bf16[896,1024]{1,0:T(8,128)(2,1)}, bf16[896,1024]{1,0:T(8,128)(2,1)}, u32[]{:S(2)}, u32[]{:S(2)}) collective-permute-start(bf16[896,1024]{1,0:T(8,128)(2,1)} %bitcast.6.weight_ref), channel_id=1, source_target_pairs={{0,256},{256,0},{1,257},{257,1},{2,258},{258,2},{3,259},{259,3},{4... | collective-permute-start | bytes 5505032 | tf_op jit(solution)/shard_map/ppermute | solution.py:70
  61.0 2.8 %own_half.1 = (f32[256,1024]{1,0:T(8,128)S(1)}, bf16[256,1024]{1,0:T(8,128)(2,1)S(1)}) custom-call(s32[2]{0:T(128)S(1)} %pad_add_fusion.where, bf16[512,896]{1,0:T(8,128)(2,1)S(1)} %bitcast.82, bf16[896,1024]{1,0:T(8,128)(2,1)} %bitcast.6.weight_ref, bf16[256,1024]{1,0:T(8,128)(2,1)S(1)} %collective-permute-done.1.arrived_ref), custom_call_target="tpu_custom_call" | custom-call | flops 469762048 | bytes 2818048 | tf_op jit(solution)/shard_map/own_half/pallas_call | solution.py:142
  63.8 5.1 %collective-permute-start.2 = (bf16[256,1024]{1,0:T(8,128)(2,1)S(1)}, bf16[256,1024]{1,0:T(8,128)(2,1)S(1)}, u32[]{:S(2)}, u32[]{:S(2)}) collective-permute-start(bf16[256,1024]{1,0:T(8,128)(2,1)S(1)} %get-tuple-element.25), channel_id=1, source_target_pairs={{0,2},{1,3},{2,0},{3,1},{4,6},{5,7},{6,4},{7,5},{8,10},{9,11},{10,... | collective-permute-start | bytes 1572872 | tf_op jit(solution)/shard_map/ppermute | solution.py:70
  68.9 2.5 %collective-permute-start.3 = (bf16[256,1024]{1,0:T(8,128)(2,1)S(1)}, bf16[256,1024]{1,0:T(8,128)(2,1)S(1)}, u32[]{:S(2)}, u32[]{:S(2)}) collective-permute-start(bf16[256,1024]{1,0:T(8,128)(2,1)S(1)} %get-tuple-element.25), channel_id=1, source_target_pairs={{0,1},{1,2},{2,3},{3,0},{4,5},{5,6},{6,7},{7,4},{8,9},{9,10},{10,1... | collective-permute-start | bytes 1572872 | tf_op jit(solution)/shard_map/ppermute | solution.py:70
  71.4 4.5 %collective-permute-start.4 = (bf16[256,1024]{1,0:T(8,128)(2,1)S(1)}, bf16[256,1024]{1,0:T(8,128)(2,1)S(1)}, u32[]{:S(2)}, u32[]{:S(2)}) collective-permute-start(bf16[256,1024]{1,0:T(8,128)(2,1)S(1)} %get-tuple-element.25), channel_id=1, source_target_pairs={{0,3},{1,0},{2,1},{3,2},{4,7},{5,4},{6,5},{7,6},{8,11},{9,8},{10,9... | collective-permute-start | bytes 1572872 | tf_op jit(solution)/shard_map/ppermute | solution.py:70
  75.9 6.2 %collective-permute-done.2 = bf16[256,1024]{1,0:T(8,128)(2,1)S(1)} collective-permute-done((bf16[256,1024]{1,0:T(8,128)(2,1)S(1)}, bf16[256,1024]{1,0:T(8,128)(2,1)S(1)}, u32[]{:S(2)}, u32[]{:S(2)}) %collective-permute-start.2) | collective-permute-done | bytes 524320 | tf_op jit(solution)/shard_map/ppermute | solution.py:70
  82.2 10.2 %collective-permute-done.3 = bf16[256,1024]{1,0:T(8,128)(2,1)S(1)} collective-permute-done((bf16[256,1024]{1,0:T(8,128)(2,1)S(1)}, bf16[256,1024]{1,0:T(8,128)(2,1)S(1)}, u32[]{:S(2)}, u32[]{:S(2)}) %collective-permute-start.3) | collective-permute-done | bytes 524320 | tf_op jit(solution)/shard_map/ppermute | solution.py:70
  92.4 0.1 collective-permute-done.4
  92.5 0.5 multiply_convert_fusion.mine_ref
  93.0 1.9 collective-permute-start.5
  94.9 1.9 collective-permute-done.5.theirs_ref
  96.8 2.8 %down_both.1 = bf16[512,896]{1,0:T(8,128)(2,1)} custom-call(s32[2]{0:T(128)S(1)} %pad_add_fusion.where, bf16[256,1024]{1,0:T(8,128)(2,1)S(1)} %multiply_convert_fusion.mine_ref, bf16[256,1024]{1,0:T(8,128)(2,1)S(1)} %collective-permute-done.5.theirs_ref, bf16[1024,896]{1,0:T(8,128)(2,1)S(1)} %bitcast.78), custom_call_target="tpu_custom_call" | custom-call | flops 939524096 | bytes 3801088 | tf_op jit(solution)/shard_map/down_both/pallas_call | solution.py:187
  99.6 2.4 %all-to-all-done.1 = bf16[64,8,1792]{2,1,0:T(8,128)(2,1)} async-done(((bf16[64,8,1792]{2,1,0:T(8,128)(2,1)}), bf16[64,8,1792]{2,1,0:T(8,128)(2,1)}, u32[]{:S(2)}, u32[]{:S(2)}) %all-to-all-start.1) | async-done | bytes 1835040 | tf_op jit(solution)/shard_map/all_to_all | solution.py:357
  102.0 5.5 %wide_product.1 = (f32[128,1024]{1,0:T(8,128)S(1)}, bf16[128,1024]{1,0:T(8,128)(2,1)S(1)}, bf16[128,1024]{1,0:T(8,128)(2,1)S(1)}, bf16[128,1024]{1,0:T(8,128)(2,1)S(1)}) custom-call(s32[2]{0:T(128)S(1)} %pad_add_fusion.where, bf16[512,1792]{1,0:T(8,128)(2,1)} %bitcast.13.rows_ref, bf16[896,1024]{1,0:T(8,128)(2,1)} %bitcast.6.weight_ref, ...), custom_call_target="tpu_custom_call" | custom-call | flops 1879048192 | bytes 6553600 | tf_op jit(solution)/shard_map/wide_product/pallas_call | solution.py:234
  107.6 4.9 %collective-permute-start.7 = (bf16[128,1024]{1,0:T(8,128)(2,1)S(1)}, bf16[128,1024]{1,0:T(8,128)(2,1)}, u32[]{:S(2)}, u32[]{:S(2)}) collective-permute-start(bf16[128,1024]{1,0:T(8,128)(2,1)S(1)} %get-tuple-element.29), channel_id=1, source_target_pairs={{0,2},{1,3},{2,0},{3,1},{4,6},{5,7},{6,4},{7,5},{8,10},{9,11},{10,... | collective-permute-start | bytes 786440 | tf_op jit(solution)/shard_map/ppermute | solution.py:70
  112.5 2.5 %collective-permute-start.8 = (bf16[128,1024]{1,0:T(8,128)(2,1)S(1)}, bf16[128,1024]{1,0:T(8,128)(2,1)}, u32[]{:S(2)}, u32[]{:S(2)}) collective-permute-start(bf16[128,1024]{1,0:T(8,128)(2,1)S(1)} %get-tuple-element.30), channel_id=1, source_target_pairs={{0,1},{1,2},{2,3},{3,0},{4,5},{5,6},{6,7},{7,4},{8,9},{9,10},{10,1... | collective-permute-start | bytes 786440 | tf_op jit(solution)/shard_map/ppermute | solution.py:70
  115.0 4.6 %collective-permute-start.9 = (bf16[128,1024]{1,0:T(8,128)(2,1)S(1)}, bf16[128,1024]{1,0:T(8,128)(2,1)}, u32[]{:S(2)}, u32[]{:S(2)}) collective-permute-start(bf16[128,1024]{1,0:T(8,128)(2,1)S(1)} %get-tuple-element.31), channel_id=1, source_target_pairs={{0,3},{1,0},{2,1},{3,2},{4,7},{5,4},{6,5},{7,6},{8,11},{9,8},{10,9... | collective-permute-start | bytes 786440 | tf_op jit(solution)/shard_map/ppermute | solution.py:70
  119.6 10.3 %all-to-all-start.2 = ((bf16[64,8,896]{2,1,0:T(8,128)(2,1)}), bf16[64,8,896]{2,1,0:T(8,128)(2,1)}, u32[]{:S(2)}, u32[]{:S(2)}) async-start(bf16[64,8,896]{2,1,0:T(8,128)(2,1)} %bitcast.14), calls=%async_computation.2 | async-start | bytes 1835008 | tf_op jit(solution)/shard_map/all_to_all | solution.py:357
  130.0 1.3 multiply_convert_fusion.1
  131.3 1.9 collective-permute-start.10
  133.2 3.4 %collective-permute-start.11 = (bf16[128,1024]{1,0:T(8,128)(2,1)S(1)}, bf16[128,1024]{1,0:T(8,128)(2,1)S(1)}, u32[]{:S(2)}, u32[]{:S(2)}) collective-permute-start(bf16[128,1024]{1,0:T(8,128)(2,1)S(1)} %multiply_convert_fusion.1), channel_id=1, source_target_pairs={{0,2},{1,3},{2,0},{3,1},{4,6},{5,7},{6,4},{7,5},{8,10},{9,11},{10,... | collective-permute-start | bytes 786440 | tf_op jit(solution)/shard_map/ppermute | solution.py:70
  136.6 3.7 %collective-permute-start.12 = (bf16[128,1024]{1,0:T(8,128)(2,1)S(1)}, bf16[128,1024]{1,0:T(8,128)(2,1)S(1)}, u32[]{:S(2)}, u32[]{:S(2)}) collective-permute-start(bf16[128,1024]{1,0:T(8,128)(2,1)S(1)} %multiply_convert_fusion.1), channel_id=1, source_target_pairs={{0,3},{1,0},{2,1},{3,2},{4,7},{5,4},{6,5},{7,6},{8,11},{9,8},{10,9... | collective-permute-start | bytes 786440 | tf_op jit(solution)/shard_map/ppermute | solution.py:70
  140.3 6.7 %collective-permute-done.10 = bf16[128,1024]{1,0:T(8,128)(2,1)S(1)} collective-permute-done((bf16[128,1024]{1,0:T(8,128)(2,1)S(1)}, bf16[128,1024]{1,0:T(8,128)(2,1)S(1)}, u32[]{:S(2)}, u32[]{:S(2)}) %collective-permute-start.10) | collective-permute-done | bytes 262176 | tf_op jit(solution)/shard_map/ppermute | solution.py:70
  147.0 2.5 %collective-permute-done.12 = bf16[128,1024]{1,0:T(8,128)(2,1)S(1)} collective-permute-done((bf16[128,1024]{1,0:T(8,128)(2,1)S(1)}, bf16[128,1024]{1,0:T(8,128)(2,1)S(1)}, u32[]{:S(2)}, u32[]{:S(2)}) %collective-permute-start.12) | collective-permute-done | bytes 262176 | tf_op jit(solution)/shard_map/ppermute | solution.py:70
  149.5 1.9 collective-permute-start.13
  151.5 2.9 %down_half.2.rest_0_ = bf16[64,2,8,896]{3,2,1,0:T(8,128)(2,1)} custom-call(s32[2]{0:T(128)S(1)} %pad_add_fusion.where, bf16[512,1024]{1,0:T(8,128)(2,1)S(1)} %pad_maximum_fusion.rows_ref, bf16[1024,896]{1,0:T(8,128)(2,1)S(1)} %bitcast.79), custom_call_target="tpu_custom_call" | custom-call | flops 939524096 | bytes 3801088 | tf_op jit(solution)/shard_map/down_half/pallas_call | solution.py:290
  154.4 3.0 %down_half.3 = bf16[64,2,8,896]{3,2,1,0:T(8,128)(2,1)} custom-call(s32[2]{0:T(128)S(1)} %pad_add_fusion.where, bf16[512,1024]{1,0:T(8,128)(2,1)S(1)} %collective-permute-done.13.rows_ref, bf16[1024,896]{1,0:T(8,128)(2,1)S(1)} %bitcast.80, bf16[64,2,8,896]{3,2,1,0:T(8,128)(2,1)} %down_half.2.rest_0_), custom_call_target="tpu_custom_call", output_to_operand_aliasing={{}: (3, {})} | custom-call | flops 939524096 | bytes 3801088 | tf_op jit(solution)/shard_map/down_half/pallas_call | solution.py:290
  157.4 12.8 %all-to-all-start.3 = ((bf16[64,2,8,896]{3,2,1,0:T(8,128)(2,1)}), bf16[64,2,8,896]{3,2,1,0:T(8,128)(2,1)S(1)}, u32[]{:S(2)}, u32[]{:S(2)}) async-start(bf16[64,2,8,896]{3,2,1,0:T(8,128)(2,1)} %down_half.3), calls=%async_computation.3 | async-start | bytes 3670016 | tf_op jit(solution)/shard_map/all_to_all | solution.py:357
  170.4 0.4 fusion.35
  170.8 0.2 fusion.20
  171.0 0.1 copy.34
  171.2 0.3 convolution_convert_fusion.2
  171.6 2.8 %collective-permute-start.14 = (bf16[2,32,640]{2,1,0:T(8,128)(2,1)S(1)}, bf16[2,32,640]{2,1,0:T(8,128)(2,1)S(1)}, u32[]{:S(2)}, u32[]{:S(2)}) collective-permute-start(bf16[2,32,640]{2,1,0:T(8,128)(2,1)S(1)} %get-tuple-element.46), channel_id=1, source_target_pairs={{0,2},{1,3},{2,0},{3,1},{4,6},{5,7},{6,4},{7,5},{8,10},{9,11},{10,... | collective-permute-start | bytes 245768 | tf_op jit(solution)/shard_map/ppermute | solution.py:70
  174.4 4.5 %collective-permute-start.15 = (bf16[2,32,640]{2,1,0:T(8,128)(2,1)S(1)}, bf16[2,32,640]{2,1,0:T(8,128)(2,1)S(1)}, u32[]{:S(2)}, u32[]{:S(2)}) collective-permute-start(bf16[2,32,640]{2,1,0:T(8,128)(2,1)S(1)} %get-tuple-element.45), channel_id=1, source_target_pairs={{0,1},{1,2},{2,3},{3,0},{4,5},{5,6},{6,7},{7,4},{8,9},{9,10},{10,1... | collective-permute-start | bytes 245768 | tf_op jit(solution)/shard_map/ppermute | solution.py:70
  178.9 2.5 %collective-permute-start.16 = (bf16[2,32,640]{2,1,0:T(8,128)(2,1)S(1)}, bf16[2,32,640]{2,1,0:T(8,128)(2,1)S(1)}, u32[]{:S(2)}, u32[]{:S(2)}) collective-permute-start(bf16[2,32,640]{2,1,0:T(8,128)(2,1)S(1)} %get-tuple-element.44), channel_id=1, source_target_pairs={{0,3},{1,0},{2,1},{3,2},{4,7},{5,4},{6,5},{7,6},{8,11},{9,8},{10,9... | collective-permute-start | bytes 245768 | tf_op jit(solution)/shard_map/ppermute | solution.py:70
  181.5 1.6 fusion.4
  183.1 2.1 collective-permute-done.16
  185.3 0.1 slice_reduce_fusion.1
  185.4 0.3 slice_reduce_fusion
  185.8 0.1 multiply_reduce_fusion
  185.9 0.7 divide_convert_fusion
  186.6 32.0 %all-to-all-done.3 = bf16[64,2,8,896]{3,2,1,0:T(8,128)(2,1)S(1)} async-done(((bf16[64,2,8,896]{3,2,1,0:T(8,128)(2,1)}), bf16[64,2,8,896]{3,2,1,0:T(8,128)(2,1)S(1)}, u32[]{:S(2)}, u32[]{:S(2)}) %all-to-all-start.3) | async-done | bytes 1835040 | tf_op jit(solution)/shard_map/all_to_all | solution.py:357
  218.7 1.8 convolution_add_fusion
  220.4 0.7 fusion.11
  (46 shorter events, 0.5 us)
Async XLA Ops:
  0.6 169.7 %copy-start = (bf16[2,128,576]{1,2,0:T(8,128)(2,1)S(1)}, bf16[2,128,576]{1,2,0:T(8,128)(2,1)}, u32[]{:S(2)}) copy-start(bf16[2,128,576]{1,2,0:T(8,128)(2,1)} %param.8) | copy-start | bytes 884740
  0.6 21.9 %copy-start.5 = (s32[128,8]{0,1:T(8,128)S(1)}, s32[128,8]{0,1:T(8,128)}, u32[]{:S(2)}) copy-start(s32[128,8]{0,1:T(8,128)} %param.12) | copy-start | bytes 12292
  0.7 19.8 %copy-start.4 = (bf16[128,896]{1,0:T(8,128)(2,1)S(1)}, bf16[128,896]{1,0:T(8,128)(2,1)}, u32[]{:S(2)}) copy-start(bf16[128,896]{1,0:T(8,128)(2,1)} %param.11) | copy-start | bytes 688132
  0.7 21.9 %copy-start.6 = (f32[128,8]{0,1:T(8,128)S(1)}, f32[128,8]{0,1:T(8,128)}, u32[]{:S(2)}) copy-start(f32[128,8]{0,1:T(8,128)} %param.13) | copy-start | bytes 12292
  4.1 43.3 %all-to-all-start = ((bf16[64,8,896]{2,1,0:T(8,128)(2,1)}), bf16[64,8,896]{2,1,0:T(8,128)(2,1)S(1)}, u32[]{:S(2)}, u32[]{:S(2)}) async-start(bf16[64,8,896]{2,1,0:T(8,128)(2,1)} %fusion.1), calls=%async_computation | async-start | bytes 1835008 | tf_op jit(solution)/shard_map/all_to_all | solution.py:357
  20.5 4.6 %collective-permute-start = (bf16[128,896]{1,0:T(8,128)(2,1)S(1)}, bf16[128,896]{1,0:T(8,128)(2,1)S(1)}, u32[]{:S(2)}, u32[]{:S(2)}) collective-permute-start(bf16[128,896]{1,0:T(8,128)(2,1)S(1)} %copy-done.4), channel_id=1, source_target_pairs={{0,256},{256,0},{1,257},{257,1},{2,258},{258,2},{3,259},{259,3},{4... | collective-permute-start | bytes 688136 | tf_op jit(solution)/shard_map/ppermute | solution.py:70
  47.4 54.6 %all-to-all-start.1 = ((bf16[64,8,1792]{2,1,0:T(8,128)(2,1)}), bf16[64,8,1792]{2,1,0:T(8,128)(2,1)}, u32[]{:S(2)}, u32[]{:S(2)}) async-start(bf16[64,8,1792]{2,1,0:T(8,128)(2,1)} %fusion), calls=%async_computation.1 | async-start | bytes 3670016 | tf_op jit(solution)/shard_map/all_to_all | solution.py:357
  56.7 4.3 %collective-permute-start.1 = (bf16[256,1024]{1,0:T(8,128)(2,1)S(1)}, bf16[256,1024]{1,0:T(8,128)(2,1)S(1)}, u32[]{:S(2)}, u32[]{:S(2)}) collective-permute-start(bf16[256,1024]{1,0:T(8,128)(2,1)S(1)} %their_half.1), channel_id=1, source_target_pairs={{0,256},{256,0},{1,257},{257,1},{2,258},{258,2},{3,259},{259,3},{4... | collective-permute-start | bytes 1572872 | tf_op jit(solution)/shard_map/ppermute | solution.py:70
  58.6 43.5 %collective-permute-start.6 = (bf16[896,1024]{1,0:T(8,128)(2,1)}, bf16[896,1024]{1,0:T(8,128)(2,1)}, u32[]{:S(2)}, u32[]{:S(2)}) collective-permute-start(bf16[896,1024]{1,0:T(8,128)(2,1)} %bitcast.6.weight_ref), channel_id=1, source_target_pairs={{0,256},{256,0},{1,257},{257,1},{2,258},{258,2},{3,259},{259,3},{4... | collective-permute-start | bytes 5505032 | tf_op jit(solution)/shard_map/ppermute | solution.py:70
  63.8 33.0 %copy-start.1 = (bf16[1,1024,896]{2,1,0:T(8,128)(2,1)S(1)}, bf16[1,1024,896]{2,1,0:T(8,128)(2,1)}, u32[]{:S(2)}) copy-start(bf16[1,1024,896]{2,1,0:T(8,128)(2,1)} %param.15) | copy-start | bytes 5505028
  63.8 18.4 %collective-permute-start.2 = (bf16[256,1024]{1,0:T(8,128)(2,1)S(1)}, bf16[256,1024]{1,0:T(8,128)(2,1)S(1)}, u32[]{:S(2)}, u32[]{:S(2)}) collective-permute-start(bf16[256,1024]{1,0:T(8,128)(2,1)S(1)} %get-tuple-element.25), channel_id=1, source_target_pairs={{0,2},{1,3},{2,0},{3,1},{4,6},{5,7},{6,4},{7,5},{8,10},{9,11},{10,... | collective-permute-start | bytes 1572872 | tf_op jit(solution)/shard_map/ppermute | solution.py:70
  68.9 23.5 %collective-permute-start.3 = (bf16[256,1024]{1,0:T(8,128)(2,1)S(1)}, bf16[256,1024]{1,0:T(8,128)(2,1)S(1)}, u32[]{:S(2)}, u32[]{:S(2)}) collective-permute-start(bf16[256,1024]{1,0:T(8,128)(2,1)S(1)} %get-tuple-element.25), channel_id=1, source_target_pairs={{0,1},{1,2},{2,3},{3,0},{4,5},{5,6},{6,7},{7,4},{8,9},{9,10},{10,1... | collective-permute-start | bytes 1572872 | tf_op jit(solution)/shard_map/ppermute | solution.py:70
  71.4 21.2 %collective-permute-start.4 = (bf16[256,1024]{1,0:T(8,128)(2,1)S(1)}, bf16[256,1024]{1,0:T(8,128)(2,1)S(1)}, u32[]{:S(2)}, u32[]{:S(2)}) collective-permute-start(bf16[256,1024]{1,0:T(8,128)(2,1)S(1)} %get-tuple-element.25), channel_id=1, source_target_pairs={{0,3},{1,0},{2,1},{3,2},{4,7},{5,4},{6,5},{7,6},{8,11},{9,8},{10,9... | collective-permute-start | bytes 1572872 | tf_op jit(solution)/shard_map/ppermute | solution.py:70
  93.0 3.8 %collective-permute-start.5 = (bf16[256,1024]{1,0:T(8,128)(2,1)S(1)}, bf16[256,1024]{1,0:T(8,128)(2,1)S(1)}, u32[]{:S(2)}, u32[]{:S(2)}) collective-permute-start(bf16[256,1024]{1,0:T(8,128)(2,1)S(1)} %multiply_convert_fusion.mine_ref), channel_id=1, source_target_pairs={{0,256},{256,0},{1,257},{257,1},{2,258},{258,2},{3,259},{259,3},{4... | collective-permute-start | bytes 1572872 | tf_op jit(solution)/shard_map/ppermute | solution.py:70
  107.6 22.4 %collective-permute-start.7 = (bf16[128,1024]{1,0:T(8,128)(2,1)S(1)}, bf16[128,1024]{1,0:T(8,128)(2,1)}, u32[]{:S(2)}, u32[]{:S(2)}) collective-permute-start(bf16[128,1024]{1,0:T(8,128)(2,1)S(1)} %get-tuple-element.29), channel_id=1, source_target_pairs={{0,2},{1,3},{2,0},{3,1},{4,6},{5,7},{6,4},{7,5},{8,10},{9,11},{10,... | collective-permute-start | bytes 786440 | tf_op jit(solution)/shard_map/ppermute | solution.py:70
  112.5 17.4 %collective-permute-start.8 = (bf16[128,1024]{1,0:T(8,128)(2,1)S(1)}, bf16[128,1024]{1,0:T(8,128)(2,1)}, u32[]{:S(2)}, u32[]{:S(2)}) collective-permute-start(bf16[128,1024]{1,0:T(8,128)(2,1)S(1)} %get-tuple-element.30), channel_id=1, source_target_pairs={{0,1},{1,2},{2,3},{3,0},{4,5},{5,6},{6,7},{7,4},{8,9},{9,10},{10,1... | collective-permute-start | bytes 786440 | tf_op jit(solution)/shard_map/ppermute | solution.py:70
  115.0 14.9 %collective-permute-start.9 = (bf16[128,1024]{1,0:T(8,128)(2,1)S(1)}, bf16[128,1024]{1,0:T(8,128)(2,1)}, u32[]{:S(2)}, u32[]{:S(2)}) collective-permute-start(bf16[128,1024]{1,0:T(8,128)(2,1)S(1)} %get-tuple-element.31), channel_id=1, source_target_pairs={{0,3},{1,0},{2,1},{3,2},{4,7},{5,4},{6,5},{7,6},{8,11},{9,8},{10,9... | collective-permute-start | bytes 786440 | tf_op jit(solution)/shard_map/ppermute | solution.py:70
  119.6 37.8 %all-to-all-start.2 = ((bf16[64,8,896]{2,1,0:T(8,128)(2,1)}), bf16[64,8,896]{2,1,0:T(8,128)(2,1)}, u32[]{:S(2)}, u32[]{:S(2)}) async-start(bf16[64,8,896]{2,1,0:T(8,128)(2,1)} %bitcast.14), calls=%async_computation.2 | async-start | bytes 1835008 | tf_op jit(solution)/shard_map/all_to_all | solution.py:357
  131.3 15.7 %collective-permute-start.10 = (bf16[128,1024]{1,0:T(8,128)(2,1)S(1)}, bf16[128,1024]{1,0:T(8,128)(2,1)S(1)}, u32[]{:S(2)}, u32[]{:S(2)}) collective-permute-start(bf16[128,1024]{1,0:T(8,128)(2,1)S(1)} %multiply_convert_fusion.1), channel_id=1, source_target_pairs={{0,1},{1,2},{2,3},{3,0},{4,5},{5,6},{6,7},{7,4},{8,9},{9,10},{10,1... | collective-permute-start | bytes 786440 | tf_op jit(solution)/shard_map/ppermute | solution.py:70
  133.2 13.7 %collective-permute-start.11 = (bf16[128,1024]{1,0:T(8,128)(2,1)S(1)}, bf16[128,1024]{1,0:T(8,128)(2,1)S(1)}, u32[]{:S(2)}, u32[]{:S(2)}) collective-permute-start(bf16[128,1024]{1,0:T(8,128)(2,1)S(1)} %multiply_convert_fusion.1), channel_id=1, source_target_pairs={{0,2},{1,3},{2,0},{3,1},{4,6},{5,7},{6,4},{7,5},{8,10},{9,11},{10,... | collective-permute-start | bytes 786440 | tf_op jit(solution)/shard_map/ppermute | solution.py:70
  136.6 12.8 %collective-permute-start.12 = (bf16[128,1024]{1,0:T(8,128)(2,1)S(1)}, bf16[128,1024]{1,0:T(8,128)(2,1)S(1)}, u32[]{:S(2)}, u32[]{:S(2)}) collective-permute-start(bf16[128,1024]{1,0:T(8,128)(2,1)S(1)} %multiply_convert_fusion.1), channel_id=1, source_target_pairs={{0,3},{1,0},{2,1},{3,2},{4,7},{5,4},{6,5},{7,6},{8,11},{9,8},{10,9... | collective-permute-start | bytes 786440 | tf_op jit(solution)/shard_map/ppermute | solution.py:70
  149.5 4.9 %collective-permute-start.13 = (bf16[512,1024]{1,0:T(8,128)(2,1)S(1)}, bf16[512,1024]{1,0:T(8,128)(2,1)S(1)}, u32[]{:S(2)}, u32[]{:S(2)}) collective-permute-start(bf16[512,1024]{1,0:T(8,128)(2,1)S(1)} %pad_maximum_fusion.rows_ref), channel_id=1, source_target_pairs={{0,256},{256,0},{1,257},{257,1},{2,258},{258,2},{3,259},{259,3},{4... | collective-permute-start | bytes 3145736 | tf_op jit(solution)/shard_map/ppermute | solution.py:70
  157.4 12.9 %copy-start.7 = (s32[2]{0:T(128)S(1)}, s32[2]{0:T(128)}, u32[]{:S(2)}) copy-start(s32[2]{0:T(128)} %param.10) | copy-start | bytes 28
  157.4 13.0 %copy-start.2 = (bf16[2,256,576]{1,2,0:T(8,128)(2,1)S(1)}, bf16[2,256,576]{1,2,0:T(8,128)(2,1)}, u32[]{:S(2)}) copy-start(bf16[2,256,576]{1,2,0:T(8,128)(2,1)} %param.9) | copy-start | bytes 1769476
  157.4 61.3 %all-to-all-start.3 = ((bf16[64,2,8,896]{3,2,1,0:T(8,128)(2,1)}), bf16[64,2,8,896]{3,2,1,0:T(8,128)(2,1)S(1)}, u32[]{:S(2)}, u32[]{:S(2)}) async-start(bf16[64,2,8,896]{3,2,1,0:T(8,128)(2,1)} %down_half.3), calls=%async_computation.3 | async-start | bytes 3670016 | tf_op jit(solution)/shard_map/all_to_all | solution.py:357
  170.4 11.1 %copy-start.3 = (bf16[256,512]{0,1:T(8,128)(2,1)S(1)}, bf16[256,512]{0,1:T(8,128)(2,1)}, u32[]{:S(2)}) copy-start(bf16[256,512]{0,1:T(8,128)(2,1)} %pad_maximum_fusion.3) | copy-start | bytes 786436
  171.6 11.5 %collective-permute-start.14 = (bf16[2,32,640]{2,1,0:T(8,128)(2,1)S(1)}, bf16[2,32,640]{2,1,0:T(8,128)(2,1)S(1)}, u32[]{:S(2)}, u32[]{:S(2)}) collective-permute-start(bf16[2,32,640]{2,1,0:T(8,128)(2,1)S(1)} %get-tuple-element.46), channel_id=1, source_target_pairs={{0,2},{1,3},{2,0},{3,1},{4,6},{5,7},{6,4},{7,5},{8,10},{9,11},{10,... | collective-permute-start | bytes 245768 | tf_op jit(solution)/shard_map/ppermute | solution.py:70
  174.4 8.7 %collective-permute-start.15 = (bf16[2,32,640]{2,1,0:T(8,128)(2,1)S(1)}, bf16[2,32,640]{2,1,0:T(8,128)(2,1)S(1)}, u32[]{:S(2)}, u32[]{:S(2)}) collective-permute-start(bf16[2,32,640]{2,1,0:T(8,128)(2,1)S(1)} %get-tuple-element.45), channel_id=1, source_target_pairs={{0,1},{1,2},{2,3},{3,0},{4,5},{5,6},{6,7},{7,4},{8,9},{9,10},{10,1... | collective-permute-start | bytes 245768 | tf_op jit(solution)/shard_map/ppermute | solution.py:70
  178.9 6.3 %collective-permute-start.16 = (bf16[2,32,640]{2,1,0:T(8,128)(2,1)S(1)}, bf16[2,32,640]{2,1,0:T(8,128)(2,1)S(1)}, u32[]{:S(2)}, u32[]{:S(2)}) collective-permute-start(bf16[2,32,640]{2,1,0:T(8,128)(2,1)S(1)} %get-tuple-element.44), channel_id=1, source_target_pairs={{0,3},{1,0},{2,1},{3,2},{4,7},{5,4},{6,5},{7,6},{8,11},{9,8},{10,9... | collective-permute-start | bytes 245768 | tf_op jit(solution)/shard_map/ppermute | solution.py:70

commit v4 on v3

--- a/solution.py
+++ b/solution.py
@@ -13,6 +13,7 @@
 EXPERTS = 64
 CAP = 24
 FIRST = 8
+TILE = 256
 VMEM = 32 * 1024 * 1024
 LANES = 128
 
@@ -78,6 +79,44 @@
     )
 
 
+def select_kernel(ids_ref, rows_ref, rank_ref, out_ref):
+    top, rows = ids_ref.shape
+    experts, slots, columns = out_ref.shape
+    named = jnp.zeros((experts, rows), jnp.float32)
+    numbers = lax.broadcasted_iota(jnp.int32, (experts, rows), 0)
+    for k in range(top):
+        named = jnp.where(ids_ref[k : k + 1, :] == numbers, 1.0, named)
+    above = lax.broadcasted_iota(jnp.int32, (rows, rows), 0)
+    right = lax.broadcasted_iota(jnp.int32, (rows, rows), 1)
+    before = jnp.dot(
+        named.astype(jnp.bfloat16),
+        jnp.where(above < right, 1.0, 0.0).astype(jnp.bfloat16),
+        preferred_element_type=jnp.float32,
+    )
+    rank = jnp.where(named > 0.5, before, -1.0)
+    rank_ref[...] = rank
+    slot = lax.broadcasted_iota(jnp.int32, (experts, slots, rows), 1).astype(jnp.float32)
+    placed = jnp.where(rank[:, None, :] == slot, 1.0, 0.0).reshape(experts * slots, rows)
+    made = jnp.dot(
+        placed.astype(jnp.bfloat16), rows_ref[...], preferred_element_type=jnp.float32
+    )
+    out_ref[...] = made.reshape(experts, slots, columns).astype(out_ref.dtype)
+
+
+def first_selection(ids, rows_in):
+    rows, columns = rows_in.shape
+    return pl.pallas_call(
+        select_kernel,
+        out_shape=[
+            jax.ShapeDtypeStruct((EXPERTS, rows), jnp.float32),
+            jax.ShapeDtypeStruct((EXPERTS, FIRST, columns), jnp.bfloat16),
+        ],
+        compiler_params=pltpu.CompilerParams(vmem_limit_bytes=VMEM),
+        cost_estimate=cost(EXPERTS * FIRST, rows, columns),
+        name="first_selection",
+    )(ids.T, rows_in)
+
+
 def their_kernel(where, rows_ref, weight_ref, out_ref):
     out_ref[...] = jnp.dot(
         rows_ref[...], weight_ref[...], preferred_element_type=jnp.float32
@@ -86,20 +125,18 @@
 
 def their_half(where, rows_in, weight):
     half, depth = rows_in.shape[0] // 2, rows_in.shape[1]
-    columns = weight.shape[1]
-    tile = min(256, half)
-    steps = half // tile
+    columns = weight.shape[2]
     return pl.pallas_call(
         their_kernel,
         out_shape=jax.ShapeDtypeStruct((half, columns), jnp.bfloat16),
         grid_spec=pltpu.PrefetchScalarGridSpec(
             num_scalar_prefetch=1,
-            grid=(steps,),
+            grid=(columns // TILE,),
             in_specs=[
-                pl.BlockSpec((tile, depth), lambda i, where: ((1 - where[0]) * steps + i, 0)),
-                pl.BlockSpec((depth, columns), lambda i, where: (0, 0)),
+                pl.BlockSpec((half, depth), lambda j, where: (1 - where[0], 0)),
+                pl.BlockSpec((None, depth, TILE), lambda j, where: (0, 0, j)),
             ],
-            out_specs=pl.BlockSpec((tile, columns), lambda i, where: (i, 0)),
+            out_specs=pl.BlockSpec((half, TILE), lambda j, where: (0, j)),
         ),
         compiler_params=pltpu.CompilerParams(vmem_limit_bytes=VMEM),
         cost_estimate=cost(half, depth, columns),
@@ -107,53 +144,32 @@
     )(where, rows_in, weight)
 
 
-def own_kernel(where, rows_ref, weight_ref, arrived_ref, own_ref, *rest):
-    piece_refs, total = rest[:-1], rest[-1]
-    tile = rows_ref.shape[0]
-    share = own_ref.shape[0]
-    size = total.shape[0] // share
-    step = pl.program_id(0)
-    here = pl.ds(pl.multiple_of(step * tile, tile), tile)
-    total[here, :] = jnp.dot(
+def own_kernel(where, rows_ref, weight_ref, arrived_ref, own_ref, rounded_ref):
+    total = jnp.dot(
         rows_ref[...], weight_ref[...], preferred_element_type=jnp.float32
     ) + arrived_ref[...].astype(jnp.float32)
-
-    @pl.when(step == pl.num_programs(0) - 1)
-    def _():
-        if size == 1:
-            own_ref[...] = total[...]
-            piece_refs[0][...] = total[...].astype(jnp.bfloat16)
-        else:
-            for ahead in range(size):
-                place = lax.rem(where[1] + ahead, size)
-                piece = total[pl.ds(pl.multiple_of(place * share, share), share), :]
-                if ahead == 0:
-                    own_ref[...] = piece
-                else:
-                    piece_refs[ahead - 1][...] = piece.astype(jnp.bfloat16)
-
-
-def own_half(where, rows_in, weight, arrived, size):
+    own_ref[...] = total
+    rounded_ref[...] = total.astype(rounded_ref.dtype)
+
+
+def own_half(where, rows_in, weight, arrived):
     half, depth = rows_in.shape[0] // 2, rows_in.shape[1]
-    columns = weight.shape[1]
-    tile = min(256, half)
-    steps = half // tile
-    share = half // size
+    columns = weight.shape[2]
     return pl.pallas_call(
         own_kernel,
-        out_shape=[jax.ShapeDtypeStruct((share, columns), jnp.float32)]
-        + [jax.ShapeDtypeStruct((share, columns), jnp.bfloat16)] * max(1, size - 1),
+        out_shape=[
+            jax.ShapeDtypeStruct((half, columns), jnp.float32),
+            jax.ShapeDtypeStruct((half, columns), jnp.bfloat16),
+        ],
         grid_spec=pltpu.PrefetchScalarGridSpec(
             num_scalar_prefetch=1,
-            grid=(steps,),
+            grid=(columns // TILE,),
             in_specs=[
-                pl.BlockSpec((tile, depth), lambda i, where: (where[0] * steps + i, 0)),
-                pl.BlockSpec((depth, columns), lambda i, where: (0, 0)),
-                pl.BlockSpec((tile, columns), lambda i, where: (i, 0)),
+                pl.BlockSpec((half, depth), lambda j, where: (where[0], 0)),
+                pl.BlockSpec((None, depth, TILE), lambda j, where: (0, 0, j)),
+                pl.BlockSpec((half, TILE), lambda j, where: (0, j)),
             ],
-            out_specs=[pl.BlockSpec((share, columns), lambda i, where: (0, 0))]
-            * max(2, size),
-            scratch_shapes=[pltpu.VMEM((half, columns), jnp.float32)],
+            out_specs=[pl.BlockSpec((half, TILE), lambda j, where: (0, j))] * 2,
         ),
         compiler_params=pltpu.CompilerParams(vmem_limit_bytes=VMEM),
         cost_estimate=cost(half, depth, columns),
@@ -175,27 +191,23 @@
         ).astype(out_ref.dtype)
 
 
-def down_both(where, mine, theirs, weight, size):
+def down_both(where, mine, theirs, weight):
     half, depth = mine.shape
-    columns = weight.shape[1]
-    share = half // size
-
-    def place(core, back, where):
-        which = where[0] + core - 2 * where[0] * core
-        return which * size + lax.rem(where[1] * (size > 1) + size - back, size), 0
-
+    columns = weight.shape[2]
     return pl.pallas_call(
         down_kernel,
         out_shape=jax.ShapeDtypeStruct((2 * half, columns), jnp.bfloat16),
         grid_spec=pltpu.PrefetchScalarGridSpec(
             num_scalar_prefetch=1,
-            grid=(2, size),
+            grid=(2,),
             in_specs=[
-                pl.BlockSpec((share, depth), lambda h, i, where: (i * (1 - h) + (size - 1) * h, 0)),
-                pl.BlockSpec((share, depth), lambda h, i, where: (i * h, 0)),
-                pl.BlockSpec((depth, columns), lambda h, i, where: (0, 0)),
+                pl.BlockSpec((half, depth), lambda h, where: (0, 0)),
+                pl.BlockSpec((half, depth), lambda h, where: (0, 0)),
+                pl.BlockSpec((None, depth, columns), lambda h, where: (0, 0, 0)),
             ],
-            out_specs=pl.BlockSpec((share, columns), place),
+            out_specs=pl.BlockSpec(
+                (half, columns), lambda h, where: (where[0] + h - 2 * where[0] * h, 0)
+            ),
         ),
         compiler_params=pltpu.CompilerParams(vmem_limit_bytes=VMEM),
         cost_estimate=cost(2 * half, depth, columns),
@@ -205,31 +217,24 @@
 
 def wide_kernel(where, rows_ref, weight_ref, other_ref, own_ref, *rest):
     piece_refs, total = rest[:-1], rest[-1]
-    tile = rows_ref.shape[0]
     depth = weight_ref.shape[0]
     share = own_ref.shape[0]
     size = total.shape[0] // share
-    step = pl.program_id(0)
-    here = pl.ds(pl.multiple_of(step * tile, tile), tile)
-    total[here, :] = jnp.dot(
+    total[...] = jnp.dot(
         rows_ref[:, :depth], weight_ref[...], preferred_element_type=jnp.float32
     ) + jnp.dot(rows_ref[:, depth:], other_ref[...], preferred_element_type=jnp.float32)
-
-    @pl.when(step == pl.num_programs(0) - 1)
-    def _():
-        for ahead in range(size):
-            place = lax.rem(where[1] + ahead, size)
-            piece = total[pl.ds(pl.multiple_of(place * share, share), share), :]
-            if ahead == 0:
-                own_ref[...] = piece
-            else:
-                piece_refs[ahead - 1][...] = piece.astype(jnp.bfloat16)
+    for ahead in range(size):
+        place = lax.rem(where[1] + ahead, size)
+        piece = total[pl.ds(pl.multiple_of(place * share, share), share), :]
+        if ahead == 0:
+            own_ref[...] = piece
+        else:
+            piece_refs[ahead - 1][...] = piece.astype(jnp.bfloat16)
 
 
 def wide_product(where, rows_in, weight, other, size):
     rows, width = rows_in.shape
-    depth, columns = weight.shape
-    tile = 256
+    _, depth, columns = weight.shape
     share = rows // size
     return pl.pallas_call(
         wide_kernel,
@@ -237,14 +242,14 @@
         + [jax.ShapeDtypeStruct((share, columns), jnp.bfloat16)] * (size - 1),
         grid_spec=pltpu.PrefetchScalarGridSpec(
             num_scalar_prefetch=1,
-            grid=(rows // tile,),
+            grid=(columns // TILE,),
             in_specs=[
-                pl.BlockSpec((tile, width), lambda i, where: (i, 0)),
-                pl.BlockSpec((depth, columns), lambda i, where: (0, 0)),
-                pl.BlockSpec((depth, columns), lambda i, where: (0, 0)),
+                pl.BlockSpec((rows, width), lambda j, where: (0, 0)),
+                pl.BlockSpec((None, depth, TILE), lambda j, where: (0, 0, j)),
+                pl.BlockSpec((None, depth, TILE), lambda j, where: (0, 0, j)),
             ],
-            out_specs=[pl.BlockSpec((share, columns), lambda i, where: (0, 0))] * size,
-            scratch_shapes=[pltpu.VMEM((rows, columns), jnp.float32)],
+            out_specs=[pl.BlockSpec((share, TILE), lambda j, where: (0, j))] * size,
+            scratch_shapes=[pltpu.VMEM((rows, TILE), jnp.float32)],
         ),
         compiler_params=pltpu.CompilerParams(vmem_limit_bytes=VMEM),
         cost_estimate=cost(rows, width, columns),
@@ -270,12 +275,12 @@
 
 def down_half(where, core, rows_in, weight, made, sources):
     rows, depth = rows_in.shape
-    columns = weight.shape[1]
+    columns = weight.shape[2]
     slots = rows // sources
     tile = rows // 2
     in_specs = [
         pl.BlockSpec((tile, depth), lambda i, where: (i, 0)),
-        pl.BlockSpec((depth, columns), lambda i, where: (0, 0)),
+        pl.BlockSpec((None, depth, columns), lambda i, where: (0, 0, 0)),
     ]
     inputs = [rows_in, weight]
     aliases = {}
@@ -305,12 +310,12 @@
 
 def narrow_rows(where, rows_in, up, down):
     arrived = turned(their_half(where, rows_in, up), "role", 1)
-    own, rounded = own_half(where, rows_in, up, arrived, 1)
+    own, rounded = own_half(where, rows_in, up, arrived)
     pieces = [turned(rounded, "tp", step) for step in (2, 1, 3)]
     for piece in pieces:
         own = own + piece.astype(jnp.float32)
     mine = jax.nn.silu(own).astype(jnp.bfloat16)
-    return down_both(where, mine, turned(mine, "role", 1), down, 1)
+    return down_both(where, mine, turned(mine, "role", 1), down)
 
 
 def wide_rows(where, rows_in, up, other_up, down, sources):
@@ -340,37 +345,24 @@
     owners = lax.axis_size("grp")
     experts = jnp.arange(EXPERTS, dtype=jnp.int32)
     where = jnp.stack([lax.axis_index("role"), lax.axis_index("tp")]).astype(jnp.int32)
-    up = up_weight[0]
-    down = down_weight[0]
-
-    named = expert_ids[:, None, :] == experts[None, :, None]
-    named_any = jnp.any(named, axis=2)
-    row_numbers = jnp.arange(rows, dtype=jnp.int32)
-    lower = (row_numbers[None, :] < row_numbers[:, None]).astype(jnp.bfloat16)
-    before = jnp.dot(
-        lower, named_any.astype(jnp.bfloat16), preferred_element_type=jnp.float32
-    ).astype(jnp.int32)
-    rank = jnp.where(named_any, before, -1)
-    rank_by_expert = rank.T
+
+    rank, first_out = first_selection(expert_ids, hidden)
 
     def exchanged(value):
         return lax.all_to_all(value, "grp", split_axis=0, concat_axis=0, tiled=True)
 
     def outgoing(first, count, source):
-        slots = first + jnp.arange(count, dtype=jnp.int32)
-        placed = rank_by_expert[:, None, :] == slots[None, :, None]
+        slots = (first + jnp.arange(count, dtype=jnp.int32)).astype(jnp.float32)
+        placed = rank[:, None, :] == slots[None, :, None]
         placed = placed.reshape(-1, rows).astype(jnp.bfloat16)
         made = jnp.dot(placed, source, preferred_element_type=jnp.float32).astype(jnp.bfloat16)
         return made.reshape(owners, count, source.shape[1])
 
     def weights(first, last):
-        slots = jnp.arange(first, last, dtype=jnp.int32)
-        taken = rank[:, :, None] == slots[None, None, :]
-        return jnp.concatenate(
-            two_halves(jnp.where(taken, weight_of[:, :, None], 0.0).reshape(rows, -1)), axis=0
-        )
-
-    first_out = outgoing(0, FIRST, hidden)
+        slots = jnp.arange(first, last, dtype=jnp.int32).astype(jnp.float32)
+        taken = rank.T[:, :, None] == slots[None, None, :]
+        return jnp.where(taken, weight_of[:, :, None], 0.0).reshape(rows, -1).astype(jnp.bfloat16)
+
     first_out, hidden = lax.optimization_barrier((first_out, hidden))
     first_in = exchanged(first_out)
 
@@ -378,20 +370,21 @@
 
     sigmoid_terms = jax.nn.sigmoid(route_logits)
     route_weights = 2.5 * sigmoid_terms / jnp.sum(sigmoid_terms, axis=-1, keepdims=True)
+    named = expert_ids[:, None, :] == experts[None, :, None]
     weight_of = jnp.sum(jnp.where(named, route_weights[:, None, :], 0.0), axis=2)
     weights_of = [weights(0, FIRST), weights(FIRST, CAP)]
 
     half = (CAP - FIRST) // 2
     begin = FIRST + where[0] * half
     second_out, first_in, passed_up, *weights_of = lax.optimization_barrier(
-        (outgoing(begin, half, wide), first_in, up, *weights_of)
+        (outgoing(begin, half, wide), first_in, up_weight, *weights_of)
     )
     second_in = exchanged(second_out)
     other_up = turned(passed_up, "role", 1)
-    first_out = narrow_rows(where, first_in.reshape(-1, width), up, down)
+    first_out = narrow_rows(where, first_in.reshape(-1, width), up_weight, down_weight)
     second_in, first_out = lax.optimization_barrier((second_in, first_out))
     first_back = exchanged(first_out.reshape(owners, FIRST, width))
-    second_out = wide_rows(where, second_in.reshape(-1, 2 * width), up, other_up, down, owners)
+    second_out = wide_rows(where, second_in.reshape(-1, 2 * width), up_weight, other_up, down_weight, owners)
     second_out, first_back, q_latent = lax.optimization_barrier((second_out, first_back, q_latent))
     second_back = exchanged(second_out)
 
@@ -409,8 +402,7 @@
     second_back = second_back.reshape(-1, width)
     result = jnp.dot(weights_of[0], first_back, preferred_element_type=jnp.float32)
     result = result + jnp.dot(weights_of[1], second_back, preferred_element_type=jnp.float32)
-    moe_output = (result[:rows] + result[rows:]).astype(jnp.bfloat16)
-    return (attn_context, moe_output)
+    return (attn_context, result.astype(jnp.bfloat16))
 
 
 def solution(mesh):

time: 222 us -> 223 us (level)
  Pallas kernels: 19.8 us -> 23.5 us
  matrix products: 8.52 us -> 5.33 us
    pallas_call x1 -> x2, Pallas kernels: 2.77 us -> 5.12 us  [the longest x1 3.66 us: own_half(): pl.pallas_call(own_kernel, out_shape=[jax.ShapeDtypeStruct((half, columns...]
    dot_general x2 -> x1, matrix products: 4.26 us -> 1.95 us  [outgoing(): jnp.dot(placed, source, preferred_element_type=jnp.float32)]
  transfers between devices with their start and end apart: 21 -> 21, of which waited for: 10 -> 10; matrix products, arithmetic and copies ran while one was open for 5% -> 5% of each run, Pallas kernels for 6% -> 7%
where the time goes in v4:
time: 223 us; the launch traced here: 222 us
  starting transfers between devices  101 us (45%)
  waiting for transfers between devices  83.4 us (37%)
  Pallas kernels  23.5 us (11%)
  other arithmetic  5.41 us (2%)
  matrix products  5.33 us (2%)
    all_to_all x4, waiting for transfers between devices, exchanged(): return lax.all_to_all(value, 'grp', split_axis=0, concat_axis=0, tiled=True)  53.5 us
    ppermute x17, starting transfers between devices, turned(): lax.ppermute(value, axis, [(k, (k + step) % size) for k in range(size)])  53.2 us
    all_to_all x4, starting transfers between devices, exchanged(): return lax.all_to_all(value, 'grp', split_axis=0, concat_axis=0, tiled=True)  47.7 us
    ppermute x17, waiting for transfers between devices, turned(): lax.ppermute(value, axis, [(k, (k + step) % size) for k in range(size)])  29.9 us
    pallas_call x1, Pallas kernels, wide_product(): pl.pallas_call(wide_kernel, out_shape=[jax.ShapeDtypeStruct((share, colum...  6.01 us
    pallas_call x2, Pallas kernels, down_half(): pl.pallas_call(down_half_kernel, out_shape=jax.ShapeDtypeStruct((sources,...  5.91 us
  transfers between devices with their start and end apart: 21, of which 10 were waited for; matrix products, arithmetic and copies ran while one was open for 5% of the time, Pallas kernels for 7%

profile of v4, /device:TPU:24, one launch (start us, length us, event | category | flops | bytes accessed | tf_op | source)
XLA Modules:
  0.0 221.7 jit_solution(10713214200144672965)
XLA Ops:
  0.6 0.0 copy-start
  0.7 1.0 copy-done.2
  1.6 0.7 copy-done.4
  2.3 1.5 first_selection.1
  3.8 16.4 %all-to-all-start = ((bf16[64,8,896]{2,1,0:T(8,128)(2,1)}), bf16[64,8,896]{2,1,0:T(8,128)(2,1)S(1)}, u32[]{:S(2)}, u32[]{:S(2)}) async-start(bf16[64,8,896]{2,1,0:T(8,128)(2,1)} %get-tuple-element.25), calls=%async_computation | async-start | bytes 1835008 | tf_op jit(solution)/shard_map/all_to_all | solution.py:352
  20.2 1.9 collective-permute-start
  22.2 0.1 select_reduce_fusion
  22.3 0.1 eq.81
  22.4 0.1 eq.96
  22.5 0.1 eq.87
  22.6 0.9 fusion.6
  23.5 0.8 fusion.12
  24.3 1.9 fusion
  26.3 20.9 %all-to-all-done = bf16[64,8,896]{2,1,0:T(8,128)(2,1)S(1)} async-done(((bf16[64,8,896]{2,1,0:T(8,128)(2,1)}), bf16[64,8,896]{2,1,0:T(8,128)(2,1)S(1)}, u32[]{:S(2)}, u32[]{:S(2)}) %all-to-all-start) | async-done | bytes 917536 | tf_op jit(solution)/shard_map/all_to_all | solution.py:352
  47.1 6.4 %all-to-all-start.1 = ((bf16[64,8,1792]{2,1,0:T(8,128)(2,1)}), bf16[64,8,1792]{2,1,0:T(8,128)(2,1)}, u32[]{:S(2)}, u32[]{:S(2)}) async-start(bf16[64,8,1792]{2,1,0:T(8,128)(2,1)} %fusion), calls=%async_computation.1 | async-start | bytes 3670016 | tf_op jit(solution)/shard_map/all_to_all | solution.py:352
  53.5 0.1 pad_add_fusion.where
  53.6 3.6 %their_half.1 = bf16[256,1024]{1,0:T(8,128)(2,1)S(1)} custom-call(s32[2]{0:T(128)S(1)} %pad_add_fusion.where, bf16[512,896]{1,0:T(8,128)(2,1)S(1)} %bitcast.51, bf16[1,896,1024]{2,1,0:T(8,128)(2,1)} %weight_ref.9), custom_call_target="tpu_custom_call" | custom-call | flops 469762048 | bytes 2818048 | tf_op jit(solution)/shard_map/their_half/pallas_call | solution.py:129
  57.2 1.9 collective-permute-start.1
  59.1 2.4 %collective-permute-start.6 = (bf16[1,896,1024]{2,1,0:T(8,128)(2,1)}, bf16[1,896,1024]{2,1,0:T(8,128)(2,1)}, u32[]{:S(2)}, u32[]{:S(2)}) collective-permute-start(bf16[1,896,1024]{2,1,0:T(8,128)(2,1)} %weight_ref.9), channel_id=1, source_target_pairs={{0,256},{256,0},{1,257},{257,1},{2,258},{258,2},{3,259},{259,3},{4... | collective-permute-start | bytes 5505032 | tf_op jit(solution)/shard_map/ppermute | solution.py:71
  61.6 3.7 %own_half.1 = (f32[256,1024]{1,0:T(8,128)S(1)}, bf16[256,1024]{1,0:T(8,128)(2,1)S(1)}) custom-call(s32[2]{0:T(128)S(1)} %pad_add_fusion.where, bf16[512,896]{1,0:T(8,128)(2,1)S(1)} %bitcast.52, bf16[1,896,1024]{2,1,0:T(8,128)(2,1)} %weight_ref.9, bf16[256,1024]{1,0:T(8,128)(2,1)S(1)} %collective-permute-done.1.arrived_ref), custom_call_target="tpu_custom_call" | custom-call | flops 469762048 | bytes 2818048 | tf_op jit(solution)/shard_map/own_half/pallas_call | solution.py:158
  65.2 5.1 %collective-permute-start.2 = (bf16[256,1024]{1,0:T(8,128)(2,1)S(1)}, bf16[256,1024]{1,0:T(8,128)(2,1)S(1)}, u32[]{:S(2)}, u32[]{:S(2)}) collective-permute-start(bf16[256,1024]{1,0:T(8,128)(2,1)S(1)} %get-tuple-element.29), channel_id=1, source_target_pairs={{0,2},{1,3},{2,0},{3,1},{4,6},{5,7},{6,4},{7,5},{8,10},{9,11},{10,... | collective-permute-start | bytes 1572872 | tf_op jit(solution)/shard_map/ppermute | solution.py:71
  70.3 2.5 %collective-permute-start.3 = (bf16[256,1024]{1,0:T(8,128)(2,1)S(1)}, bf16[256,1024]{1,0:T(8,128)(2,1)S(1)}, u32[]{:S(2)}, u32[]{:S(2)}) collective-permute-start(bf16[256,1024]{1,0:T(8,128)(2,1)S(1)} %get-tuple-element.29), channel_id=1, source_target_pairs={{0,1},{1,2},{2,3},{3,0},{4,5},{5,6},{6,7},{7,4},{8,9},{9,10},{10,1... | collective-permute-start | bytes 1572872 | tf_op jit(solution)/shard_map/ppermute | solution.py:71
  72.8 4.6 %collective-permute-start.4 = (bf16[256,1024]{1,0:T(8,128)(2,1)S(1)}, bf16[256,1024]{1,0:T(8,128)(2,1)S(1)}, u32[]{:S(2)}, u32[]{:S(2)}) collective-permute-start(bf16[256,1024]{1,0:T(8,128)(2,1)S(1)} %get-tuple-element.29), channel_id=1, source_target_pairs={{0,3},{1,0},{2,1},{3,2},{4,7},{5,4},{6,5},{7,6},{8,11},{9,8},{10,9... | collective-permute-start | bytes 1572872 | tf_op jit(solution)/shard_map/ppermute | solution.py:71
  77.4 6.2 %collective-permute-done.2 = bf16[256,1024]{1,0:T(8,128)(2,1)S(1)} collective-permute-done((bf16[256,1024]{1,0:T(8,128)(2,1)S(1)}, bf16[256,1024]{1,0:T(8,128)(2,1)S(1)}, u32[]{:S(2)}, u32[]{:S(2)}) %collective-permute-start.2) | collective-permute-done | bytes 524320 | tf_op jit(solution)/shard_map/ppermute | solution.py:71
  83.6 10.2 %collective-permute-done.3 = bf16[256,1024]{1,0:T(8,128)(2,1)S(1)} collective-permute-done((bf16[256,1024]{1,0:T(8,128)(2,1)S(1)}, bf16[256,1024]{1,0:T(8,128)(2,1)S(1)}, u32[]{:S(2)}, u32[]{:S(2)}) %collective-permute-start.3) | collective-permute-done | bytes 524320 | tf_op jit(solution)/shard_map/ppermute | solution.py:71
  93.8 0.1 collective-permute-done.4
  94.0 0.4 multiply_convert_fusion.mine_ref
  94.4 1.9 collective-permute-start.5
  96.3 1.9 collective-permute-done.5.theirs_ref
  98.2 2.8 %down_both.1 = bf16[512,896]{1,0:T(8,128)(2,1)} custom-call(s32[2]{0:T(128)S(1)} %pad_add_fusion.where, bf16[256,1024]{1,0:T(8,128)(2,1)S(1)} %multiply_convert_fusion.mine_ref, bf16[256,1024]{1,0:T(8,128)(2,1)S(1)} %collective-permute-done.5.theirs_ref, bf16[1,1024,896]{2,1,0:T(8,128)(2,1)S(1)} %copy-done.1), custom_call_target="tpu_custom_call" | custom-call | flops 939524096 | bytes 3801088 | tf_op jit(solution)/shard_map/down_both/pallas_call | solution.py:197
  101.1 0.7 all-to-all-done.1
  101.7 6.0 %wide_product.1 = (f32[128,1024]{1,0:T(8,128)S(1)}, bf16[128,1024]{1,0:T(8,128)(2,1)S(1)}, bf16[128,1024]{1,0:T(8,128)(2,1)S(1)}, bf16[128,1024]{1,0:T(8,128)(2,1)S(1)}) custom-call(s32[2]{0:T(128)S(1)} %pad_add_fusion.where, bf16[512,1792]{1,0:T(8,128)(2,1)} %bitcast.11.rows_ref, bf16[1,896,1024]{2,1,0:T(8,128)(2,1)} %weight_ref.9, ...), custom_call_target="tpu_custom_call" | custom-call | flops 1879048192 | bytes 6553600 | tf_op jit(solution)/shard_map/wide_product/pallas_call | solution.py:239
  107.8 4.9 %collective-permute-start.7 = (bf16[128,1024]{1,0:T(8,128)(2,1)S(1)}, bf16[128,1024]{1,0:T(8,128)(2,1)}, u32[]{:S(2)}, u32[]{:S(2)}) collective-permute-start(bf16[128,1024]{1,0:T(8,128)(2,1)S(1)} %get-tuple-element.33), channel_id=1, source_target_pairs={{0,2},{1,3},{2,0},{3,1},{4,6},{5,7},{6,4},{7,5},{8,10},{9,11},{10,... | collective-permute-start | bytes 786440 | tf_op jit(solution)/shard_map/ppermute | solution.py:71
  112.7 2.5 %collective-permute-start.8 = (bf16[128,1024]{1,0:T(8,128)(2,1)S(1)}, bf16[128,1024]{1,0:T(8,128)(2,1)}, u32[]{:S(2)}, u32[]{:S(2)}) collective-permute-start(bf16[128,1024]{1,0:T(8,128)(2,1)S(1)} %get-tuple-element.34), channel_id=1, source_target_pairs={{0,1},{1,2},{2,3},{3,0},{4,5},{5,6},{6,7},{7,4},{8,9},{9,10},{10,1... | collective-permute-start | bytes 786440 | tf_op jit(solution)/shard_map/ppermute | solution.py:71
  115.2 4.6 %collective-permute-start.9 = (bf16[128,1024]{1,0:T(8,128)(2,1)S(1)}, bf16[128,1024]{1,0:T(8,128)(2,1)}, u32[]{:S(2)}, u32[]{:S(2)}) collective-permute-start(bf16[128,1024]{1,0:T(8,128)(2,1)S(1)} %get-tuple-element.35), channel_id=1, source_target_pairs={{0,3},{1,0},{2,1},{3,2},{4,7},{5,4},{6,5},{7,6},{8,11},{9,8},{10,9... | collective-permute-start | bytes 786440 | tf_op jit(solution)/shard_map/ppermute | solution.py:71
  119.8 12.1 %all-to-all-start.2 = ((bf16[64,8,896]{2,1,0:T(8,128)(2,1)}), bf16[64,8,896]{2,1,0:T(8,128)(2,1)}, u32[]{:S(2)}, u32[]{:S(2)}) async-start(bf16[64,8,896]{2,1,0:T(8,128)(2,1)} %bitcast.12), calls=%async_computation.2 | async-start | bytes 1835008 | tf_op jit(solution)/shard_map/all_to_all | solution.py:352
  131.9 1.3 multiply_convert_fusion.1
  133.2 1.9 collective-permute-start.10
  135.1 3.4 %collective-permute-start.11 = (bf16[128,1024]{1,0:T(8,128)(2,1)S(1)}, bf16[128,1024]{1,0:T(8,128)(2,1)S(1)}, u32[]{:S(2)}, u32[]{:S(2)}) collective-permute-start(bf16[128,1024]{1,0:T(8,128)(2,1)S(1)} %multiply_convert_fusion.1), channel_id=1, source_target_pairs={{0,2},{1,3},{2,0},{3,1},{4,6},{5,7},{6,4},{7,5},{8,10},{9,11},{10,... | collective-permute-start | bytes 786440 | tf_op jit(solution)/shard_map/ppermute | solution.py:71
  138.5 3.7 %collective-permute-start.12 = (bf16[128,1024]{1,0:T(8,128)(2,1)S(1)}, bf16[128,1024]{1,0:T(8,128)(2,1)S(1)}, u32[]{:S(2)}, u32[]{:S(2)}) collective-permute-start(bf16[128,1024]{1,0:T(8,128)(2,1)S(1)} %multiply_convert_fusion.1), channel_id=1, source_target_pairs={{0,3},{1,0},{2,1},{3,2},{4,7},{5,4},{6,5},{7,6},{8,11},{9,8},{10,9... | collective-permute-start | bytes 786440 | tf_op jit(solution)/shard_map/ppermute | solution.py:71
  142.2 6.7 %collective-permute-done.10 = bf16[128,1024]{1,0:T(8,128)(2,1)S(1)} collective-permute-done((bf16[128,1024]{1,0:T(8,128)(2,1)S(1)}, bf16[128,1024]{1,0:T(8,128)(2,1)S(1)}, u32[]{:S(2)}, u32[]{:S(2)}) %collective-permute-start.10) | collective-permute-done | bytes 262176 | tf_op jit(solution)/shard_map/ppermute | solution.py:71
  148.9 2.5 %collective-permute-done.12 = bf16[128,1024]{1,0:T(8,128)(2,1)S(1)} collective-permute-done((bf16[128,1024]{1,0:T(8,128)(2,1)S(1)}, bf16[128,1024]{1,0:T(8,128)(2,1)S(1)}, u32[]{:S(2)}, u32[]{:S(2)}) %collective-permute-start.12) | collective-permute-done | bytes 262176 | tf_op jit(solution)/shard_map/ppermute | solution.py:71
  151.4 0.1 pad_maximum_fusion.rows_ref
  151.4 1.9 collective-permute-start.13
  153.4 2.9 %down_half.2.rest_0_ = bf16[64,2,8,896]{3,2,1,0:T(8,128)(2,1)} custom-call(s32[2]{0:T(128)S(1)} %pad_add_fusion.where, bf16[512,1024]{1,0:T(8,128)(2,1)S(1)} %pad_maximum_fusion.rows_ref, bf16[1,1024,896]{2,1,0:T(8,128)(2,1)S(1)} %copy-done.1), custom_call_target="tpu_custom_call" | custom-call | flops 939524096 | bytes 3801088 | tf_op jit(solution)/shard_map/down_half/pallas_call | solution.py:295
  156.3 3.0 %down_half.3 = bf16[64,2,8,896]{3,2,1,0:T(8,128)(2,1)} custom-call(s32[2]{0:T(128)S(1)} %pad_add_fusion.where, bf16[512,1024]{1,0:T(8,128)(2,1)S(1)} %collective-permute-done.13.rows_ref, bf16[1,1024,896]{2,1,0:T(8,128)(2,1)S(1)} %copy-done.1, bf16[64,2,8,896]{3,2,1,0:T(8,128)(2,1)} %down_half.2.rest_0_), custom_call_target="tpu_custom_call", output_to_operand_aliasing={{}: (3, {})} | custom-call | flops 939524096 | bytes 3801088 | tf_op jit(solution)/shard_map/down_half/pallas_call | solution.py:295
  159.3 12.8 %all-to-all-start.3 = ((bf16[64,2,8,896]{3,2,1,0:T(8,128)(2,1)}), bf16[64,2,8,896]{3,2,1,0:T(8,128)(2,1)S(1)}, u32[]{:S(2)}, u32[]{:S(2)}) async-start(bf16[64,2,8,896]{3,2,1,0:T(8,128)(2,1)} %down_half.3), calls=%async_computation.3 | async-start | bytes 3670016 | tf_op jit(solution)/shard_map/all_to_all | solution.py:352
  172.2 0.1 broadcast_compare_fusion
  172.3 0.4 fusion.26
  172.7 0.2 fusion.13
  172.9 0.1 copy.34
  173.1 0.3 convolution_convert_fusion.1
  173.5 2.8 %collective-permute-start.14 = (bf16[2,32,640]{2,1,0:T(8,128)(2,1)S(1)}, bf16[2,32,640]{2,1,0:T(8,128)(2,1)S(1)}, u32[]{:S(2)}, u32[]{:S(2)}) collective-permute-start(bf16[2,32,640]{2,1,0:T(8,128)(2,1)S(1)} %get-tuple-element.50), channel_id=1, source_target_pairs={{0,2},{1,3},{2,0},{3,1},{4,6},{5,7},{6,4},{7,5},{8,10},{9,11},{10,... | collective-permute-start | bytes 245768 | tf_op jit(solution)/shard_map/ppermute | solution.py:71
  176.3 4.5 %collective-permute-start.15 = (bf16[2,32,640]{2,1,0:T(8,128)(2,1)S(1)}, bf16[2,32,640]{2,1,0:T(8,128)(2,1)S(1)}, u32[]{:S(2)}, u32[]{:S(2)}) collective-permute-start(bf16[2,32,640]{2,1,0:T(8,128)(2,1)S(1)} %get-tuple-element.49), channel_id=1, source_target_pairs={{0,1},{1,2},{2,3},{3,0},{4,5},{5,6},{6,7},{7,4},{8,9},{9,10},{10,1... | collective-permute-start | bytes 245768 | tf_op jit(solution)/shard_map/ppermute | solution.py:71
  180.8 2.6 %collective-permute-start.16 = (bf16[2,32,640]{2,1,0:T(8,128)(2,1)S(1)}, bf16[2,32,640]{2,1,0:T(8,128)(2,1)S(1)}, u32[]{:S(2)}, u32[]{:S(2)}) collective-permute-start(bf16[2,32,640]{2,1,0:T(8,128)(2,1)S(1)} %get-tuple-element.48), channel_id=1, source_target_pairs={{0,3},{1,0},{2,1},{3,2},{4,7},{5,4},{6,5},{7,6},{8,11},{9,8},{10,9... | collective-permute-start | bytes 245768 | tf_op jit(solution)/shard_map/ppermute | solution.py:71
  183.5 1.5 fusion.3
  185.0 2.3 %collective-permute-done.16 = bf16[2,32,640]{2,1,0:T(8,128)(2,1)S(1)} collective-permute-done((bf16[2,32,640]{2,1,0:T(8,128)(2,1)S(1)}, bf16[2,32,640]{2,1,0:T(8,128)(2,1)S(1)}, u32[]{:S(2)}, u32[]{:S(2)}) %collective-permute-start.16) | collective-permute-done | bytes 81952 | tf_op jit(solution)/shard_map/ppermute | solution.py:71
  187.3 0.1 slice_reduce_fusion.1
  187.4 0.3 slice_reduce_fusion
  187.7 0.1 pad_maximum_fusion.1
  187.8 0.1 multiply_reduce_fusion
  187.9 0.7 divide_convert_fusion
  188.6 31.9 %all-to-all-done.3 = bf16[64,2,8,896]{3,2,1,0:T(8,128)(2,1)S(1)} async-done(((bf16[64,2,8,896]{3,2,1,0:T(8,128)(2,1)}), bf16[64,2,8,896]{3,2,1,0:T(8,128)(2,1)S(1)}, u32[]{:S(2)}, u32[]{:S(2)}) %all-to-all-start.3) | async-done | bytes 1835040 | tf_op jit(solution)/shard_map/all_to_all | solution.py:352
  220.5 1.2 fusion.1
  (46 shorter events, 0.3 us)
Async XLA Ops:
  0.6 171.6 %copy-start = (bf16[2,128,576]{1,2,0:T(8,128)(2,1)S(1)}, bf16[2,128,576]{1,2,0:T(8,128)(2,1)}, u32[]{:S(2)}) copy-start(bf16[2,128,576]{1,2,0:T(8,128)(2,1)} %param.8) | copy-start | bytes 884740
  0.6 1.0 copy-start.2
  1.6 0.7 copy-start.4
  2.3 17.9 %copy-start.3 = (bf16[128,896]{1,0:T(8,128)(2,1)S(1)}, bf16[128,896]{1,0:T(8,128)(2,1)}, u32[]{:S(2)}) copy-start(bf16[128,896]{1,0:T(8,128)(2,1)} %rows_ref.1) | copy-start | bytes 688132
  2.3 19.8 %copy-start.9 = (f32[128,8]{0,1:T(8,128)S(1)}, f32[128,8]{0,1:T(8,128)}, u32[]{:S(2)}) copy-start(f32[128,8]{0,1:T(8,128)} %param.13) | copy-start | bytes 12292
  2.3 19.9 %copy-start.5 = (s32[128,8]{0,1:T(8,128)S(1)}, s32[128,8]{0,1:T(8,128)}, u32[]{:S(2)}) copy-start(s32[128,8]{0,1:T(8,128)} %param.12) | copy-start | bytes 12292
  3.8 43.3 %all-to-all-start = ((bf16[64,8,896]{2,1,0:T(8,128)(2,1)}), bf16[64,8,896]{2,1,0:T(8,128)(2,1)S(1)}, u32[]{:S(2)}, u32[]{:S(2)}) async-start(bf16[64,8,896]{2,1,0:T(8,128)(2,1)} %get-tuple-element.25), calls=%async_computation | async-start | bytes 1835008 | tf_op jit(solution)/shard_map/all_to_all | solution.py:352
  20.2 4.1 %collective-permute-start = (bf16[128,896]{1,0:T(8,128)(2,1)S(1)}, bf16[128,896]{1,0:T(8,128)(2,1)S(1)}, u32[]{:S(2)}, u32[]{:S(2)}) collective-permute-start(bf16[128,896]{1,0:T(8,128)(2,1)S(1)} %copy-done.3), channel_id=1, source_target_pairs={{0,256},{256,0},{1,257},{257,1},{2,258},{258,2},{3,259},{259,3},{4... | collective-permute-start | bytes 688136 | tf_op jit(solution)/shard_map/ppermute | solution.py:71
  47.1 54.6 %all-to-all-start.1 = ((bf16[64,8,1792]{2,1,0:T(8,128)(2,1)}), bf16[64,8,1792]{2,1,0:T(8,128)(2,1)}, u32[]{:S(2)}, u32[]{:S(2)}) async-start(bf16[64,8,1792]{2,1,0:T(8,128)(2,1)} %fusion), calls=%async_computation.1 | async-start | bytes 3670016 | tf_op jit(solution)/shard_map/all_to_all | solution.py:352
  57.2 4.3 %collective-permute-start.1 = (bf16[256,1024]{1,0:T(8,128)(2,1)S(1)}, bf16[256,1024]{1,0:T(8,128)(2,1)S(1)}, u32[]{:S(2)}, u32[]{:S(2)}) collective-permute-start(bf16[256,1024]{1,0:T(8,128)(2,1)S(1)} %their_half.1), channel_id=1, source_target_pairs={{0,256},{256,0},{1,257},{257,1},{2,258},{258,2},{3,259},{259,3},{4... | collective-permute-start | bytes 1572872 | tf_op jit(solution)/shard_map/ppermute | solution.py:71
  59.1 42.6 %collective-permute-start.6 = (bf16[1,896,1024]{2,1,0:T(8,128)(2,1)}, bf16[1,896,1024]{2,1,0:T(8,128)(2,1)}, u32[]{:S(2)}, u32[]{:S(2)}) collective-permute-start(bf16[1,896,1024]{2,1,0:T(8,128)(2,1)} %weight_ref.9), channel_id=1, source_target_pairs={{0,256},{256,0},{1,257},{257,1},{2,258},{258,2},{3,259},{259,3},{4... | collective-permute-start | bytes 5505032 | tf_op jit(solution)/shard_map/ppermute | solution.py:71
  65.2 33.0 %copy-start.1 = (bf16[1,1024,896]{2,1,0:T(8,128)(2,1)S(1)}, bf16[1,1024,896]{2,1,0:T(8,128)(2,1)}, u32[]{:S(2)}) copy-start(bf16[1,1024,896]{2,1,0:T(8,128)(2,1)} %weight_ref.11) | copy-start | bytes 5505028
  65.2 18.4 %collective-permute-start.2 = (bf16[256,1024]{1,0:T(8,128)(2,1)S(1)}, bf16[256,1024]{1,0:T(8,128)(2,1)S(1)}, u32[]{:S(2)}, u32[]{:S(2)}) collective-permute-start(bf16[256,1024]{1,0:T(8,128)(2,1)S(1)} %get-tuple-element.29), channel_id=1, source_target_pairs={{0,2},{1,3},{2,0},{3,1},{4,6},{5,7},{6,4},{7,5},{8,10},{9,11},{10,... | collective-permute-start | bytes 1572872 | tf_op jit(solution)/shard_map/ppermute | solution.py:71
  70.3 23.5 %collective-permute-start.3 = (bf16[256,1024]{1,0:T(8,128)(2,1)S(1)}, bf16[256,1024]{1,0:T(8,128)(2,1)S(1)}, u32[]{:S(2)}, u32[]{:S(2)}) collective-permute-start(bf16[256,1024]{1,0:T(8,128)(2,1)S(1)} %get-tuple-element.29), channel_id=1, source_target_pairs={{0,1},{1,2},{2,3},{3,0},{4,5},{5,6},{6,7},{7,4},{8,9},{9,10},{10,1... | collective-permute-start | bytes 1572872 | tf_op jit(solution)/shard_map/ppermute | solution.py:71
  72.8 21.2 %collective-permute-start.4 = (bf16[256,1024]{1,0:T(8,128)(2,1)S(1)}, bf16[256,1024]{1,0:T(8,128)(2,1)S(1)}, u32[]{:S(2)}, u32[]{:S(2)}) collective-permute-start(bf16[256,1024]{1,0:T(8,128)(2,1)S(1)} %get-tuple-element.29), channel_id=1, source_target_pairs={{0,3},{1,0},{2,1},{3,2},{4,7},{5,4},{6,5},{7,6},{8,11},{9,8},{10,9... | collective-permute-start | bytes 1572872 | tf_op jit(solution)/shard_map/ppermute | solution.py:71
  94.4 3.8 %collective-permute-start.5 = (bf16[256,1024]{1,0:T(8,128)(2,1)S(1)}, bf16[256,1024]{1,0:T(8,128)(2,1)S(1)}, u32[]{:S(2)}, u32[]{:S(2)}) collective-permute-start(bf16[256,1024]{1,0:T(8,128)(2,1)S(1)} %multiply_convert_fusion.mine_ref), channel_id=1, source_target_pairs={{0,256},{256,0},{1,257},{257,1},{2,258},{258,2},{3,259},{259,3},{4... | collective-permute-start | bytes 1572872 | tf_op jit(solution)/shard_map/ppermute | solution.py:71
  107.8 24.1 %collective-permute-start.7 = (bf16[128,1024]{1,0:T(8,128)(2,1)S(1)}, bf16[128,1024]{1,0:T(8,128)(2,1)}, u32[]{:S(2)}, u32[]{:S(2)}) collective-permute-start(bf16[128,1024]{1,0:T(8,128)(2,1)S(1)} %get-tuple-element.33), channel_id=1, source_target_pairs={{0,2},{1,3},{2,0},{3,1},{4,6},{5,7},{6,4},{7,5},{8,10},{9,11},{10,... | collective-permute-start | bytes 786440 | tf_op jit(solution)/shard_map/ppermute | solution.py:71
  112.7 19.2 %collective-permute-start.8 = (bf16[128,1024]{1,0:T(8,128)(2,1)S(1)}, bf16[128,1024]{1,0:T(8,128)(2,1)}, u32[]{:S(2)}, u32[]{:S(2)}) collective-permute-start(bf16[128,1024]{1,0:T(8,128)(2,1)S(1)} %get-tuple-element.34), channel_id=1, source_target_pairs={{0,1},{1,2},{2,3},{3,0},{4,5},{5,6},{6,7},{7,4},{8,9},{9,10},{10,1... | collective-permute-start | bytes 786440 | tf_op jit(solution)/shard_map/ppermute | solution.py:71
  115.2 16.7 %collective-permute-start.9 = (bf16[128,1024]{1,0:T(8,128)(2,1)S(1)}, bf16[128,1024]{1,0:T(8,128)(2,1)}, u32[]{:S(2)}, u32[]{:S(2)}) collective-permute-start(bf16[128,1024]{1,0:T(8,128)(2,1)S(1)} %get-tuple-element.35), channel_id=1, source_target_pairs={{0,3},{1,0},{2,1},{3,2},{4,7},{5,4},{6,5},{7,6},{8,11},{9,8},{10,9... | collective-permute-start | bytes 786440 | tf_op jit(solution)/shard_map/ppermute | solution.py:71
  119.8 39.5 %all-to-all-start.2 = ((bf16[64,8,896]{2,1,0:T(8,128)(2,1)}), bf16[64,8,896]{2,1,0:T(8,128)(2,1)}, u32[]{:S(2)}, u32[]{:S(2)}) async-start(bf16[64,8,896]{2,1,0:T(8,128)(2,1)} %bitcast.12), calls=%async_computation.2 | async-start | bytes 1835008 | tf_op jit(solution)/shard_map/all_to_all | solution.py:352
  133.2 15.6 %collective-permute-start.10 = (bf16[128,1024]{1,0:T(8,128)(2,1)S(1)}, bf16[128,1024]{1,0:T(8,128)(2,1)S(1)}, u32[]{:S(2)}, u32[]{:S(2)}) collective-permute-start(bf16[128,1024]{1,0:T(8,128)(2,1)S(1)} %multiply_convert_fusion.1), channel_id=1, source_target_pairs={{0,1},{1,2},{2,3},{3,0},{4,5},{5,6},{6,7},{7,4},{8,9},{9,10},{10,1... | collective-permute-start | bytes 786440 | tf_op jit(solution)/shard_map/ppermute | solution.py:71
  135.1 13.7 %collective-permute-start.11 = (bf16[128,1024]{1,0:T(8,128)(2,1)S(1)}, bf16[128,1024]{1,0:T(8,128)(2,1)S(1)}, u32[]{:S(2)}, u32[]{:S(2)}) collective-permute-start(bf16[128,1024]{1,0:T(8,128)(2,1)S(1)} %multiply_convert_fusion.1), channel_id=1, source_target_pairs={{0,2},{1,3},{2,0},{3,1},{4,6},{5,7},{6,4},{7,5},{8,10},{9,11},{10,... | collective-permute-start | bytes 786440 | tf_op jit(solution)/shard_map/ppermute | solution.py:71
  138.5 12.8 %collective-permute-start.12 = (bf16[128,1024]{1,0:T(8,128)(2,1)S(1)}, bf16[128,1024]{1,0:T(8,128)(2,1)S(1)}, u32[]{:S(2)}, u32[]{:S(2)}) collective-permute-start(bf16[128,1024]{1,0:T(8,128)(2,1)S(1)} %multiply_convert_fusion.1), channel_id=1, source_target_pairs={{0,3},{1,0},{2,1},{3,2},{4,7},{5,4},{6,5},{7,6},{8,11},{9,8},{10,9... | collective-permute-start | bytes 786440 | tf_op jit(solution)/shard_map/ppermute | solution.py:71
  151.4 4.9 %collective-permute-start.13 = (bf16[512,1024]{1,0:T(8,128)(2,1)S(1)}, bf16[512,1024]{1,0:T(8,128)(2,1)S(1)}, u32[]{:S(2)}, u32[]{:S(2)}) collective-permute-start(bf16[512,1024]{1,0:T(8,128)(2,1)S(1)} %pad_maximum_fusion.rows_ref), channel_id=1, source_target_pairs={{0,256},{256,0},{1,257},{257,1},{2,258},{258,2},{3,259},{259,3},{4... | collective-permute-start | bytes 3145736 | tf_op jit(solution)/shard_map/ppermute | solution.py:71
  159.3 12.9 %copy-start.10 = (s32[2]{0:T(128)S(1)}, s32[2]{0:T(128)}, u32[]{:S(2)}) copy-start(s32[2]{0:T(128)} %param.10) | copy-start | bytes 28
  159.3 13.0 %copy-start.6 = (bf16[2,256,576]{1,2,0:T(8,128)(2,1)S(1)}, bf16[2,256,576]{1,2,0:T(8,128)(2,1)}, u32[]{:S(2)}) copy-start(bf16[2,256,576]{1,2,0:T(8,128)(2,1)} %param.9) | copy-start | bytes 1769476
  159.3 61.3 %all-to-all-start.3 = ((bf16[64,2,8,896]{3,2,1,0:T(8,128)(2,1)}), bf16[64,2,8,896]{3,2,1,0:T(8,128)(2,1)S(1)}, u32[]{:S(2)}, u32[]{:S(2)}) async-start(bf16[64,2,8,896]{3,2,1,0:T(8,128)(2,1)} %down_half.3), calls=%async_computation.3 | async-start | bytes 3670016 | tf_op jit(solution)/shard_map/all_to_all | solution.py:352
  172.3 11.2 %copy-start.8 = (bf16[128,512]{0,1:T(8,128)(2,1)S(1)}, bf16[128,512]{0,1:T(8,128)(2,1)}, u32[]{:S(2)}) copy-start(bf16[128,512]{0,1:T(8,128)(2,1)} %fusion.12) | copy-start | bytes 393220
  173.5 11.6 %collective-permute-start.14 = (bf16[2,32,640]{2,1,0:T(8,128)(2,1)S(1)}, bf16[2,32,640]{2,1,0:T(8,128)(2,1)S(1)}, u32[]{:S(2)}, u32[]{:S(2)}) collective-permute-start(bf16[2,32,640]{2,1,0:T(8,128)(2,1)S(1)} %get-tuple-element.50), channel_id=1, source_target_pairs={{0,2},{1,3},{2,0},{3,1},{4,6},{5,7},{6,4},{7,5},{8,10},{9,11},{10,... | collective-permute-start | bytes 245768 | tf_op jit(solution)/shard_map/ppermute | solution.py:71
  176.3 8.8 %collective-permute-start.15 = (bf16[2,32,640]{2,1,0:T(8,128)(2,1)S(1)}, bf16[2,32,640]{2,1,0:T(8,128)(2,1)S(1)}, u32[]{:S(2)}, u32[]{:S(2)}) collective-permute-start(bf16[2,32,640]{2,1,0:T(8,128)(2,1)S(1)} %get-tuple-element.49), channel_id=1, source_target_pairs={{0,1},{1,2},{2,3},{3,0},{4,5},{5,6},{6,7},{7,4},{8,9},{9,10},{10,1... | collective-permute-start | bytes 245768 | tf_op jit(solution)/shard_map/ppermute | solution.py:71
  180.8 39.7 %copy-start.7 = (bf16[128,1024]{0,1:T(8,128)(2,1)S(1)}, bf16[128,1024]{0,1:T(8,128)(2,1)}, u32[]{:S(2)}) copy-start(bf16[128,1024]{0,1:T(8,128)(2,1)} %fusion.6) | copy-start | bytes 786436
  180.8 6.5 %collective-permute-start.16 = (bf16[2,32,640]{2,1,0:T(8,128)(2,1)S(1)}, bf16[2,32,640]{2,1,0:T(8,128)(2,1)S(1)}, u32[]{:S(2)}, u32[]{:S(2)}) collective-permute-start(bf16[2,32,640]{2,1,0:T(8,128)(2,1)S(1)} %get-tuple-element.48), channel_id=1, source_target_pairs={{0,3},{1,0},{2,1},{3,2},{4,7},{5,4},{6,5},{7,6},{8,11},{9,8},{10,9... | collective-permute-start | bytes 245768 | tf_op jit(solution)/shard_map/ppermute | solution.py:71

commit v5 on v3

--- a/solution.py
+++ b/solution.py
@@ -76,6 +76,44 @@
         bytes_accessed=2 * (rows * depth + depth * columns + rows * columns),
         transcendentals=0,
     )
+
+
+def select_kernel(ids_ref, rows_ref, rank_ref, out_ref):
+    top, rows = ids_ref.shape
+    experts, slots, columns = out_ref.shape
+    named = jnp.zeros((experts, rows), jnp.float32)
+    numbers = lax.broadcasted_iota(jnp.int32, (experts, rows), 0)
+    for k in range(top):
+        named = jnp.where(ids_ref[k : k + 1, :] == numbers, 1.0, named)
+    above = lax.broadcasted_iota(jnp.int32, (rows, rows), 0)
+    right = lax.broadcasted_iota(jnp.int32, (rows, rows), 1)
+    before = jnp.dot(
+        named.astype(jnp.bfloat16),
+        jnp.where(above < right, 1.0, 0.0).astype(jnp.bfloat16),
+        preferred_element_type=jnp.float32,
+    )
+    rank = jnp.where(named > 0.5, before, -1.0)
+    rank_ref[...] = rank
+    slot = lax.broadcasted_iota(jnp.int32, (experts, slots, rows), 1).astype(jnp.float32)
+    placed = jnp.where(rank[:, None, :] == slot, 1.0, 0.0).reshape(experts * slots, rows)
+    made = jnp.dot(
+        placed.astype(jnp.bfloat16), rows_ref[...], preferred_element_type=jnp.float32
+    )
+    out_ref[...] = made.reshape(experts, slots, columns).astype(out_ref.dtype)
+
+
+def first_selection(ids, rows_in):
+    rows, columns = rows_in.shape
+    return pl.pallas_call(
+        select_kernel,
+        out_shape=[
+            jax.ShapeDtypeStruct((EXPERTS, rows), jnp.float32),
+            jax.ShapeDtypeStruct((EXPERTS, FIRST, columns), jnp.bfloat16),
+        ],
+        compiler_params=pltpu.CompilerParams(vmem_limit_bytes=VMEM),
+        cost_estimate=cost(EXPERTS * FIRST, rows, columns),
+        name="first_selection",
+    )(ids.T, rows_in)
 
 
 def their_kernel(where, rows_ref, weight_ref, out_ref):
@@ -161,6 +199,23 @@
     )(where, rows_in, weight, arrived)
 
 
+def copy_kernel(from_ref, to_ref, sem):
+    copy = pltpu.make_async_copy(from_ref, to_ref, sem)
+    copy.start()
+    copy.wait()
+
+
+def copied(value):
+    return pl.pallas_call(
+        copy_kernel,
+        out_shape=jax.ShapeDtypeStruct(value.shape, value.dtype),
+        in_specs=[pl.BlockSpec(memory_space=pl.ANY)],
+        out_specs=pl.BlockSpec(memory_space=pl.ANY),
+        scratch_shapes=[pltpu.SemaphoreType.DMA],
+        name="copied",
+    )(value)
+
+
 def down_kernel(where, mine_ref, theirs_ref, weight_ref, out_ref):
     @pl.when(pl.program_id(0) == 0)
     def _():
@@ -175,27 +230,23 @@
         ).astype(out_ref.dtype)
 
 
-def down_both(where, mine, theirs, weight, size):
+def down_both(where, mine, theirs, weight):
     half, depth = mine.shape
-    columns = weight.shape[1]
-    share = half // size
-
-    def place(core, back, where):
-        which = where[0] + core - 2 * where[0] * core
-        return which * size + lax.rem(where[1] * (size > 1) + size - back, size), 0
-
+    columns = weight.shape[2]
     return pl.pallas_call(
         down_kernel,
         out_shape=jax.ShapeDtypeStruct((2 * half, columns), jnp.bfloat16),
         grid_spec=pltpu.PrefetchScalarGridSpec(
             num_scalar_prefetch=1,
-            grid=(2, size),
+            grid=(2,),
             in_specs=[
-                pl.BlockSpec((share, depth), lambda h, i, where: (i * (1 - h) + (size - 1) * h, 0)),
-                pl.BlockSpec((share, depth), lambda h, i, where: (i * h, 0)),
-                pl.BlockSpec((depth, columns), lambda h, i, where: (0, 0)),
+                pl.BlockSpec((half, depth), lambda h, where: (0, 0)),
+                pl.BlockSpec((half, depth), lambda h, where: (0, 0)),
+                pl.BlockSpec((None, depth, columns), lambda h, where: (0, 0, 0)),
             ],
-            out_specs=pl.BlockSpec((share, columns), place),
+            out_specs=pl.BlockSpec(
+                (half, columns), lambda h, where: (where[0] + h - 2 * where[0] * h, 0)
+            ),
         ),
         compiler_params=pltpu.CompilerParams(vmem_limit_bytes=VMEM),
         cost_estimate=cost(2 * half, depth, columns),
@@ -270,12 +321,12 @@
 
 def down_half(where, core, rows_in, weight, made, sources):
     rows, depth = rows_in.shape
-    columns = weight.shape[1]
+    columns = weight.shape[2]
     slots = rows // sources
     tile = rows // 2
     in_specs = [
         pl.BlockSpec((tile, depth), lambda i, where: (i, 0)),
-        pl.BlockSpec((depth, columns), lambda i, where: (0, 0)),
+        pl.BlockSpec((None, depth, columns), lambda i, where: (0, 0, 0)),
     ]
     inputs = [rows_in, weight]
     aliases = {}
@@ -310,7 +361,7 @@
     for piece in pieces:
         own = own + piece.astype(jnp.float32)
     mine = jax.nn.silu(own).astype(jnp.bfloat16)
-    return down_both(where, mine, turned(mine, "role", 1), down, 1)
+    return down_both(where, mine, turned(mine, "role", 1), down)
 
 
 def wide_rows(where, rows_in, up, other_up, down, sources):
@@ -340,58 +391,47 @@
     owners = lax.axis_size("grp")
     experts = jnp.arange(EXPERTS, dtype=jnp.int32)
     where = jnp.stack([lax.axis_index("role"), lax.axis_index("tp")]).astype(jnp.int32)
-    up = up_weight[0]
-    down = down_weight[0]
-
-    named = expert_ids[:, None, :] == experts[None, :, None]
-    named_any = jnp.any(named, axis=2)
-    row_numbers = jnp.arange(rows, dtype=jnp.int32)
-    lower = (row_numbers[None, :] < row_numbers[:, None]).astype(jnp.bfloat16)
-    before = jnp.dot(
-        lower, named_any.astype(jnp.bfloat16), preferred_element_type=jnp.float32
-    ).astype(jnp.int32)
-    rank = jnp.where(named_any, before, -1)
-    rank_by_expert = rank.T
+
+    rank, first_out = first_selection(expert_ids, hidden)
 
     def exchanged(value):
         return lax.all_to_all(value, "grp", split_axis=0, concat_axis=0, tiled=True)
 
     def outgoing(first, count, source):
-        slots = first + jnp.arange(count, dtype=jnp.int32)
-        placed = rank_by_expert[:, None, :] == slots[None, :, None]
+        slots = (first + jnp.arange(count, dtype=jnp.int32)).astype(jnp.float32)
+        placed = rank[:, None, :] == slots[None, :, None]
         placed = placed.reshape(-1, rows).astype(jnp.bfloat16)
         made = jnp.dot(placed, source, preferred_element_type=jnp.float32).astype(jnp.bfloat16)
         return made.reshape(owners, count, source.shape[1])
 
     def weights(first, last):
-        slots = jnp.arange(first, last, dtype=jnp.int32)
-        taken = rank[:, :, None] == slots[None, None, :]
-        return jnp.concatenate(
-            two_halves(jnp.where(taken, weight_of[:, :, None], 0.0).reshape(rows, -1)), axis=0
-        )
-
-    first_out = outgoing(0, FIRST, hidden)
+        slots = jnp.arange(first, last, dtype=jnp.int32).astype(jnp.float32)
+        taken = rank.T[:, :, None] == slots[None, None, :]
+        return jnp.where(taken, weight_of[:, :, None], 0.0).reshape(rows, -1).astype(jnp.bfloat16)
+
     first_out, hidden = lax.optimization_barrier((first_out, hidden))
     first_in = exchanged(first_out)
 
     wide = jnp.concatenate([hidden, turned(hidden, "role", 1)], axis=1)
+    passed_up = copied(up_weight[0])
 
     sigmoid_terms = jax.nn.sigmoid(route_logits)
     route_weights = 2.5 * sigmoid_terms / jnp.sum(sigmoid_terms, axis=-1, keepdims=True)
+    named = expert_ids[:, None, :] == experts[None, :, None]
     weight_of = jnp.sum(jnp.where(named, route_weights[:, None, :], 0.0), axis=2)
     weights_of = [weights(0, FIRST), weights(FIRST, CAP)]
 
     half = (CAP - FIRST) // 2
     begin = FIRST + where[0] * half
     second_out, first_in, passed_up, *weights_of = lax.optimization_barrier(
-        (outgoing(begin, half, wide), first_in, up, *weights_of)
+        (outgoing(begin, half, wide), first_in, passed_up, *weights_of)
     )
     second_in = exchanged(second_out)
     other_up = turned(passed_up, "role", 1)
-    first_out = narrow_rows(where, first_in.reshape(-1, width), up, down)
+    first_out = narrow_rows(where, first_in.reshape(-1, width), up_weight[0], down_weight)
     second_in, first_out = lax.optimization_barrier((second_in, first_out))
     first_back = exchanged(first_out.reshape(owners, FIRST, width))
-    second_out = wide_rows(where, second_in.reshape(-1, 2 * width), up, other_up, down, owners)
+    second_out = wide_rows(where, second_in.reshape(-1, 2 * width), up_weight[0], other_up, down_weight, owners)
     second_out, first_back, q_latent = lax.optimization_barrier((second_out, first_back, q_latent))
     second_back = exchanged(second_out)
 
@@ -409,8 +449,7 @@
     second_back = second_back.reshape(-1, width)
     result = jnp.dot(weights_of[0], first_back, preferred_element_type=jnp.float32)
     result = result + jnp.dot(weights_of[1], second_back, preferred_element_type=jnp.float32)
-    moe_output = (result[:rows] + result[rows:]).astype(jnp.bfloat16)
-    return (attn_context, moe_output)
+    return (attn_context, result.astype(jnp.bfloat16))
 
 
 def solution(mesh):

time: 222 us -> 262 us (1.18)
  Pallas kernels: 19.8 us -> 75.1 us
  waiting for transfers between devices: 84.6 us -> 67.6 us
  starting transfers between devices: 99 us -> 103 us
  other arithmetic: 7.55 us -> 4.32 us
    pallas_call x0 -> x2, Pallas kernels: none -> 58.2 us  [the longest x1 56.7 us: copied(): pl.pallas_call(copy_kernel, out_shape=jax.ShapeDtypeStruct(value.shape, v...]
    all_to_all x4, waiting for transfers between devices: 54.8 us -> 31.5 us  [exchanged(): return lax.all_to_all(value, 'grp', split_axis=0, concat_axis=0, tiled=True)]
    ppermute x17, waiting for transfers between devices: 29.8 us -> 36 us  [turned(): lax.ppermute(value, axis, [(k, (k + step) % size) for k in range(size)])]
    all_to_all x4, starting transfers between devices: 45.9 us -> 52 us  [exchanged(): return lax.all_to_all(value, 'grp', split_axis=0, concat_axis=0, tiled=True)]
  transfers between devices with their start and end apart: 21 -> 21, of which waited for: 10 -> 10; matrix products, arithmetic and copies ran while one was open for 5% -> 4% of each run, Pallas kernels for 6% -> 26%
where the time goes in v5:
time: 262 us; the launch traced here: 261 us
  starting transfers between devices  103 us (39%)
  Pallas kernels  75.1 us (29%)
  waiting for transfers between devices  67.6 us (26%)
  matrix products  8.12 us (3%)
  other arithmetic  4.32 us (2%)
    pallas_call x1, Pallas kernels, copied(): pl.pallas_call(copy_kernel, out_shape=jax.ShapeDtypeStruct(value.shape, v...  56.7 us
    all_to_all x4, starting transfers between devices, exchanged(): return lax.all_to_all(value, 'grp', split_axis=0, concat_axis=0, tiled=True)  52 us
    ppermute x17, starting transfers between devices, turned(): lax.ppermute(value, axis, [(k, (k + step) % size) for k in range(size)])  50.9 us
    ppermute x17, waiting for transfers between devices, turned(): lax.ppermute(value, axis, [(k, (k + step) % size) for k in range(size)])  36 us
    all_to_all x4, waiting for transfers between devices, exchanged(): return lax.all_to_all(value, 'grp', split_axis=0, concat_axis=0, tiled=True)  31.5 us
    pallas_call x2, Pallas kernels, down_half(): pl.pallas_call(down_half_kernel, out_shape=jax.ShapeDtypeStruct((sources,...  5.91 us
    pallas_call x1, Pallas kernels, wide_product(): pl.pallas_call(wide_kernel, out_shape=[jax.ShapeDtypeStruct((share, colum...  5.69 us
  transfers between devices with their start and end apart: 21, of which 10 were waited for; matrix products, arithmetic and copies ran while one was open for 4% of the time, Pallas kernels for 26%

profile of v5, /device:TPU:24, one launch (start us, length us, event | category | flops | bytes accessed | tf_op | source)
XLA Modules:
  0.0 261.3 jit_solution(8910087440937750904)
XLA Ops:
  0.7 1.0 copy-done.4
  1.6 0.7 copy-done.6
  2.3 1.5 first_selection.1
  3.8 16.4 %all-to-all-start = ((bf16[64,8,896]{2,1,0:T(8,128)(2,1)}), bf16[64,8,896]{2,1,0:T(8,128)(2,1)S(1)}, u32[]{:S(2)}, u32[]{:S(2)}) async-start(bf16[64,8,896]{2,1,0:T(8,128)(2,1)} %get-tuple-element.25), calls=%async_computation | async-start | bytes 1835008 | tf_op jit(solution)/shard_map/all_to_all | solution.py:398
  20.2 1.9 collective-permute-start
  22.2 0.1 select_reduce_fusion
  22.3 0.1 eq.81
  22.4 56.7 %copied.1 = bf16[896,1024]{1,0:T(8,128)(2,1)} custom-call(bf16[896,1024]{1,0:T(8,128)(2,1)} %bitcast.52), custom_call_target="tpu_custom_call" | custom-call | tf_op jit(solution)/shard_map/copied/pallas_call | solution.py:209
  79.1 0.1 eq.87
  79.2 0.1 eq.96
  79.3 0.9 fusion.6
  80.2 0.8 fusion.12
  81.0 2.0 fusion
  83.0 13.0 %all-to-all-start.1 = ((bf16[64,8,1792]{2,1,0:T(8,128)(2,1)}), bf16[64,8,1792]{2,1,0:T(8,128)(2,1)}, u32[]{:S(2)}, u32[]{:S(2)}) async-start(bf16[64,8,1792]{2,1,0:T(8,128)(2,1)} %fusion), calls=%async_computation.1 | async-start | bytes 3670016 | tf_op jit(solution)/shard_map/all_to_all | solution.py:398
  96.0 0.1 pad_add_fusion.where
  96.1 1.2 their_half.1
  97.3 1.9 collective-permute-start.1
  99.3 2.4 collective-permute-start.6
  101.7 1.3 own_half.1
  103.0 4.8 %collective-permute-start.4 = (bf16[256,1024]{1,0:T(8,128)(2,1)S(1)}, bf16[256,1024]{1,0:T(8,128)(2,1)S(1)}, u32[]{:S(2)}, u32[]{:S(2)}) collective-permute-start(bf16[256,1024]{1,0:T(8,128)(2,1)S(1)} %get-tuple-element.29), channel_id=1, source_target_pairs={{0,3},{1,0},{2,1},{3,2},{4,7},{5,4},{6,5},{7,6},{8,11},{9,8},{10,9... | collective-permute-start | bytes 1572872 | tf_op jit(solution)/shard_map/ppermute | solution.py:70
  107.8 1.9 collective-permute-start.3
  109.7 4.2 %collective-permute-start.2 = (bf16[256,1024]{1,0:T(8,128)(2,1)S(1)}, bf16[256,1024]{1,0:T(8,128)(2,1)S(1)}, u32[]{:S(2)}, u32[]{:S(2)}) collective-permute-start(bf16[256,1024]{1,0:T(8,128)(2,1)S(1)} %get-tuple-element.29), channel_id=1, source_target_pairs={{0,2},{1,3},{2,0},{3,1},{4,6},{5,7},{6,4},{7,5},{8,10},{9,11},{10,... | collective-permute-start | bytes 1572872 | tf_op jit(solution)/shard_map/ppermute | solution.py:70
  113.9 16.5 %collective-permute-done.4 = bf16[256,1024]{1,0:T(8,128)(2,1)S(1)} collective-permute-done((bf16[256,1024]{1,0:T(8,128)(2,1)S(1)}, bf16[256,1024]{1,0:T(8,128)(2,1)S(1)}, u32[]{:S(2)}, u32[]{:S(2)}) %collective-permute-start.4) | collective-permute-done | bytes 524320 | tf_op jit(solution)/shard_map/ppermute | solution.py:70
  130.4 5.3 %collective-permute-done.3 = bf16[256,1024]{1,0:T(8,128)(2,1)S(1)} collective-permute-done((bf16[256,1024]{1,0:T(8,128)(2,1)S(1)}, bf16[256,1024]{1,0:T(8,128)(2,1)S(1)}, u32[]{:S(2)}, u32[]{:S(2)}) %collective-permute-start.3) | collective-permute-done | bytes 524320 | tf_op jit(solution)/shard_map/ppermute | solution.py:70
  135.7 0.5 multiply_convert_fusion.mine_ref
  136.1 1.9 collective-permute-start.5
  138.1 1.9 collective-permute-done.5.theirs_ref
  140.0 2.8 %down_both.1 = bf16[512,896]{1,0:T(8,128)(2,1)} custom-call(s32[2]{0:T(128)S(1)} %pad_add_fusion.where, bf16[256,1024]{1,0:T(8,128)(2,1)S(1)} %multiply_convert_fusion.mine_ref, bf16[256,1024]{1,0:T(8,128)(2,1)S(1)} %collective-permute-done.5.theirs_ref, bf16[1,1024,896]{2,1,0:T(8,128)(2,1)S(1)} %copy-done.2), custom_call_target="tpu_custom_call" | custom-call | flops 939524096 | bytes 3801088 | tf_op jit(solution)/shard_map/down_both/pallas_call | solution.py:236
  142.8 1.6 all-to-all-done.1
  144.4 5.7 %wide_product.1 = (f32[128,1024]{1,0:T(8,128)S(1)}, bf16[128,1024]{1,0:T(8,128)(2,1)S(1)}, bf16[128,1024]{1,0:T(8,128)(2,1)S(1)}, bf16[128,1024]{1,0:T(8,128)(2,1)}) custom-call(s32[2]{0:T(128)S(1)} %pad_add_fusion.where, bf16[512,1792]{1,0:T(8,128)(2,1)} %bitcast.12.rows_ref, bf16[896,1024]{1,0:T(8,128)(2,1)S(1)} %bitcast.55, ...), custom_call_target="tpu_custom_call" | custom-call | flops 1879048192 | bytes 6553600 | tf_op jit(solution)/shard_map/wide_product/pallas_call | solution.py:285
  150.1 4.7 %collective-permute-start.9 = (bf16[128,1024]{1,0:T(8,128)(2,1)}, bf16[128,1024]{1,0:T(8,128)(2,1)S(1)}, u32[]{:S(2)}, u32[]{:S(2)}) collective-permute-start(bf16[128,1024]{1,0:T(8,128)(2,1)} %get-tuple-element.35), channel_id=1, source_target_pairs={{0,3},{1,0},{2,1},{3,2},{4,7},{5,4},{6,5},{7,6},{8,11},{9,8},{10,9... | collective-permute-start | bytes 786440 | tf_op jit(solution)/shard_map/ppermute | solution.py:70
  154.8 1.9 collective-permute-start.8
  156.7 4.2 %collective-permute-start.7 = (bf16[128,1024]{1,0:T(8,128)(2,1)S(1)}, bf16[128,1024]{1,0:T(8,128)(2,1)S(1)}, u32[]{:S(2)}, u32[]{:S(2)}) collective-permute-start(bf16[128,1024]{1,0:T(8,128)(2,1)S(1)} %get-tuple-element.33), channel_id=1, source_target_pairs={{0,2},{1,3},{2,0},{3,1},{4,6},{5,7},{6,4},{7,5},{8,10},{9,11},{10,... | collective-permute-start | bytes 786440 | tf_op jit(solution)/shard_map/ppermute | solution.py:70
  160.9 9.7 %all-to-all-start.2 = ((bf16[64,8,896]{2,1,0:T(8,128)(2,1)}), bf16[64,8,896]{2,1,0:T(8,128)(2,1)S(1)}, u32[]{:S(2)}, u32[]{:S(2)}) async-start(bf16[64,8,896]{2,1,0:T(8,128)(2,1)} %bitcast.13), calls=%async_computation.2 | async-start | bytes 1835008 | tf_op jit(solution)/shard_map/all_to_all | solution.py:398
  170.6 0.3 collective-permute-done.8
  170.9 0.2 multiply_convert_fusion.1
  171.2 2.9 %collective-permute-start.12 = (bf16[128,1024]{1,0:T(8,128)(2,1)S(1)}, bf16[128,1024]{1,0:T(8,128)(2,1)S(1)}, u32[]{:S(2)}, u32[]{:S(2)}) collective-permute-start(bf16[128,1024]{1,0:T(8,128)(2,1)S(1)} %multiply_convert_fusion.1), channel_id=1, source_target_pairs={{0,3},{1,0},{2,1},{3,2},{4,7},{5,4},{6,5},{7,6},{8,11},{9,8},{10,9... | collective-permute-start | bytes 786440 | tf_op jit(solution)/shard_map/ppermute | solution.py:70
  174.1 4.7 %collective-permute-start.11 = (bf16[128,1024]{1,0:T(8,128)(2,1)S(1)}, bf16[128,1024]{1,0:T(8,128)(2,1)S(1)}, u32[]{:S(2)}, u32[]{:S(2)}) collective-permute-start(bf16[128,1024]{1,0:T(8,128)(2,1)S(1)} %multiply_convert_fusion.1), channel_id=1, source_target_pairs={{0,2},{1,3},{2,0},{3,1},{4,6},{5,7},{6,4},{7,5},{8,10},{9,11},{10,... | collective-permute-start | bytes 786440 | tf_op jit(solution)/shard_map/ppermute | solution.py:70
  178.8 1.9 collective-permute-start.10
  180.7 1.4 collective-permute-done.12
  182.1 4.7 %collective-permute-done.11 = bf16[128,1024]{1,0:T(8,128)(2,1)S(1)} collective-permute-done((bf16[128,1024]{1,0:T(8,128)(2,1)S(1)}, bf16[128,1024]{1,0:T(8,128)(2,1)S(1)}, u32[]{:S(2)}, u32[]{:S(2)}) %collective-permute-start.11) | collective-permute-done | bytes 262176 | tf_op jit(solution)/shard_map/ppermute | solution.py:70
  186.7 3.2 %collective-permute-done.10 = bf16[128,1024]{1,0:T(8,128)(2,1)S(1)} collective-permute-done((bf16[128,1024]{1,0:T(8,128)(2,1)S(1)}, bf16[128,1024]{1,0:T(8,128)(2,1)S(1)}, u32[]{:S(2)}, u32[]{:S(2)}) %collective-permute-start.10) | collective-permute-done | bytes 262176 | tf_op jit(solution)/shard_map/ppermute | solution.py:70
  190.0 0.1 pad_maximum_fusion.rows_ref
  190.0 1.9 collective-permute-start.13
  192.0 3.0 %down_half.2.rest_0_ = bf16[64,2,8,896]{3,2,1,0:T(8,128)(2,1)} custom-call(s32[2]{0:T(128)S(1)} %pad_add_fusion.where, bf16[512,1024]{1,0:T(8,128)(2,1)S(1)} %pad_maximum_fusion.rows_ref, bf16[1,1024,896]{2,1,0:T(8,128)(2,1)S(1)} %copy-done.3), custom_call_target="tpu_custom_call" | custom-call | flops 939524096 | bytes 3801088 | tf_op jit(solution)/shard_map/down_half/pallas_call | solution.py:341
  194.9 2.9 %down_half.3 = bf16[64,2,8,896]{3,2,1,0:T(8,128)(2,1)} custom-call(s32[2]{0:T(128)S(1)} %pad_add_fusion.where, bf16[512,1024]{1,0:T(8,128)(2,1)S(1)} %collective-permute-done.13.rows_ref, bf16[1,1024,896]{2,1,0:T(8,128)(2,1)S(1)} %copy-done.3, bf16[64,2,8,896]{3,2,1,0:T(8,128)(2,1)} %down_half.2.rest_0_), custom_call_target="tpu_custom_call", output_to_operand_aliasing={{}: (3, {})} | custom-call | flops 939524096 | bytes 3801088 | tf_op jit(solution)/shard_map/down_half/pallas_call | solution.py:341
  197.9 12.8 %all-to-all-start.3 = ((bf16[64,2,8,896]{3,2,1,0:T(8,128)(2,1)}), bf16[64,2,8,896]{3,2,1,0:T(8,128)(2,1)S(1)}, u32[]{:S(2)}, u32[]{:S(2)}) async-start(bf16[64,2,8,896]{3,2,1,0:T(8,128)(2,1)} %down_half.3), calls=%async_computation.3 | async-start | bytes 3670016 | tf_op jit(solution)/shard_map/all_to_all | solution.py:398
  210.8 0.1 broadcast_compare_fusion
  210.9 1.5 fusion.26
  212.3 0.2 fusion.13
  212.6 0.1 copy.34
  212.7 1.4 convolution_convert_fusion.1
  214.2 2.4 collective-permute-start.16
  216.6 3.4 %collective-permute-start.15 = (bf16[2,32,640]{2,1,0:T(8,128)(2,1)S(1)}, bf16[2,32,640]{2,1,0:T(8,128)(2,1)S(1)}, u32[]{:S(2)}, u32[]{:S(2)}) collective-permute-start(bf16[2,32,640]{2,1,0:T(8,128)(2,1)S(1)} %get-tuple-element.49), channel_id=1, source_target_pairs={{0,1},{1,2},{2,3},{3,0},{4,5},{5,6},{6,7},{7,4},{8,9},{9,10},{10,1... | collective-permute-start | bytes 245768 | tf_op jit(solution)/shard_map/ppermute | solution.py:70
  220.0 3.8 %collective-permute-start.14 = (bf16[2,32,640]{2,1,0:T(8,128)(2,1)S(1)}, bf16[2,32,640]{2,1,0:T(8,128)(2,1)S(1)}, u32[]{:S(2)}, u32[]{:S(2)}) collective-permute-start(bf16[2,32,640]{2,1,0:T(8,128)(2,1)S(1)} %get-tuple-element.50), channel_id=1, source_target_pairs={{0,2},{1,3},{2,0},{3,1},{4,6},{5,7},{6,4},{7,5},{8,10},{9,11},{10,... | collective-permute-start | bytes 245768 | tf_op jit(solution)/shard_map/ppermute | solution.py:70
  223.8 1.2 fusion.3
  225.1 2.8 %collective-permute-done.14 = bf16[2,32,640]{2,1,0:T(8,128)(2,1)S(1)} collective-permute-done((bf16[2,32,640]{2,1,0:T(8,128)(2,1)S(1)}, bf16[2,32,640]{2,1,0:T(8,128)(2,1)S(1)}, u32[]{:S(2)}, u32[]{:S(2)}) %collective-permute-start.14) | collective-permute-done | bytes 81952 | tf_op jit(solution)/shard_map/ppermute | solution.py:70
  227.9 0.1 slice_reduce_fusion.1
  228.0 0.3 slice_reduce_fusion
  228.3 0.1 pad_maximum_fusion.1
  228.4 0.1 multiply_reduce_fusion
  228.5 0.7 divide_convert_fusion
  229.2 29.9 %all-to-all-done.3 = bf16[64,2,8,896]{3,2,1,0:T(8,128)(2,1)S(1)} async-done(((bf16[64,2,8,896]{3,2,1,0:T(8,128)(2,1)}), bf16[64,2,8,896]{3,2,1,0:T(8,128)(2,1)S(1)}, u32[]{:S(2)}, u32[]{:S(2)}) %all-to-all-start.3) | async-done | bytes 1835040 | tf_op jit(solution)/shard_map/all_to_all | solution.py:398
  259.2 2.1 fusion.1
  (45 shorter events, 0.3 us)
Async XLA Ops:
  0.6 210.2 %copy-start = (bf16[2,128,576]{1,2,0:T(8,128)(2,1)S(1)}, bf16[2,128,576]{1,2,0:T(8,128)(2,1)}, u32[]{:S(2)}) copy-start(bf16[2,128,576]{1,2,0:T(8,128)(2,1)} %param.8) | copy-start | bytes 884740
  0.6 1.0 copy-start.4
  1.6 0.7 copy-start.6
  2.3 17.9 %copy-start.5 = (bf16[128,896]{1,0:T(8,128)(2,1)S(1)}, bf16[128,896]{1,0:T(8,128)(2,1)}, u32[]{:S(2)}) copy-start(bf16[128,896]{1,0:T(8,128)(2,1)} %rows_ref.1) | copy-start | bytes 688132
  2.3 19.8 %copy-start.8 = (f32[128,8]{0,1:T(8,128)S(1)}, f32[128,8]{0,1:T(8,128)}, u32[]{:S(2)}) copy-start(f32[128,8]{0,1:T(8,128)} %param.13) | copy-start | bytes 12292
  2.3 19.9 %copy-start.7 = (s32[128,8]{0,1:T(8,128)S(1)}, s32[128,8]{0,1:T(8,128)}, u32[]{:S(2)}) copy-start(s32[128,8]{0,1:T(8,128)} %param.12) | copy-start | bytes 12292
  3.8 79.2 %all-to-all-start = ((bf16[64,8,896]{2,1,0:T(8,128)(2,1)}), bf16[64,8,896]{2,1,0:T(8,128)(2,1)S(1)}, u32[]{:S(2)}, u32[]{:S(2)}) async-start(bf16[64,8,896]{2,1,0:T(8,128)(2,1)} %get-tuple-element.25), calls=%async_computation | async-start | bytes 1835008 | tf_op jit(solution)/shard_map/all_to_all | solution.py:398
  20.2 60.8 %collective-permute-start = (bf16[128,896]{1,0:T(8,128)(2,1)S(1)}, bf16[128,896]{1,0:T(8,128)(2,1)S(1)}, u32[]{:S(2)}, u32[]{:S(2)}) collective-permute-start(bf16[128,896]{1,0:T(8,128)(2,1)S(1)} %copy-done.5), channel_id=1, source_target_pairs={{0,256},{256,0},{1,257},{257,1},{2,258},{258,2},{3,259},{259,3},{4... | collective-permute-start | bytes 688136 | tf_op jit(solution)/shard_map/ppermute | solution.py:70
  83.0 13.1 %copy-start.1 = (bf16[1,896,1024]{2,1,0:T(8,128)(2,1)S(1)}, bf16[1,896,1024]{2,1,0:T(8,128)(2,1)}, u32[]{:S(2)}) copy-start(bf16[1,896,1024]{2,1,0:T(8,128)(2,1)} %param.14) | copy-start | bytes 5505028
  83.0 61.4 %all-to-all-start.1 = ((bf16[64,8,1792]{2,1,0:T(8,128)(2,1)}), bf16[64,8,1792]{2,1,0:T(8,128)(2,1)}, u32[]{:S(2)}, u32[]{:S(2)}) async-start(bf16[64,8,1792]{2,1,0:T(8,128)(2,1)} %fusion), calls=%async_computation.1 | async-start | bytes 3670016 | tf_op jit(solution)/shard_map/all_to_all | solution.py:398
  97.3 4.3 %collective-permute-start.1 = (bf16[256,1024]{1,0:T(8,128)(2,1)S(1)}, bf16[256,1024]{1,0:T(8,128)(2,1)S(1)}, u32[]{:S(2)}, u32[]{:S(2)}) collective-permute-start(bf16[256,1024]{1,0:T(8,128)(2,1)S(1)} %their_half.1), channel_id=1, source_target_pairs={{0,256},{256,0},{1,257},{257,1},{2,258},{258,2},{3,259},{259,3},{4... | collective-permute-start | bytes 1572872 | tf_op jit(solution)/shard_map/ppermute | solution.py:70
  99.3 45.1 %collective-permute-start.6 = (bf16[896,1024]{1,0:T(8,128)(2,1)}, bf16[896,1024]{1,0:T(8,128)(2,1)}, u32[]{:S(2)}, u32[]{:S(2)}) collective-permute-start(bf16[896,1024]{1,0:T(8,128)(2,1)} %copied.1), channel_id=1, source_target_pairs={{0,256},{256,0},{1,257},{257,1},{2,258},{258,2},{3,259},{259,3},{4... | collective-permute-start | bytes 5505032 | tf_op jit(solution)/shard_map/ppermute | solution.py:70
  103.0 37.0 %copy-start.2 = (bf16[1,1024,896]{2,1,0:T(8,128)(2,1)S(1)}, bf16[1,1024,896]{2,1,0:T(8,128)(2,1)}, u32[]{:S(2)}) copy-start(bf16[1,1024,896]{2,1,0:T(8,128)(2,1)} %weight_ref.5) | copy-start | bytes 5505028
  103.0 27.4 %collective-permute-start.4 = (bf16[256,1024]{1,0:T(8,128)(2,1)S(1)}, bf16[256,1024]{1,0:T(8,128)(2,1)S(1)}, u32[]{:S(2)}, u32[]{:S(2)}) collective-permute-start(bf16[256,1024]{1,0:T(8,128)(2,1)S(1)} %get-tuple-element.29), channel_id=1, source_target_pairs={{0,3},{1,0},{2,1},{3,2},{4,7},{5,4},{6,5},{7,6},{8,11},{9,8},{10,9... | collective-permute-start | bytes 1572872 | tf_op jit(solution)/shard_map/ppermute | solution.py:70
  107.8 27.9 %collective-permute-start.3 = (bf16[256,1024]{1,0:T(8,128)(2,1)S(1)}, bf16[256,1024]{1,0:T(8,128)(2,1)S(1)}, u32[]{:S(2)}, u32[]{:S(2)}) collective-permute-start(bf16[256,1024]{1,0:T(8,128)(2,1)S(1)} %get-tuple-element.29), channel_id=1, source_target_pairs={{0,1},{1,2},{2,3},{3,0},{4,5},{5,6},{6,7},{7,4},{8,9},{9,10},{10,1... | collective-permute-start | bytes 1572872 | tf_op jit(solution)/shard_map/ppermute | solution.py:70
  109.7 26.0 %collective-permute-start.2 = (bf16[256,1024]{1,0:T(8,128)(2,1)S(1)}, bf16[256,1024]{1,0:T(8,128)(2,1)S(1)}, u32[]{:S(2)}, u32[]{:S(2)}) collective-permute-start(bf16[256,1024]{1,0:T(8,128)(2,1)S(1)} %get-tuple-element.29), channel_id=1, source_target_pairs={{0,2},{1,3},{2,0},{3,1},{4,6},{5,7},{6,4},{7,5},{8,10},{9,11},{10,... | collective-permute-start | bytes 1572872 | tf_op jit(solution)/shard_map/ppermute | solution.py:70
  136.1 3.8 %collective-permute-start.5 = (bf16[256,1024]{1,0:T(8,128)(2,1)S(1)}, bf16[256,1024]{1,0:T(8,128)(2,1)S(1)}, u32[]{:S(2)}, u32[]{:S(2)}) collective-permute-start(bf16[256,1024]{1,0:T(8,128)(2,1)S(1)} %multiply_convert_fusion.mine_ref), channel_id=1, source_target_pairs={{0,256},{256,0},{1,257},{257,1},{2,258},{258,2},{3,259},{259,3},{4... | collective-permute-start | bytes 1572872 | tf_op jit(solution)/shard_map/ppermute | solution.py:70
  150.1 20.5 %collective-permute-start.9 = (bf16[128,1024]{1,0:T(8,128)(2,1)}, bf16[128,1024]{1,0:T(8,128)(2,1)S(1)}, u32[]{:S(2)}, u32[]{:S(2)}) collective-permute-start(bf16[128,1024]{1,0:T(8,128)(2,1)} %get-tuple-element.35), channel_id=1, source_target_pairs={{0,3},{1,0},{2,1},{3,2},{4,7},{5,4},{6,5},{7,6},{8,11},{9,8},{10,9... | collective-permute-start | bytes 786440 | tf_op jit(solution)/shard_map/ppermute | solution.py:70
  154.8 16.2 %collective-permute-start.8 = (bf16[128,1024]{1,0:T(8,128)(2,1)S(1)}, bf16[128,1024]{1,0:T(8,128)(2,1)S(1)}, u32[]{:S(2)}, u32[]{:S(2)}) collective-permute-start(bf16[128,1024]{1,0:T(8,128)(2,1)S(1)} %get-tuple-element.34), channel_id=1, source_target_pairs={{0,1},{1,2},{2,3},{3,0},{4,5},{5,6},{6,7},{7,4},{8,9},{9,10},{10,1... | collective-permute-start | bytes 786440 | tf_op jit(solution)/shard_map/ppermute | solution.py:70
  156.7 14.2 %collective-permute-start.7 = (bf16[128,1024]{1,0:T(8,128)(2,1)S(1)}, bf16[128,1024]{1,0:T(8,128)(2,1)S(1)}, u32[]{:S(2)}, u32[]{:S(2)}) collective-permute-start(bf16[128,1024]{1,0:T(8,128)(2,1)S(1)} %get-tuple-element.33), channel_id=1, source_target_pairs={{0,2},{1,3},{2,0},{3,1},{4,6},{5,7},{6,4},{7,5},{8,10},{9,11},{10,... | collective-permute-start | bytes 786440 | tf_op jit(solution)/shard_map/ppermute | solution.py:70
  160.9 37.0 %all-to-all-start.2 = ((bf16[64,8,896]{2,1,0:T(8,128)(2,1)}), bf16[64,8,896]{2,1,0:T(8,128)(2,1)S(1)}, u32[]{:S(2)}, u32[]{:S(2)}) async-start(bf16[64,8,896]{2,1,0:T(8,128)(2,1)} %bitcast.13), calls=%async_computation.2 | async-start | bytes 1835008 | tf_op jit(solution)/shard_map/all_to_all | solution.py:398
  170.9 21.0 %copy-start.3 = (bf16[1,1024,896]{2,1,0:T(8,128)(2,1)S(1)}, bf16[1,1024,896]{2,1,0:T(8,128)(2,1)}, u32[]{:S(2)}) copy-start(bf16[1,1024,896]{2,1,0:T(8,128)(2,1)} %weight_ref.5) | copy-start | bytes 5505028
  171.2 10.9 %collective-permute-start.12 = (bf16[128,1024]{1,0:T(8,128)(2,1)S(1)}, bf16[128,1024]{1,0:T(8,128)(2,1)S(1)}, u32[]{:S(2)}, u32[]{:S(2)}) collective-permute-start(bf16[128,1024]{1,0:T(8,128)(2,1)S(1)} %multiply_convert_fusion.1), channel_id=1, source_target_pairs={{0,3},{1,0},{2,1},{3,2},{4,7},{5,4},{6,5},{7,6},{8,11},{9,8},{10,9... | collective-permute-start | bytes 786440 | tf_op jit(solution)/shard_map/ppermute | solution.py:70
  174.1 12.6 %collective-permute-start.11 = (bf16[128,1024]{1,0:T(8,128)(2,1)S(1)}, bf16[128,1024]{1,0:T(8,128)(2,1)S(1)}, u32[]{:S(2)}, u32[]{:S(2)}) collective-permute-start(bf16[128,1024]{1,0:T(8,128)(2,1)S(1)} %multiply_convert_fusion.1), channel_id=1, source_target_pairs={{0,2},{1,3},{2,0},{3,1},{4,6},{5,7},{6,4},{7,5},{8,10},{9,11},{10,... | collective-permute-start | bytes 786440 | tf_op jit(solution)/shard_map/ppermute | solution.py:70
  178.8 11.2 %collective-permute-start.10 = (bf16[128,1024]{1,0:T(8,128)(2,1)S(1)}, bf16[128,1024]{1,0:T(8,128)(2,1)S(1)}, u32[]{:S(2)}, u32[]{:S(2)}) collective-permute-start(bf16[128,1024]{1,0:T(8,128)(2,1)S(1)} %multiply_convert_fusion.1), channel_id=1, source_target_pairs={{0,1},{1,2},{2,3},{3,0},{4,5},{5,6},{6,7},{7,4},{8,9},{9,10},{10,1... | collective-permute-start | bytes 786440 | tf_op jit(solution)/shard_map/ppermute | solution.py:70
  190.0 4.9 %collective-permute-start.13 = (bf16[512,1024]{1,0:T(8,128)(2,1)S(1)}, bf16[512,1024]{1,0:T(8,128)(2,1)S(1)}, u32[]{:S(2)}, u32[]{:S(2)}) collective-permute-start(bf16[512,1024]{1,0:T(8,128)(2,1)S(1)} %pad_maximum_fusion.rows_ref), channel_id=1, source_target_pairs={{0,256},{256,0},{1,257},{257,1},{2,258},{258,2},{3,259},{259,3},{4... | collective-permute-start | bytes 3145736 | tf_op jit(solution)/shard_map/ppermute | solution.py:70
  197.9 12.9 %copy-start.9 = (s32[2]{0:T(128)S(1)}, s32[2]{0:T(128)}, u32[]{:S(2)}) copy-start(s32[2]{0:T(128)} %param.10) | copy-start | bytes 28
  197.9 61.3 %all-to-all-start.3 = ((bf16[64,2,8,896]{3,2,1,0:T(8,128)(2,1)}), bf16[64,2,8,896]{3,2,1,0:T(8,128)(2,1)S(1)}, u32[]{:S(2)}, u32[]{:S(2)}) async-start(bf16[64,2,8,896]{3,2,1,0:T(8,128)(2,1)} %down_half.3), calls=%async_computation.3 | async-start | bytes 3670016 | tf_op jit(solution)/shard_map/all_to_all | solution.py:398
  214.2 10.9 %collective-permute-start.16 = (bf16[2,32,640]{2,1,0:T(8,128)(2,1)S(1)}, bf16[2,32,640]{2,1,0:T(8,128)(2,1)S(1)}, u32[]{:S(2)}, u32[]{:S(2)}) collective-permute-start(bf16[2,32,640]{2,1,0:T(8,128)(2,1)S(1)} %get-tuple-element.48), channel_id=1, source_target_pairs={{0,3},{1,0},{2,1},{3,2},{4,7},{5,4},{6,5},{7,6},{8,11},{9,8},{10,9... | collective-permute-start | bytes 245768 | tf_op jit(solution)/shard_map/ppermute | solution.py:70
  216.6 8.5 %collective-permute-start.15 = (bf16[2,32,640]{2,1,0:T(8,128)(2,1)S(1)}, bf16[2,32,640]{2,1,0:T(8,128)(2,1)S(1)}, u32[]{:S(2)}, u32[]{:S(2)}) collective-permute-start(bf16[2,32,640]{2,1,0:T(8,128)(2,1)S(1)} %get-tuple-element.49), channel_id=1, source_target_pairs={{0,1},{1,2},{2,3},{3,0},{4,5},{5,6},{6,7},{7,4},{8,9},{9,10},{10,1... | collective-permute-start | bytes 245768 | tf_op jit(solution)/shard_map/ppermute | solution.py:70
  220.0 7.8 %collective-permute-start.14 = (bf16[2,32,640]{2,1,0:T(8,128)(2,1)S(1)}, bf16[2,32,640]{2,1,0:T(8,128)(2,1)S(1)}, u32[]{:S(2)}, u32[]{:S(2)}) collective-permute-start(bf16[2,32,640]{2,1,0:T(8,128)(2,1)S(1)} %get-tuple-element.50), channel_id=1, source_target_pairs={{0,2},{1,3},{2,0},{3,1},{4,6},{5,7},{6,4},{7,5},{8,10},{9,11},{10,... | collective-permute-start | bytes 245768 | tf_op jit(solution)/shard_map/ppermute | solution.py:70

commit v6 on v5

--- a/solution.py
+++ b/solution.py
@@ -199,19 +199,23 @@
     )(where, rows_in, weight, arrived)
 
 
-def copy_kernel(from_ref, to_ref, sem):
-    copy = pltpu.make_async_copy(from_ref, to_ref, sem)
-    copy.start()
-    copy.wait()
+def copy_kernel(from_ref, to_ref):
+    to_ref[...] = from_ref[...]
 
 
 def copied(value):
+    rows, columns = value.shape
+    tile = 128
     return pl.pallas_call(
         copy_kernel,
         out_shape=jax.ShapeDtypeStruct(value.shape, value.dtype),
-        in_specs=[pl.BlockSpec(memory_space=pl.ANY)],
-        out_specs=pl.BlockSpec(memory_space=pl.ANY),
-        scratch_shapes=[pltpu.SemaphoreType.DMA],
+        grid=(rows // tile,),
+        in_specs=[pl.BlockSpec((tile, columns), lambda i: (i, 0))],
+        out_specs=pl.BlockSpec((tile, columns), lambda i: (i, 0)),
+        compiler_params=pltpu.CompilerParams(vmem_limit_bytes=VMEM),
+        cost_estimate=pl.CostEstimate(
+            flops=0, bytes_accessed=4 * rows * columns, transcendentals=0
+        ),
         name="copied",
     )(value)
 
@@ -312,7 +316,8 @@
     made = jnp.dot(rows_ref[...], weight_ref[...], preferred_element_type=jnp.float32)
     for k in range(together):
         back = pl.program_id(0) * together + k
-        place = lax.rem(where[1] + size - back, size)
+        step = jnp.where(back < 2, back, 5 - back)
+        place = lax.rem(where[1] + size - step, size)
         piece = made[k * share * slots : (k + 1) * share * slots]
         out_ref[pl.ds(place * share, share), 0] = piece.reshape(share, slots, columns).astype(
             out_ref.dtype
@@ -357,7 +362,7 @@
 def narrow_rows(where, rows_in, up, down):
     arrived = turned(their_half(where, rows_in, up), "role", 1)
     own, rounded = own_half(where, rows_in, up, arrived, 1)
-    pieces = [turned(rounded, "tp", step) for step in (2, 1, 3)]
+    pieces = [turned(rounded, "tp", step) for step in (3, 1, 2)]
     for piece in pieces:
         own = own + piece.astype(jnp.float32)
     mine = jax.nn.silu(own).astype(jnp.bfloat16)
@@ -367,11 +372,11 @@
 def wide_rows(where, rows_in, up, other_up, down, sources):
     size = lax.axis_size("tp")
     own, *pieces = wide_product(where, rows_in, up, other_up, size)
-    for step in (2, 1, 3):
+    for step in (3, 1, 2):
         own = own + turned(pieces[step - 1], "tp", step).astype(jnp.float32)
     mine = jax.nn.silu(own).astype(jnp.bfloat16)
-    others = {step: turned(mine, "tp", step) for step in (2, 1, 3)}
-    mine = jnp.concatenate([mine] + [others[step] for step in range(1, size)], axis=0)
+    others = {step: turned(mine, "tp", step) for step in (3, 1, 2)}
+    mine = jnp.concatenate([mine, others[1], others[3], others[2]], axis=0)
     theirs = turned(mine, "role", 1)
     made = down_half(where, 0, mine, down, None, sources)
     return down_half(where, 1, theirs, down, made, sources)

time: 262 us -> 217 us (0.83)
  Pallas kernels: 75.1 us -> 20.4 us
  starting transfers between devices: 103 us -> 90.9 us
  waiting for transfers between devices: 67.6 us -> 79.4 us
  local copies, waits for them, and re-layouts: 2.16 us -> 8.27 us
    pallas_call x1, Pallas kernels: 56.7 us -> 2.93 us  [copied(): pl.pallas_call(copy_kernel, out_shape=jax.ShapeDtypeStruct(value.shape, v...]
    all_to_all x4, waiting for transfers between devices: 31.5 us -> 48.6 us  [exchanged(): return lax.all_to_all(value, 'grp', split_axis=0, concat_axis=0, tiled=True)]
    all_to_all x4, starting transfers between devices: 52 us -> 40.8 us  [exchanged(): return lax.all_to_all(value, 'grp', split_axis=0, concat_axis=0, tiled=True)]
    ppermute x17, waiting for transfers between devices: 36 us -> 30.7 us  [turned(): lax.ppermute(value, axis, [(k, (k + step) % size) for k in range(size)])]
    eq x4, local copies, waits for them, and re-layouts: 0.17 us -> 2.92 us  [weights(): taken = rank.T[:, :, None] == slots[None, None, :]]
  transfers between devices with their start and end apart: 21 -> 21, of which waited for: 10 -> 13; matrix products, arithmetic and copies ran while one was open for 4% -> 8% of each run, Pallas kernels for 26% -> 7%
where the time goes in v6:
time: 217 us; the launch traced here: 215 us
  starting transfers between devices  90.9 us (42%)
  waiting for transfers between devices  79.4 us (37%)
  Pallas kernels  20.4 us (9%)
  local copies, waits for them, and re-layouts  8.27 us (4%)
  matrix products  8.2 us (4%)
  other arithmetic  6.87 us (3%)
    ppermute x17, starting transfers between devices, turned(): lax.ppermute(value, axis, [(k, (k + step) % size) for k in range(size)])  50.1 us
    all_to_all x4, waiting for transfers between devices, exchanged(): return lax.all_to_all(value, 'grp', split_axis=0, concat_axis=0, tiled=True)  48.6 us
    all_to_all x4, starting transfers between devices, exchanged(): return lax.all_to_all(value, 'grp', split_axis=0, concat_axis=0, tiled=True)  40.8 us
    ppermute x17, waiting for transfers between devices, turned(): lax.ppermute(value, axis, [(k, (k + step) % size) for k in range(size)])  30.7 us
    pallas_call x2, Pallas kernels, down_half(): pl.pallas_call(down_half_kernel, out_shape=jax.ShapeDtypeStruct((sources,...  5.9 us
    pallas_call x1, Pallas kernels, wide_product(): pl.pallas_call(wide_kernel, out_shape=[jax.ShapeDtypeStruct((share, colum...  5.66 us
  transfers between devices with their start and end apart: 21, of which 13 were waited for; matrix products, arithmetic and copies ran while one was open for 8% of the time, Pallas kernels for 7%

profile of v6, /device:TPU:24, one launch (start us, length us, event | category | flops | bytes accessed | tf_op | source)
XLA Modules:
  0.0 215.2 jit_solution(2977389935697039605)
XLA Ops:
  0.7 1.1 copy-done.5
  1.7 0.7 copy-done.7
  2.4 0.5 first_selection.1
  3.0 0.9 copy-done.4
  3.9 16.4 %all-to-all-start = ((bf16[64,8,896]{2,1,0:T(8,128)(2,1)}), bf16[64,8,896]{2,1,0:T(8,128)(2,1)S(1)}, u32[]{:S(2)}, u32[]{:S(2)}) async-start(bf16[64,8,896]{2,1,0:T(8,128)(2,1)} %copy-done.4), calls=%async_computation | async-start | bytes 1835008 | tf_op jit(solution)/shard_map/all_to_all | solution.py:403
  20.3 1.9 collective-permute-start
  22.3 0.5 iota_convert_fusion
  22.8 0.7 select_reduce_fusion
  23.5 0.6 eq.80
  24.1 0.8 eq.81
  25.0 2.9 %copied.1 = bf16[896,1024]{1,0:T(8,128)(2,1)} custom-call(bf16[896,1024]{1,0:T(8,128)(2,1)S(1)} %bitcast.52), custom_call_target="tpu_custom_call" | custom-call | bytes 3670016 | tf_op jit(solution)/shard_map/copied/pallas_call | solution.py:209
  27.9 0.6 eq.86
  28.6 0.8 eq.87
  29.4 0.6 eq.95
  30.0 0.8 eq.96
  30.9 1.6 fusion.6
  32.5 1.5 fusion.12
  34.0 2.0 fusion
  36.0 11.3 %all-to-all-done = bf16[64,8,896]{2,1,0:T(8,128)(2,1)S(1)} async-done(((bf16[64,8,896]{2,1,0:T(8,128)(2,1)}), bf16[64,8,896]{2,1,0:T(8,128)(2,1)S(1)}, u32[]{:S(2)}, u32[]{:S(2)}) %all-to-all-start) | async-done | bytes 917536 | tf_op jit(solution)/shard_map/all_to_all | solution.py:403
  47.2 6.4 %all-to-all-start.1 = ((bf16[64,8,1792]{2,1,0:T(8,128)(2,1)}), bf16[64,8,1792]{2,1,0:T(8,128)(2,1)}, u32[]{:S(2)}, u32[]{:S(2)}) async-start(bf16[64,8,1792]{2,1,0:T(8,128)(2,1)} %fusion), calls=%async_computation.1 | async-start | bytes 3670016 | tf_op jit(solution)/shard_map/all_to_all | solution.py:403
  53.7 1.2 their_half.1
  55.0 1.9 collective-permute-start.1
  56.9 2.4 %collective-permute-start.6 = (bf16[896,1024]{1,0:T(8,128)(2,1)}, bf16[896,1024]{1,0:T(8,128)(2,1)}, u32[]{:S(2)}, u32[]{:S(2)}) collective-permute-start(bf16[896,1024]{1,0:T(8,128)(2,1)} %copied.1), channel_id=1, source_target_pairs={{0,256},{256,0},{1,257},{257,1},{2,258},{258,2},{3,259},{259,3},{4... | collective-permute-start | bytes 5505032 | tf_op jit(solution)/shard_map/ppermute | solution.py:70
  59.3 1.3 own_half.1
  60.6 5.1 %collective-permute-start.4 = (bf16[256,1024]{1,0:T(8,128)(2,1)S(1)}, bf16[256,1024]{1,0:T(8,128)(2,1)S(1)}, u32[]{:S(2)}, u32[]{:S(2)}) collective-permute-start(bf16[256,1024]{1,0:T(8,128)(2,1)S(1)} %get-tuple-element.29), channel_id=1, source_target_pairs={{0,2},{1,3},{2,0},{3,1},{4,6},{5,7},{6,4},{7,5},{8,10},{9,11},{10,... | collective-permute-start | bytes 1572872 | tf_op jit(solution)/shard_map/ppermute | solution.py:70
  65.7 2.5 %collective-permute-start.3 = (bf16[256,1024]{1,0:T(8,128)(2,1)S(1)}, bf16[256,1024]{1,0:T(8,128)(2,1)S(1)}, u32[]{:S(2)}, u32[]{:S(2)}) collective-permute-start(bf16[256,1024]{1,0:T(8,128)(2,1)S(1)} %get-tuple-element.29), channel_id=1, source_target_pairs={{0,1},{1,2},{2,3},{3,0},{4,5},{5,6},{6,7},{7,4},{8,9},{9,10},{10,1... | collective-permute-start | bytes 1572872 | tf_op jit(solution)/shard_map/ppermute | solution.py:70
  68.2 4.6 %collective-permute-start.2 = (bf16[256,1024]{1,0:T(8,128)(2,1)S(1)}, bf16[256,1024]{1,0:T(8,128)(2,1)S(1)}, u32[]{:S(2)}, u32[]{:S(2)}) collective-permute-start(bf16[256,1024]{1,0:T(8,128)(2,1)S(1)} %get-tuple-element.29), channel_id=1, source_target_pairs={{0,3},{1,0},{2,1},{3,2},{4,7},{5,4},{6,5},{7,6},{8,11},{9,8},{10,9... | collective-permute-start | bytes 1572872 | tf_op jit(solution)/shard_map/ppermute | solution.py:70
  72.8 6.2 %collective-permute-done.4 = bf16[256,1024]{1,0:T(8,128)(2,1)S(1)} collective-permute-done((bf16[256,1024]{1,0:T(8,128)(2,1)S(1)}, bf16[256,1024]{1,0:T(8,128)(2,1)S(1)}, u32[]{:S(2)}, u32[]{:S(2)}) %collective-permute-start.4) | collective-permute-done | bytes 524320 | tf_op jit(solution)/shard_map/ppermute | solution.py:70
  79.0 10.2 %collective-permute-done.3 = bf16[256,1024]{1,0:T(8,128)(2,1)S(1)} collective-permute-done((bf16[256,1024]{1,0:T(8,128)(2,1)S(1)}, bf16[256,1024]{1,0:T(8,128)(2,1)S(1)}, u32[]{:S(2)}, u32[]{:S(2)}) %collective-permute-start.3) | collective-permute-done | bytes 524320 | tf_op jit(solution)/shard_map/ppermute | solution.py:70
  89.3 0.5 multiply_convert_fusion.mine_ref
  89.8 1.9 collective-permute-start.5
  91.7 1.9 collective-permute-done.5.theirs_ref
  93.6 2.8 %down_both.1 = bf16[512,896]{1,0:T(8,128)(2,1)} custom-call(s32[2]{0:T(128)S(1)} %pad_add_fusion.where, bf16[256,1024]{1,0:T(8,128)(2,1)S(1)} %multiply_convert_fusion.mine_ref, bf16[256,1024]{1,0:T(8,128)(2,1)S(1)} %collective-permute-done.5.theirs_ref, bf16[1,1024,896]{2,1,0:T(8,128)(2,1)S(1)} %copy-done.2), custom_call_target="tpu_custom_call" | custom-call | flops 939524096 | bytes 3801088 | tf_op jit(solution)/shard_map/down_both/pallas_call | solution.py:240
  96.5 5.4 %all-to-all-done.1 = bf16[64,8,1792]{2,1,0:T(8,128)(2,1)} async-done(((bf16[64,8,1792]{2,1,0:T(8,128)(2,1)}), bf16[64,8,1792]{2,1,0:T(8,128)(2,1)}, u32[]{:S(2)}, u32[]{:S(2)}) %all-to-all-start.1) | async-done | bytes 1835040 | tf_op jit(solution)/shard_map/all_to_all | solution.py:403
  101.9 5.7 %wide_product.1 = (f32[128,1024]{1,0:T(8,128)S(1)}, bf16[128,1024]{1,0:T(8,128)(2,1)S(1)}, bf16[128,1024]{1,0:T(8,128)(2,1)}, bf16[128,1024]{1,0:T(8,128)(2,1)S(1)}) custom-call(s32[2]{0:T(128)S(1)} %pad_add_fusion.where, bf16[512,1792]{1,0:T(8,128)(2,1)} %bitcast.12.rows_ref, bf16[896,1024]{1,0:T(8,128)(2,1)S(1)} %bitcast.55, ...), custom_call_target="tpu_custom_call" | custom-call | flops 1879048192 | bytes 6553600 | tf_op jit(solution)/shard_map/wide_product/pallas_call | solution.py:289
  107.5 4.9 %collective-permute-start.9 = (bf16[128,1024]{1,0:T(8,128)(2,1)}, bf16[128,1024]{1,0:T(8,128)(2,1)S(1)}, u32[]{:S(2)}, u32[]{:S(2)}) collective-permute-start(bf16[128,1024]{1,0:T(8,128)(2,1)} %get-tuple-element.35), channel_id=1, source_target_pairs={{0,2},{1,3},{2,0},{3,1},{4,6},{5,7},{6,4},{7,5},{8,10},{9,11},{10,... | collective-permute-start | bytes 786440 | tf_op jit(solution)/shard_map/ppermute | solution.py:70
  112.4 2.5 %collective-permute-start.8 = (bf16[128,1024]{1,0:T(8,128)(2,1)S(1)}, bf16[128,1024]{1,0:T(8,128)(2,1)S(1)}, u32[]{:S(2)}, u32[]{:S(2)}) collective-permute-start(bf16[128,1024]{1,0:T(8,128)(2,1)S(1)} %get-tuple-element.34), channel_id=1, source_target_pairs={{0,1},{1,2},{2,3},{3,0},{4,5},{5,6},{6,7},{7,4},{8,9},{9,10},{10,1... | collective-permute-start | bytes 786440 | tf_op jit(solution)/shard_map/ppermute | solution.py:70
  115.0 4.5 %collective-permute-start.7 = (bf16[128,1024]{1,0:T(8,128)(2,1)S(1)}, bf16[128,1024]{1,0:T(8,128)(2,1)S(1)}, u32[]{:S(2)}, u32[]{:S(2)}) collective-permute-start(bf16[128,1024]{1,0:T(8,128)(2,1)S(1)} %get-tuple-element.33), channel_id=1, source_target_pairs={{0,3},{1,0},{2,1},{3,2},{4,7},{5,4},{6,5},{7,6},{8,11},{9,8},{10,9... | collective-permute-start | bytes 786440 | tf_op jit(solution)/shard_map/ppermute | solution.py:70
  119.5 7.4 %all-to-all-start.2 = ((bf16[64,8,896]{2,1,0:T(8,128)(2,1)}), bf16[64,8,896]{2,1,0:T(8,128)(2,1)S(1)}, u32[]{:S(2)}, u32[]{:S(2)}) async-start(bf16[64,8,896]{2,1,0:T(8,128)(2,1)} %bitcast.13), calls=%async_computation.2 | async-start | bytes 1835008 | tf_op jit(solution)/shard_map/all_to_all | solution.py:403
  127.0 0.2 multiply_convert_fusion.1
  127.2 2.1 collective-permute-start.12
  129.3 4.0 %collective-permute-start.11 = (bf16[128,1024]{1,0:T(8,128)(2,1)S(1)}, bf16[128,1024]{1,0:T(8,128)(2,1)S(1)}, u32[]{:S(2)}, u32[]{:S(2)}) collective-permute-start(bf16[128,1024]{1,0:T(8,128)(2,1)S(1)} %multiply_convert_fusion.1), channel_id=1, source_target_pairs={{0,3},{1,0},{2,1},{3,2},{4,7},{5,4},{6,5},{7,6},{8,11},{9,8},{10,9... | collective-permute-start | bytes 786440 | tf_op jit(solution)/shard_map/ppermute | solution.py:70
  133.2 1.9 collective-permute-start.10
  135.2 2.5 %collective-permute-done.12 = bf16[128,1024]{1,0:T(8,128)(2,1)S(1)} collective-permute-done((bf16[128,1024]{1,0:T(8,128)(2,1)S(1)}, bf16[128,1024]{1,0:T(8,128)(2,1)S(1)}, u32[]{:S(2)}, u32[]{:S(2)}) %collective-permute-start.12) | collective-permute-done | bytes 262176 | tf_op jit(solution)/shard_map/ppermute | solution.py:70
  137.7 3.0 %collective-permute-done.11 = bf16[128,1024]{1,0:T(8,128)(2,1)S(1)} collective-permute-done((bf16[128,1024]{1,0:T(8,128)(2,1)S(1)}, bf16[128,1024]{1,0:T(8,128)(2,1)S(1)}, u32[]{:S(2)}, u32[]{:S(2)}) %collective-permute-start.11) | collective-permute-done | bytes 262176 | tf_op jit(solution)/shard_map/ppermute | solution.py:70
  140.7 2.4 %collective-permute-done.10 = bf16[128,1024]{1,0:T(8,128)(2,1)S(1)} collective-permute-done((bf16[128,1024]{1,0:T(8,128)(2,1)S(1)}, bf16[128,1024]{1,0:T(8,128)(2,1)S(1)}, u32[]{:S(2)}, u32[]{:S(2)}) %collective-permute-start.10) | collective-permute-done | bytes 262176 | tf_op jit(solution)/shard_map/ppermute | solution.py:70
  143.1 1.9 collective-permute-start.13
  145.0 2.9 %down_half.2.rest_0_ = bf16[64,2,8,896]{3,2,1,0:T(8,128)(2,1)} custom-call(s32[2]{0:T(128)S(1)} %pad_add_fusion.where, bf16[512,1024]{1,0:T(8,128)(2,1)S(1)} %pad_maximum_fusion.rows_ref, bf16[1,1024,896]{2,1,0:T(8,128)(2,1)S(1)} %copy-done.3), custom_call_target="tpu_custom_call" | custom-call | flops 939524096 | bytes 3801088 | tf_op jit(solution)/shard_map/down_half/pallas_call | solution.py:346
  148.0 3.0 %down_half.3 = bf16[64,2,8,896]{3,2,1,0:T(8,128)(2,1)} custom-call(s32[2]{0:T(128)S(1)} %pad_add_fusion.where, bf16[512,1024]{1,0:T(8,128)(2,1)S(1)} %collective-permute-done.13.rows_ref, bf16[1,1024,896]{2,1,0:T(8,128)(2,1)S(1)} %copy-done.3, bf16[64,2,8,896]{3,2,1,0:T(8,128)(2,1)} %down_half.2.rest_0_), custom_call_target="tpu_custom_call", output_to_operand_aliasing={{}: (3, {})} | custom-call | flops 939524096 | bytes 3801088 | tf_op jit(solution)/shard_map/down_half/pallas_call | solution.py:346
  151.0 2.1 all-to-all-done.2
  153.1 0.9 copy-done.9
  154.0 10.6 %all-to-all-start.3 = ((bf16[64,2,8,896]{3,2,1,0:T(8,128)(2,1)}), bf16[64,2,8,896]{3,2,1,0:T(8,128)(2,1)S(1)}, u32[]{:S(2)}, u32[]{:S(2)}) async-start(bf16[64,2,8,896]{3,2,1,0:T(8,128)(2,1)} %down_half.3), calls=%async_computation.3 | async-start | bytes 3670016 | tf_op jit(solution)/shard_map/all_to_all | solution.py:403
  164.8 1.5 fusion.26
  166.7 1.4 convolution_convert_fusion.1
  168.1 2.5 %collective-permute-start.16 = (bf16[2,32,640]{2,1,0:T(8,128)(2,1)S(1)}, bf16[2,32,640]{2,1,0:T(8,128)(2,1)S(1)}, u32[]{:S(2)}, u32[]{:S(2)}) collective-permute-start(bf16[2,32,640]{2,1,0:T(8,128)(2,1)S(1)} %get-tuple-element.48), channel_id=1, source_target_pairs={{0,3},{1,0},{2,1},{3,2},{4,7},{5,4},{6,5},{7,6},{8,11},{9,8},{10,9... | collective-permute-start | bytes 245768 | tf_op jit(solution)/shard_map/ppermute | solution.py:70
  170.6 3.4 %collective-permute-start.15 = (bf16[2,32,640]{2,1,0:T(8,128)(2,1)S(1)}, bf16[2,32,640]{2,1,0:T(8,128)(2,1)S(1)}, u32[]{:S(2)}, u32[]{:S(2)}) collective-permute-start(bf16[2,32,640]{2,1,0:T(8,128)(2,1)S(1)} %get-tuple-element.49), channel_id=1, source_target_pairs={{0,1},{1,2},{2,3},{3,0},{4,5},{5,6},{6,7},{7,4},{8,9},{9,10},{10,1... | collective-permute-start | bytes 245768 | tf_op jit(solution)/shard_map/ppermute | solution.py:70
  174.0 2.2 %collective-permute-start.14 = (bf16[2,32,640]{2,1,0:T(8,128)(2,1)S(1)}, bf16[2,32,640]{2,1,0:T(8,128)(2,1)S(1)}, u32[]{:S(2)}, u32[]{:S(2)}) collective-permute-start(bf16[2,32,640]{2,1,0:T(8,128)(2,1)S(1)} %get-tuple-element.50), channel_id=1, source_target_pairs={{0,2},{1,3},{2,0},{3,1},{4,6},{5,7},{6,4},{7,5},{8,10},{9,11},{10,... | collective-permute-start | bytes 245768 | tf_op jit(solution)/shard_map/ppermute | solution.py:70
  176.2 1.2 fusion.3
  177.5 0.7 collective-permute-done.15
  178.2 3.7 %collective-permute-done.14 = bf16[2,32,640]{2,1,0:T(8,128)(2,1)S(1)} collective-permute-done((bf16[2,32,640]{2,1,0:T(8,128)(2,1)S(1)}, bf16[2,32,640]{2,1,0:T(8,128)(2,1)S(1)}, u32[]{:S(2)}, u32[]{:S(2)}) %collective-permute-start.14) | collective-permute-done | bytes 81952 | tf_op jit(solution)/shard_map/ppermute | solution.py:70
  182.0 0.3 slice_reduce_fusion
  182.5 0.7 divide_convert_fusion
  183.2 29.9 %all-to-all-done.3 = bf16[64,2,8,896]{3,2,1,0:T(8,128)(2,1)S(1)} async-done(((bf16[64,2,8,896]{3,2,1,0:T(8,128)(2,1)}), bf16[64,2,8,896]{3,2,1,0:T(8,128)(2,1)S(1)}, u32[]{:S(2)}, u32[]{:S(2)}) %all-to-all-start.3) | async-done | bytes 1835040 | tf_op jit(solution)/shard_map/all_to_all | solution.py:403
  213.0 2.1 fusion.1
  (53 shorter events, 1.2 us)
Async XLA Ops:
  0.6 164.1 %copy-start = (bf16[2,128,576]{1,2,0:T(8,128)(2,1)S(1)}, bf16[2,128,576]{1,2,0:T(8,128)(2,1)}, u32[]{:S(2)}) copy-start(bf16[2,128,576]{1,2,0:T(8,128)(2,1)} %param.8) | copy-start | bytes 884740
  0.6 24.3 %copy-start.1 = (bf16[1,896,1024]{2,1,0:T(8,128)(2,1)S(1)}, bf16[1,896,1024]{2,1,0:T(8,128)(2,1)}, u32[]{:S(2)}) copy-start(bf16[1,896,1024]{2,1,0:T(8,128)(2,1)} %param.14) | copy-start | bytes 5505028
  0.7 1.1 copy-start.5
  1.7 0.7 copy-start.7
  2.4 17.9 %copy-start.6 = (bf16[128,896]{1,0:T(8,128)(2,1)S(1)}, bf16[128,896]{1,0:T(8,128)(2,1)}, u32[]{:S(2)}) copy-start(bf16[128,896]{1,0:T(8,128)(2,1)} %rows_ref.1) | copy-start | bytes 688132
  2.4 20.3 %copy-start.11 = (f32[128,8]{0,1:T(8,128)S(1)}, f32[128,8]{0,1:T(8,128)}, u32[]{:S(2)}) copy-start(f32[128,8]{0,1:T(8,128)} %param.13) | copy-start | bytes 12292
  2.4 20.4 %copy-start.8 = (s32[128,8]{0,1:T(8,128)S(1)}, s32[128,8]{0,1:T(8,128)}, u32[]{:S(2)}) copy-start(s32[128,8]{0,1:T(8,128)} %param.12) | copy-start | bytes 12292
  3.0 0.9 copy-start.4
  3.9 43.3 %all-to-all-start = ((bf16[64,8,896]{2,1,0:T(8,128)(2,1)}), bf16[64,8,896]{2,1,0:T(8,128)(2,1)S(1)}, u32[]{:S(2)}, u32[]{:S(2)}) async-start(bf16[64,8,896]{2,1,0:T(8,128)(2,1)} %copy-done.4), calls=%async_computation | async-start | bytes 1835008 | tf_op jit(solution)/shard_map/all_to_all | solution.py:403
  20.3 13.7 %collective-permute-start = (bf16[128,896]{1,0:T(8,128)(2,1)S(1)}, bf16[128,896]{1,0:T(8,128)(2,1)S(1)}, u32[]{:S(2)}, u32[]{:S(2)}) collective-permute-start(bf16[128,896]{1,0:T(8,128)(2,1)S(1)} %copy-done.6), channel_id=1, source_target_pairs={{0,256},{256,0},{1,257},{257,1},{2,258},{258,2},{3,259},{259,3},{4... | collective-permute-start | bytes 688136 | tf_op jit(solution)/shard_map/ppermute | solution.py:70
  25.0 2.9 %copy-start.12 = (f32[8]{0:T(128)S(1)}, f32[8]{0:T(128)}, u32[]{:S(2)}) copy-start(f32[8]{0:T(128)} %iota_convert_fusion) | copy-start | bytes 100
  47.2 54.6 %all-to-all-start.1 = ((bf16[64,8,1792]{2,1,0:T(8,128)(2,1)}), bf16[64,8,1792]{2,1,0:T(8,128)(2,1)}, u32[]{:S(2)}, u32[]{:S(2)}) async-start(bf16[64,8,1792]{2,1,0:T(8,128)(2,1)} %fusion), calls=%async_computation.1 | async-start | bytes 3670016 | tf_op jit(solution)/shard_map/all_to_all | solution.py:403
  55.0 4.3 %collective-permute-start.1 = (bf16[256,1024]{1,0:T(8,128)(2,1)S(1)}, bf16[256,1024]{1,0:T(8,128)(2,1)S(1)}, u32[]{:S(2)}, u32[]{:S(2)}) collective-permute-start(bf16[256,1024]{1,0:T(8,128)(2,1)S(1)} %their_half.1), channel_id=1, source_target_pairs={{0,256},{256,0},{1,257},{257,1},{2,258},{258,2},{3,259},{259,3},{4... | collective-permute-start | bytes 1572872 | tf_op jit(solution)/shard_map/ppermute | solution.py:70
  56.9 45.0 %collective-permute-start.6 = (bf16[896,1024]{1,0:T(8,128)(2,1)}, bf16[896,1024]{1,0:T(8,128)(2,1)}, u32[]{:S(2)}, u32[]{:S(2)}) collective-permute-start(bf16[896,1024]{1,0:T(8,128)(2,1)} %copied.1), channel_id=1, source_target_pairs={{0,256},{256,0},{1,257},{257,1},{2,258},{258,2},{3,259},{259,3},{4... | collective-permute-start | bytes 5505032 | tf_op jit(solution)/shard_map/ppermute | solution.py:70
  60.6 33.0 %copy-start.2 = (bf16[1,1024,896]{2,1,0:T(8,128)(2,1)S(1)}, bf16[1,1024,896]{2,1,0:T(8,128)(2,1)}, u32[]{:S(2)}) copy-start(bf16[1,1024,896]{2,1,0:T(8,128)(2,1)} %weight_ref.5) | copy-start | bytes 5505028
  60.6 18.4 %collective-permute-start.4 = (bf16[256,1024]{1,0:T(8,128)(2,1)S(1)}, bf16[256,1024]{1,0:T(8,128)(2,1)S(1)}, u32[]{:S(2)}, u32[]{:S(2)}) collective-permute-start(bf16[256,1024]{1,0:T(8,128)(2,1)S(1)} %get-tuple-element.29), channel_id=1, source_target_pairs={{0,2},{1,3},{2,0},{3,1},{4,6},{5,7},{6,4},{7,5},{8,10},{9,11},{10,... | collective-permute-start | bytes 1572872 | tf_op jit(solution)/shard_map/ppermute | solution.py:70
  65.7 23.5 %collective-permute-start.3 = (bf16[256,1024]{1,0:T(8,128)(2,1)S(1)}, bf16[256,1024]{1,0:T(8,128)(2,1)S(1)}, u32[]{:S(2)}, u32[]{:S(2)}) collective-permute-start(bf16[256,1024]{1,0:T(8,128)(2,1)S(1)} %get-tuple-element.29), channel_id=1, source_target_pairs={{0,1},{1,2},{2,3},{3,0},{4,5},{5,6},{6,7},{7,4},{8,9},{9,10},{10,1... | collective-permute-start | bytes 1572872 | tf_op jit(solution)/shard_map/ppermute | solution.py:70
  68.2 21.2 %collective-permute-start.2 = (bf16[256,1024]{1,0:T(8,128)(2,1)S(1)}, bf16[256,1024]{1,0:T(8,128)(2,1)S(1)}, u32[]{:S(2)}, u32[]{:S(2)}) collective-permute-start(bf16[256,1024]{1,0:T(8,128)(2,1)S(1)} %get-tuple-element.29), channel_id=1, source_target_pairs={{0,3},{1,0},{2,1},{3,2},{4,7},{5,4},{6,5},{7,6},{8,11},{9,8},{10,9... | collective-permute-start | bytes 1572872 | tf_op jit(solution)/shard_map/ppermute | solution.py:70
  89.8 3.8 %collective-permute-start.5 = (bf16[256,1024]{1,0:T(8,128)(2,1)S(1)}, bf16[256,1024]{1,0:T(8,128)(2,1)S(1)}, u32[]{:S(2)}, u32[]{:S(2)}) collective-permute-start(bf16[256,1024]{1,0:T(8,128)(2,1)S(1)} %multiply_convert_fusion.mine_ref), channel_id=1, source_target_pairs={{0,256},{256,0},{1,257},{257,1},{2,258},{258,2},{3,259},{259,3},{4... | collective-permute-start | bytes 1572872 | tf_op jit(solution)/shard_map/ppermute | solution.py:70
  107.5 19.4 %collective-permute-start.9 = (bf16[128,1024]{1,0:T(8,128)(2,1)}, bf16[128,1024]{1,0:T(8,128)(2,1)S(1)}, u32[]{:S(2)}, u32[]{:S(2)}) collective-permute-start(bf16[128,1024]{1,0:T(8,128)(2,1)} %get-tuple-element.35), channel_id=1, source_target_pairs={{0,2},{1,3},{2,0},{3,1},{4,6},{5,7},{6,4},{7,5},{8,10},{9,11},{10,... | collective-permute-start | bytes 786440 | tf_op jit(solution)/shard_map/ppermute | solution.py:70
  112.4 14.5 %collective-permute-start.8 = (bf16[128,1024]{1,0:T(8,128)(2,1)S(1)}, bf16[128,1024]{1,0:T(8,128)(2,1)S(1)}, u32[]{:S(2)}, u32[]{:S(2)}) collective-permute-start(bf16[128,1024]{1,0:T(8,128)(2,1)S(1)} %get-tuple-element.34), channel_id=1, source_target_pairs={{0,1},{1,2},{2,3},{3,0},{4,5},{5,6},{6,7},{7,4},{8,9},{9,10},{10,1... | collective-permute-start | bytes 786440 | tf_op jit(solution)/shard_map/ppermute | solution.py:70
  115.0 12.0 %collective-permute-start.7 = (bf16[128,1024]{1,0:T(8,128)(2,1)S(1)}, bf16[128,1024]{1,0:T(8,128)(2,1)S(1)}, u32[]{:S(2)}, u32[]{:S(2)}) collective-permute-start(bf16[128,1024]{1,0:T(8,128)(2,1)S(1)} %get-tuple-element.33), channel_id=1, source_target_pairs={{0,3},{1,0},{2,1},{3,2},{4,7},{5,4},{6,5},{7,6},{8,11},{9,8},{10,9... | collective-permute-start | bytes 786440 | tf_op jit(solution)/shard_map/ppermute | solution.py:70
  119.5 33.5 %all-to-all-start.2 = ((bf16[64,8,896]{2,1,0:T(8,128)(2,1)}), bf16[64,8,896]{2,1,0:T(8,128)(2,1)S(1)}, u32[]{:S(2)}, u32[]{:S(2)}) async-start(bf16[64,8,896]{2,1,0:T(8,128)(2,1)} %bitcast.13), calls=%async_computation.2 | async-start | bytes 1835008 | tf_op jit(solution)/shard_map/all_to_all | solution.py:403
  127.0 18.1 %copy-start.3 = (bf16[1,1024,896]{2,1,0:T(8,128)(2,1)S(1)}, bf16[1,1024,896]{2,1,0:T(8,128)(2,1)}, u32[]{:S(2)}) copy-start(bf16[1,1024,896]{2,1,0:T(8,128)(2,1)} %weight_ref.5) | copy-start | bytes 5505028
  127.2 10.5 %collective-permute-start.12 = (bf16[128,1024]{1,0:T(8,128)(2,1)S(1)}, bf16[128,1024]{1,0:T(8,128)(2,1)S(1)}, u32[]{:S(2)}, u32[]{:S(2)}) collective-permute-start(bf16[128,1024]{1,0:T(8,128)(2,1)S(1)} %multiply_convert_fusion.1), channel_id=1, source_target_pairs={{0,2},{1,3},{2,0},{3,1},{4,6},{5,7},{6,4},{7,5},{8,10},{9,11},{10,... | collective-permute-start | bytes 786440 | tf_op jit(solution)/shard_map/ppermute | solution.py:70
  129.3 11.4 %collective-permute-start.11 = (bf16[128,1024]{1,0:T(8,128)(2,1)S(1)}, bf16[128,1024]{1,0:T(8,128)(2,1)S(1)}, u32[]{:S(2)}, u32[]{:S(2)}) collective-permute-start(bf16[128,1024]{1,0:T(8,128)(2,1)S(1)} %multiply_convert_fusion.1), channel_id=1, source_target_pairs={{0,3},{1,0},{2,1},{3,2},{4,7},{5,4},{6,5},{7,6},{8,11},{9,8},{10,9... | collective-permute-start | bytes 786440 | tf_op jit(solution)/shard_map/ppermute | solution.py:70
  133.2 9.8 %collective-permute-start.10 = (bf16[128,1024]{1,0:T(8,128)(2,1)S(1)}, bf16[128,1024]{1,0:T(8,128)(2,1)S(1)}, u32[]{:S(2)}, u32[]{:S(2)}) collective-permute-start(bf16[128,1024]{1,0:T(8,128)(2,1)S(1)} %multiply_convert_fusion.1), channel_id=1, source_target_pairs={{0,1},{1,2},{2,3},{3,0},{4,5},{5,6},{6,7},{7,4},{8,9},{9,10},{10,1... | collective-permute-start | bytes 786440 | tf_op jit(solution)/shard_map/ppermute | solution.py:70
  143.1 4.9 %collective-permute-start.13 = (bf16[512,1024]{1,0:T(8,128)(2,1)S(1)}, bf16[512,1024]{1,0:T(8,128)(2,1)S(1)}, u32[]{:S(2)}, u32[]{:S(2)}) collective-permute-start(bf16[512,1024]{1,0:T(8,128)(2,1)S(1)} %pad_maximum_fusion.rows_ref), channel_id=1, source_target_pairs={{0,256},{256,0},{1,257},{257,1},{2,258},{258,2},{3,259},{259,3},{4... | collective-permute-start | bytes 3145736 | tf_op jit(solution)/shard_map/ppermute | solution.py:70
  151.0 13.7 %copy-start.13 = (s32[2]{0:T(128)S(1)}, s32[2]{0:T(128)}, u32[]{:S(2)}) copy-start(s32[2]{0:T(128)} %param.10) | copy-start | bytes 28
  153.1 0.9 copy-start.9
  154.0 59.0 %all-to-all-start.3 = ((bf16[64,2,8,896]{3,2,1,0:T(8,128)(2,1)}), bf16[64,2,8,896]{3,2,1,0:T(8,128)(2,1)S(1)}, u32[]{:S(2)}, u32[]{:S(2)}) async-start(bf16[64,2,8,896]{3,2,1,0:T(8,128)(2,1)} %down_half.3), calls=%async_computation.3 | async-start | bytes 3670016 | tf_op jit(solution)/shard_map/all_to_all | solution.py:403
  164.8 11.5 %copy-start.10 = (bf16[64,8,896]{2,1,0:T(8,128)(2,1)S(1)}, bf16[64,8,896]{2,1,0:T(8,128)(2,1)}, u32[]{:S(2)}) copy-start(bf16[64,8,896]{2,1,0:T(8,128)(2,1)} %copy-done.9) | copy-start | bytes 2752516
  168.1 9.3 %collective-permute-start.16 = (bf16[2,32,640]{2,1,0:T(8,128)(2,1)S(1)}, bf16[2,32,640]{2,1,0:T(8,128)(2,1)S(1)}, u32[]{:S(2)}, u32[]{:S(2)}) collective-permute-start(bf16[2,32,640]{2,1,0:T(8,128)(2,1)S(1)} %get-tuple-element.48), channel_id=1, source_target_pairs={{0,3},{1,0},{2,1},{3,2},{4,7},{5,4},{6,5},{7,6},{8,11},{9,8},{10,9... | collective-permute-start | bytes 245768 | tf_op jit(solution)/shard_map/ppermute | solution.py:70
  170.6 7.5 %collective-permute-start.15 = (bf16[2,32,640]{2,1,0:T(8,128)(2,1)S(1)}, bf16[2,32,640]{2,1,0:T(8,128)(2,1)S(1)}, u32[]{:S(2)}, u32[]{:S(2)}) collective-permute-start(bf16[2,32,640]{2,1,0:T(8,128)(2,1)S(1)} %get-tuple-element.49), channel_id=1, source_target_pairs={{0,1},{1,2},{2,3},{3,0},{4,5},{5,6},{6,7},{7,4},{8,9},{9,10},{10,1... | collective-permute-start | bytes 245768 | tf_op jit(solution)/shard_map/ppermute | solution.py:70
  174.0 7.8 %collective-permute-start.14 = (bf16[2,32,640]{2,1,0:T(8,128)(2,1)S(1)}, bf16[2,32,640]{2,1,0:T(8,128)(2,1)S(1)}, u32[]{:S(2)}, u32[]{:S(2)}) collective-permute-start(bf16[2,32,640]{2,1,0:T(8,128)(2,1)S(1)} %get-tuple-element.50), channel_id=1, source_target_pairs={{0,2},{1,3},{2,0},{3,1},{4,6},{5,7},{6,4},{7,5},{8,10},{9,11},{10,... | collective-permute-start | bytes 245768 | tf_op jit(solution)/shard_map/ppermute | solution.py:70

commit v7 on v6

--- a/solution.py
+++ b/solution.py
@@ -14,6 +14,7 @@
 CAP = 24
 FIRST = 8
 VMEM = 32 * 1024 * 1024
+MOST = 60 * 1024 * 1024
 LANES = 128
 
 NEGATIVE = -1e30
@@ -110,7 +111,7 @@
             jax.ShapeDtypeStruct((EXPERTS, rows), jnp.float32),
             jax.ShapeDtypeStruct((EXPERTS, FIRST, columns), jnp.bfloat16),
         ],
-        compiler_params=pltpu.CompilerParams(vmem_limit_bytes=VMEM),
+        compiler_params=pltpu.CompilerParams(vmem_limit_bytes=MOST),
         cost_estimate=cost(EXPERTS * FIRST, rows, columns),
         name="first_selection",
     )(ids.T, rows_in)
@@ -197,6 +198,22 @@
         cost_estimate=cost(half, depth, columns),
         name="own_half",
     )(where, rows_in, weight, arrived)
+
+
+def combine_kernel(weights_ref, rows_ref, out_ref):
+    out_ref[...] = jnp.dot(weights_ref[...], rows_ref[...], preferred_element_type=jnp.float32)
+
+
+def combined(weights, rows_in):
+    rows, depth = weights.shape
+    columns = rows_in.shape[1]
+    return pl.pallas_call(
+        combine_kernel,
+        out_shape=jax.ShapeDtypeStruct((rows, columns), jnp.float32),
+        compiler_params=pltpu.CompilerParams(vmem_limit_bytes=MOST),
+        cost_estimate=cost(rows, depth, columns),
+        name="combined",
+    )(weights, rows_in)
 
 
 def copy_kernel(from_ref, to_ref):
@@ -452,7 +469,7 @@
     attn_context = attention_join(pieces)
     first_back = first_back.reshape(-1, width)
     second_back = second_back.reshape(-1, width)
-    result = jnp.dot(weights_of[0], first_back, preferred_element_type=jnp.float32)
+    result = combined(weights_of[0], first_back)
     result = result + jnp.dot(weights_of[1], second_back, preferred_element_type=jnp.float32)
     return (attn_context, result.astype(jnp.bfloat16))
 

time: 217 us -> 215 us (level)
  local copies, waits for them, and re-layouts: 8.27 us -> 3.41 us
  waiting for transfers between devices: 79.4 us -> 84.1 us
  Pallas kernels: 20.4 us -> 24.8 us
  matrix products: 8.2 us -> 4.86 us
  other arithmetic: 6.87 us -> 4.23 us
    all_to_all x4, waiting for transfers between devices: 48.6 us -> 54.5 us  [exchanged(): return lax.all_to_all(value, 'grp', split_axis=0, concat_axis=0, tiled=True)]
    unnamed x28 -> x24, local copies, waits for them, and re-layouts: 3.7 us -> 0.99 us
    pallas_call x0 -> x1, Pallas kernels: none -> 2.38 us  [combined(): pl.pallas_call(combine_kernel, out_shape=jax.ShapeDtypeStruct((rows, colu...]
  transfers between devices with their start and end apart: 21 -> 21, of which waited for: 13 -> 12; matrix products, arithmetic and copies ran while one was open for 8% -> 5% of each run, Pallas kernels for 7% -> 8%
where the time goes in v7:
time: 215 us; the launch traced here: 214 us
  starting transfers between devices  91 us (42%)
  waiting for transfers between devices  84.1 us (39%)
  Pallas kernels  24.8 us (12%)
  matrix products  4.86 us (2%)
  other arithmetic  4.23 us (2%)
  local copies, waits for them, and re-layouts  3.41 us (2%)
    all_to_all x4, waiting for transfers between devices, exchanged(): return lax.all_to_all(value, 'grp', split_axis=0, concat_axis=0, tiled=True)  54.5 us
    ppermute x17, starting transfers between devices, turned(): lax.ppermute(value, axis, [(k, (k + step) % size) for k in range(size)])  50.2 us
    all_to_all x4, starting transfers between devices, exchanged(): return lax.all_to_all(value, 'grp', split_axis=0, concat_axis=0, tiled=True)  40.8 us
    ppermute x17, waiting for transfers between devices, turned(): lax.ppermute(value, axis, [(k, (k + step) % size) for k in range(size)])  29.6 us
    pallas_call x2, Pallas kernels, down_half(): pl.pallas_call(down_half_kernel, out_shape=jax.ShapeDtypeStruct((sources,...  5.92 us
    pallas_call x1, Pallas kernels, wide_product(): pl.pallas_call(wide_kernel, out_shape=[jax.ShapeDtypeStruct((share, colum...  5.67 us
  transfers between devices with their start and end apart: 21, of which 12 were waited for; matrix products, arithmetic and copies ran while one was open for 5% of the time, Pallas kernels for 8%

profile of v7, /device:TPU:24, one launch (start us, length us, event | category | flops | bytes accessed | tf_op | source)
XLA Modules:
  0.0 213.5 jit_solution(4065031704031868528)
XLA Ops:
  0.7 2.6 %first_selection.1 = (f32[64,128]{1,0:T(8,128)}, bf16[64,8,896]{2,1,0:T(8,128)(2,1)}) custom-call(s32[8,128]{1,0:T(8,128)} %bitcast.61, bf16[128,896]{1,0:T(8,128)(2,1)} %rows_ref.1), custom_call_target="tpu_custom_call" | custom-call | flops 117440512 | bytes 1277952 | tf_op jit(solution)/shard_map/first_selection/pallas_call | solution.py:108
  3.2 16.4 %all-to-all-start = ((bf16[64,8,896]{2,1,0:T(8,128)(2,1)}), bf16[64,8,896]{2,1,0:T(8,128)(2,1)S(1)}, u32[]{:S(2)}, u32[]{:S(2)}) async-start(bf16[64,8,896]{2,1,0:T(8,128)(2,1)} %get-tuple-element.25), calls=%async_computation | async-start | bytes 1835008 | tf_op jit(solution)/shard_map/all_to_all | solution.py:420
  19.6 1.9 collective-permute-start
  21.6 0.1 eq.81
  21.7 3.0 %copied.1 = bf16[896,1024]{1,0:T(8,128)(2,1)} custom-call(bf16[896,1024]{1,0:T(8,128)(2,1)S(1)} %bitcast.45), custom_call_target="tpu_custom_call" | custom-call | bytes 3670016 | tf_op jit(solution)/shard_map/copied/pallas_call | solution.py:226
  24.7 0.1 select_reduce_fusion
  24.8 0.1 copy.40
  25.0 0.7 broadcast_bitcast_fusion.1
  25.7 1.1 copy.39
  26.8 0.1 eq.87
  26.9 0.1 eq.96
  27.0 0.9 fusion.4
  27.9 0.7 select_convert_fusion.weights_ref
  28.6 3.0 %fusion = bf16[64,8,1792]{2,1,0:T(8,128)(2,1)} fusion(bf16[128,896]{1,0:T(8,128)(2,1)} %collective-permute-done, bf16[128,896]{1,0:T(8,128)(2,1)} %rows_ref.1, f32[512]{0:T(512)S(1)} %eq.81, f32[64,128]{1,0:T(8,128)S(1)} %copy-done.8), kind=kOutput, calls=%fused_computation.1 | convolution fusion | flops 236781568 | bytes 2328576 | tf_op jit(solution)/shard_map/dot_general | solution.py:426
  31.6 14.9 %all-to-all-done = bf16[64,8,896]{2,1,0:T(8,128)(2,1)S(1)} async-done(((bf16[64,8,896]{2,1,0:T(8,128)(2,1)}), bf16[64,8,896]{2,1,0:T(8,128)(2,1)S(1)}, u32[]{:S(2)}, u32[]{:S(2)}) %all-to-all-start) | async-done | bytes 917536 | tf_op jit(solution)/shard_map/all_to_all | solution.py:420
  46.6 6.4 %all-to-all-start.1 = ((bf16[64,8,1792]{2,1,0:T(8,128)(2,1)}), bf16[64,8,1792]{2,1,0:T(8,128)(2,1)}, u32[]{:S(2)}, u32[]{:S(2)}) async-start(bf16[64,8,1792]{2,1,0:T(8,128)(2,1)} %fusion), calls=%async_computation.1 | async-start | bytes 3670016 | tf_op jit(solution)/shard_map/all_to_all | solution.py:420
  53.0 1.2 their_half.1
  54.3 1.9 collective-permute-start.1
  56.2 2.4 %collective-permute-start.6 = (bf16[896,1024]{1,0:T(8,128)(2,1)}, bf16[896,1024]{1,0:T(8,128)(2,1)}, u32[]{:S(2)}, u32[]{:S(2)}) collective-permute-start(bf16[896,1024]{1,0:T(8,128)(2,1)} %copied.1), channel_id=1, source_target_pairs={{0,256},{256,0},{1,257},{257,1},{2,258},{258,2},{3,259},{259,3},{4... | collective-permute-start | bytes 5505032 | tf_op jit(solution)/shard_map/ppermute | solution.py:71
  58.6 1.3 own_half.1
  59.9 5.1 %collective-permute-start.4 = (bf16[256,1024]{1,0:T(8,128)(2,1)S(1)}, bf16[256,1024]{1,0:T(8,128)(2,1)S(1)}, u32[]{:S(2)}, u32[]{:S(2)}) collective-permute-start(bf16[256,1024]{1,0:T(8,128)(2,1)S(1)} %get-tuple-element.29), channel_id=1, source_target_pairs={{0,2},{1,3},{2,0},{3,1},{4,6},{5,7},{6,4},{7,5},{8,10},{9,11},{10,... | collective-permute-start | bytes 1572872 | tf_op jit(solution)/shard_map/ppermute | solution.py:71
  65.0 2.5 %collective-permute-start.3 = (bf16[256,1024]{1,0:T(8,128)(2,1)S(1)}, bf16[256,1024]{1,0:T(8,128)(2,1)S(1)}, u32[]{:S(2)}, u32[]{:S(2)}) collective-permute-start(bf16[256,1024]{1,0:T(8,128)(2,1)S(1)} %get-tuple-element.29), channel_id=1, source_target_pairs={{0,1},{1,2},{2,3},{3,0},{4,5},{5,6},{6,7},{7,4},{8,9},{9,10},{10,1... | collective-permute-start | bytes 1572872 | tf_op jit(solution)/shard_map/ppermute | solution.py:71
  67.5 4.6 %collective-permute-start.2 = (bf16[256,1024]{1,0:T(8,128)(2,1)S(1)}, bf16[256,1024]{1,0:T(8,128)(2,1)S(1)}, u32[]{:S(2)}, u32[]{:S(2)}) collective-permute-start(bf16[256,1024]{1,0:T(8,128)(2,1)S(1)} %get-tuple-element.29), channel_id=1, source_target_pairs={{0,3},{1,0},{2,1},{3,2},{4,7},{5,4},{6,5},{7,6},{8,11},{9,8},{10,9... | collective-permute-start | bytes 1572872 | tf_op jit(solution)/shard_map/ppermute | solution.py:71
  72.1 6.2 %collective-permute-done.4 = bf16[256,1024]{1,0:T(8,128)(2,1)S(1)} collective-permute-done((bf16[256,1024]{1,0:T(8,128)(2,1)S(1)}, bf16[256,1024]{1,0:T(8,128)(2,1)S(1)}, u32[]{:S(2)}, u32[]{:S(2)}) %collective-permute-start.4) | collective-permute-done | bytes 524320 | tf_op jit(solution)/shard_map/ppermute | solution.py:71
  78.3 10.2 %collective-permute-done.3 = bf16[256,1024]{1,0:T(8,128)(2,1)S(1)} collective-permute-done((bf16[256,1024]{1,0:T(8,128)(2,1)S(1)}, bf16[256,1024]{1,0:T(8,128)(2,1)S(1)}, u32[]{:S(2)}, u32[]{:S(2)}) %collective-permute-start.3) | collective-permute-done | bytes 524320 | tf_op jit(solution)/shard_map/ppermute | solution.py:71
  88.5 0.1 collective-permute-done.2
  88.7 0.5 multiply_convert_fusion.mine_ref
  89.1 1.9 collective-permute-start.5
  91.0 1.9 collective-permute-done.5.theirs_ref
  92.9 2.8 %down_both.1 = bf16[512,896]{1,0:T(8,128)(2,1)} custom-call(s32[2]{0:T(128)S(1)} %pad_add_fusion.where, bf16[256,1024]{1,0:T(8,128)(2,1)S(1)} %multiply_convert_fusion.mine_ref, bf16[256,1024]{1,0:T(8,128)(2,1)S(1)} %collective-permute-done.5.theirs_ref, bf16[1,1024,896]{2,1,0:T(8,128)(2,1)S(1)} %copy-done.2), custom_call_target="tpu_custom_call" | custom-call | flops 939524096 | bytes 3801088 | tf_op jit(solution)/shard_map/down_both/pallas_call | solution.py:257
  95.8 5.4 %all-to-all-done.1 = bf16[64,8,1792]{2,1,0:T(8,128)(2,1)} async-done(((bf16[64,8,1792]{2,1,0:T(8,128)(2,1)}), bf16[64,8,1792]{2,1,0:T(8,128)(2,1)}, u32[]{:S(2)}, u32[]{:S(2)}) %all-to-all-start.1) | async-done | bytes 1835040 | tf_op jit(solution)/shard_map/all_to_all | solution.py:420
  101.2 5.7 %wide_product.1 = (f32[128,1024]{1,0:T(8,128)S(1)}, bf16[128,1024]{1,0:T(8,128)(2,1)S(1)}, bf16[128,1024]{1,0:T(8,128)(2,1)}, bf16[128,1024]{1,0:T(8,128)(2,1)S(1)}) custom-call(s32[2]{0:T(128)S(1)} %pad_add_fusion.where, bf16[512,1792]{1,0:T(8,128)(2,1)} %bitcast.12.rows_ref, bf16[896,1024]{1,0:T(8,128)(2,1)S(1)} %bitcast.48, ...), custom_call_target="tpu_custom_call" | custom-call | flops 1879048192 | bytes 6553600 | tf_op jit(solution)/shard_map/wide_product/pallas_call | solution.py:306
  106.8 4.9 %collective-permute-start.9 = (bf16[128,1024]{1,0:T(8,128)(2,1)}, bf16[128,1024]{1,0:T(8,128)(2,1)S(1)}, u32[]{:S(2)}, u32[]{:S(2)}) collective-permute-start(bf16[128,1024]{1,0:T(8,128)(2,1)} %get-tuple-element.35), channel_id=1, source_target_pairs={{0,2},{1,3},{2,0},{3,1},{4,6},{5,7},{6,4},{7,5},{8,10},{9,11},{10,... | collective-permute-start | bytes 786440 | tf_op jit(solution)/shard_map/ppermute | solution.py:71
  111.8 2.5 %collective-permute-start.8 = (bf16[128,1024]{1,0:T(8,128)(2,1)S(1)}, bf16[128,1024]{1,0:T(8,128)(2,1)S(1)}, u32[]{:S(2)}, u32[]{:S(2)}) collective-permute-start(bf16[128,1024]{1,0:T(8,128)(2,1)S(1)} %get-tuple-element.34), channel_id=1, source_target_pairs={{0,1},{1,2},{2,3},{3,0},{4,5},{5,6},{6,7},{7,4},{8,9},{9,10},{10,1... | collective-permute-start | bytes 786440 | tf_op jit(solution)/shard_map/ppermute | solution.py:71
  114.3 4.6 %collective-permute-start.7 = (bf16[128,1024]{1,0:T(8,128)(2,1)S(1)}, bf16[128,1024]{1,0:T(8,128)(2,1)S(1)}, u32[]{:S(2)}, u32[]{:S(2)}) collective-permute-start(bf16[128,1024]{1,0:T(8,128)(2,1)S(1)} %get-tuple-element.33), channel_id=1, source_target_pairs={{0,3},{1,0},{2,1},{3,2},{4,7},{5,4},{6,5},{7,6},{8,11},{9,8},{10,9... | collective-permute-start | bytes 786440 | tf_op jit(solution)/shard_map/ppermute | solution.py:71
  118.8 7.4 %all-to-all-start.2 = ((bf16[64,8,896]{2,1,0:T(8,128)(2,1)}), bf16[64,8,896]{2,1,0:T(8,128)(2,1)S(1)}, u32[]{:S(2)}, u32[]{:S(2)}) async-start(bf16[64,8,896]{2,1,0:T(8,128)(2,1)} %bitcast.13), calls=%async_computation.2 | async-start | bytes 1835008 | tf_op jit(solution)/shard_map/all_to_all | solution.py:420
  126.3 0.2 multiply_convert_fusion.1
  126.5 2.1 collective-permute-start.12
  128.6 4.0 %collective-permute-start.11 = (bf16[128,1024]{1,0:T(8,128)(2,1)S(1)}, bf16[128,1024]{1,0:T(8,128)(2,1)S(1)}, u32[]{:S(2)}, u32[]{:S(2)}) collective-permute-start(bf16[128,1024]{1,0:T(8,128)(2,1)S(1)} %multiply_convert_fusion.1), channel_id=1, source_target_pairs={{0,3},{1,0},{2,1},{3,2},{4,7},{5,4},{6,5},{7,6},{8,11},{9,8},{10,9... | collective-permute-start | bytes 786440 | tf_op jit(solution)/shard_map/ppermute | solution.py:71
  132.6 1.9 collective-permute-start.10
  134.5 2.5 %collective-permute-done.12 = bf16[128,1024]{1,0:T(8,128)(2,1)S(1)} collective-permute-done((bf16[128,1024]{1,0:T(8,128)(2,1)S(1)}, bf16[128,1024]{1,0:T(8,128)(2,1)S(1)}, u32[]{:S(2)}, u32[]{:S(2)}) %collective-permute-start.12) | collective-permute-done | bytes 262176 | tf_op jit(solution)/shard_map/ppermute | solution.py:71
  137.0 3.0 %collective-permute-done.11 = bf16[128,1024]{1,0:T(8,128)(2,1)S(1)} collective-permute-done((bf16[128,1024]{1,0:T(8,128)(2,1)S(1)}, bf16[128,1024]{1,0:T(8,128)(2,1)S(1)}, u32[]{:S(2)}, u32[]{:S(2)}) %collective-permute-start.11) | collective-permute-done | bytes 262176 | tf_op jit(solution)/shard_map/ppermute | solution.py:71
  140.0 2.4 %collective-permute-done.10 = bf16[128,1024]{1,0:T(8,128)(2,1)S(1)} collective-permute-done((bf16[128,1024]{1,0:T(8,128)(2,1)S(1)}, bf16[128,1024]{1,0:T(8,128)(2,1)S(1)}, u32[]{:S(2)}, u32[]{:S(2)}) %collective-permute-start.10) | collective-permute-done | bytes 262176 | tf_op jit(solution)/shard_map/ppermute | solution.py:71
  142.4 1.9 collective-permute-start.13
  144.4 3.0 %down_half.2.rest_0_ = bf16[64,2,8,896]{3,2,1,0:T(8,128)(2,1)} custom-call(s32[2]{0:T(128)S(1)} %pad_add_fusion.where, bf16[512,1024]{1,0:T(8,128)(2,1)S(1)} %pad_maximum_fusion.rows_ref, bf16[1,1024,896]{2,1,0:T(8,128)(2,1)S(1)} %copy-done.3), custom_call_target="tpu_custom_call" | custom-call | flops 939524096 | bytes 3801088 | tf_op jit(solution)/shard_map/down_half/pallas_call | solution.py:363
  147.3 2.9 %down_half.3 = bf16[64,2,8,896]{3,2,1,0:T(8,128)(2,1)} custom-call(s32[2]{0:T(128)S(1)} %pad_add_fusion.where, bf16[512,1024]{1,0:T(8,128)(2,1)S(1)} %collective-permute-done.13.rows_ref, bf16[1,1024,896]{2,1,0:T(8,128)(2,1)S(1)} %copy-done.3, bf16[64,2,8,896]{3,2,1,0:T(8,128)(2,1)} %down_half.2.rest_0_), custom_call_target="tpu_custom_call", output_to_operand_aliasing={{}: (3, {})} | custom-call | flops 939524096 | bytes 3801088 | tf_op jit(solution)/shard_map/down_half/pallas_call | solution.py:363
  150.3 2.1 all-to-all-done.2
  152.4 0.9 copy-done.4
  153.3 10.6 %all-to-all-start.3 = ((bf16[64,2,8,896]{3,2,1,0:T(8,128)(2,1)}), bf16[64,2,8,896]{3,2,1,0:T(8,128)(2,1)S(1)}, u32[]{:S(2)}, u32[]{:S(2)}) async-start(bf16[64,2,8,896]{3,2,1,0:T(8,128)(2,1)} %down_half.3), calls=%async_computation.3 | async-start | bytes 3670016 | tf_op jit(solution)/shard_map/all_to_all | solution.py:420
  164.1 0.4 fusion.23
  164.5 0.2 fusion.10
  164.7 0.1 copy.42
  164.9 0.3 convolution_convert_fusion.1
  165.3 2.5 %collective-permute-start.16 = (bf16[2,32,640]{2,1,0:T(8,128)(2,1)S(1)}, bf16[2,32,640]{2,1,0:T(8,128)(2,1)S(1)}, u32[]{:S(2)}, u32[]{:S(2)}) collective-permute-start(bf16[2,32,640]{2,1,0:T(8,128)(2,1)S(1)} %get-tuple-element.48), channel_id=1, source_target_pairs={{0,3},{1,0},{2,1},{3,2},{4,7},{5,4},{6,5},{7,6},{8,11},{9,8},{10,9... | collective-permute-start | bytes 245768 | tf_op jit(solution)/shard_map/ppermute | solution.py:71
  167.8 3.4 %collective-permute-start.15 = (bf16[2,32,640]{2,1,0:T(8,128)(2,1)S(1)}, bf16[2,32,640]{2,1,0:T(8,128)(2,1)S(1)}, u32[]{:S(2)}, u32[]{:S(2)}) collective-permute-start(bf16[2,32,640]{2,1,0:T(8,128)(2,1)S(1)} %get-tuple-element.49), channel_id=1, source_target_pairs={{0,1},{1,2},{2,3},{3,0},{4,5},{5,6},{6,7},{7,4},{8,9},{9,10},{10,1... | collective-permute-start | bytes 245768 | tf_op jit(solution)/shard_map/ppermute | solution.py:71
  171.1 2.2 %collective-permute-start.14 = (bf16[2,32,640]{2,1,0:T(8,128)(2,1)S(1)}, bf16[2,32,640]{2,1,0:T(8,128)(2,1)S(1)}, u32[]{:S(2)}, u32[]{:S(2)}) collective-permute-start(bf16[2,32,640]{2,1,0:T(8,128)(2,1)S(1)} %get-tuple-element.50), channel_id=1, source_target_pairs={{0,2},{1,3},{2,0},{3,1},{4,6},{5,7},{6,4},{7,5},{8,10},{9,11},{10,... | collective-permute-start | bytes 245768 | tf_op jit(solution)/shard_map/ppermute | solution.py:71
  173.4 2.4 %combined.1 = f32[128,896]{1,0:T(8,128)} custom-call(bf16[128,512]{1,0:T(8,128)(2,1)} %select_convert_fusion.weights_ref, bf16[512,896]{1,0:T(8,128)(2,1)} %bitcast.52), custom_call_target="tpu_custom_call" | custom-call | flops 117440512 | bytes 1277952 | tf_op jit(solution)/shard_map/combined/pallas_call | solution.py:210
  175.8 3.2 %collective-permute-done.14 = bf16[2,32,640]{2,1,0:T(8,128)(2,1)S(1)} collective-permute-done((bf16[2,32,640]{2,1,0:T(8,128)(2,1)S(1)}, bf16[2,32,640]{2,1,0:T(8,128)(2,1)S(1)}, u32[]{:S(2)}, u32[]{:S(2)}) %collective-permute-start.14) | collective-permute-done | bytes 81952 | tf_op jit(solution)/shard_map/ppermute | solution.py:71
  179.0 0.1 slice_reduce_fusion.1
  179.1 0.3 slice_reduce_fusion
  179.5 0.1 multiply_reduce_fusion
  179.6 0.7 divide_convert_fusion
  180.3 32.1 %all-to-all-done.3 = bf16[64,2,8,896]{3,2,1,0:T(8,128)(2,1)S(1)} async-done(((bf16[64,2,8,896]{3,2,1,0:T(8,128)(2,1)}), bf16[64,2,8,896]{3,2,1,0:T(8,128)(2,1)S(1)}, u32[]{:S(2)}, u32[]{:S(2)}) %all-to-all-start.3) | async-done | bytes 1835040 | tf_op jit(solution)/shard_map/all_to_all | solution.py:420
  212.4 1.2 fusion.1
  (53 shorter events, 0.6 us)
Async XLA Ops:
  0.6 163.5 %copy-start = (bf16[2,128,576]{1,2,0:T(8,128)(2,1)S(1)}, bf16[2,128,576]{1,2,0:T(8,128)(2,1)}, u32[]{:S(2)}) copy-start(bf16[2,128,576]{1,2,0:T(8,128)(2,1)} %param.8) | copy-start | bytes 884740
  0.6 21.0 %copy-start.1 = (bf16[1,896,1024]{2,1,0:T(8,128)(2,1)S(1)}, bf16[1,896,1024]{2,1,0:T(8,128)(2,1)}, u32[]{:S(2)}) copy-start(bf16[1,896,1024]{2,1,0:T(8,128)(2,1)} %param.14) | copy-start | bytes 5505028
  3.2 43.3 %all-to-all-start = ((bf16[64,8,896]{2,1,0:T(8,128)(2,1)}), bf16[64,8,896]{2,1,0:T(8,128)(2,1)S(1)}, u32[]{:S(2)}, u32[]{:S(2)}) async-start(bf16[64,8,896]{2,1,0:T(8,128)(2,1)} %get-tuple-element.25), calls=%async_computation | async-start | bytes 1835008 | tf_op jit(solution)/shard_map/all_to_all | solution.py:420
  19.6 9.0 %collective-permute-start = (bf16[128,896]{1,0:T(8,128)(2,1)}, bf16[128,896]{1,0:T(8,128)(2,1)}, u32[]{:S(2)}, u32[]{:S(2)}) collective-permute-start(bf16[128,896]{1,0:T(8,128)(2,1)} %rows_ref.1), channel_id=1, source_target_pairs={{0,256},{256,0},{1,257},{257,1},{2,258},{258,2},{3,259},{259,3},{4... | collective-permute-start | bytes 688136 | tf_op jit(solution)/shard_map/ppermute | solution.py:71
  21.7 3.0 %copy-start.9 = (f32[128,8]{0,1:T(8,128)S(1)}, f32[128,8]{0,1:T(8,128)}, u32[]{:S(2)}) copy-start(f32[128,8]{0,1:T(8,128)} %param.13) | copy-start | bytes 12292
  21.7 3.0 %copy-start.10 = (s32[128,8]{0,1:T(8,128)S(1)}, s32[128,8]{0,1:T(8,128)}, u32[]{:S(2)}) copy-start(s32[128,8]{0,1:T(8,128)} %param.12) | copy-start | bytes 12292
  21.7 3.3 %copy-start.8 = (f32[64,128]{1,0:T(8,128)S(1)}, f32[64,128]{1,0:T(8,128)}, u32[]{:S(2)}) copy-start(f32[64,128]{1,0:T(8,128)} %get-tuple-element.22) | copy-start | bytes 98308
  46.6 54.6 %all-to-all-start.1 = ((bf16[64,8,1792]{2,1,0:T(8,128)(2,1)}), bf16[64,8,1792]{2,1,0:T(8,128)(2,1)}, u32[]{:S(2)}, u32[]{:S(2)}) async-start(bf16[64,8,1792]{2,1,0:T(8,128)(2,1)} %fusion), calls=%async_computation.1 | async-start | bytes 3670016 | tf_op jit(solution)/shard_map/all_to_all | solution.py:420
  54.3 4.3 %collective-permute-start.1 = (bf16[256,1024]{1,0:T(8,128)(2,1)S(1)}, bf16[256,1024]{1,0:T(8,128)(2,1)S(1)}, u32[]{:S(2)}, u32[]{:S(2)}) collective-permute-start(bf16[256,1024]{1,0:T(8,128)(2,1)S(1)} %their_half.1), channel_id=1, source_target_pairs={{0,256},{256,0},{1,257},{257,1},{2,258},{258,2},{3,259},{259,3},{4... | collective-permute-start | bytes 1572872 | tf_op jit(solution)/shard_map/ppermute | solution.py:71
  56.2 45.0 %collective-permute-start.6 = (bf16[896,1024]{1,0:T(8,128)(2,1)}, bf16[896,1024]{1,0:T(8,128)(2,1)}, u32[]{:S(2)}, u32[]{:S(2)}) collective-permute-start(bf16[896,1024]{1,0:T(8,128)(2,1)} %copied.1), channel_id=1, source_target_pairs={{0,256},{256,0},{1,257},{257,1},{2,258},{258,2},{3,259},{259,3},{4... | collective-permute-start | bytes 5505032 | tf_op jit(solution)/shard_map/ppermute | solution.py:71
  59.9 33.0 %copy-start.2 = (bf16[1,1024,896]{2,1,0:T(8,128)(2,1)S(1)}, bf16[1,1024,896]{2,1,0:T(8,128)(2,1)}, u32[]{:S(2)}) copy-start(bf16[1,1024,896]{2,1,0:T(8,128)(2,1)} %weight_ref.5) | copy-start | bytes 5505028
  59.9 18.4 %collective-permute-start.4 = (bf16[256,1024]{1,0:T(8,128)(2,1)S(1)}, bf16[256,1024]{1,0:T(8,128)(2,1)S(1)}, u32[]{:S(2)}, u32[]{:S(2)}) collective-permute-start(bf16[256,1024]{1,0:T(8,128)(2,1)S(1)} %get-tuple-element.29), channel_id=1, source_target_pairs={{0,2},{1,3},{2,0},{3,1},{4,6},{5,7},{6,4},{7,5},{8,10},{9,11},{10,... | collective-permute-start | bytes 1572872 | tf_op jit(solution)/shard_map/ppermute | solution.py:71
  65.0 23.5 %collective-permute-start.3 = (bf16[256,1024]{1,0:T(8,128)(2,1)S(1)}, bf16[256,1024]{1,0:T(8,128)(2,1)S(1)}, u32[]{:S(2)}, u32[]{:S(2)}) collective-permute-start(bf16[256,1024]{1,0:T(8,128)(2,1)S(1)} %get-tuple-element.29), channel_id=1, source_target_pairs={{0,1},{1,2},{2,3},{3,0},{4,5},{5,6},{6,7},{7,4},{8,9},{9,10},{10,1... | collective-permute-start | bytes 1572872 | tf_op jit(solution)/shard_map/ppermute | solution.py:71
  67.5 21.2 %collective-permute-start.2 = (bf16[256,1024]{1,0:T(8,128)(2,1)S(1)}, bf16[256,1024]{1,0:T(8,128)(2,1)S(1)}, u32[]{:S(2)}, u32[]{:S(2)}) collective-permute-start(bf16[256,1024]{1,0:T(8,128)(2,1)S(1)} %get-tuple-element.29), channel_id=1, source_target_pairs={{0,3},{1,0},{2,1},{3,2},{4,7},{5,4},{6,5},{7,6},{8,11},{9,8},{10,9... | collective-permute-start | bytes 1572872 | tf_op jit(solution)/shard_map/ppermute | solution.py:71
  89.1 3.8 %collective-permute-start.5 = (bf16[256,1024]{1,0:T(8,128)(2,1)S(1)}, bf16[256,1024]{1,0:T(8,128)(2,1)S(1)}, u32[]{:S(2)}, u32[]{:S(2)}) collective-permute-start(bf16[256,1024]{1,0:T(8,128)(2,1)S(1)} %multiply_convert_fusion.mine_ref), channel_id=1, source_target_pairs={{0,256},{256,0},{1,257},{257,1},{2,258},{258,2},{3,259},{259,3},{4... | collective-permute-start | bytes 1572872 | tf_op jit(solution)/shard_map/ppermute | solution.py:71
  106.8 19.4 %collective-permute-start.9 = (bf16[128,1024]{1,0:T(8,128)(2,1)}, bf16[128,1024]{1,0:T(8,128)(2,1)S(1)}, u32[]{:S(2)}, u32[]{:S(2)}) collective-permute-start(bf16[128,1024]{1,0:T(8,128)(2,1)} %get-tuple-element.35), channel_id=1, source_target_pairs={{0,2},{1,3},{2,0},{3,1},{4,6},{5,7},{6,4},{7,5},{8,10},{9,11},{10,... | collective-permute-start | bytes 786440 | tf_op jit(solution)/shard_map/ppermute | solution.py:71
  111.8 14.5 %collective-permute-start.8 = (bf16[128,1024]{1,0:T(8,128)(2,1)S(1)}, bf16[128,1024]{1,0:T(8,128)(2,1)S(1)}, u32[]{:S(2)}, u32[]{:S(2)}) collective-permute-start(bf16[128,1024]{1,0:T(8,128)(2,1)S(1)} %get-tuple-element.34), channel_id=1, source_target_pairs={{0,1},{1,2},{2,3},{3,0},{4,5},{5,6},{6,7},{7,4},{8,9},{9,10},{10,1... | collective-permute-start | bytes 786440 | tf_op jit(solution)/shard_map/ppermute | solution.py:71
  114.3 12.0 %collective-permute-start.7 = (bf16[128,1024]{1,0:T(8,128)(2,1)S(1)}, bf16[128,1024]{1,0:T(8,128)(2,1)S(1)}, u32[]{:S(2)}, u32[]{:S(2)}) collective-permute-start(bf16[128,1024]{1,0:T(8,128)(2,1)S(1)} %get-tuple-element.33), channel_id=1, source_target_pairs={{0,3},{1,0},{2,1},{3,2},{4,7},{5,4},{6,5},{7,6},{8,11},{9,8},{10,9... | collective-permute-start | bytes 786440 | tf_op jit(solution)/shard_map/ppermute | solution.py:71
  118.8 33.5 %all-to-all-start.2 = ((bf16[64,8,896]{2,1,0:T(8,128)(2,1)}), bf16[64,8,896]{2,1,0:T(8,128)(2,1)S(1)}, u32[]{:S(2)}, u32[]{:S(2)}) async-start(bf16[64,8,896]{2,1,0:T(8,128)(2,1)} %bitcast.13), calls=%async_computation.2 | async-start | bytes 1835008 | tf_op jit(solution)/shard_map/all_to_all | solution.py:420
  126.3 18.1 %copy-start.3 = (bf16[1,1024,896]{2,1,0:T(8,128)(2,1)S(1)}, bf16[1,1024,896]{2,1,0:T(8,128)(2,1)}, u32[]{:S(2)}) copy-start(bf16[1,1024,896]{2,1,0:T(8,128)(2,1)} %weight_ref.5) | copy-start | bytes 5505028
  126.5 10.5 %collective-permute-start.12 = (bf16[128,1024]{1,0:T(8,128)(2,1)S(1)}, bf16[128,1024]{1,0:T(8,128)(2,1)S(1)}, u32[]{:S(2)}, u32[]{:S(2)}) collective-permute-start(bf16[128,1024]{1,0:T(8,128)(2,1)S(1)} %multiply_convert_fusion.1), channel_id=1, source_target_pairs={{0,2},{1,3},{2,0},{3,1},{4,6},{5,7},{6,4},{7,5},{8,10},{9,11},{10,... | collective-permute-start | bytes 786440 | tf_op jit(solution)/shard_map/ppermute | solution.py:71
  128.6 11.4 %collective-permute-start.11 = (bf16[128,1024]{1,0:T(8,128)(2,1)S(1)}, bf16[128,1024]{1,0:T(8,128)(2,1)S(1)}, u32[]{:S(2)}, u32[]{:S(2)}) collective-permute-start(bf16[128,1024]{1,0:T(8,128)(2,1)S(1)} %multiply_convert_fusion.1), channel_id=1, source_target_pairs={{0,3},{1,0},{2,1},{3,2},{4,7},{5,4},{6,5},{7,6},{8,11},{9,8},{10,9... | collective-permute-start | bytes 786440 | tf_op jit(solution)/shard_map/ppermute | solution.py:71
  132.6 9.8 %collective-permute-start.10 = (bf16[128,1024]{1,0:T(8,128)(2,1)S(1)}, bf16[128,1024]{1,0:T(8,128)(2,1)S(1)}, u32[]{:S(2)}, u32[]{:S(2)}) collective-permute-start(bf16[128,1024]{1,0:T(8,128)(2,1)S(1)} %multiply_convert_fusion.1), channel_id=1, source_target_pairs={{0,1},{1,2},{2,3},{3,0},{4,5},{5,6},{6,7},{7,4},{8,9},{9,10},{10,1... | collective-permute-start | bytes 786440 | tf_op jit(solution)/shard_map/ppermute | solution.py:71
  142.4 4.9 %collective-permute-start.13 = (bf16[512,1024]{1,0:T(8,128)(2,1)S(1)}, bf16[512,1024]{1,0:T(8,128)(2,1)S(1)}, u32[]{:S(2)}, u32[]{:S(2)}) collective-permute-start(bf16[512,1024]{1,0:T(8,128)(2,1)S(1)} %pad_maximum_fusion.rows_ref), channel_id=1, source_target_pairs={{0,256},{256,0},{1,257},{257,1},{2,258},{258,2},{3,259},{259,3},{4... | collective-permute-start | bytes 3145736 | tf_op jit(solution)/shard_map/ppermute | solution.py:71
  150.3 13.7 %copy-start.11 = (s32[2]{0:T(128)S(1)}, s32[2]{0:T(128)}, u32[]{:S(2)}) copy-start(s32[2]{0:T(128)} %param.10) | copy-start | bytes 28
  150.3 13.8 %copy-start.5 = (bf16[2,256,576]{1,2,0:T(8,128)(2,1)S(1)}, bf16[2,256,576]{1,2,0:T(8,128)(2,1)}, u32[]{:S(2)}) copy-start(bf16[2,256,576]{1,2,0:T(8,128)(2,1)} %param.9) | copy-start | bytes 1769476
  152.4 0.9 copy-start.4
  153.3 59.1 %all-to-all-start.3 = ((bf16[64,2,8,896]{3,2,1,0:T(8,128)(2,1)}), bf16[64,2,8,896]{3,2,1,0:T(8,128)(2,1)S(1)}, u32[]{:S(2)}, u32[]{:S(2)}) async-start(bf16[64,2,8,896]{3,2,1,0:T(8,128)(2,1)} %down_half.3), calls=%async_computation.3 | async-start | bytes 3670016 | tf_op jit(solution)/shard_map/all_to_all | solution.py:420
  165.3 10.5 %collective-permute-start.16 = (bf16[2,32,640]{2,1,0:T(8,128)(2,1)S(1)}, bf16[2,32,640]{2,1,0:T(8,128)(2,1)S(1)}, u32[]{:S(2)}, u32[]{:S(2)}) collective-permute-start(bf16[2,32,640]{2,1,0:T(8,128)(2,1)S(1)} %get-tuple-element.48), channel_id=1, source_target_pairs={{0,3},{1,0},{2,1},{3,2},{4,7},{5,4},{6,5},{7,6},{8,11},{9,8},{10,9... | collective-permute-start | bytes 245768 | tf_op jit(solution)/shard_map/ppermute | solution.py:71
  167.8 8.0 %collective-permute-start.15 = (bf16[2,32,640]{2,1,0:T(8,128)(2,1)S(1)}, bf16[2,32,640]{2,1,0:T(8,128)(2,1)S(1)}, u32[]{:S(2)}, u32[]{:S(2)}) collective-permute-start(bf16[2,32,640]{2,1,0:T(8,128)(2,1)S(1)} %get-tuple-element.49), channel_id=1, source_target_pairs={{0,1},{1,2},{2,3},{3,0},{4,5},{5,6},{6,7},{7,4},{8,9},{9,10},{10,1... | collective-permute-start | bytes 245768 | tf_op jit(solution)/shard_map/ppermute | solution.py:71
  171.1 7.8 %collective-permute-start.14 = (bf16[2,32,640]{2,1,0:T(8,128)(2,1)S(1)}, bf16[2,32,640]{2,1,0:T(8,128)(2,1)S(1)}, u32[]{:S(2)}, u32[]{:S(2)}) collective-permute-start(bf16[2,32,640]{2,1,0:T(8,128)(2,1)S(1)} %get-tuple-element.50), channel_id=1, source_target_pairs={{0,2},{1,3},{2,0},{3,1},{4,6},{5,7},{6,4},{7,5},{8,10},{9,11},{10,... | collective-permute-start | bytes 245768 | tf_op jit(solution)/shard_map/ppermute | solution.py:71
  173.3 39.0 %copy-start.7 = (bf16[128,1024]{0,1:T(8,128)(2,1)S(1)}, bf16[128,1024]{0,1:T(8,128)(2,1)}, u32[]{:S(2)}) copy-start(bf16[128,1024]{0,1:T(8,128)(2,1)} %fusion.4) | copy-start | bytes 786436
  175.7 36.6 %copy-start.6 = (f32[128,896]{1,0:T(8,128)S(1)}, f32[128,896]{1,0:T(8,128)}, u32[]{:S(2)}) copy-start(f32[128,896]{1,0:T(8,128)} %combined.1) | copy-start | bytes 1376260

commit v8 on v7

--- a/solution.py
+++ b/solution.py
@@ -275,33 +275,22 @@
     )(where, mine, theirs, weight)
 
 
-def wide_kernel(where, rows_ref, weight_ref, other_ref, own_ref, *rest):
-    piece_refs, total = rest[:-1], rest[-1]
-    tile = rows_ref.shape[0]
+def wide_kernel(where, rows_ref, weight_ref, other_ref, *out_refs):
     depth = weight_ref.shape[0]
-    share = own_ref.shape[0]
-    size = total.shape[0] // share
-    step = pl.program_id(0)
-    here = pl.ds(pl.multiple_of(step * tile, tile), tile)
-    total[here, :] = jnp.dot(
-        rows_ref[:, :depth], weight_ref[...], preferred_element_type=jnp.float32
-    ) + jnp.dot(rows_ref[:, depth:], other_ref[...], preferred_element_type=jnp.float32)
-
-    @pl.when(step == pl.num_programs(0) - 1)
-    def _():
-        for ahead in range(size):
-            place = lax.rem(where[1] + ahead, size)
-            piece = total[pl.ds(pl.multiple_of(place * share, share), share), :]
-            if ahead == 0:
-                own_ref[...] = piece
-            else:
-                piece_refs[ahead - 1][...] = piece.astype(jnp.bfloat16)
+    share = out_refs[0].shape[0]
+    size = len(out_refs)
+    for ahead, out_ref in enumerate(out_refs):
+        place = lax.rem(where[1] + ahead, size)
+        rows = rows_ref[pl.ds(pl.multiple_of(place * share, share), share), :]
+        made = jnp.dot(
+            rows[:, :depth], weight_ref[...], preferred_element_type=jnp.float32
+        ) + jnp.dot(rows[:, depth:], other_ref[...], preferred_element_type=jnp.float32)
+        out_ref[...] = made.astype(out_ref.dtype)
 
 
 def wide_product(where, rows_in, weight, other, size):
     rows, width = rows_in.shape
     depth, columns = weight.shape
-    tile = 256
     share = rows // size
     return pl.pallas_call(
         wide_kernel,
@@ -309,14 +298,13 @@
         + [jax.ShapeDtypeStruct((share, columns), jnp.bfloat16)] * (size - 1),
         grid_spec=pltpu.PrefetchScalarGridSpec(
             num_scalar_prefetch=1,
-            grid=(rows // tile,),
+            grid=(1,),
             in_specs=[
-                pl.BlockSpec((tile, width), lambda i, where: (i, 0)),
+                pl.BlockSpec((rows, width), lambda i, where: (0, 0)),
                 pl.BlockSpec((depth, columns), lambda i, where: (0, 0)),
                 pl.BlockSpec((depth, columns), lambda i, where: (0, 0)),
             ],
             out_specs=[pl.BlockSpec((share, columns), lambda i, where: (0, 0))] * size,
-            scratch_shapes=[pltpu.VMEM((rows, columns), jnp.float32)],
         ),
         compiler_params=pltpu.CompilerParams(vmem_limit_bytes=VMEM),
         cost_estimate=cost(rows, width, columns),
@@ -389,7 +377,7 @@
 def wide_rows(where, rows_in, up, other_up, down, sources):
     size = lax.axis_size("tp")
     own, *pieces = wide_product(where, rows_in, up, other_up, size)
-    for step in (3, 1, 2):
+    for step in (2, 1, 3):
         own = own + turned(pieces[step - 1], "tp", step).astype(jnp.float32)
     mine = jax.nn.silu(own).astype(jnp.bfloat16)
     others = {step: turned(mine, "tp", step) for step in (3, 1, 2)}

time: 215 us -> 216 us (level)
  no operation moved by 1% of the time
where the time goes in v8:
time: 216 us; the launch traced here: 215 us
  starting transfers between devices  92.3 us (43%)
  waiting for transfers between devices  83.8 us (39%)
  Pallas kernels  24.8 us (11%)
  matrix products  4.86 us (2%)
  other arithmetic  4.23 us (2%)
  local copies, waits for them, and re-layouts  3.4 us (2%)
    all_to_all x4, waiting for transfers between devices, exchanged(): return lax.all_to_all(value, 'grp', split_axis=0, concat_axis=0, tiled=True)  52.4 us
    ppermute x17, starting transfers between devices, turned(): lax.ppermute(value, axis, [(k, (k + step) % size) for k in range(size)])  49.7 us
    all_to_all x4, starting transfers between devices, exchanged(): return lax.all_to_all(value, 'grp', split_axis=0, concat_axis=0, tiled=True)  42.6 us
    ppermute x17, waiting for transfers between devices, turned(): lax.ppermute(value, axis, [(k, (k + step) % size) for k in range(size)])  31.4 us
    pallas_call x2, Pallas kernels, down_half(): pl.pallas_call(down_half_kernel, out_shape=jax.ShapeDtypeStruct((sources,...  5.92 us
    pallas_call x1, Pallas kernels, wide_product(): pl.pallas_call(wide_kernel, out_shape=[jax.ShapeDtypeStruct((share, colum...  5.64 us
  transfers between devices with their start and end apart: 21, of which 12 were waited for; matrix products, arithmetic and copies ran while one was open for 5% of the time, Pallas kernels for 8%

profile of v8, /device:TPU:24, one launch (start us, length us, event | category | flops | bytes accessed | tf_op | source)
XLA Modules:
  0.0 214.6 jit_solution(2128339168716277699)
XLA Ops:
  0.7 2.6 %first_selection.1 = (f32[64,128]{1,0:T(8,128)}, bf16[64,8,896]{2,1,0:T(8,128)(2,1)}) custom-call(s32[8,128]{1,0:T(8,128)} %bitcast.61, bf16[128,896]{1,0:T(8,128)(2,1)} %rows_ref.1), custom_call_target="tpu_custom_call" | custom-call | flops 117440512 | bytes 1277952 | tf_op jit(solution)/shard_map/first_selection/pallas_call | solution.py:108
  3.2 16.4 %all-to-all-start = ((bf16[64,8,896]{2,1,0:T(8,128)(2,1)}), bf16[64,8,896]{2,1,0:T(8,128)(2,1)S(1)}, u32[]{:S(2)}, u32[]{:S(2)}) async-start(bf16[64,8,896]{2,1,0:T(8,128)(2,1)} %get-tuple-element.25), calls=%async_computation | async-start | bytes 1835008 | tf_op jit(solution)/shard_map/all_to_all | solution.py:408
  19.6 1.9 collective-permute-start
  21.6 0.1 eq.81
  21.7 3.0 %copied.1 = bf16[896,1024]{1,0:T(8,128)(2,1)} custom-call(bf16[896,1024]{1,0:T(8,128)(2,1)S(1)} %bitcast.45), custom_call_target="tpu_custom_call" | custom-call | bytes 3670016 | tf_op jit(solution)/shard_map/copied/pallas_call | solution.py:226
  24.7 0.1 select_reduce_fusion
  24.8 0.1 copy.40
  25.0 0.7 broadcast_bitcast_fusion.1
  25.7 1.1 copy.39
  26.8 0.1 eq.87
  26.9 0.1 eq.96
  27.0 0.9 fusion.4
  27.9 0.7 select_convert_fusion.weights_ref
  28.6 3.0 %fusion = bf16[64,8,1792]{2,1,0:T(8,128)(2,1)} fusion(bf16[128,896]{1,0:T(8,128)(2,1)} %collective-permute-done, bf16[128,896]{1,0:T(8,128)(2,1)} %rows_ref.1, f32[512]{0:T(512)S(1)} %eq.81, f32[64,128]{1,0:T(8,128)S(1)} %copy-done.8), kind=kOutput, calls=%fused_computation.1 | convolution fusion | flops 236781568 | bytes 2328576 | tf_op jit(solution)/shard_map/dot_general | solution.py:414
  31.6 14.9 %all-to-all-done = bf16[64,8,896]{2,1,0:T(8,128)(2,1)S(1)} async-done(((bf16[64,8,896]{2,1,0:T(8,128)(2,1)}), bf16[64,8,896]{2,1,0:T(8,128)(2,1)S(1)}, u32[]{:S(2)}, u32[]{:S(2)}) %all-to-all-start) | async-done | bytes 917536 | tf_op jit(solution)/shard_map/all_to_all | solution.py:408
  46.6 6.4 %all-to-all-start.1 = ((bf16[64,8,1792]{2,1,0:T(8,128)(2,1)}), bf16[64,8,1792]{2,1,0:T(8,128)(2,1)}, u32[]{:S(2)}, u32[]{:S(2)}) async-start(bf16[64,8,1792]{2,1,0:T(8,128)(2,1)} %fusion), calls=%async_computation.1 | async-start | bytes 3670016 | tf_op jit(solution)/shard_map/all_to_all | solution.py:408
  53.0 1.3 their_half.1
  54.3 1.9 collective-permute-start.1
  56.2 2.4 %collective-permute-start.6 = (bf16[896,1024]{1,0:T(8,128)(2,1)}, bf16[896,1024]{1,0:T(8,128)(2,1)}, u32[]{:S(2)}, u32[]{:S(2)}) collective-permute-start(bf16[896,1024]{1,0:T(8,128)(2,1)} %copied.1), channel_id=1, source_target_pairs={{0,256},{256,0},{1,257},{257,1},{2,258},{258,2},{3,259},{259,3},{4... | collective-permute-start | bytes 5505032 | tf_op jit(solution)/shard_map/ppermute | solution.py:71
  58.6 1.3 own_half.1
  59.9 5.1 %collective-permute-start.4 = (bf16[256,1024]{1,0:T(8,128)(2,1)S(1)}, bf16[256,1024]{1,0:T(8,128)(2,1)S(1)}, u32[]{:S(2)}, u32[]{:S(2)}) collective-permute-start(bf16[256,1024]{1,0:T(8,128)(2,1)S(1)} %get-tuple-element.29), channel_id=1, source_target_pairs={{0,2},{1,3},{2,0},{3,1},{4,6},{5,7},{6,4},{7,5},{8,10},{9,11},{10,... | collective-permute-start | bytes 1572872 | tf_op jit(solution)/shard_map/ppermute | solution.py:71
  65.0 2.5 %collective-permute-start.3 = (bf16[256,1024]{1,0:T(8,128)(2,1)S(1)}, bf16[256,1024]{1,0:T(8,128)(2,1)S(1)}, u32[]{:S(2)}, u32[]{:S(2)}) collective-permute-start(bf16[256,1024]{1,0:T(8,128)(2,1)S(1)} %get-tuple-element.29), channel_id=1, source_target_pairs={{0,1},{1,2},{2,3},{3,0},{4,5},{5,6},{6,7},{7,4},{8,9},{9,10},{10,1... | collective-permute-start | bytes 1572872 | tf_op jit(solution)/shard_map/ppermute | solution.py:71
  67.5 4.5 %collective-permute-start.2 = (bf16[256,1024]{1,0:T(8,128)(2,1)S(1)}, bf16[256,1024]{1,0:T(8,128)(2,1)S(1)}, u32[]{:S(2)}, u32[]{:S(2)}) collective-permute-start(bf16[256,1024]{1,0:T(8,128)(2,1)S(1)} %get-tuple-element.29), channel_id=1, source_target_pairs={{0,3},{1,0},{2,1},{3,2},{4,7},{5,4},{6,5},{7,6},{8,11},{9,8},{10,9... | collective-permute-start | bytes 1572872 | tf_op jit(solution)/shard_map/ppermute | solution.py:71
  72.1 6.2 %collective-permute-done.4 = bf16[256,1024]{1,0:T(8,128)(2,1)S(1)} collective-permute-done((bf16[256,1024]{1,0:T(8,128)(2,1)S(1)}, bf16[256,1024]{1,0:T(8,128)(2,1)S(1)}, u32[]{:S(2)}, u32[]{:S(2)}) %collective-permute-start.4) | collective-permute-done | bytes 524320 | tf_op jit(solution)/shard_map/ppermute | solution.py:71
  78.3 10.2 %collective-permute-done.3 = bf16[256,1024]{1,0:T(8,128)(2,1)S(1)} collective-permute-done((bf16[256,1024]{1,0:T(8,128)(2,1)S(1)}, bf16[256,1024]{1,0:T(8,128)(2,1)S(1)}, u32[]{:S(2)}, u32[]{:S(2)}) %collective-permute-start.3) | collective-permute-done | bytes 524320 | tf_op jit(solution)/shard_map/ppermute | solution.py:71
  88.5 0.1 collective-permute-done.2
  88.7 0.5 multiply_convert_fusion.mine_ref
  89.1 1.9 collective-permute-start.5
  91.0 1.9 collective-permute-done.5.theirs_ref
  92.9 2.8 %down_both.1 = bf16[512,896]{1,0:T(8,128)(2,1)} custom-call(s32[2]{0:T(128)S(1)} %pad_add_fusion.where, bf16[256,1024]{1,0:T(8,128)(2,1)S(1)} %multiply_convert_fusion.mine_ref, bf16[256,1024]{1,0:T(8,128)(2,1)S(1)} %collective-permute-done.5.theirs_ref, bf16[1,1024,896]{2,1,0:T(8,128)(2,1)S(1)} %copy-done.2), custom_call_target="tpu_custom_call" | custom-call | flops 939524096 | bytes 3801088 | tf_op jit(solution)/shard_map/down_both/pallas_call | solution.py:257
  95.8 5.4 %all-to-all-done.1 = bf16[64,8,1792]{2,1,0:T(8,128)(2,1)} async-done(((bf16[64,8,1792]{2,1,0:T(8,128)(2,1)}), bf16[64,8,1792]{2,1,0:T(8,128)(2,1)}, u32[]{:S(2)}, u32[]{:S(2)}) %all-to-all-start.1) | async-done | bytes 1835040 | tf_op jit(solution)/shard_map/all_to_all | solution.py:408
  101.2 5.6 %wide_product.1 = (f32[128,1024]{1,0:T(8,128)S(1)}, bf16[128,1024]{1,0:T(8,128)(2,1)S(1)}, bf16[128,1024]{1,0:T(8,128)(2,1)S(1)}, bf16[128,1024]{1,0:T(8,128)(2,1)}) custom-call(s32[2]{0:T(128)S(1)} %pad_add_fusion.where, bf16[512,1792]{1,0:T(8,128)(2,1)} %bitcast.12.rows_ref, bf16[896,1024]{1,0:T(8,128)(2,1)S(1)} %bitcast.48, ...), custom_call_target="tpu_custom_call" | custom-call | flops 1879048192 | bytes 6553600 | tf_op jit(solution)/shard_map/wide_product/pallas_call | solution.py:295
  106.8 4.7 %collective-permute-start.9 = (bf16[128,1024]{1,0:T(8,128)(2,1)}, bf16[128,1024]{1,0:T(8,128)(2,1)S(1)}, u32[]{:S(2)}, u32[]{:S(2)}) collective-permute-start(bf16[128,1024]{1,0:T(8,128)(2,1)} %get-tuple-element.35), channel_id=1, source_target_pairs={{0,3},{1,0},{2,1},{3,2},{4,7},{5,4},{6,5},{7,6},{8,11},{9,8},{10,9... | collective-permute-start | bytes 786440 | tf_op jit(solution)/shard_map/ppermute | solution.py:71
  111.5 1.9 collective-permute-start.8
  113.4 4.2 %collective-permute-start.7 = (bf16[128,1024]{1,0:T(8,128)(2,1)S(1)}, bf16[128,1024]{1,0:T(8,128)(2,1)S(1)}, u32[]{:S(2)}, u32[]{:S(2)}) collective-permute-start(bf16[128,1024]{1,0:T(8,128)(2,1)S(1)} %get-tuple-element.33), channel_id=1, source_target_pairs={{0,2},{1,3},{2,0},{3,1},{4,6},{5,7},{6,4},{7,5},{8,10},{9,11},{10,... | collective-permute-start | bytes 786440 | tf_op jit(solution)/shard_map/ppermute | solution.py:71
  117.6 7.4 %all-to-all-start.2 = ((bf16[64,8,896]{2,1,0:T(8,128)(2,1)}), bf16[64,8,896]{2,1,0:T(8,128)(2,1)S(1)}, u32[]{:S(2)}, u32[]{:S(2)}) async-start(bf16[64,8,896]{2,1,0:T(8,128)(2,1)} %bitcast.13), calls=%async_computation.2 | async-start | bytes 1835008 | tf_op jit(solution)/shard_map/all_to_all | solution.py:408
  125.0 2.0 collective-permute-done.8
  127.1 0.2 multiply_convert_fusion.1
  127.3 2.6 %collective-permute-start.12 = (bf16[128,1024]{1,0:T(8,128)(2,1)S(1)}, bf16[128,1024]{1,0:T(8,128)(2,1)S(1)}, u32[]{:S(2)}, u32[]{:S(2)}) collective-permute-start(bf16[128,1024]{1,0:T(8,128)(2,1)S(1)} %multiply_convert_fusion.1), channel_id=1, source_target_pairs={{0,2},{1,3},{2,0},{3,1},{4,6},{5,7},{6,4},{7,5},{8,10},{9,11},{10,... | collective-permute-start | bytes 786440 | tf_op jit(solution)/shard_map/ppermute | solution.py:71
  129.9 3.8 %collective-permute-start.11 = (bf16[128,1024]{1,0:T(8,128)(2,1)S(1)}, bf16[128,1024]{1,0:T(8,128)(2,1)S(1)}, u32[]{:S(2)}, u32[]{:S(2)}) collective-permute-start(bf16[128,1024]{1,0:T(8,128)(2,1)S(1)} %multiply_convert_fusion.1), channel_id=1, source_target_pairs={{0,3},{1,0},{2,1},{3,2},{4,7},{5,4},{6,5},{7,6},{8,11},{9,8},{10,9... | collective-permute-start | bytes 786440 | tf_op jit(solution)/shard_map/ppermute | solution.py:71
  133.7 2.0 collective-permute-start.10
  135.8 2.7 %collective-permute-done.12 = bf16[128,1024]{1,0:T(8,128)(2,1)S(1)} collective-permute-done((bf16[128,1024]{1,0:T(8,128)(2,1)S(1)}, bf16[128,1024]{1,0:T(8,128)(2,1)S(1)}, u32[]{:S(2)}, u32[]{:S(2)}) %collective-permute-start.12) | collective-permute-done | bytes 262176 | tf_op jit(solution)/shard_map/ppermute | solution.py:71
  138.4 1.3 collective-permute-done.11
  139.7 3.8 %collective-permute-done.10 = bf16[128,1024]{1,0:T(8,128)(2,1)S(1)} collective-permute-done((bf16[128,1024]{1,0:T(8,128)(2,1)S(1)}, bf16[128,1024]{1,0:T(8,128)(2,1)S(1)}, u32[]{:S(2)}, u32[]{:S(2)}) %collective-permute-start.10) | collective-permute-done | bytes 262176 | tf_op jit(solution)/shard_map/ppermute | solution.py:71
  143.6 2.1 collective-permute-start.13
  145.7 3.0 %down_half.2.rest_0_ = bf16[64,2,8,896]{3,2,1,0:T(8,128)(2,1)} custom-call(s32[2]{0:T(128)S(1)} %pad_add_fusion.where, bf16[512,1024]{1,0:T(8,128)(2,1)S(1)} %pad_maximum_fusion.rows_ref, bf16[1,1024,896]{2,1,0:T(8,128)(2,1)S(1)} %copy-done.3), custom_call_target="tpu_custom_call" | custom-call | flops 939524096 | bytes 3801088 | tf_op jit(solution)/shard_map/down_half/pallas_call | solution.py:351
  148.7 2.9 %down_half.3 = bf16[64,2,8,896]{3,2,1,0:T(8,128)(2,1)} custom-call(s32[2]{0:T(128)S(1)} %pad_add_fusion.where, bf16[512,1024]{1,0:T(8,128)(2,1)S(1)} %collective-permute-done.13.rows_ref, bf16[1,1024,896]{2,1,0:T(8,128)(2,1)S(1)} %copy-done.3, bf16[64,2,8,896]{3,2,1,0:T(8,128)(2,1)} %down_half.2.rest_0_), custom_call_target="tpu_custom_call", output_to_operand_aliasing={{}: (3, {})} | custom-call | flops 939524096 | bytes 3801088 | tf_op jit(solution)/shard_map/down_half/pallas_call | solution.py:351
  151.6 0.9 copy-done.4
  152.6 12.4 %all-to-all-start.3 = ((bf16[64,2,8,896]{3,2,1,0:T(8,128)(2,1)}), bf16[64,2,8,896]{3,2,1,0:T(8,128)(2,1)S(1)}, u32[]{:S(2)}, u32[]{:S(2)}) async-start(bf16[64,2,8,896]{3,2,1,0:T(8,128)(2,1)} %down_half.3), calls=%async_computation.3 | async-start | bytes 3670016 | tf_op jit(solution)/shard_map/all_to_all | solution.py:408
  165.1 0.4 fusion.23
  165.5 0.2 fusion.10
  165.8 0.1 copy.42
  165.9 0.3 convolution_convert_fusion.1
  166.3 1.9 collective-permute-start.16
  168.3 3.9 %collective-permute-start.15 = (bf16[2,32,640]{2,1,0:T(8,128)(2,1)S(1)}, bf16[2,32,640]{2,1,0:T(8,128)(2,1)S(1)}, u32[]{:S(2)}, u32[]{:S(2)}) collective-permute-start(bf16[2,32,640]{2,1,0:T(8,128)(2,1)S(1)} %get-tuple-element.49), channel_id=1, source_target_pairs={{0,1},{1,2},{2,3},{3,0},{4,5},{5,6},{6,7},{7,4},{8,9},{9,10},{10,1... | collective-permute-start | bytes 245768 | tf_op jit(solution)/shard_map/ppermute | solution.py:71
  172.2 2.3 %collective-permute-start.14 = (bf16[2,32,640]{2,1,0:T(8,128)(2,1)S(1)}, bf16[2,32,640]{2,1,0:T(8,128)(2,1)S(1)}, u32[]{:S(2)}, u32[]{:S(2)}) collective-permute-start(bf16[2,32,640]{2,1,0:T(8,128)(2,1)S(1)} %get-tuple-element.50), channel_id=1, source_target_pairs={{0,2},{1,3},{2,0},{3,1},{4,6},{5,7},{6,4},{7,5},{8,10},{9,11},{10,... | collective-permute-start | bytes 245768 | tf_op jit(solution)/shard_map/ppermute | solution.py:71
  174.5 2.4 %combined.1 = f32[128,896]{1,0:T(8,128)} custom-call(bf16[128,512]{1,0:T(8,128)(2,1)} %select_convert_fusion.weights_ref, bf16[512,896]{1,0:T(8,128)(2,1)} %bitcast.52), custom_call_target="tpu_custom_call" | custom-call | flops 117440512 | bytes 1277952 | tf_op jit(solution)/shard_map/combined/pallas_call | solution.py:210
  176.9 3.2 %collective-permute-done.14 = bf16[2,32,640]{2,1,0:T(8,128)(2,1)S(1)} collective-permute-done((bf16[2,32,640]{2,1,0:T(8,128)(2,1)S(1)}, bf16[2,32,640]{2,1,0:T(8,128)(2,1)S(1)}, u32[]{:S(2)}, u32[]{:S(2)}) %collective-permute-start.14) | collective-permute-done | bytes 81952 | tf_op jit(solution)/shard_map/ppermute | solution.py:71
  180.0 0.1 slice_reduce_fusion.1
  180.1 0.3 slice_reduce_fusion
  180.5 0.1 multiply_reduce_fusion
  180.7 0.7 divide_convert_fusion
  181.4 32.0 %all-to-all-done.3 = bf16[64,2,8,896]{3,2,1,0:T(8,128)(2,1)S(1)} async-done(((bf16[64,2,8,896]{3,2,1,0:T(8,128)(2,1)}), bf16[64,2,8,896]{3,2,1,0:T(8,128)(2,1)S(1)}, u32[]{:S(2)}, u32[]{:S(2)}) %all-to-all-start.3) | async-done | bytes 1835040 | tf_op jit(solution)/shard_map/all_to_all | solution.py:408
  213.4 1.2 fusion.1
  (53 shorter events, 0.6 us)
Async XLA Ops:
  0.6 164.5 %copy-start = (bf16[2,128,576]{1,2,0:T(8,128)(2,1)S(1)}, bf16[2,128,576]{1,2,0:T(8,128)(2,1)}, u32[]{:S(2)}) copy-start(bf16[2,128,576]{1,2,0:T(8,128)(2,1)} %param.8) | copy-start | bytes 884740
  0.6 21.0 %copy-start.1 = (bf16[1,896,1024]{2,1,0:T(8,128)(2,1)S(1)}, bf16[1,896,1024]{2,1,0:T(8,128)(2,1)}, u32[]{:S(2)}) copy-start(bf16[1,896,1024]{2,1,0:T(8,128)(2,1)} %param.14) | copy-start | bytes 5505028
  3.2 43.3 %all-to-all-start = ((bf16[64,8,896]{2,1,0:T(8,128)(2,1)}), bf16[64,8,896]{2,1,0:T(8,128)(2,1)S(1)}, u32[]{:S(2)}, u32[]{:S(2)}) async-start(bf16[64,8,896]{2,1,0:T(8,128)(2,1)} %get-tuple-element.25), calls=%async_computation | async-start | bytes 1835008 | tf_op jit(solution)/shard_map/all_to_all | solution.py:408
  19.6 9.0 %collective-permute-start = (bf16[128,896]{1,0:T(8,128)(2,1)}, bf16[128,896]{1,0:T(8,128)(2,1)}, u32[]{:S(2)}, u32[]{:S(2)}) collective-permute-start(bf16[128,896]{1,0:T(8,128)(2,1)} %rows_ref.1), channel_id=1, source_target_pairs={{0,256},{256,0},{1,257},{257,1},{2,258},{258,2},{3,259},{259,3},{4... | collective-permute-start | bytes 688136 | tf_op jit(solution)/shard_map/ppermute | solution.py:71
  21.7 3.0 %copy-start.9 = (f32[128,8]{0,1:T(8,128)S(1)}, f32[128,8]{0,1:T(8,128)}, u32[]{:S(2)}) copy-start(f32[128,8]{0,1:T(8,128)} %param.13) | copy-start | bytes 12292
  21.7 3.0 %copy-start.10 = (s32[128,8]{0,1:T(8,128)S(1)}, s32[128,8]{0,1:T(8,128)}, u32[]{:S(2)}) copy-start(s32[128,8]{0,1:T(8,128)} %param.12) | copy-start | bytes 12292
  21.7 3.3 %copy-start.8 = (f32[64,128]{1,0:T(8,128)S(1)}, f32[64,128]{1,0:T(8,128)}, u32[]{:S(2)}) copy-start(f32[64,128]{1,0:T(8,128)} %get-tuple-element.22) | copy-start | bytes 98308
  46.6 54.6 %all-to-all-start.1 = ((bf16[64,8,1792]{2,1,0:T(8,128)(2,1)}), bf16[64,8,1792]{2,1,0:T(8,128)(2,1)}, u32[]{:S(2)}, u32[]{:S(2)}) async-start(bf16[64,8,1792]{2,1,0:T(8,128)(2,1)} %fusion), calls=%async_computation.1 | async-start | bytes 3670016 | tf_op jit(solution)/shard_map/all_to_all | solution.py:408
  54.3 4.3 %collective-permute-start.1 = (bf16[256,1024]{1,0:T(8,128)(2,1)S(1)}, bf16[256,1024]{1,0:T(8,128)(2,1)S(1)}, u32[]{:S(2)}, u32[]{:S(2)}) collective-permute-start(bf16[256,1024]{1,0:T(8,128)(2,1)S(1)} %their_half.1), channel_id=1, source_target_pairs={{0,256},{256,0},{1,257},{257,1},{2,258},{258,2},{3,259},{259,3},{4... | collective-permute-start | bytes 1572872 | tf_op jit(solution)/shard_map/ppermute | solution.py:71
  56.2 45.0 %collective-permute-start.6 = (bf16[896,1024]{1,0:T(8,128)(2,1)}, bf16[896,1024]{1,0:T(8,128)(2,1)}, u32[]{:S(2)}, u32[]{:S(2)}) collective-permute-start(bf16[896,1024]{1,0:T(8,128)(2,1)} %copied.1), channel_id=1, source_target_pairs={{0,256},{256,0},{1,257},{257,1},{2,258},{258,2},{3,259},{259,3},{4... | collective-permute-start | bytes 5505032 | tf_op jit(solution)/shard_map/ppermute | solution.py:71
  59.9 33.0 %copy-start.2 = (bf16[1,1024,896]{2,1,0:T(8,128)(2,1)S(1)}, bf16[1,1024,896]{2,1,0:T(8,128)(2,1)}, u32[]{:S(2)}) copy-start(bf16[1,1024,896]{2,1,0:T(8,128)(2,1)} %weight_ref.5) | copy-start | bytes 5505028
  59.9 18.4 %collective-permute-start.4 = (bf16[256,1024]{1,0:T(8,128)(2,1)S(1)}, bf16[256,1024]{1,0:T(8,128)(2,1)S(1)}, u32[]{:S(2)}, u32[]{:S(2)}) collective-permute-start(bf16[256,1024]{1,0:T(8,128)(2,1)S(1)} %get-tuple-element.29), channel_id=1, source_target_pairs={{0,2},{1,3},{2,0},{3,1},{4,6},{5,7},{6,4},{7,5},{8,10},{9,11},{10,... | collective-permute-start | bytes 1572872 | tf_op jit(solution)/shard_map/ppermute | solution.py:71
  65.0 23.5 %collective-permute-start.3 = (bf16[256,1024]{1,0:T(8,128)(2,1)S(1)}, bf16[256,1024]{1,0:T(8,128)(2,1)S(1)}, u32[]{:S(2)}, u32[]{:S(2)}) collective-permute-start(bf16[256,1024]{1,0:T(8,128)(2,1)S(1)} %get-tuple-element.29), channel_id=1, source_target_pairs={{0,1},{1,2},{2,3},{3,0},{4,5},{5,6},{6,7},{7,4},{8,9},{9,10},{10,1... | collective-permute-start | bytes 1572872 | tf_op jit(solution)/shard_map/ppermute | solution.py:71
  67.5 21.2 %collective-permute-start.2 = (bf16[256,1024]{1,0:T(8,128)(2,1)S(1)}, bf16[256,1024]{1,0:T(8,128)(2,1)S(1)}, u32[]{:S(2)}, u32[]{:S(2)}) collective-permute-start(bf16[256,1024]{1,0:T(8,128)(2,1)S(1)} %get-tuple-element.29), channel_id=1, source_target_pairs={{0,3},{1,0},{2,1},{3,2},{4,7},{5,4},{6,5},{7,6},{8,11},{9,8},{10,9... | collective-permute-start | bytes 1572872 | tf_op jit(solution)/shard_map/ppermute | solution.py:71
  89.1 3.8 %collective-permute-start.5 = (bf16[256,1024]{1,0:T(8,128)(2,1)S(1)}, bf16[256,1024]{1,0:T(8,128)(2,1)S(1)}, u32[]{:S(2)}, u32[]{:S(2)}) collective-permute-start(bf16[256,1024]{1,0:T(8,128)(2,1)S(1)} %multiply_convert_fusion.mine_ref), channel_id=1, source_target_pairs={{0,256},{256,0},{1,257},{257,1},{2,258},{258,2},{3,259},{259,3},{4... | collective-permute-start | bytes 1572872 | tf_op jit(solution)/shard_map/ppermute | solution.py:71
  106.8 18.2 %collective-permute-start.9 = (bf16[128,1024]{1,0:T(8,128)(2,1)}, bf16[128,1024]{1,0:T(8,128)(2,1)S(1)}, u32[]{:S(2)}, u32[]{:S(2)}) collective-permute-start(bf16[128,1024]{1,0:T(8,128)(2,1)} %get-tuple-element.35), channel_id=1, source_target_pairs={{0,3},{1,0},{2,1},{3,2},{4,7},{5,4},{6,5},{7,6},{8,11},{9,8},{10,9... | collective-permute-start | bytes 786440 | tf_op jit(solution)/shard_map/ppermute | solution.py:71
  111.5 15.6 %collective-permute-start.8 = (bf16[128,1024]{1,0:T(8,128)(2,1)S(1)}, bf16[128,1024]{1,0:T(8,128)(2,1)S(1)}, u32[]{:S(2)}, u32[]{:S(2)}) collective-permute-start(bf16[128,1024]{1,0:T(8,128)(2,1)S(1)} %get-tuple-element.34), channel_id=1, source_target_pairs={{0,1},{1,2},{2,3},{3,0},{4,5},{5,6},{6,7},{7,4},{8,9},{9,10},{10,1... | collective-permute-start | bytes 786440 | tf_op jit(solution)/shard_map/ppermute | solution.py:71
  113.4 13.6 %collective-permute-start.7 = (bf16[128,1024]{1,0:T(8,128)(2,1)S(1)}, bf16[128,1024]{1,0:T(8,128)(2,1)S(1)}, u32[]{:S(2)}, u32[]{:S(2)}) collective-permute-start(bf16[128,1024]{1,0:T(8,128)(2,1)S(1)} %get-tuple-element.33), channel_id=1, source_target_pairs={{0,2},{1,3},{2,0},{3,1},{4,6},{5,7},{6,4},{7,5},{8,10},{9,11},{10,... | collective-permute-start | bytes 786440 | tf_op jit(solution)/shard_map/ppermute | solution.py:71
  117.6 34.0 %all-to-all-start.2 = ((bf16[64,8,896]{2,1,0:T(8,128)(2,1)}), bf16[64,8,896]{2,1,0:T(8,128)(2,1)S(1)}, u32[]{:S(2)}, u32[]{:S(2)}) async-start(bf16[64,8,896]{2,1,0:T(8,128)(2,1)} %bitcast.13), calls=%async_computation.2 | async-start | bytes 1835008 | tf_op jit(solution)/shard_map/all_to_all | solution.py:408
  127.1 18.6 %copy-start.3 = (bf16[1,1024,896]{2,1,0:T(8,128)(2,1)S(1)}, bf16[1,1024,896]{2,1,0:T(8,128)(2,1)}, u32[]{:S(2)}) copy-start(bf16[1,1024,896]{2,1,0:T(8,128)(2,1)} %weight_ref.5) | copy-start | bytes 5505028
  127.3 11.2 %collective-permute-start.12 = (bf16[128,1024]{1,0:T(8,128)(2,1)S(1)}, bf16[128,1024]{1,0:T(8,128)(2,1)S(1)}, u32[]{:S(2)}, u32[]{:S(2)}) collective-permute-start(bf16[128,1024]{1,0:T(8,128)(2,1)S(1)} %multiply_convert_fusion.1), channel_id=1, source_target_pairs={{0,2},{1,3},{2,0},{3,1},{4,6},{5,7},{6,4},{7,5},{8,10},{9,11},{10,... | collective-permute-start | bytes 786440 | tf_op jit(solution)/shard_map/ppermute | solution.py:71
  129.9 9.8 %collective-permute-start.11 = (bf16[128,1024]{1,0:T(8,128)(2,1)S(1)}, bf16[128,1024]{1,0:T(8,128)(2,1)S(1)}, u32[]{:S(2)}, u32[]{:S(2)}) collective-permute-start(bf16[128,1024]{1,0:T(8,128)(2,1)S(1)} %multiply_convert_fusion.1), channel_id=1, source_target_pairs={{0,3},{1,0},{2,1},{3,2},{4,7},{5,4},{6,5},{7,6},{8,11},{9,8},{10,9... | collective-permute-start | bytes 786440 | tf_op jit(solution)/shard_map/ppermute | solution.py:71
  133.7 9.8 %collective-permute-start.10 = (bf16[128,1024]{1,0:T(8,128)(2,1)S(1)}, bf16[128,1024]{1,0:T(8,128)(2,1)S(1)}, u32[]{:S(2)}, u32[]{:S(2)}) collective-permute-start(bf16[128,1024]{1,0:T(8,128)(2,1)S(1)} %multiply_convert_fusion.1), channel_id=1, source_target_pairs={{0,1},{1,2},{2,3},{3,0},{4,5},{5,6},{6,7},{7,4},{8,9},{9,10},{10,1... | collective-permute-start | bytes 786440 | tf_op jit(solution)/shard_map/ppermute | solution.py:71
  143.6 5.1 %collective-permute-start.13 = (bf16[512,1024]{1,0:T(8,128)(2,1)S(1)}, bf16[512,1024]{1,0:T(8,128)(2,1)S(1)}, u32[]{:S(2)}, u32[]{:S(2)}) collective-permute-start(bf16[512,1024]{1,0:T(8,128)(2,1)S(1)} %pad_maximum_fusion.rows_ref), channel_id=1, source_target_pairs={{0,256},{256,0},{1,257},{257,1},{2,258},{258,2},{3,259},{259,3},{4... | collective-permute-start | bytes 3145736 | tf_op jit(solution)/shard_map/ppermute | solution.py:71
  151.6 13.4 %copy-start.11 = (s32[2]{0:T(128)S(1)}, s32[2]{0:T(128)}, u32[]{:S(2)}) copy-start(s32[2]{0:T(128)} %param.10) | copy-start | bytes 28
  151.6 13.5 %copy-start.5 = (bf16[2,256,576]{1,2,0:T(8,128)(2,1)S(1)}, bf16[2,256,576]{1,2,0:T(8,128)(2,1)}, u32[]{:S(2)}) copy-start(bf16[2,256,576]{1,2,0:T(8,128)(2,1)} %param.9) | copy-start | bytes 1769476
  151.6 0.9 copy-start.4
  152.6 60.8 %all-to-all-start.3 = ((bf16[64,2,8,896]{3,2,1,0:T(8,128)(2,1)}), bf16[64,2,8,896]{3,2,1,0:T(8,128)(2,1)S(1)}, u32[]{:S(2)}, u32[]{:S(2)}) async-start(bf16[64,2,8,896]{3,2,1,0:T(8,128)(2,1)} %down_half.3), calls=%async_computation.3 | async-start | bytes 3670016 | tf_op jit(solution)/shard_map/all_to_all | solution.py:408
  166.3 10.5 %collective-permute-start.16 = (bf16[2,32,640]{2,1,0:T(8,128)(2,1)S(1)}, bf16[2,32,640]{2,1,0:T(8,128)(2,1)S(1)}, u32[]{:S(2)}, u32[]{:S(2)}) collective-permute-start(bf16[2,32,640]{2,1,0:T(8,128)(2,1)S(1)} %get-tuple-element.48), channel_id=1, source_target_pairs={{0,3},{1,0},{2,1},{3,2},{4,7},{5,4},{6,5},{7,6},{8,11},{9,8},{10,9... | collective-permute-start | bytes 245768 | tf_op jit(solution)/shard_map/ppermute | solution.py:71
  168.3 8.6 %collective-permute-start.15 = (bf16[2,32,640]{2,1,0:T(8,128)(2,1)S(1)}, bf16[2,32,640]{2,1,0:T(8,128)(2,1)S(1)}, u32[]{:S(2)}, u32[]{:S(2)}) collective-permute-start(bf16[2,32,640]{2,1,0:T(8,128)(2,1)S(1)} %get-tuple-element.49), channel_id=1, source_target_pairs={{0,1},{1,2},{2,3},{3,0},{4,5},{5,6},{6,7},{7,4},{8,9},{9,10},{10,1... | collective-permute-start | bytes 245768 | tf_op jit(solution)/shard_map/ppermute | solution.py:71
  172.2 7.8 %collective-permute-start.14 = (bf16[2,32,640]{2,1,0:T(8,128)(2,1)S(1)}, bf16[2,32,640]{2,1,0:T(8,128)(2,1)S(1)}, u32[]{:S(2)}, u32[]{:S(2)}) collective-permute-start(bf16[2,32,640]{2,1,0:T(8,128)(2,1)S(1)} %get-tuple-element.50), channel_id=1, source_target_pairs={{0,2},{1,3},{2,0},{3,1},{4,6},{5,7},{6,4},{7,5},{8,10},{9,11},{10,... | collective-permute-start | bytes 245768 | tf_op jit(solution)/shard_map/ppermute | solution.py:71
  174.5 39.0 %copy-start.7 = (bf16[128,1024]{0,1:T(8,128)(2,1)S(1)}, bf16[128,1024]{0,1:T(8,128)(2,1)}, u32[]{:S(2)}) copy-start(bf16[128,1024]{0,1:T(8,128)(2,1)} %fusion.4) | copy-start | bytes 786436
  176.9 36.6 %copy-start.6 = (f32[128,896]{1,0:T(8,128)S(1)}, f32[128,896]{1,0:T(8,128)}, u32[]{:S(2)}) copy-start(f32[128,896]{1,0:T(8,128)} %combined.1) | copy-start | bytes 1376260

commit v9 on v8

--- a/solution.py
+++ b/solution.py
@@ -83,7 +83,7 @@
     top, rows = ids_ref.shape
     experts, slots, columns = out_ref.shape
     named = jnp.zeros((experts, rows), jnp.float32)
-    numbers = lax.broadcasted_iota(jnp.int32, (experts, rows), 0)
+    numbers = lax.broadcasted_iota(jnp.int32, (experts, rows), 0) + pl.program_id(0) * experts
     for k in range(top):
         named = jnp.where(ids_ref[k : k + 1, :] == numbers, 1.0, named)
     above = lax.broadcasted_iota(jnp.int32, (rows, rows), 0)
@@ -105,11 +105,22 @@
 
 def first_selection(ids, rows_in):
     rows, columns = rows_in.shape
+    top = ids.shape[1]
+    together = EXPERTS // 4
     return pl.pallas_call(
         select_kernel,
         out_shape=[
             jax.ShapeDtypeStruct((EXPERTS, rows), jnp.float32),
             jax.ShapeDtypeStruct((EXPERTS, FIRST, columns), jnp.bfloat16),
+        ],
+        grid=(EXPERTS // together,),
+        in_specs=[
+            pl.BlockSpec((top, rows), lambda i: (0, 0)),
+            pl.BlockSpec((rows, columns), lambda i: (0, 0)),
+        ],
+        out_specs=[
+            pl.BlockSpec((together, rows), lambda i: (i, 0)),
+            pl.BlockSpec((together, FIRST, columns), lambda i: (i, 0, 0)),
         ],
         compiler_params=pltpu.CompilerParams(vmem_limit_bytes=MOST),
         cost_estimate=cost(EXPERTS * FIRST, rows, columns),
@@ -377,7 +388,7 @@
 def wide_rows(where, rows_in, up, other_up, down, sources):
     size = lax.axis_size("tp")
     own, *pieces = wide_product(where, rows_in, up, other_up, size)
-    for step in (2, 1, 3):
+    for step in (3, 1, 2):
         own = own + turned(pieces[step - 1], "tp", step).astype(jnp.float32)
     mine = jax.nn.silu(own).astype(jnp.bfloat16)
     others = {step: turned(mine, "tp", step) for step in (3, 1, 2)}

time: 216 us -> 215 us (level)
  no operation moved by 1% of the time
where the time goes in v9:
time: 215 us; the launch traced here: 214 us
  starting transfers between devices  91.2 us (42%)
  waiting for transfers between devices  84 us (39%)
  Pallas kernels  25.3 us (12%)
  matrix products  4.85 us (2%)
  other arithmetic  4.23 us (2%)
  local copies, waits for them, and re-layouts  3.41 us (2%)
    all_to_all x4, waiting for transfers between devices, exchanged(): return lax.all_to_all(value, 'grp', split_axis=0, concat_axis=0, tiled=True)  54.4 us
    ppermute x17, starting transfers between devices, turned(): lax.ppermute(value, axis, [(k, (k + step) % size) for k in range(size)])  50.2 us
    all_to_all x4, starting transfers between devices, exchanged(): return lax.all_to_all(value, 'grp', split_axis=0, concat_axis=0, tiled=True)  41 us
    ppermute x17, waiting for transfers between devices, turned(): lax.ppermute(value, axis, [(k, (k + step) % size) for k in range(size)])  29.6 us
    pallas_call x2, Pallas kernels, down_half(): pl.pallas_call(down_half_kernel, out_shape=jax.ShapeDtypeStruct((sources,...  5.92 us
    pallas_call x1, Pallas kernels, wide_product(): pl.pallas_call(wide_kernel, out_shape=[jax.ShapeDtypeStruct((share, colum...  5.1 us
  transfers between devices with their start and end apart: 21, of which 12 were waited for; matrix products, arithmetic and copies ran while one was open for 5% of the time, Pallas kernels for 8%

profile of v9, /device:TPU:24, one launch (start us, length us, event | category | flops | bytes accessed | tf_op | source)
XLA Modules:
  0.0 214.1 jit_solution(728721534581236767)
XLA Ops:
  0.7 3.6 %first_selection.1 = (f32[64,128]{1,0:T(8,128)}, bf16[64,8,896]{2,1,0:T(8,128)(2,1)}) custom-call(s32[8,128]{1,0:T(8,128)} %bitcast.61, bf16[128,896]{1,0:T(8,128)(2,1)} %rows_ref.1), custom_call_target="tpu_custom_call" | custom-call | flops 117440512 | bytes 1277952 | tf_op jit(solution)/shard_map/first_selection/pallas_call | solution.py:110
  4.2 16.4 %all-to-all-start = ((bf16[64,8,896]{2,1,0:T(8,128)(2,1)}), bf16[64,8,896]{2,1,0:T(8,128)(2,1)S(1)}, u32[]{:S(2)}, u32[]{:S(2)}) async-start(bf16[64,8,896]{2,1,0:T(8,128)(2,1)} %get-tuple-element.25), calls=%async_computation | async-start | bytes 1835008 | tf_op jit(solution)/shard_map/all_to_all | solution.py:419
  20.6 1.9 collective-permute-start
  22.6 0.1 eq.81
  22.7 3.0 %copied.1 = bf16[896,1024]{1,0:T(8,128)(2,1)} custom-call(bf16[896,1024]{1,0:T(8,128)(2,1)S(1)} %bitcast.45), custom_call_target="tpu_custom_call" | custom-call | bytes 3670016 | tf_op jit(solution)/shard_map/copied/pallas_call | solution.py:237
  25.7 0.1 select_reduce_fusion
  25.8 0.1 copy.40
  26.0 0.7 broadcast_bitcast_fusion.1
  26.7 1.1 copy.39
  27.8 0.1 eq.87
  27.9 0.1 eq.96
  28.0 0.9 fusion.4
  28.9 0.7 select_convert_fusion.weights_ref
  29.6 3.0 %fusion = bf16[64,8,1792]{2,1,0:T(8,128)(2,1)} fusion(bf16[128,896]{1,0:T(8,128)(2,1)} %collective-permute-done, bf16[128,896]{1,0:T(8,128)(2,1)} %rows_ref.1, f32[512]{0:T(512)S(1)} %eq.81, f32[64,128]{1,0:T(8,128)S(1)} %copy-done.8), kind=kOutput, calls=%fused_computation.1 | convolution fusion | flops 236781568 | bytes 2328576 | tf_op jit(solution)/shard_map/dot_general | solution.py:425
  32.6 14.9 %all-to-all-done = bf16[64,8,896]{2,1,0:T(8,128)(2,1)S(1)} async-done(((bf16[64,8,896]{2,1,0:T(8,128)(2,1)}), bf16[64,8,896]{2,1,0:T(8,128)(2,1)S(1)}, u32[]{:S(2)}, u32[]{:S(2)}) %all-to-all-start) | async-done | bytes 917536 | tf_op jit(solution)/shard_map/all_to_all | solution.py:419
  47.5 6.4 %all-to-all-start.1 = ((bf16[64,8,1792]{2,1,0:T(8,128)(2,1)}), bf16[64,8,1792]{2,1,0:T(8,128)(2,1)}, u32[]{:S(2)}, u32[]{:S(2)}) async-start(bf16[64,8,1792]{2,1,0:T(8,128)(2,1)} %fusion), calls=%async_computation.1 | async-start | bytes 3670016 | tf_op jit(solution)/shard_map/all_to_all | solution.py:419
  54.0 1.3 their_half.1
  55.3 1.9 collective-permute-start.1
  57.2 2.4 %collective-permute-start.6 = (bf16[896,1024]{1,0:T(8,128)(2,1)}, bf16[896,1024]{1,0:T(8,128)(2,1)}, u32[]{:S(2)}, u32[]{:S(2)}) collective-permute-start(bf16[896,1024]{1,0:T(8,128)(2,1)} %copied.1), channel_id=1, source_target_pairs={{0,256},{256,0},{1,257},{257,1},{2,258},{258,2},{3,259},{259,3},{4... | collective-permute-start | bytes 5505032 | tf_op jit(solution)/shard_map/ppermute | solution.py:71
  59.6 1.3 own_half.1
  60.9 5.1 %collective-permute-start.4 = (bf16[256,1024]{1,0:T(8,128)(2,1)S(1)}, bf16[256,1024]{1,0:T(8,128)(2,1)S(1)}, u32[]{:S(2)}, u32[]{:S(2)}) collective-permute-start(bf16[256,1024]{1,0:T(8,128)(2,1)S(1)} %get-tuple-element.29), channel_id=1, source_target_pairs={{0,2},{1,3},{2,0},{3,1},{4,6},{5,7},{6,4},{7,5},{8,10},{9,11},{10,... | collective-permute-start | bytes 1572872 | tf_op jit(solution)/shard_map/ppermute | solution.py:71
  66.0 2.5 %collective-permute-start.3 = (bf16[256,1024]{1,0:T(8,128)(2,1)S(1)}, bf16[256,1024]{1,0:T(8,128)(2,1)S(1)}, u32[]{:S(2)}, u32[]{:S(2)}) collective-permute-start(bf16[256,1024]{1,0:T(8,128)(2,1)S(1)} %get-tuple-element.29), channel_id=1, source_target_pairs={{0,1},{1,2},{2,3},{3,0},{4,5},{5,6},{6,7},{7,4},{8,9},{9,10},{10,1... | collective-permute-start | bytes 1572872 | tf_op jit(solution)/shard_map/ppermute | solution.py:71
  68.5 4.6 %collective-permute-start.2 = (bf16[256,1024]{1,0:T(8,128)(2,1)S(1)}, bf16[256,1024]{1,0:T(8,128)(2,1)S(1)}, u32[]{:S(2)}, u32[]{:S(2)}) collective-permute-start(bf16[256,1024]{1,0:T(8,128)(2,1)S(1)} %get-tuple-element.29), channel_id=1, source_target_pairs={{0,3},{1,0},{2,1},{3,2},{4,7},{5,4},{6,5},{7,6},{8,11},{9,8},{10,9... | collective-permute-start | bytes 1572872 | tf_op jit(solution)/shard_map/ppermute | solution.py:71
  73.0 6.2 %collective-permute-done.4 = bf16[256,1024]{1,0:T(8,128)(2,1)S(1)} collective-permute-done((bf16[256,1024]{1,0:T(8,128)(2,1)S(1)}, bf16[256,1024]{1,0:T(8,128)(2,1)S(1)}, u32[]{:S(2)}, u32[]{:S(2)}) %collective-permute-start.4) | collective-permute-done | bytes 524320 | tf_op jit(solution)/shard_map/ppermute | solution.py:71
  79.3 10.3 %collective-permute-done.3 = bf16[256,1024]{1,0:T(8,128)(2,1)S(1)} collective-permute-done((bf16[256,1024]{1,0:T(8,128)(2,1)S(1)}, bf16[256,1024]{1,0:T(8,128)(2,1)S(1)}, u32[]{:S(2)}, u32[]{:S(2)}) %collective-permute-start.3) | collective-permute-done | bytes 524320 | tf_op jit(solution)/shard_map/ppermute | solution.py:71
  89.5 0.1 collective-permute-done.2
  89.6 0.5 multiply_convert_fusion.mine_ref
  90.1 1.9 collective-permute-start.5
  92.0 1.9 collective-permute-done.5.theirs_ref
  93.9 2.8 %down_both.1 = bf16[512,896]{1,0:T(8,128)(2,1)} custom-call(s32[2]{0:T(128)S(1)} %pad_add_fusion.where, bf16[256,1024]{1,0:T(8,128)(2,1)S(1)} %multiply_convert_fusion.mine_ref, bf16[256,1024]{1,0:T(8,128)(2,1)S(1)} %collective-permute-done.5.theirs_ref, bf16[1,1024,896]{2,1,0:T(8,128)(2,1)S(1)} %copy-done.2), custom_call_target="tpu_custom_call" | custom-call | flops 939524096 | bytes 3801088 | tf_op jit(solution)/shard_map/down_both/pallas_call | solution.py:268
  96.7 5.5 %all-to-all-done.1 = bf16[64,8,1792]{2,1,0:T(8,128)(2,1)} async-done(((bf16[64,8,1792]{2,1,0:T(8,128)(2,1)}), bf16[64,8,1792]{2,1,0:T(8,128)(2,1)}, u32[]{:S(2)}, u32[]{:S(2)}) %all-to-all-start.1) | async-done | bytes 1835040 | tf_op jit(solution)/shard_map/all_to_all | solution.py:419
  102.2 5.1 %wide_product.1 = (f32[128,1024]{1,0:T(8,128)S(1)}, bf16[128,1024]{1,0:T(8,128)(2,1)S(1)}, bf16[128,1024]{1,0:T(8,128)(2,1)}, bf16[128,1024]{1,0:T(8,128)(2,1)S(1)}) custom-call(s32[2]{0:T(128)S(1)} %pad_add_fusion.where, bf16[512,1792]{1,0:T(8,128)(2,1)} %bitcast.12.rows_ref, bf16[896,1024]{1,0:T(8,128)(2,1)S(1)} %bitcast.48, ...), custom_call_target="tpu_custom_call" | custom-call | flops 1879048192 | bytes 6553600 | tf_op jit(solution)/shard_map/wide_product/pallas_call | solution.py:306
  107.3 4.8 %collective-permute-start.9 = (bf16[128,1024]{1,0:T(8,128)(2,1)}, bf16[128,1024]{1,0:T(8,128)(2,1)S(1)}, u32[]{:S(2)}, u32[]{:S(2)}) collective-permute-start(bf16[128,1024]{1,0:T(8,128)(2,1)} %get-tuple-element.35), channel_id=1, source_target_pairs={{0,2},{1,3},{2,0},{3,1},{4,6},{5,7},{6,4},{7,5},{8,10},{9,11},{10,... | collective-permute-start | bytes 786440 | tf_op jit(solution)/shard_map/ppermute | solution.py:71
  112.2 2.5 %collective-permute-start.8 = (bf16[128,1024]{1,0:T(8,128)(2,1)S(1)}, bf16[128,1024]{1,0:T(8,128)(2,1)S(1)}, u32[]{:S(2)}, u32[]{:S(2)}) collective-permute-start(bf16[128,1024]{1,0:T(8,128)(2,1)S(1)} %get-tuple-element.34), channel_id=1, source_target_pairs={{0,1},{1,2},{2,3},{3,0},{4,5},{5,6},{6,7},{7,4},{8,9},{9,10},{10,1... | collective-permute-start | bytes 786440 | tf_op jit(solution)/shard_map/ppermute | solution.py:71
  114.7 4.5 %collective-permute-start.7 = (bf16[128,1024]{1,0:T(8,128)(2,1)S(1)}, bf16[128,1024]{1,0:T(8,128)(2,1)S(1)}, u32[]{:S(2)}, u32[]{:S(2)}) collective-permute-start(bf16[128,1024]{1,0:T(8,128)(2,1)S(1)} %get-tuple-element.33), channel_id=1, source_target_pairs={{0,3},{1,0},{2,1},{3,2},{4,7},{5,4},{6,5},{7,6},{8,11},{9,8},{10,9... | collective-permute-start | bytes 786440 | tf_op jit(solution)/shard_map/ppermute | solution.py:71
  119.3 7.4 %all-to-all-start.2 = ((bf16[64,8,896]{2,1,0:T(8,128)(2,1)}), bf16[64,8,896]{2,1,0:T(8,128)(2,1)S(1)}, u32[]{:S(2)}, u32[]{:S(2)}) async-start(bf16[64,8,896]{2,1,0:T(8,128)(2,1)} %bitcast.13), calls=%async_computation.2 | async-start | bytes 1835008 | tf_op jit(solution)/shard_map/all_to_all | solution.py:419
  126.7 0.2 multiply_convert_fusion.1
  127.0 2.1 collective-permute-start.12
  129.0 4.0 %collective-permute-start.11 = (bf16[128,1024]{1,0:T(8,128)(2,1)S(1)}, bf16[128,1024]{1,0:T(8,128)(2,1)S(1)}, u32[]{:S(2)}, u32[]{:S(2)}) collective-permute-start(bf16[128,1024]{1,0:T(8,128)(2,1)S(1)} %multiply_convert_fusion.1), channel_id=1, source_target_pairs={{0,3},{1,0},{2,1},{3,2},{4,7},{5,4},{6,5},{7,6},{8,11},{9,8},{10,9... | collective-permute-start | bytes 786440 | tf_op jit(solution)/shard_map/ppermute | solution.py:71
  133.0 1.9 collective-permute-start.10
  134.9 2.5 %collective-permute-done.12 = bf16[128,1024]{1,0:T(8,128)(2,1)S(1)} collective-permute-done((bf16[128,1024]{1,0:T(8,128)(2,1)S(1)}, bf16[128,1024]{1,0:T(8,128)(2,1)S(1)}, u32[]{:S(2)}, u32[]{:S(2)}) %collective-permute-start.12) | collective-permute-done | bytes 262176 | tf_op jit(solution)/shard_map/ppermute | solution.py:71
  137.4 3.0 %collective-permute-done.11 = bf16[128,1024]{1,0:T(8,128)(2,1)S(1)} collective-permute-done((bf16[128,1024]{1,0:T(8,128)(2,1)S(1)}, bf16[128,1024]{1,0:T(8,128)(2,1)S(1)}, u32[]{:S(2)}, u32[]{:S(2)}) %collective-permute-start.11) | collective-permute-done | bytes 262176 | tf_op jit(solution)/shard_map/ppermute | solution.py:71
  140.4 2.4 %collective-permute-done.10 = bf16[128,1024]{1,0:T(8,128)(2,1)S(1)} collective-permute-done((bf16[128,1024]{1,0:T(8,128)(2,1)S(1)}, bf16[128,1024]{1,0:T(8,128)(2,1)S(1)}, u32[]{:S(2)}, u32[]{:S(2)}) %collective-permute-start.10) | collective-permute-done | bytes 262176 | tf_op jit(solution)/shard_map/ppermute | solution.py:71
  142.8 2.1 collective-permute-start.13
  145.0 3.0 %down_half.2.rest_0_ = bf16[64,2,8,896]{3,2,1,0:T(8,128)(2,1)} custom-call(s32[2]{0:T(128)S(1)} %pad_add_fusion.where, bf16[512,1024]{1,0:T(8,128)(2,1)S(1)} %pad_maximum_fusion.rows_ref, bf16[1,1024,896]{2,1,0:T(8,128)(2,1)S(1)} %copy-done.3), custom_call_target="tpu_custom_call" | custom-call | flops 939524096 | bytes 3801088 | tf_op jit(solution)/shard_map/down_half/pallas_call | solution.py:362
  147.9 2.9 %down_half.3 = bf16[64,2,8,896]{3,2,1,0:T(8,128)(2,1)} custom-call(s32[2]{0:T(128)S(1)} %pad_add_fusion.where, bf16[512,1024]{1,0:T(8,128)(2,1)S(1)} %collective-permute-done.13.rows_ref, bf16[1,1024,896]{2,1,0:T(8,128)(2,1)S(1)} %copy-done.3, bf16[64,2,8,896]{3,2,1,0:T(8,128)(2,1)} %down_half.2.rest_0_), custom_call_target="tpu_custom_call", output_to_operand_aliasing={{}: (3, {})} | custom-call | flops 939524096 | bytes 3801088 | tf_op jit(solution)/shard_map/down_half/pallas_call | solution.py:362
  150.9 1.9 all-to-all-done.2
  152.8 0.9 copy-done.4
  153.7 10.8 %all-to-all-start.3 = ((bf16[64,2,8,896]{3,2,1,0:T(8,128)(2,1)}), bf16[64,2,8,896]{3,2,1,0:T(8,128)(2,1)S(1)}, u32[]{:S(2)}, u32[]{:S(2)}) async-start(bf16[64,2,8,896]{3,2,1,0:T(8,128)(2,1)} %down_half.3), calls=%async_computation.3 | async-start | bytes 3670016 | tf_op jit(solution)/shard_map/all_to_all | solution.py:419
  164.7 0.4 fusion.23
  165.1 0.2 fusion.10
  165.3 0.1 copy.42
  165.5 0.3 convolution_convert_fusion.1
  165.9 2.5 %collective-permute-start.16 = (bf16[2,32,640]{2,1,0:T(8,128)(2,1)S(1)}, bf16[2,32,640]{2,1,0:T(8,128)(2,1)S(1)}, u32[]{:S(2)}, u32[]{:S(2)}) collective-permute-start(bf16[2,32,640]{2,1,0:T(8,128)(2,1)S(1)} %get-tuple-element.48), channel_id=1, source_target_pairs={{0,3},{1,0},{2,1},{3,2},{4,7},{5,4},{6,5},{7,6},{8,11},{9,8},{10,9... | collective-permute-start | bytes 245768 | tf_op jit(solution)/shard_map/ppermute | solution.py:71
  168.4 3.4 %collective-permute-start.15 = (bf16[2,32,640]{2,1,0:T(8,128)(2,1)S(1)}, bf16[2,32,640]{2,1,0:T(8,128)(2,1)S(1)}, u32[]{:S(2)}, u32[]{:S(2)}) collective-permute-start(bf16[2,32,640]{2,1,0:T(8,128)(2,1)S(1)} %get-tuple-element.49), channel_id=1, source_target_pairs={{0,1},{1,2},{2,3},{3,0},{4,5},{5,6},{6,7},{7,4},{8,9},{9,10},{10,1... | collective-permute-start | bytes 245768 | tf_op jit(solution)/shard_map/ppermute | solution.py:71
  171.7 2.2 %collective-permute-start.14 = (bf16[2,32,640]{2,1,0:T(8,128)(2,1)S(1)}, bf16[2,32,640]{2,1,0:T(8,128)(2,1)S(1)}, u32[]{:S(2)}, u32[]{:S(2)}) collective-permute-start(bf16[2,32,640]{2,1,0:T(8,128)(2,1)S(1)} %get-tuple-element.50), channel_id=1, source_target_pairs={{0,2},{1,3},{2,0},{3,1},{4,6},{5,7},{6,4},{7,5},{8,10},{9,11},{10,... | collective-permute-start | bytes 245768 | tf_op jit(solution)/shard_map/ppermute | solution.py:71
  174.0 2.4 %combined.1 = f32[128,896]{1,0:T(8,128)} custom-call(bf16[128,512]{1,0:T(8,128)(2,1)} %select_convert_fusion.weights_ref, bf16[512,896]{1,0:T(8,128)(2,1)} %bitcast.52), custom_call_target="tpu_custom_call" | custom-call | flops 117440512 | bytes 1277952 | tf_op jit(solution)/shard_map/combined/pallas_call | solution.py:221
  176.4 3.2 %collective-permute-done.14 = bf16[2,32,640]{2,1,0:T(8,128)(2,1)S(1)} collective-permute-done((bf16[2,32,640]{2,1,0:T(8,128)(2,1)S(1)}, bf16[2,32,640]{2,1,0:T(8,128)(2,1)S(1)}, u32[]{:S(2)}, u32[]{:S(2)}) %collective-permute-start.14) | collective-permute-done | bytes 81952 | tf_op jit(solution)/shard_map/ppermute | solution.py:71
  179.6 0.1 slice_reduce_fusion.1
  179.7 0.3 slice_reduce_fusion
  180.1 0.1 multiply_reduce_fusion
  180.2 0.7 divide_convert_fusion
  180.9 32.1 %all-to-all-done.3 = bf16[64,2,8,896]{3,2,1,0:T(8,128)(2,1)S(1)} async-done(((bf16[64,2,8,896]{3,2,1,0:T(8,128)(2,1)}), bf16[64,2,8,896]{3,2,1,0:T(8,128)(2,1)S(1)}, u32[]{:S(2)}, u32[]{:S(2)}) %all-to-all-start.3) | async-done | bytes 1835040 | tf_op jit(solution)/shard_map/all_to_all | solution.py:419
  213.0 1.2 fusion.1
  (53 shorter events, 0.6 us)
Async XLA Ops:
  0.6 164.1 %copy-start = (bf16[2,128,576]{1,2,0:T(8,128)(2,1)S(1)}, bf16[2,128,576]{1,2,0:T(8,128)(2,1)}, u32[]{:S(2)}) copy-start(bf16[2,128,576]{1,2,0:T(8,128)(2,1)} %param.8) | copy-start | bytes 884740
  0.6 22.0 %copy-start.1 = (bf16[1,896,1024]{2,1,0:T(8,128)(2,1)S(1)}, bf16[1,896,1024]{2,1,0:T(8,128)(2,1)}, u32[]{:S(2)}) copy-start(bf16[1,896,1024]{2,1,0:T(8,128)(2,1)} %param.14) | copy-start | bytes 5505028
  4.2 43.3 %all-to-all-start = ((bf16[64,8,896]{2,1,0:T(8,128)(2,1)}), bf16[64,8,896]{2,1,0:T(8,128)(2,1)S(1)}, u32[]{:S(2)}, u32[]{:S(2)}) async-start(bf16[64,8,896]{2,1,0:T(8,128)(2,1)} %get-tuple-element.25), calls=%async_computation | async-start | bytes 1835008 | tf_op jit(solution)/shard_map/all_to_all | solution.py:419
  20.6 9.0 %collective-permute-start = (bf16[128,896]{1,0:T(8,128)(2,1)}, bf16[128,896]{1,0:T(8,128)(2,1)}, u32[]{:S(2)}, u32[]{:S(2)}) collective-permute-start(bf16[128,896]{1,0:T(8,128)(2,1)} %rows_ref.1), channel_id=1, source_target_pairs={{0,256},{256,0},{1,257},{257,1},{2,258},{258,2},{3,259},{259,3},{4... | collective-permute-start | bytes 688136 | tf_op jit(solution)/shard_map/ppermute | solution.py:71
  22.7 3.0 %copy-start.9 = (f32[128,8]{0,1:T(8,128)S(1)}, f32[128,8]{0,1:T(8,128)}, u32[]{:S(2)}) copy-start(f32[128,8]{0,1:T(8,128)} %param.13) | copy-start | bytes 12292
  22.7 3.0 %copy-start.10 = (s32[128,8]{0,1:T(8,128)S(1)}, s32[128,8]{0,1:T(8,128)}, u32[]{:S(2)}) copy-start(s32[128,8]{0,1:T(8,128)} %param.12) | copy-start | bytes 12292
  22.7 3.3 %copy-start.8 = (f32[64,128]{1,0:T(8,128)S(1)}, f32[64,128]{1,0:T(8,128)}, u32[]{:S(2)}) copy-start(f32[64,128]{1,0:T(8,128)} %get-tuple-element.22) | copy-start | bytes 98308
  47.5 54.7 %all-to-all-start.1 = ((bf16[64,8,1792]{2,1,0:T(8,128)(2,1)}), bf16[64,8,1792]{2,1,0:T(8,128)(2,1)}, u32[]{:S(2)}, u32[]{:S(2)}) async-start(bf16[64,8,1792]{2,1,0:T(8,128)(2,1)} %fusion), calls=%async_computation.1 | async-start | bytes 3670016 | tf_op jit(solution)/shard_map/all_to_all | solution.py:419
  55.3 4.3 %collective-permute-start.1 = (bf16[256,1024]{1,0:T(8,128)(2,1)S(1)}, bf16[256,1024]{1,0:T(8,128)(2,1)S(1)}, u32[]{:S(2)}, u32[]{:S(2)}) collective-permute-start(bf16[256,1024]{1,0:T(8,128)(2,1)S(1)} %their_half.1), channel_id=1, source_target_pairs={{0,256},{256,0},{1,257},{257,1},{2,258},{258,2},{3,259},{259,3},{4... | collective-permute-start | bytes 1572872 | tf_op jit(solution)/shard_map/ppermute | solution.py:71
  57.2 45.0 %collective-permute-start.6 = (bf16[896,1024]{1,0:T(8,128)(2,1)}, bf16[896,1024]{1,0:T(8,128)(2,1)}, u32[]{:S(2)}, u32[]{:S(2)}) collective-permute-start(bf16[896,1024]{1,0:T(8,128)(2,1)} %copied.1), channel_id=1, source_target_pairs={{0,256},{256,0},{1,257},{257,1},{2,258},{258,2},{3,259},{259,3},{4... | collective-permute-start | bytes 5505032 | tf_op jit(solution)/shard_map/ppermute | solution.py:71
  60.9 33.0 %copy-start.2 = (bf16[1,1024,896]{2,1,0:T(8,128)(2,1)S(1)}, bf16[1,1024,896]{2,1,0:T(8,128)(2,1)}, u32[]{:S(2)}) copy-start(bf16[1,1024,896]{2,1,0:T(8,128)(2,1)} %weight_ref.5) | copy-start | bytes 5505028
  60.9 18.4 %collective-permute-start.4 = (bf16[256,1024]{1,0:T(8,128)(2,1)S(1)}, bf16[256,1024]{1,0:T(8,128)(2,1)S(1)}, u32[]{:S(2)}, u32[]{:S(2)}) collective-permute-start(bf16[256,1024]{1,0:T(8,128)(2,1)S(1)} %get-tuple-element.29), channel_id=1, source_target_pairs={{0,2},{1,3},{2,0},{3,1},{4,6},{5,7},{6,4},{7,5},{8,10},{9,11},{10,... | collective-permute-start | bytes 1572872 | tf_op jit(solution)/shard_map/ppermute | solution.py:71
  66.0 23.5 %collective-permute-start.3 = (bf16[256,1024]{1,0:T(8,128)(2,1)S(1)}, bf16[256,1024]{1,0:T(8,128)(2,1)S(1)}, u32[]{:S(2)}, u32[]{:S(2)}) collective-permute-start(bf16[256,1024]{1,0:T(8,128)(2,1)S(1)} %get-tuple-element.29), channel_id=1, source_target_pairs={{0,1},{1,2},{2,3},{3,0},{4,5},{5,6},{6,7},{7,4},{8,9},{9,10},{10,1... | collective-permute-start | bytes 1572872 | tf_op jit(solution)/shard_map/ppermute | solution.py:71
  68.5 21.2 %collective-permute-start.2 = (bf16[256,1024]{1,0:T(8,128)(2,1)S(1)}, bf16[256,1024]{1,0:T(8,128)(2,1)S(1)}, u32[]{:S(2)}, u32[]{:S(2)}) collective-permute-start(bf16[256,1024]{1,0:T(8,128)(2,1)S(1)} %get-tuple-element.29), channel_id=1, source_target_pairs={{0,3},{1,0},{2,1},{3,2},{4,7},{5,4},{6,5},{7,6},{8,11},{9,8},{10,9... | collective-permute-start | bytes 1572872 | tf_op jit(solution)/shard_map/ppermute | solution.py:71
  90.1 3.8 %collective-permute-start.5 = (bf16[256,1024]{1,0:T(8,128)(2,1)S(1)}, bf16[256,1024]{1,0:T(8,128)(2,1)S(1)}, u32[]{:S(2)}, u32[]{:S(2)}) collective-permute-start(bf16[256,1024]{1,0:T(8,128)(2,1)S(1)} %multiply_convert_fusion.mine_ref), channel_id=1, source_target_pairs={{0,256},{256,0},{1,257},{257,1},{2,258},{258,2},{3,259},{259,3},{4... | collective-permute-start | bytes 1572872 | tf_op jit(solution)/shard_map/ppermute | solution.py:71
  107.3 19.3 %collective-permute-start.9 = (bf16[128,1024]{1,0:T(8,128)(2,1)}, bf16[128,1024]{1,0:T(8,128)(2,1)S(1)}, u32[]{:S(2)}, u32[]{:S(2)}) collective-permute-start(bf16[128,1024]{1,0:T(8,128)(2,1)} %get-tuple-element.35), channel_id=1, source_target_pairs={{0,2},{1,3},{2,0},{3,1},{4,6},{5,7},{6,4},{7,5},{8,10},{9,11},{10,... | collective-permute-start | bytes 786440 | tf_op jit(solution)/shard_map/ppermute | solution.py:71
  112.2 14.5 %collective-permute-start.8 = (bf16[128,1024]{1,0:T(8,128)(2,1)S(1)}, bf16[128,1024]{1,0:T(8,128)(2,1)S(1)}, u32[]{:S(2)}, u32[]{:S(2)}) collective-permute-start(bf16[128,1024]{1,0:T(8,128)(2,1)S(1)} %get-tuple-element.34), channel_id=1, source_target_pairs={{0,1},{1,2},{2,3},{3,0},{4,5},{5,6},{6,7},{7,4},{8,9},{9,10},{10,1... | collective-permute-start | bytes 786440 | tf_op jit(solution)/shard_map/ppermute | solution.py:71
  114.7 12.0 %collective-permute-start.7 = (bf16[128,1024]{1,0:T(8,128)(2,1)S(1)}, bf16[128,1024]{1,0:T(8,128)(2,1)S(1)}, u32[]{:S(2)}, u32[]{:S(2)}) collective-permute-start(bf16[128,1024]{1,0:T(8,128)(2,1)S(1)} %get-tuple-element.33), channel_id=1, source_target_pairs={{0,3},{1,0},{2,1},{3,2},{4,7},{5,4},{6,5},{7,6},{8,11},{9,8},{10,9... | collective-permute-start | bytes 786440 | tf_op jit(solution)/shard_map/ppermute | solution.py:71
  119.3 33.5 %all-to-all-start.2 = ((bf16[64,8,896]{2,1,0:T(8,128)(2,1)}), bf16[64,8,896]{2,1,0:T(8,128)(2,1)S(1)}, u32[]{:S(2)}, u32[]{:S(2)}) async-start(bf16[64,8,896]{2,1,0:T(8,128)(2,1)} %bitcast.13), calls=%async_computation.2 | async-start | bytes 1835008 | tf_op jit(solution)/shard_map/all_to_all | solution.py:419
  126.7 18.3 %copy-start.3 = (bf16[1,1024,896]{2,1,0:T(8,128)(2,1)S(1)}, bf16[1,1024,896]{2,1,0:T(8,128)(2,1)}, u32[]{:S(2)}) copy-start(bf16[1,1024,896]{2,1,0:T(8,128)(2,1)} %weight_ref.5) | copy-start | bytes 5505028
  127.0 10.5 %collective-permute-start.12 = (bf16[128,1024]{1,0:T(8,128)(2,1)S(1)}, bf16[128,1024]{1,0:T(8,128)(2,1)S(1)}, u32[]{:S(2)}, u32[]{:S(2)}) collective-permute-start(bf16[128,1024]{1,0:T(8,128)(2,1)S(1)} %multiply_convert_fusion.1), channel_id=1, source_target_pairs={{0,2},{1,3},{2,0},{3,1},{4,6},{5,7},{6,4},{7,5},{8,10},{9,11},{10,... | collective-permute-start | bytes 786440 | tf_op jit(solution)/shard_map/ppermute | solution.py:71
  129.0 11.4 %collective-permute-start.11 = (bf16[128,1024]{1,0:T(8,128)(2,1)S(1)}, bf16[128,1024]{1,0:T(8,128)(2,1)S(1)}, u32[]{:S(2)}, u32[]{:S(2)}) collective-permute-start(bf16[128,1024]{1,0:T(8,128)(2,1)S(1)} %multiply_convert_fusion.1), channel_id=1, source_target_pairs={{0,3},{1,0},{2,1},{3,2},{4,7},{5,4},{6,5},{7,6},{8,11},{9,8},{10,9... | collective-permute-start | bytes 786440 | tf_op jit(solution)/shard_map/ppermute | solution.py:71
  133.0 9.8 %collective-permute-start.10 = (bf16[128,1024]{1,0:T(8,128)(2,1)S(1)}, bf16[128,1024]{1,0:T(8,128)(2,1)S(1)}, u32[]{:S(2)}, u32[]{:S(2)}) collective-permute-start(bf16[128,1024]{1,0:T(8,128)(2,1)S(1)} %multiply_convert_fusion.1), channel_id=1, source_target_pairs={{0,1},{1,2},{2,3},{3,0},{4,5},{5,6},{6,7},{7,4},{8,9},{9,10},{10,1... | collective-permute-start | bytes 786440 | tf_op jit(solution)/shard_map/ppermute | solution.py:71
  142.8 5.1 %collective-permute-start.13 = (bf16[512,1024]{1,0:T(8,128)(2,1)S(1)}, bf16[512,1024]{1,0:T(8,128)(2,1)S(1)}, u32[]{:S(2)}, u32[]{:S(2)}) collective-permute-start(bf16[512,1024]{1,0:T(8,128)(2,1)S(1)} %pad_maximum_fusion.rows_ref), channel_id=1, source_target_pairs={{0,256},{256,0},{1,257},{257,1},{2,258},{258,2},{3,259},{259,3},{4... | collective-permute-start | bytes 3145736 | tf_op jit(solution)/shard_map/ppermute | solution.py:71
  150.9 13.7 %copy-start.11 = (s32[2]{0:T(128)S(1)}, s32[2]{0:T(128)}, u32[]{:S(2)}) copy-start(s32[2]{0:T(128)} %param.10) | copy-start | bytes 28
  150.9 13.8 %copy-start.5 = (bf16[2,256,576]{1,2,0:T(8,128)(2,1)S(1)}, bf16[2,256,576]{1,2,0:T(8,128)(2,1)}, u32[]{:S(2)}) copy-start(bf16[2,256,576]{1,2,0:T(8,128)(2,1)} %param.9) | copy-start | bytes 1769476
  152.8 0.9 copy-start.4
  153.7 59.2 %all-to-all-start.3 = ((bf16[64,2,8,896]{3,2,1,0:T(8,128)(2,1)}), bf16[64,2,8,896]{3,2,1,0:T(8,128)(2,1)S(1)}, u32[]{:S(2)}, u32[]{:S(2)}) async-start(bf16[64,2,8,896]{3,2,1,0:T(8,128)(2,1)} %down_half.3), calls=%async_computation.3 | async-start | bytes 3670016 | tf_op jit(solution)/shard_map/all_to_all | solution.py:419
  165.9 10.5 %collective-permute-start.16 = (bf16[2,32,640]{2,1,0:T(8,128)(2,1)S(1)}, bf16[2,32,640]{2,1,0:T(8,128)(2,1)S(1)}, u32[]{:S(2)}, u32[]{:S(2)}) collective-permute-start(bf16[2,32,640]{2,1,0:T(8,128)(2,1)S(1)} %get-tuple-element.48), channel_id=1, source_target_pairs={{0,3},{1,0},{2,1},{3,2},{4,7},{5,4},{6,5},{7,6},{8,11},{9,8},{10,9... | collective-permute-start | bytes 245768 | tf_op jit(solution)/shard_map/ppermute | solution.py:71
  168.4 8.0 %collective-permute-start.15 = (bf16[2,32,640]{2,1,0:T(8,128)(2,1)S(1)}, bf16[2,32,640]{2,1,0:T(8,128)(2,1)S(1)}, u32[]{:S(2)}, u32[]{:S(2)}) collective-permute-start(bf16[2,32,640]{2,1,0:T(8,128)(2,1)S(1)} %get-tuple-element.49), channel_id=1, source_target_pairs={{0,1},{1,2},{2,3},{3,0},{4,5},{5,6},{6,7},{7,4},{8,9},{9,10},{10,1... | collective-permute-start | bytes 245768 | tf_op jit(solution)/shard_map/ppermute | solution.py:71
  171.7 7.8 %collective-permute-start.14 = (bf16[2,32,640]{2,1,0:T(8,128)(2,1)S(1)}, bf16[2,32,640]{2,1,0:T(8,128)(2,1)S(1)}, u32[]{:S(2)}, u32[]{:S(2)}) collective-permute-start(bf16[2,32,640]{2,1,0:T(8,128)(2,1)S(1)} %get-tuple-element.50), channel_id=1, source_target_pairs={{0,2},{1,3},{2,0},{3,1},{4,6},{5,7},{6,4},{7,5},{8,10},{9,11},{10,... | collective-permute-start | bytes 245768 | tf_op jit(solution)/shard_map/ppermute | solution.py:71
  174.0 39.0 %copy-start.7 = (bf16[128,1024]{0,1:T(8,128)(2,1)S(1)}, bf16[128,1024]{0,1:T(8,128)(2,1)}, u32[]{:S(2)}) copy-start(bf16[128,1024]{0,1:T(8,128)(2,1)} %fusion.4) | copy-start | bytes 786436
  176.3 36.6 %copy-start.6 = (f32[128,896]{1,0:T(8,128)S(1)}, f32[128,896]{1,0:T(8,128)}, u32[]{:S(2)}) copy-start(f32[128,896]{1,0:T(8,128)} %combined.1) | copy-start | bytes 1376260

commit v10 on v8

--- a/solution.py
+++ b/solution.py
@@ -377,7 +377,7 @@
 def wide_rows(where, rows_in, up, other_up, down, sources):
     size = lax.axis_size("tp")
     own, *pieces = wide_product(where, rows_in, up, other_up, size)
-    for step in (2, 1, 3):
+    for step in (3, 1, 2):
         own = own + turned(pieces[step - 1], "tp", step).astype(jnp.float32)
     mine = jax.nn.silu(own).astype(jnp.bfloat16)
     others = {step: turned(mine, "tp", step) for step in (3, 1, 2)}

time: 216 us -> 214 us (level)
  no operation moved by 1% of the time
where the time goes in v10:
time: 214 us; the launch traced here: 213 us
  starting transfers between devices  91.3 us (43%)
  waiting for transfers between devices  83.9 us (39%)
  Pallas kernels  24.3 us (11%)
  matrix products  4.86 us (2%)
  other arithmetic  4.23 us (2%)
  local copies, waits for them, and re-layouts  3.41 us (2%)
    all_to_all x4, waiting for transfers between devices, exchanged(): return lax.all_to_all(value, 'grp', split_axis=0, concat_axis=0, tiled=True)  54.3 us
    ppermute x17, starting transfers between devices, turned(): lax.ppermute(value, axis, [(k, (k + step) % size) for k in range(size)])  50.3 us
    all_to_all x4, starting transfers between devices, exchanged(): return lax.all_to_all(value, 'grp', split_axis=0, concat_axis=0, tiled=True)  41 us
    ppermute x17, waiting for transfers between devices, turned(): lax.ppermute(value, axis, [(k, (k + step) % size) for k in range(size)])  29.6 us
    pallas_call x2, Pallas kernels, down_half(): pl.pallas_call(down_half_kernel, out_shape=jax.ShapeDtypeStruct((sources,...  5.92 us
    pallas_call x1, Pallas kernels, wide_product(): pl.pallas_call(wide_kernel, out_shape=[jax.ShapeDtypeStruct((share, colum...  5.1 us
  transfers between devices with their start and end apart: 21, of which 12 were waited for; matrix products, arithmetic and copies ran while one was open for 5% of the time, Pallas kernels for 8%

profile of v10, /device:TPU:24, one launch (start us, length us, event | category | flops | bytes accessed | tf_op | source)
XLA Modules:
  0.0 213.2 jit_solution(5016222763499273574)
XLA Ops:
  0.7 2.6 %first_selection.1 = (f32[64,128]{1,0:T(8,128)}, bf16[64,8,896]{2,1,0:T(8,128)(2,1)}) custom-call(s32[8,128]{1,0:T(8,128)} %bitcast.61, bf16[128,896]{1,0:T(8,128)(2,1)} %rows_ref.1), custom_call_target="tpu_custom_call" | custom-call | flops 117440512 | bytes 1277952 | tf_op jit(solution)/shard_map/first_selection/pallas_call | solution.py:108
  3.2 16.4 %all-to-all-start = ((bf16[64,8,896]{2,1,0:T(8,128)(2,1)}), bf16[64,8,896]{2,1,0:T(8,128)(2,1)S(1)}, u32[]{:S(2)}, u32[]{:S(2)}) async-start(bf16[64,8,896]{2,1,0:T(8,128)(2,1)} %get-tuple-element.25), calls=%async_computation | async-start | bytes 1835008 | tf_op jit(solution)/shard_map/all_to_all | solution.py:408
  19.6 1.9 collective-permute-start
  21.6 0.1 eq.81
  21.7 3.0 %copied.1 = bf16[896,1024]{1,0:T(8,128)(2,1)} custom-call(bf16[896,1024]{1,0:T(8,128)(2,1)S(1)} %bitcast.45), custom_call_target="tpu_custom_call" | custom-call | bytes 3670016 | tf_op jit(solution)/shard_map/copied/pallas_call | solution.py:226
  24.7 0.1 select_reduce_fusion
  24.8 0.1 copy.40
  25.0 0.7 broadcast_bitcast_fusion.1
  25.7 1.1 copy.39
  26.8 0.1 eq.87
  26.9 0.1 eq.96
  27.0 0.9 fusion.4
  27.9 0.7 select_convert_fusion.weights_ref
  28.6 3.0 %fusion = bf16[64,8,1792]{2,1,0:T(8,128)(2,1)} fusion(bf16[128,896]{1,0:T(8,128)(2,1)} %collective-permute-done, bf16[128,896]{1,0:T(8,128)(2,1)} %rows_ref.1, f32[512]{0:T(512)S(1)} %eq.81, f32[64,128]{1,0:T(8,128)S(1)} %copy-done.8), kind=kOutput, calls=%fused_computation.1 | convolution fusion | flops 236781568 | bytes 2328576 | tf_op jit(solution)/shard_map/dot_general | solution.py:414
  31.6 14.9 %all-to-all-done = bf16[64,8,896]{2,1,0:T(8,128)(2,1)S(1)} async-done(((bf16[64,8,896]{2,1,0:T(8,128)(2,1)}), bf16[64,8,896]{2,1,0:T(8,128)(2,1)S(1)}, u32[]{:S(2)}, u32[]{:S(2)}) %all-to-all-start) | async-done | bytes 917536 | tf_op jit(solution)/shard_map/all_to_all | solution.py:408
  46.6 6.4 %all-to-all-start.1 = ((bf16[64,8,1792]{2,1,0:T(8,128)(2,1)}), bf16[64,8,1792]{2,1,0:T(8,128)(2,1)}, u32[]{:S(2)}, u32[]{:S(2)}) async-start(bf16[64,8,1792]{2,1,0:T(8,128)(2,1)} %fusion), calls=%async_computation.1 | async-start | bytes 3670016 | tf_op jit(solution)/shard_map/all_to_all | solution.py:408
  53.0 1.3 their_half.1
  54.3 1.9 collective-permute-start.1
  56.2 2.4 %collective-permute-start.6 = (bf16[896,1024]{1,0:T(8,128)(2,1)}, bf16[896,1024]{1,0:T(8,128)(2,1)}, u32[]{:S(2)}, u32[]{:S(2)}) collective-permute-start(bf16[896,1024]{1,0:T(8,128)(2,1)} %copied.1), channel_id=1, source_target_pairs={{0,256},{256,0},{1,257},{257,1},{2,258},{258,2},{3,259},{259,3},{4... | collective-permute-start | bytes 5505032 | tf_op jit(solution)/shard_map/ppermute | solution.py:71
  58.6 1.3 own_half.1
  59.9 5.1 %collective-permute-start.4 = (bf16[256,1024]{1,0:T(8,128)(2,1)S(1)}, bf16[256,1024]{1,0:T(8,128)(2,1)S(1)}, u32[]{:S(2)}, u32[]{:S(2)}) collective-permute-start(bf16[256,1024]{1,0:T(8,128)(2,1)S(1)} %get-tuple-element.29), channel_id=1, source_target_pairs={{0,2},{1,3},{2,0},{3,1},{4,6},{5,7},{6,4},{7,5},{8,10},{9,11},{10,... | collective-permute-start | bytes 1572872 | tf_op jit(solution)/shard_map/ppermute | solution.py:71
  65.0 2.5 %collective-permute-start.3 = (bf16[256,1024]{1,0:T(8,128)(2,1)S(1)}, bf16[256,1024]{1,0:T(8,128)(2,1)S(1)}, u32[]{:S(2)}, u32[]{:S(2)}) collective-permute-start(bf16[256,1024]{1,0:T(8,128)(2,1)S(1)} %get-tuple-element.29), channel_id=1, source_target_pairs={{0,1},{1,2},{2,3},{3,0},{4,5},{5,6},{6,7},{7,4},{8,9},{9,10},{10,1... | collective-permute-start | bytes 1572872 | tf_op jit(solution)/shard_map/ppermute | solution.py:71
  67.5 4.5 %collective-permute-start.2 = (bf16[256,1024]{1,0:T(8,128)(2,1)S(1)}, bf16[256,1024]{1,0:T(8,128)(2,1)S(1)}, u32[]{:S(2)}, u32[]{:S(2)}) collective-permute-start(bf16[256,1024]{1,0:T(8,128)(2,1)S(1)} %get-tuple-element.29), channel_id=1, source_target_pairs={{0,3},{1,0},{2,1},{3,2},{4,7},{5,4},{6,5},{7,6},{8,11},{9,8},{10,9... | collective-permute-start | bytes 1572872 | tf_op jit(solution)/shard_map/ppermute | solution.py:71
  72.1 6.2 %collective-permute-done.4 = bf16[256,1024]{1,0:T(8,128)(2,1)S(1)} collective-permute-done((bf16[256,1024]{1,0:T(8,128)(2,1)S(1)}, bf16[256,1024]{1,0:T(8,128)(2,1)S(1)}, u32[]{:S(2)}, u32[]{:S(2)}) %collective-permute-start.4) | collective-permute-done | bytes 524320 | tf_op jit(solution)/shard_map/ppermute | solution.py:71
  78.3 10.2 %collective-permute-done.3 = bf16[256,1024]{1,0:T(8,128)(2,1)S(1)} collective-permute-done((bf16[256,1024]{1,0:T(8,128)(2,1)S(1)}, bf16[256,1024]{1,0:T(8,128)(2,1)S(1)}, u32[]{:S(2)}, u32[]{:S(2)}) %collective-permute-start.3) | collective-permute-done | bytes 524320 | tf_op jit(solution)/shard_map/ppermute | solution.py:71
  88.5 0.1 collective-permute-done.2
  88.7 0.5 multiply_convert_fusion.mine_ref
  89.1 1.9 collective-permute-start.5
  91.0 1.9 collective-permute-done.5.theirs_ref
  92.9 2.8 %down_both.1 = bf16[512,896]{1,0:T(8,128)(2,1)} custom-call(s32[2]{0:T(128)S(1)} %pad_add_fusion.where, bf16[256,1024]{1,0:T(8,128)(2,1)S(1)} %multiply_convert_fusion.mine_ref, bf16[256,1024]{1,0:T(8,128)(2,1)S(1)} %collective-permute-done.5.theirs_ref, bf16[1,1024,896]{2,1,0:T(8,128)(2,1)S(1)} %copy-done.2), custom_call_target="tpu_custom_call" | custom-call | flops 939524096 | bytes 3801088 | tf_op jit(solution)/shard_map/down_both/pallas_call | solution.py:257
  95.8 5.4 %all-to-all-done.1 = bf16[64,8,1792]{2,1,0:T(8,128)(2,1)} async-done(((bf16[64,8,1792]{2,1,0:T(8,128)(2,1)}), bf16[64,8,1792]{2,1,0:T(8,128)(2,1)}, u32[]{:S(2)}, u32[]{:S(2)}) %all-to-all-start.1) | async-done | bytes 1835040 | tf_op jit(solution)/shard_map/all_to_all | solution.py:408
  101.2 5.1 %wide_product.1 = (f32[128,1024]{1,0:T(8,128)S(1)}, bf16[128,1024]{1,0:T(8,128)(2,1)S(1)}, bf16[128,1024]{1,0:T(8,128)(2,1)}, bf16[128,1024]{1,0:T(8,128)(2,1)S(1)}) custom-call(s32[2]{0:T(128)S(1)} %pad_add_fusion.where, bf16[512,1792]{1,0:T(8,128)(2,1)} %bitcast.12.rows_ref, bf16[896,1024]{1,0:T(8,128)(2,1)S(1)} %bitcast.48, ...), custom_call_target="tpu_custom_call" | custom-call | flops 1879048192 | bytes 6553600 | tf_op jit(solution)/shard_map/wide_product/pallas_call | solution.py:295
  106.3 4.9 %collective-permute-start.9 = (bf16[128,1024]{1,0:T(8,128)(2,1)}, bf16[128,1024]{1,0:T(8,128)(2,1)S(1)}, u32[]{:S(2)}, u32[]{:S(2)}) collective-permute-start(bf16[128,1024]{1,0:T(8,128)(2,1)} %get-tuple-element.35), channel_id=1, source_target_pairs={{0,2},{1,3},{2,0},{3,1},{4,6},{5,7},{6,4},{7,5},{8,10},{9,11},{10,... | collective-permute-start | bytes 786440 | tf_op jit(solution)/shard_map/ppermute | solution.py:71
  111.2 2.5 %collective-permute-start.8 = (bf16[128,1024]{1,0:T(8,128)(2,1)S(1)}, bf16[128,1024]{1,0:T(8,128)(2,1)S(1)}, u32[]{:S(2)}, u32[]{:S(2)}) collective-permute-start(bf16[128,1024]{1,0:T(8,128)(2,1)S(1)} %get-tuple-element.34), channel_id=1, source_target_pairs={{0,1},{1,2},{2,3},{3,0},{4,5},{5,6},{6,7},{7,4},{8,9},{9,10},{10,1... | collective-permute-start | bytes 786440 | tf_op jit(solution)/shard_map/ppermute | solution.py:71
  113.7 4.6 %collective-permute-start.7 = (bf16[128,1024]{1,0:T(8,128)(2,1)S(1)}, bf16[128,1024]{1,0:T(8,128)(2,1)S(1)}, u32[]{:S(2)}, u32[]{:S(2)}) collective-permute-start(bf16[128,1024]{1,0:T(8,128)(2,1)S(1)} %get-tuple-element.33), channel_id=1, source_target_pairs={{0,3},{1,0},{2,1},{3,2},{4,7},{5,4},{6,5},{7,6},{8,11},{9,8},{10,9... | collective-permute-start | bytes 786440 | tf_op jit(solution)/shard_map/ppermute | solution.py:71
  118.3 7.4 %all-to-all-start.2 = ((bf16[64,8,896]{2,1,0:T(8,128)(2,1)}), bf16[64,8,896]{2,1,0:T(8,128)(2,1)S(1)}, u32[]{:S(2)}, u32[]{:S(2)}) async-start(bf16[64,8,896]{2,1,0:T(8,128)(2,1)} %bitcast.13), calls=%async_computation.2 | async-start | bytes 1835008 | tf_op jit(solution)/shard_map/all_to_all | solution.py:408
  125.7 0.2 multiply_convert_fusion.1
  126.0 2.1 collective-permute-start.12
  128.0 4.0 %collective-permute-start.11 = (bf16[128,1024]{1,0:T(8,128)(2,1)S(1)}, bf16[128,1024]{1,0:T(8,128)(2,1)S(1)}, u32[]{:S(2)}, u32[]{:S(2)}) collective-permute-start(bf16[128,1024]{1,0:T(8,128)(2,1)S(1)} %multiply_convert_fusion.1), channel_id=1, source_target_pairs={{0,3},{1,0},{2,1},{3,2},{4,7},{5,4},{6,5},{7,6},{8,11},{9,8},{10,9... | collective-permute-start | bytes 786440 | tf_op jit(solution)/shard_map/ppermute | solution.py:71
  132.0 1.9 collective-permute-start.10
  133.9 2.5 %collective-permute-done.12 = bf16[128,1024]{1,0:T(8,128)(2,1)S(1)} collective-permute-done((bf16[128,1024]{1,0:T(8,128)(2,1)S(1)}, bf16[128,1024]{1,0:T(8,128)(2,1)S(1)}, u32[]{:S(2)}, u32[]{:S(2)}) %collective-permute-start.12) | collective-permute-done | bytes 262176 | tf_op jit(solution)/shard_map/ppermute | solution.py:71
  136.4 3.0 %collective-permute-done.11 = bf16[128,1024]{1,0:T(8,128)(2,1)S(1)} collective-permute-done((bf16[128,1024]{1,0:T(8,128)(2,1)S(1)}, bf16[128,1024]{1,0:T(8,128)(2,1)S(1)}, u32[]{:S(2)}, u32[]{:S(2)}) %collective-permute-start.11) | collective-permute-done | bytes 262176 | tf_op jit(solution)/shard_map/ppermute | solution.py:71
  139.4 2.4 %collective-permute-done.10 = bf16[128,1024]{1,0:T(8,128)(2,1)S(1)} collective-permute-done((bf16[128,1024]{1,0:T(8,128)(2,1)S(1)}, bf16[128,1024]{1,0:T(8,128)(2,1)S(1)}, u32[]{:S(2)}, u32[]{:S(2)}) %collective-permute-start.10) | collective-permute-done | bytes 262176 | tf_op jit(solution)/shard_map/ppermute | solution.py:71
  141.9 2.1 collective-permute-start.13
  144.0 3.0 %down_half.2.rest_0_ = bf16[64,2,8,896]{3,2,1,0:T(8,128)(2,1)} custom-call(s32[2]{0:T(128)S(1)} %pad_add_fusion.where, bf16[512,1024]{1,0:T(8,128)(2,1)S(1)} %pad_maximum_fusion.rows_ref, bf16[1,1024,896]{2,1,0:T(8,128)(2,1)S(1)} %copy-done.3), custom_call_target="tpu_custom_call" | custom-call | flops 939524096 | bytes 3801088 | tf_op jit(solution)/shard_map/down_half/pallas_call | solution.py:351
  147.0 2.9 %down_half.3 = bf16[64,2,8,896]{3,2,1,0:T(8,128)(2,1)} custom-call(s32[2]{0:T(128)S(1)} %pad_add_fusion.where, bf16[512,1024]{1,0:T(8,128)(2,1)S(1)} %collective-permute-done.13.rows_ref, bf16[1,1024,896]{2,1,0:T(8,128)(2,1)S(1)} %copy-done.3, bf16[64,2,8,896]{3,2,1,0:T(8,128)(2,1)} %down_half.2.rest_0_), custom_call_target="tpu_custom_call", output_to_operand_aliasing={{}: (3, {})} | custom-call | flops 939524096 | bytes 3801088 | tf_op jit(solution)/shard_map/down_half/pallas_call | solution.py:351
  149.9 1.9 all-to-all-done.2
  151.8 0.9 copy-done.4
  152.8 10.8 %all-to-all-start.3 = ((bf16[64,2,8,896]{3,2,1,0:T(8,128)(2,1)}), bf16[64,2,8,896]{3,2,1,0:T(8,128)(2,1)S(1)}, u32[]{:S(2)}, u32[]{:S(2)}) async-start(bf16[64,2,8,896]{3,2,1,0:T(8,128)(2,1)} %down_half.3), calls=%async_computation.3 | async-start | bytes 3670016 | tf_op jit(solution)/shard_map/all_to_all | solution.py:408
  163.7 0.4 fusion.23
  164.1 0.2 fusion.10
  164.4 0.1 copy.42
  164.5 0.3 convolution_convert_fusion.1
  164.9 2.5 %collective-permute-start.16 = (bf16[2,32,640]{2,1,0:T(8,128)(2,1)S(1)}, bf16[2,32,640]{2,1,0:T(8,128)(2,1)S(1)}, u32[]{:S(2)}, u32[]{:S(2)}) collective-permute-start(bf16[2,32,640]{2,1,0:T(8,128)(2,1)S(1)} %get-tuple-element.48), channel_id=1, source_target_pairs={{0,3},{1,0},{2,1},{3,2},{4,7},{5,4},{6,5},{7,6},{8,11},{9,8},{10,9... | collective-permute-start | bytes 245768 | tf_op jit(solution)/shard_map/ppermute | solution.py:71
  167.4 3.4 %collective-permute-start.15 = (bf16[2,32,640]{2,1,0:T(8,128)(2,1)S(1)}, bf16[2,32,640]{2,1,0:T(8,128)(2,1)S(1)}, u32[]{:S(2)}, u32[]{:S(2)}) collective-permute-start(bf16[2,32,640]{2,1,0:T(8,128)(2,1)S(1)} %get-tuple-element.49), channel_id=1, source_target_pairs={{0,1},{1,2},{2,3},{3,0},{4,5},{5,6},{6,7},{7,4},{8,9},{9,10},{10,1... | collective-permute-start | bytes 245768 | tf_op jit(solution)/shard_map/ppermute | solution.py:71
  170.8 2.2 %collective-permute-start.14 = (bf16[2,32,640]{2,1,0:T(8,128)(2,1)S(1)}, bf16[2,32,640]{2,1,0:T(8,128)(2,1)S(1)}, u32[]{:S(2)}, u32[]{:S(2)}) collective-permute-start(bf16[2,32,640]{2,1,0:T(8,128)(2,1)S(1)} %get-tuple-element.50), channel_id=1, source_target_pairs={{0,2},{1,3},{2,0},{3,1},{4,6},{5,7},{6,4},{7,5},{8,10},{9,11},{10,... | collective-permute-start | bytes 245768 | tf_op jit(solution)/shard_map/ppermute | solution.py:71
  173.0 2.4 %combined.1 = f32[128,896]{1,0:T(8,128)} custom-call(bf16[128,512]{1,0:T(8,128)(2,1)} %select_convert_fusion.weights_ref, bf16[512,896]{1,0:T(8,128)(2,1)} %bitcast.52), custom_call_target="tpu_custom_call" | custom-call | flops 117440512 | bytes 1277952 | tf_op jit(solution)/shard_map/combined/pallas_call | solution.py:210
  175.4 3.2 %collective-permute-done.14 = bf16[2,32,640]{2,1,0:T(8,128)(2,1)S(1)} collective-permute-done((bf16[2,32,640]{2,1,0:T(8,128)(2,1)S(1)}, bf16[2,32,640]{2,1,0:T(8,128)(2,1)S(1)}, u32[]{:S(2)}, u32[]{:S(2)}) %collective-permute-start.14) | collective-permute-done | bytes 81952 | tf_op jit(solution)/shard_map/ppermute | solution.py:71
  178.6 0.1 slice_reduce_fusion.1
  178.7 0.3 slice_reduce_fusion
  179.1 0.1 multiply_reduce_fusion
  179.2 0.7 divide_convert_fusion
  179.9 32.1 %all-to-all-done.3 = bf16[64,2,8,896]{3,2,1,0:T(8,128)(2,1)S(1)} async-done(((bf16[64,2,8,896]{3,2,1,0:T(8,128)(2,1)}), bf16[64,2,8,896]{3,2,1,0:T(8,128)(2,1)S(1)}, u32[]{:S(2)}, u32[]{:S(2)}) %all-to-all-start.3) | async-done | bytes 1835040 | tf_op jit(solution)/shard_map/all_to_all | solution.py:408
  212.0 1.2 fusion.1
  (53 shorter events, 0.6 us)
Async XLA Ops:
  0.6 163.1 %copy-start = (bf16[2,128,576]{1,2,0:T(8,128)(2,1)S(1)}, bf16[2,128,576]{1,2,0:T(8,128)(2,1)}, u32[]{:S(2)}) copy-start(bf16[2,128,576]{1,2,0:T(8,128)(2,1)} %param.8) | copy-start | bytes 884740
  0.6 21.0 %copy-start.1 = (bf16[1,896,1024]{2,1,0:T(8,128)(2,1)S(1)}, bf16[1,896,1024]{2,1,0:T(8,128)(2,1)}, u32[]{:S(2)}) copy-start(bf16[1,896,1024]{2,1,0:T(8,128)(2,1)} %param.14) | copy-start | bytes 5505028
  3.2 43.3 %all-to-all-start = ((bf16[64,8,896]{2,1,0:T(8,128)(2,1)}), bf16[64,8,896]{2,1,0:T(8,128)(2,1)S(1)}, u32[]{:S(2)}, u32[]{:S(2)}) async-start(bf16[64,8,896]{2,1,0:T(8,128)(2,1)} %get-tuple-element.25), calls=%async_computation | async-start | bytes 1835008 | tf_op jit(solution)/shard_map/all_to_all | solution.py:408
  19.6 9.0 %collective-permute-start = (bf16[128,896]{1,0:T(8,128)(2,1)}, bf16[128,896]{1,0:T(8,128)(2,1)}, u32[]{:S(2)}, u32[]{:S(2)}) collective-permute-start(bf16[128,896]{1,0:T(8,128)(2,1)} %rows_ref.1), channel_id=1, source_target_pairs={{0,256},{256,0},{1,257},{257,1},{2,258},{258,2},{3,259},{259,3},{4... | collective-permute-start | bytes 688136 | tf_op jit(solution)/shard_map/ppermute | solution.py:71
  21.7 3.0 %copy-start.9 = (f32[128,8]{0,1:T(8,128)S(1)}, f32[128,8]{0,1:T(8,128)}, u32[]{:S(2)}) copy-start(f32[128,8]{0,1:T(8,128)} %param.13) | copy-start | bytes 12292
  21.7 3.0 %copy-start.10 = (s32[128,8]{0,1:T(8,128)S(1)}, s32[128,8]{0,1:T(8,128)}, u32[]{:S(2)}) copy-start(s32[128,8]{0,1:T(8,128)} %param.12) | copy-start | bytes 12292
  21.7 3.3 %copy-start.8 = (f32[64,128]{1,0:T(8,128)S(1)}, f32[64,128]{1,0:T(8,128)}, u32[]{:S(2)}) copy-start(f32[64,128]{1,0:T(8,128)} %get-tuple-element.22) | copy-start | bytes 98308
  46.6 54.6 %all-to-all-start.1 = ((bf16[64,8,1792]{2,1,0:T(8,128)(2,1)}), bf16[64,8,1792]{2,1,0:T(8,128)(2,1)}, u32[]{:S(2)}, u32[]{:S(2)}) async-start(bf16[64,8,1792]{2,1,0:T(8,128)(2,1)} %fusion), calls=%async_computation.1 | async-start | bytes 3670016 | tf_op jit(solution)/shard_map/all_to_all | solution.py:408
  54.3 4.3 %collective-permute-start.1 = (bf16[256,1024]{1,0:T(8,128)(2,1)S(1)}, bf16[256,1024]{1,0:T(8,128)(2,1)S(1)}, u32[]{:S(2)}, u32[]{:S(2)}) collective-permute-start(bf16[256,1024]{1,0:T(8,128)(2,1)S(1)} %their_half.1), channel_id=1, source_target_pairs={{0,256},{256,0},{1,257},{257,1},{2,258},{258,2},{3,259},{259,3},{4... | collective-permute-start | bytes 1572872 | tf_op jit(solution)/shard_map/ppermute | solution.py:71
  56.2 45.0 %collective-permute-start.6 = (bf16[896,1024]{1,0:T(8,128)(2,1)}, bf16[896,1024]{1,0:T(8,128)(2,1)}, u32[]{:S(2)}, u32[]{:S(2)}) collective-permute-start(bf16[896,1024]{1,0:T(8,128)(2,1)} %copied.1), channel_id=1, source_target_pairs={{0,256},{256,0},{1,257},{257,1},{2,258},{258,2},{3,259},{259,3},{4... | collective-permute-start | bytes 5505032 | tf_op jit(solution)/shard_map/ppermute | solution.py:71
  59.9 33.0 %copy-start.2 = (bf16[1,1024,896]{2,1,0:T(8,128)(2,1)S(1)}, bf16[1,1024,896]{2,1,0:T(8,128)(2,1)}, u32[]{:S(2)}) copy-start(bf16[1,1024,896]{2,1,0:T(8,128)(2,1)} %weight_ref.5) | copy-start | bytes 5505028
  59.9 18.4 %collective-permute-start.4 = (bf16[256,1024]{1,0:T(8,128)(2,1)S(1)}, bf16[256,1024]{1,0:T(8,128)(2,1)S(1)}, u32[]{:S(2)}, u32[]{:S(2)}) collective-permute-start(bf16[256,1024]{1,0:T(8,128)(2,1)S(1)} %get-tuple-element.29), channel_id=1, source_target_pairs={{0,2},{1,3},{2,0},{3,1},{4,6},{5,7},{6,4},{7,5},{8,10},{9,11},{10,... | collective-permute-start | bytes 1572872 | tf_op jit(solution)/shard_map/ppermute | solution.py:71
  65.0 23.5 %collective-permute-start.3 = (bf16[256,1024]{1,0:T(8,128)(2,1)S(1)}, bf16[256,1024]{1,0:T(8,128)(2,1)S(1)}, u32[]{:S(2)}, u32[]{:S(2)}) collective-permute-start(bf16[256,1024]{1,0:T(8,128)(2,1)S(1)} %get-tuple-element.29), channel_id=1, source_target_pairs={{0,1},{1,2},{2,3},{3,0},{4,5},{5,6},{6,7},{7,4},{8,9},{9,10},{10,1... | collective-permute-start | bytes 1572872 | tf_op jit(solution)/shard_map/ppermute | solution.py:71
  67.5 21.2 %collective-permute-start.2 = (bf16[256,1024]{1,0:T(8,128)(2,1)S(1)}, bf16[256,1024]{1,0:T(8,128)(2,1)S(1)}, u32[]{:S(2)}, u32[]{:S(2)}) collective-permute-start(bf16[256,1024]{1,0:T(8,128)(2,1)S(1)} %get-tuple-element.29), channel_id=1, source_target_pairs={{0,3},{1,0},{2,1},{3,2},{4,7},{5,4},{6,5},{7,6},{8,11},{9,8},{10,9... | collective-permute-start | bytes 1572872 | tf_op jit(solution)/shard_map/ppermute | solution.py:71
  89.1 3.8 %collective-permute-start.5 = (bf16[256,1024]{1,0:T(8,128)(2,1)S(1)}, bf16[256,1024]{1,0:T(8,128)(2,1)S(1)}, u32[]{:S(2)}, u32[]{:S(2)}) collective-permute-start(bf16[256,1024]{1,0:T(8,128)(2,1)S(1)} %multiply_convert_fusion.mine_ref), channel_id=1, source_target_pairs={{0,256},{256,0},{1,257},{257,1},{2,258},{258,2},{3,259},{259,3},{4... | collective-permute-start | bytes 1572872 | tf_op jit(solution)/shard_map/ppermute | solution.py:71
  106.3 19.4 %collective-permute-start.9 = (bf16[128,1024]{1,0:T(8,128)(2,1)}, bf16[128,1024]{1,0:T(8,128)(2,1)S(1)}, u32[]{:S(2)}, u32[]{:S(2)}) collective-permute-start(bf16[128,1024]{1,0:T(8,128)(2,1)} %get-tuple-element.35), channel_id=1, source_target_pairs={{0,2},{1,3},{2,0},{3,1},{4,6},{5,7},{6,4},{7,5},{8,10},{9,11},{10,... | collective-permute-start | bytes 786440 | tf_op jit(solution)/shard_map/ppermute | solution.py:71
  111.2 14.5 %collective-permute-start.8 = (bf16[128,1024]{1,0:T(8,128)(2,1)S(1)}, bf16[128,1024]{1,0:T(8,128)(2,1)S(1)}, u32[]{:S(2)}, u32[]{:S(2)}) collective-permute-start(bf16[128,1024]{1,0:T(8,128)(2,1)S(1)} %get-tuple-element.34), channel_id=1, source_target_pairs={{0,1},{1,2},{2,3},{3,0},{4,5},{5,6},{6,7},{7,4},{8,9},{9,10},{10,1... | collective-permute-start | bytes 786440 | tf_op jit(solution)/shard_map/ppermute | solution.py:71
  113.7 12.0 %collective-permute-start.7 = (bf16[128,1024]{1,0:T(8,128)(2,1)S(1)}, bf16[128,1024]{1,0:T(8,128)(2,1)S(1)}, u32[]{:S(2)}, u32[]{:S(2)}) collective-permute-start(bf16[128,1024]{1,0:T(8,128)(2,1)S(1)} %get-tuple-element.33), channel_id=1, source_target_pairs={{0,3},{1,0},{2,1},{3,2},{4,7},{5,4},{6,5},{7,6},{8,11},{9,8},{10,9... | collective-permute-start | bytes 786440 | tf_op jit(solution)/shard_map/ppermute | solution.py:71
  118.3 33.6 %all-to-all-start.2 = ((bf16[64,8,896]{2,1,0:T(8,128)(2,1)}), bf16[64,8,896]{2,1,0:T(8,128)(2,1)S(1)}, u32[]{:S(2)}, u32[]{:S(2)}) async-start(bf16[64,8,896]{2,1,0:T(8,128)(2,1)} %bitcast.13), calls=%async_computation.2 | async-start | bytes 1835008 | tf_op jit(solution)/shard_map/all_to_all | solution.py:408
  125.7 18.3 %copy-start.3 = (bf16[1,1024,896]{2,1,0:T(8,128)(2,1)S(1)}, bf16[1,1024,896]{2,1,0:T(8,128)(2,1)}, u32[]{:S(2)}) copy-start(bf16[1,1024,896]{2,1,0:T(8,128)(2,1)} %weight_ref.5) | copy-start | bytes 5505028
  126.0 10.5 %collective-permute-start.12 = (bf16[128,1024]{1,0:T(8,128)(2,1)S(1)}, bf16[128,1024]{1,0:T(8,128)(2,1)S(1)}, u32[]{:S(2)}, u32[]{:S(2)}) collective-permute-start(bf16[128,1024]{1,0:T(8,128)(2,1)S(1)} %multiply_convert_fusion.1), channel_id=1, source_target_pairs={{0,2},{1,3},{2,0},{3,1},{4,6},{5,7},{6,4},{7,5},{8,10},{9,11},{10,... | collective-permute-start | bytes 786440 | tf_op jit(solution)/shard_map/ppermute | solution.py:71
  128.0 11.4 %collective-permute-start.11 = (bf16[128,1024]{1,0:T(8,128)(2,1)S(1)}, bf16[128,1024]{1,0:T(8,128)(2,1)S(1)}, u32[]{:S(2)}, u32[]{:S(2)}) collective-permute-start(bf16[128,1024]{1,0:T(8,128)(2,1)S(1)} %multiply_convert_fusion.1), channel_id=1, source_target_pairs={{0,3},{1,0},{2,1},{3,2},{4,7},{5,4},{6,5},{7,6},{8,11},{9,8},{10,9... | collective-permute-start | bytes 786440 | tf_op jit(solution)/shard_map/ppermute | solution.py:71
  132.0 9.8 %collective-permute-start.10 = (bf16[128,1024]{1,0:T(8,128)(2,1)S(1)}, bf16[128,1024]{1,0:T(8,128)(2,1)S(1)}, u32[]{:S(2)}, u32[]{:S(2)}) collective-permute-start(bf16[128,1024]{1,0:T(8,128)(2,1)S(1)} %multiply_convert_fusion.1), channel_id=1, source_target_pairs={{0,1},{1,2},{2,3},{3,0},{4,5},{5,6},{6,7},{7,4},{8,9},{9,10},{10,1... | collective-permute-start | bytes 786440 | tf_op jit(solution)/shard_map/ppermute | solution.py:71
  141.9 5.1 %collective-permute-start.13 = (bf16[512,1024]{1,0:T(8,128)(2,1)S(1)}, bf16[512,1024]{1,0:T(8,128)(2,1)S(1)}, u32[]{:S(2)}, u32[]{:S(2)}) collective-permute-start(bf16[512,1024]{1,0:T(8,128)(2,1)S(1)} %pad_maximum_fusion.rows_ref), channel_id=1, source_target_pairs={{0,256},{256,0},{1,257},{257,1},{2,258},{258,2},{3,259},{259,3},{4... | collective-permute-start | bytes 3145736 | tf_op jit(solution)/shard_map/ppermute | solution.py:71
  149.9 13.7 %copy-start.11 = (s32[2]{0:T(128)S(1)}, s32[2]{0:T(128)}, u32[]{:S(2)}) copy-start(s32[2]{0:T(128)} %param.10) | copy-start | bytes 28
  149.9 13.8 %copy-start.5 = (bf16[2,256,576]{1,2,0:T(8,128)(2,1)S(1)}, bf16[2,256,576]{1,2,0:T(8,128)(2,1)}, u32[]{:S(2)}) copy-start(bf16[2,256,576]{1,2,0:T(8,128)(2,1)} %param.9) | copy-start | bytes 1769476
  151.8 0.9 copy-start.4
  152.8 59.2 %all-to-all-start.3 = ((bf16[64,2,8,896]{3,2,1,0:T(8,128)(2,1)}), bf16[64,2,8,896]{3,2,1,0:T(8,128)(2,1)S(1)}, u32[]{:S(2)}, u32[]{:S(2)}) async-start(bf16[64,2,8,896]{3,2,1,0:T(8,128)(2,1)} %down_half.3), calls=%async_computation.3 | async-start | bytes 3670016 | tf_op jit(solution)/shard_map/all_to_all | solution.py:408
  164.9 10.5 %collective-permute-start.16 = (bf16[2,32,640]{2,1,0:T(8,128)(2,1)S(1)}, bf16[2,32,640]{2,1,0:T(8,128)(2,1)S(1)}, u32[]{:S(2)}, u32[]{:S(2)}) collective-permute-start(bf16[2,32,640]{2,1,0:T(8,128)(2,1)S(1)} %get-tuple-element.48), channel_id=1, source_target_pairs={{0,3},{1,0},{2,1},{3,2},{4,7},{5,4},{6,5},{7,6},{8,11},{9,8},{10,9... | collective-permute-start | bytes 245768 | tf_op jit(solution)/shard_map/ppermute | solution.py:71
  167.4 8.0 %collective-permute-start.15 = (bf16[2,32,640]{2,1,0:T(8,128)(2,1)S(1)}, bf16[2,32,640]{2,1,0:T(8,128)(2,1)S(1)}, u32[]{:S(2)}, u32[]{:S(2)}) collective-permute-start(bf16[2,32,640]{2,1,0:T(8,128)(2,1)S(1)} %get-tuple-element.49), channel_id=1, source_target_pairs={{0,1},{1,2},{2,3},{3,0},{4,5},{5,6},{6,7},{7,4},{8,9},{9,10},{10,1... | collective-permute-start | bytes 245768 | tf_op jit(solution)/shard_map/ppermute | solution.py:71
  170.8 7.8 %collective-permute-start.14 = (bf16[2,32,640]{2,1,0:T(8,128)(2,1)S(1)}, bf16[2,32,640]{2,1,0:T(8,128)(2,1)S(1)}, u32[]{:S(2)}, u32[]{:S(2)}) collective-permute-start(bf16[2,32,640]{2,1,0:T(8,128)(2,1)S(1)} %get-tuple-element.50), channel_id=1, source_target_pairs={{0,2},{1,3},{2,0},{3,1},{4,6},{5,7},{6,4},{7,5},{8,10},{9,11},{10,... | collective-permute-start | bytes 245768 | tf_op jit(solution)/shard_map/ppermute | solution.py:71
  173.0 39.0 %copy-start.7 = (bf16[128,1024]{0,1:T(8,128)(2,1)S(1)}, bf16[128,1024]{0,1:T(8,128)(2,1)}, u32[]{:S(2)}) copy-start(bf16[128,1024]{0,1:T(8,128)(2,1)} %fusion.4) | copy-start | bytes 786436
  175.4 36.6 %copy-start.6 = (f32[128,896]{1,0:T(8,128)S(1)}, f32[128,896]{1,0:T(8,128)}, u32[]{:S(2)}) copy-start(f32[128,896]{1,0:T(8,128)} %combined.1) | copy-start | bytes 1376260
